TPU v7x, 32 devices: a whole 2x2x4 slice. The times are simulated.
32 devices in a mesh: copies: 2 (over y), tile: 4 (over z), sub: 4 (over x, core), lev: 1.
Axes of the slice: x: 2, y: 2, z: 4, core: 2. Of those that a mesh axis runs over, the one named last changes fastest.
Arguments:
- water_heat_state: float32 [4, 512, 512], P('lev', ('copies', 'tile'), 'sub'), parts along dimension 1, may hold values from -6 to 6
- diffusion_coefficient: float32 [256, 512], P('tile', 'sub'), may hold values from 0.004 to 0.03
- upper_current_vector: float32 [2, 512, 512], P(None, ('copies', 'tile'), 'sub'), parts along dimension 1, may hold values from -4 to 4
- remap_blocks: int32 [16, 4], P(('tile', 'sub', 'lev')), may hold values from 0 to 15, as said below
- remap_rows: bfloat16 [16, 4, 128, 64], P(('tile', 'sub', 'lev')), may hold values from -0.75 to 0.75
- remap_cols: bfloat16 [16, 4, 128, 128], P(('tile', 'sub', 'lev')), may hold values from -0.5 to 0.5
- neighbors: int32 [1, 16, 4], P(None, ('tile', 'sub', 'lev')), may hold values from -1 to 15, as said below
- thickness: float32 [1, 32, 5, 16384], P(None, ('copies', 'tile', 'sub', 'lev')), parts along dimension 1, may hold values from 0.5 to 6
- concentration: float32 [1, 32, 5, 16384], P(None, ('copies', 'tile', 'sub', 'lev')), parts along dimension 1, may hold values from 0.18 to 0.2
- ice_velocity: float32 [1, 32, 2, 16384], P(None, ('copies', 'tile', 'sub', 'lev')), parts along dimension 1, may hold values from -3 to 3
- wind_stress: float32 [1, 32, 2, 16384], P(None, ('copies', 'tile', 'sub', 'lev')), parts along dimension 1, may hold values from -6 to 6
Outputs:
- updated_heat_state: float32 [4, 512, 512], P('lev', ('copies', 'tile'), 'sub'), parts along dimension 1
- current_out: float32 [2, 512, 512], P(None, ('copies', 'tile'), 'sub'), parts along dimension 1
- velocity_out: float32 [1, 32, 2, 16384], P(None, ('copies', 'tile', 'sub', 'lev')), parts along dimension 1
There are 2 independent parts, one for each index of `copies`. A program takes and returns all parts, laid end to end along the dimension named above; an argument that names none is the same for every part. Nothing has to cross between parts.
Inputs may be any that keep to these rules, and one draw needn't show every extreme that they name: `remap_blocks`: every ice block is named by exactly four pairs over all devices. The block n lives on device n mod 16; the pairs of device e name only blocks living on devices with the same position along `tile` as e (e // 4); the pairs of one device name at most 1 block living on any one device, and this is reached. `neighbors`: -1 marks a coast. Links are mutual: if b is the north (east) neighbour of a, then a is the south (west) neighbour of b. For each direction, the blocks of one device have their neighbours on distinct devices.
All inputs are finite; a program needn't handle non-finite values.
Results may differ from a plain program's by a relative error of at most 0.0044.
Values may be sent and summed in bfloat16 or wider, within the bound.
No kernel may reach another device: no remote copies, remote signals or barrier semaphores. Data moves between devices by JAX's collectives and lax.ppermute only.
A program may use at most 64 MiB of HBM per device.

v0:
```python
import jax
import jax.numpy as jnp
from jax import lax
from jax.sharding import PartitionSpec as P

SUBCYCLES = 4


STRENGTH_DECAY = 5.0
VISCOUS_STEP = 0.24
SUBCYCLE_STEP = 0.5
CORIOLIS_TURN = 0.1
BASE_MASS = 0.5
HEAT_RATE = 0.2
THIN_ICE = 0.1
THERMAL_DIFFUSE = 0.5
STRESS_MIXING = 0.5
OPPOSITE = (1, 0, 3, 2)


def extended(value, sides, width):
    for axis, dim in sides:
        size, length = (lax.axis_size(axis), value.shape[dim])
        up = [(i, (i + 1) % size) for i in range(size - 1)]
        down = [(j, i) for i, j in up]
        last = lax.slice_in_dim(value, length - width, length, axis=dim)
        leading = lax.slice_in_dim(value, 0, width, axis=dim)
        before = lax.ppermute(last, axis, up)
        after = lax.ppermute(leading, axis, down)
        value = jnp.concatenate([before, value, after], axis=dim)
    return value


def second_derivative(padded):
    return (
        padded[..., 2:, 1:-1]
        + padded[..., :-2, 1:-1]
        + padded[..., 1:-1, 2:]
        + padded[..., 1:-1, :-2]
        - 4.0 * padded[..., 1:-1, 1:-1]
    )


def block_edges(velocity):
    return jnp.stack(
        [velocity[:, :, -1, :], velocity[:, :, 0, :], velocity[:, :, :, -1], velocity[:, :, :, 0]],
        axis=1,
    )


def with_halo(velocity, rim_halos):
    padded = jnp.pad(velocity, ((0, 0), (0, 0), (1, 1), (1, 1)))
    padded = padded.at[:, :, -1, 1:-1].set(rim_halos[:, 0])
    padded = padded.at[:, :, 0, 1:-1].set(rim_halos[:, 1])
    padded = padded.at[:, :, 1:-1, -1].set(rim_halos[:, 2])
    padded = padded.at[:, :, 1:-1, 0].set(rim_halos[:, 3])
    return padded


def ice_coefficients(thickness, concentration):
    total_cover = jnp.sum(concentration, axis=1)
    volume = jnp.sum(concentration * thickness, axis=1)
    ice_mass = volume + BASE_MASS
    strength = volume * jnp.exp(-STRENGTH_DECAY * (1.0 - total_cover))
    conduct = jnp.sum(concentration / (thickness + THIN_ICE), axis=1)
    return (VISCOUS_STEP * strength / ice_mass, SUBCYCLE_STEP / ice_mass, total_cover, conduct)


def subcycle(velocity, rim_halos, viscous, step_mass, drag_rate, wind_force, current_ice):
    spread = second_derivative(with_halo(velocity, rim_halos))
    pushed = (
        velocity
        + viscous[:, None] * spread
        + step_mass[:, None] * (wind_force + drag_rate[:, None] * current_ice)
    )
    turned = jnp.stack(
        [
            pushed[:, 0] + CORIOLIS_TURN * velocity[:, 1],
            pushed[:, 1] - CORIOLIS_TURN * velocity[:, 0],
        ],
        axis=1,
    )
    return turned / (1.0 + step_mass * drag_rate)[:, None]


def ice_fluxes(velocity, conduct, drag_rate, forcing):
    heat_flux = -HEAT_RATE * conduct * forcing[:, 0]
    stress = drag_rate[:, None] * (velocity - forcing[:, 1:])
    return jnp.concatenate([heat_flux[:, None], stress], axis=1)


def shards(
    water_heat_state,
    diffusion_coefficient,
    upper_current_vector,
    remap_blocks,
    remap_rows,
    remap_cols,
    neighbors,
    thickness,
    concentration,
    ice_velocity,
    wind_stress,
):
    tile_count = lax.axis_size("tile")
    group_count = lax.axis_size("sub") * lax.axis_size("lev")
    device_count = tile_count * group_count
    vertical_total = water_heat_state.shape[0] * lax.axis_size("lev")
    bordered_heat_state = extended(water_heat_state, (("tile", 1), ("sub", 2)), 2)
    diffused_warmth = water_heat_state - diffusion_coefficient * second_derivative(
        second_derivative(bordered_heat_state)
    )
    topmost_warmth = lax.psum(jnp.sum(diffused_warmth, axis=0), "lev") / vertical_total
    topmost_slab = jnp.concatenate([topmost_warmth[None], upper_current_vector], axis=0).astype(
        jnp.bfloat16
    )
    row_weights = remap_rows[0]
    col_weights = remap_cols[0]
    target_blocks = remap_blocks[0]
    pair_count = target_blocks.shape[0]
    block_side = row_weights.shape[1]
    item_width = 3 * block_side * block_side
    capacity = (pair_count + group_count - 1) // group_count
    partial_rows = jnp.einsum(
        "mbx,fxy->mfby", row_weights, topmost_slab, preferred_element_type=jnp.float32
    ).astype(jnp.bfloat16)
    pieces = (
        jnp.einsum("mfby,mcy->mfbc", partial_rows, col_weights, preferred_element_type=jnp.float32)
        .astype(jnp.bfloat16)
        .reshape(pair_count, item_width)
    )
    owner_member = target_blocks % device_count % group_count
    owner_slot = target_blocks // device_count
    pair_order = jnp.arange(pair_count)
    slot_rank = jnp.sum(
        (owner_member[None, :] == owner_member[:, None])
        & (pair_order[None, :] < pair_order[:, None]),
        axis=1,
    )
    outgoing = (
        jnp.zeros((group_count, capacity, item_width), jnp.bfloat16)
        .at[owner_member, slot_rank]
        .set(pieces)
    )
    labels = (
        jnp.full((group_count, capacity), -1, jnp.int32).at[owner_member, slot_rank].set(owner_slot)
    )
    incoming, in_labels = (
        lax.all_to_all(outgoing, ("sub", "lev"), split_axis=0, concat_axis=0, tiled=True),
        lax.all_to_all(labels, ("sub", "lev"), split_axis=0, concat_axis=0, tiled=True),
    )
    incoming = incoming.reshape(group_count * capacity, item_width)
    block_count = thickness.shape[0]
    selector = (in_labels.reshape(1, -1) == jnp.arange(block_count)[:, None]).astype(jnp.bfloat16)
    forcing = jnp.dot(selector, incoming, preferred_element_type=jnp.float32).reshape(
        block_count, 3, block_side, block_side
    )
    category_count = thickness.shape[2]
    thick_blocks = thickness[:, 0].reshape(block_count, category_count, block_side, block_side)
    cover_blocks = concentration[:, 0].reshape(block_count, category_count, block_side, block_side)
    velocity = ice_velocity[:, 0].reshape(block_count, 2, block_side, block_side)
    wind_force = wind_stress[:, 0].reshape(block_count, 2, block_side, block_side)
    neighbor_ids = neighbors[:, 0, :]
    linked = neighbor_ids >= 0
    mask_edges = linked.astype(jnp.float32)[:, :, None, None]
    opposite = jnp.array(OPPOSITE, jnp.int32)[None, :]
    source_dev = jnp.where(linked, neighbor_ids % device_count, 0)
    source_slot = jnp.where(linked, neighbor_ids // device_count, 0)
    viscous, step_mass, drag_rate, conduct = ice_coefficients(thick_blocks, cover_blocks)
    current_ice = forcing[:, 1:]
    for subcycle_index in range(SUBCYCLES):
        rim_edges = block_edges(velocity)
        everything = lax.all_gather(
            rim_edges.reshape(block_count, 8 * block_side),
            ("tile", "sub", "lev"),
            axis=0,
            tiled=True,
        )
        rim_halos = everything.reshape(device_count * block_count * 4, 2, block_side)[
            (source_dev * block_count + source_slot) * 4 + opposite
        ]
        velocity = subcycle(
            velocity, rim_halos * mask_edges, viscous, step_mass, drag_rate, wind_force, current_ice
        )
    fluxes = (
        ice_fluxes(velocity, conduct, drag_rate, forcing)
        .astype(jnp.bfloat16)
        .reshape(block_count, item_width)
    )
    replies = jnp.dot(selector.T, fluxes, preferred_element_type=jnp.float32).astype(jnp.bfloat16)
    returned = lax.all_to_all(
        replies.reshape(group_count, capacity, item_width),
        ("sub", "lev"),
        split_axis=0,
        concat_axis=0,
        tiled=True,
    )
    answers = returned.reshape(group_count * capacity, item_width)[
        owner_member * capacity + slot_rank
    ]
    answers = answers.reshape(pair_count, 3, block_side, block_side)
    partial_cols = jnp.einsum(
        "mbx,mfbc->mfxc", row_weights, answers, preferred_element_type=jnp.float32
    ).astype(jnp.bfloat16)
    exchange_parts = jnp.einsum(
        "mfxc,mcy->fxy", partial_cols, col_weights, preferred_element_type=jnp.float32
    )
    exchange_parts = lax.psum(exchange_parts, "lev")
    updated_heat_state = diffused_warmth + THERMAL_DIFFUSE * exchange_parts[0]
    current_out = upper_current_vector + STRESS_MIXING * exchange_parts[1:]
    return (
        updated_heat_state,
        current_out,
        velocity.reshape(block_count, 1, 2, block_side * block_side),
    )


def solution(mesh):
    return jax.shard_map(
        shards,
        mesh=mesh,
        in_specs=(
            P("lev", ("copies", "tile"), "sub"),
            P("tile", "sub"),
            P(None, ("copies", "tile"), "sub"),
            P(("tile", "sub", "lev"), None),
            P(("tile", "sub", "lev"), None, None, None),
            P(("tile", "sub", "lev"), None, None, None),
            P(None, ("tile", "sub", "lev"), None),
            P(None, ("copies", "tile", "sub", "lev"), None, None),
            P(None, ("copies", "tile", "sub", "lev"), None, None),
            P(None, ("copies", "tile", "sub", "lev"), None, None),
            P(None, ("copies", "tile", "sub", "lev"), None, None),
        ),
        out_specs=(
            P("lev", ("copies", "tile"), "sub"),
            P(None, ("copies", "tile"), "sub"),
            P(None, ("copies", "tile", "sub", "lev"), None, None),
        ),
        check_vma=False,
    )
```

profile of v0, /device:TPU:0, one launch (start us, length us, event | category | flops | bytes accessed | tf_op | source)
XLA Modules:
  0.0 156.9 jit_solution(6172388742929699705)
XLA Ops:
  0.6 0.8 fusion.91
  1.4 5.0 %collective-permute-start = (f32[4,2,128]{2,1,0:T(2,128)S(1)}, f32[4,2,128]{2,1,0:T(2,128)S(1)}, u32[]{:S(2)}, u32[]{:S(2)}) collective-permute-start(f32[4,2,128]{2,1,0:T(2,128)S(1)} %get-tuple-element.234), channel_id=1, source_target_pairs={{0,4},{4,8},{8,12},{1,5},{5,9},{9,13},{2,6},{6,10},{10,14},{3,7},{... | collective-permute-start | bytes 12296 | tf_op jit(solution)/shard_map/ppermute | solution.py:28
  6.5 1.3 collective-permute-start.1
  8.0 0.6 scatter_custom_fusion
  8.7 0.7 copy.190
  9.3 3.2 %all-to-all-start = ((s32[4,1,1]{2,1,0:T(1,128)}), s32[4,1,1]{2,1,0:T(1,128)S(1)}, u32[]{:S(2)}, u32[]{:S(2)}) async-start(s32[4,1,1]{2,1,0:T(1,128)} %copy.190), calls=%async_computation | async-start | bytes 4096 | tf_op jit(solution)/shard_map/all_to_all | solution.py:150
  12.6 1.0 copy.250
  13.6 0.2 slice_reduce_fusion.7
  13.8 23.3 %all-gather = f32[16,1,1024]{2,1,0:T(1,128)S(1)} all-gather(f32[1,1,1024]{2,1,0:T(1,128)S(1)} %bitcast.277), channel_id=1, replica_groups=mesh['copies'=2,'tile'=4,'sub'=4,'lev'=1] {'tile','sub','lev'}, dimensions={0}, use_global_device_ids=true | all-gather | bytes 69632 | tf_op jit(solution)/shard_map/all_gather | solution.py:173
  37.2 0.6 gather_fusion
  37.8 1.2 fusion.10
  39.1 0.6 fusion.92
  39.7 0.3 copy-done.1
  40.1 2.3 %collective-permute-start.2 = (f32[4,68,2]{2,1,0:T(8,128)S(1)}, f32[4,68,2]{2,1,0:T(8,128)S(1)}, u32[]{:S(2)}, u32[]{:S(2)}) collective-permute-start(f32[4,68,2]{2,1,0:T(8,128)S(1)} %get-tuple-element.220), channel_id=1, source_target_pairs={{0,1},{1,2},{2,3},{4,5},{5,6},{6,7},{8,9},{9,10},{10,11},{12,13},{... | collective-permute-start | bytes 6536 | tf_op jit(solution)/shard_map/ppermute | solution.py:28
  42.3 1.3 collective-permute-start.3
  44.0 0.7 copy-done.5
  44.8 0.5 scatter.70
  45.3 1.8 %scatter.71 = f32[1,2,130,130]{3,2,1,0:T(8,128)S(1)} dynamic-update-slice(f32[1,2,130,130]{3,2,1,0:T(8,128)S(1)} %scatter.70, f32[1,2,1,128]{3,2,1,0:T(1,128)S(1)} %bitcast.289, s32[]{:T(128)} %constant.453.clone.1, s32[]{:T(128)} %constant.453.clone.1, s32[]{:T(128)} %bitcast.37, s32[]{:T(128)} %bitcast.38) | dynamic-update-slice | bytes 2052 | tf_op jit(solution)/shard_map/scatter | solution.py:54
  47.0 1.0 scatter.74
  48.1 0.6 scatter.75
  48.9 0.4 fusion.11
  49.3 0.4 copy-done.8
  49.9 0.6 copy-done.6
  50.5 0.5 convolution_convert_fusion
  51.0 1.9 %scatter_custom_fusion.1 = bf16[4,49152]{1,0:T(4,128)(2,1)S(1)} fusion(s32[4]{0:T(128)S(1)} %fusion.77, bf16[1,4,384,128]{3,2,1,0:T(8,128)(2,1)S(1)} %bitcast.259, bf16[]{:T(256)} %constant.462.clone.1), kind=kCustom, calls=%fused_computation.16 | custom fusion | bytes 786434 | tf_op jit(solution)/shard_map/scatter | solution.py:143
  53.0 0.6 broadcast.767
  53.5 1.1 reduce.57
  54.7 1.2 reshape.1402
  55.8 3.5 %all-to-all-start.1 = ((bf16[4,2,24576]{2,1,0:T(2,128)(2,1)}), bf16[4,2,24576]{2,1,0:T(2,128)(2,1)S(1)}, u32[]{:S(2)}, u32[]{:S(2)}) async-start(bf16[4,2,24576]{2,1,0:T(2,128)(2,1)} %reshape.1402), calls=%async_computation.1 | async-start | bytes 786432 | tf_op jit(solution)/shard_map/all_to_all | solution.py:149
  59.6 7.2 %all-to-all-done.1 = bf16[4,2,24576]{2,1,0:T(2,128)(2,1)S(1)} async-done(((bf16[4,2,24576]{2,1,0:T(2,128)(2,1)}), bf16[4,2,24576]{2,1,0:T(2,128)(2,1)S(1)}, u32[]{:S(2)}, u32[]{:S(2)}) %all-to-all-start.1) | async-done | bytes 393248 | tf_op jit(solution)/shard_map/all_to_all | solution.py:149
  66.8 0.4 reshape.1403
  67.2 0.5 copy.225
  67.8 0.4 fusion.65
  68.1 0.5 copy-done.2
  69.4 17.5 %all-gather.1 = f32[16,1,1024]{2,1,0:T(1,128)S(1)} all-gather(f32[1,1,1024]{2,1,0:T(1,128)S(1)} %bitcast.278), channel_id=1, replica_groups=mesh['copies'=2,'tile'=4,'sub'=4,'lev'=1] {'tile','sub','lev'}, dimensions={0}, use_global_device_ids=true | all-gather | bytes 69632 | tf_op jit(solution)/shard_map/all_gather | solution.py:173
  86.8 0.6 gather_fusion.1
  87.8 0.5 scatter.76
  88.2 1.8 %scatter.79 = f32[1,2,130,130]{3,2,1,0:T(8,128)S(1)} dynamic-update-slice(f32[1,2,130,130]{3,2,1,0:T(8,128)S(1)} %scatter.76, f32[1,2,1,128]{3,2,1,0:T(1,128)S(1)} %bitcast.292, s32[]{:T(128)} %constant.453.clone.1, s32[]{:T(128)} %constant.453.clone.1, s32[]{:T(128)} %bitcast.37, s32[]{:T(128)} %bitcast.38) | dynamic-update-slice | bytes 2052 | tf_op jit(solution)/shard_map/scatter | solution.py:54
  90.0 1.0 scatter.80
  91.0 0.6 scatter.81
  92.3 19.3 %all-gather.2 = f32[16,1,1024]{2,1,0:T(1,128)S(1)} all-gather(f32[1,1,1024]{2,1,0:T(1,128)S(1)} %bitcast.279), channel_id=1, replica_groups=mesh['copies'=2,'tile'=4,'sub'=4,'lev'=1] {'tile','sub','lev'}, dimensions={0}, use_global_device_ids=true | all-gather | bytes 69632 | tf_op jit(solution)/shard_map/all_gather | solution.py:173
  111.6 0.6 gather_fusion.2
  112.5 0.5 scatter.84
  113.0 1.8 %scatter.85 = f32[1,2,130,130]{3,2,1,0:T(8,128)S(1)} dynamic-update-slice(f32[1,2,130,130]{3,2,1,0:T(8,128)S(1)} %scatter.84, f32[1,2,1,128]{3,2,1,0:T(1,128)S(1)} %bitcast.293, s32[]{:T(128)} %constant.453.clone.1, s32[]{:T(128)} %constant.453.clone.1, s32[]{:T(128)} %bitcast.37, s32[]{:T(128)} %bitcast.38) | dynamic-update-slice | bytes 2052 | tf_op jit(solution)/shard_map/scatter | solution.py:54
  114.8 1.0 scatter.86
  115.8 0.6 scatter.89
  116.7 0.2 slice_reduce_fusion.1
  117.1 17.6 %all-gather.3 = f32[16,1,1024]{2,1,0:T(1,128)S(1)} all-gather(f32[1,1,1024]{2,1,0:T(1,128)S(1)} %bitcast.280), channel_id=1, replica_groups=mesh['copies'=2,'tile'=4,'sub'=4,'lev'=1] {'tile','sub','lev'}, dimensions={0}, use_global_device_ids=true | all-gather | bytes 69632 | tf_op jit(solution)/shard_map/all_gather | solution.py:173
  134.7 0.6 gather_fusion.3
  135.6 0.5 scatter.108
  136.1 1.8 %scatter.109 = f32[1,2,130,130]{3,2,1,0:T(8,128)S(1)} dynamic-update-slice(f32[1,2,130,130]{3,2,1,0:T(8,128)S(1)} %scatter.108, f32[1,2,1,128]{3,2,1,0:T(1,128)S(1)} %bitcast.291, s32[]{:T(128)} %constant.453.clone.1, s32[]{:T(128)} %constant.453.clone.1, s32[]{:T(128)} %bitcast.37, s32[]{:T(128)} %bitcast.38) | dynamic-update-slice | bytes 2052 | tf_op jit(solution)/shard_map/scatter | solution.py:54
  137.9 1.0 scatter.110
  138.9 0.6 scatter.111
  140.1 1.1 reduce.58
  141.2 1.2 reshape.1404
  142.4 3.5 %all-to-all-start.2 = ((bf16[4,2,24576]{2,1,0:T(2,128)(2,1)}), bf16[4,2,24576]{2,1,0:T(2,128)(2,1)S(1)}, u32[]{:S(2)}, u32[]{:S(2)}) async-start(bf16[4,2,24576]{2,1,0:T(2,128)(2,1)} %reshape.1404), calls=%async_computation.2 | async-start | bytes 786432 | tf_op jit(solution)/shard_map/all_to_all | solution.py:191
  145.8 0.8 maximum_divide_fusion.4
  146.6 6.6 %all-to-all-done.2 = bf16[4,2,24576]{2,1,0:T(2,128)(2,1)S(1)} async-done(((bf16[4,2,24576]{2,1,0:T(2,128)(2,1)}), bf16[4,2,24576]{2,1,0:T(2,128)(2,1)S(1)}, u32[]{:S(2)}, u32[]{:S(2)}) %all-to-all-start.2) | async-done | bytes 393248 | tf_op jit(solution)/shard_map/all_to_all | solution.py:191
  153.2 0.4 reshape.1405
  153.6 0.5 copy.249
  154.2 0.9 gather_fusion.4
  155.2 0.4 fusion.3
  155.5 0.6 fusion.41
  156.2 0.7 broadcast_add_fusion
  (92 shorter events, 4.9 us)
Async XLA Ops:
  0.6 49.3 %copy-start = (bf16[1,4,128,128]{3,2,1,0:T(8,128)(2,1)S(1)}, bf16[1,4,128,128]{3,2,1,0:T(8,128)(2,1)}, u32[]{:S(2)}) copy-start(bf16[1,4,128,128]{3,2,1,0:T(8,128)(2,1)} %param.49) | copy-start | bytes 393220
  1.4 6.4 %copy-start.9 = (s32[1,4]{1,0:T(1,128)S(1)}, s32[1,4]{1,0:T(1,128)}, u32[]{:S(2)}) copy-start(s32[1,4]{1,0:T(1,128)} %param.47) | copy-start | bytes 52
  1.4 38.3 %collective-permute-start = (f32[4,2,128]{2,1,0:T(2,128)S(1)}, f32[4,2,128]{2,1,0:T(2,128)S(1)}, u32[]{:S(2)}, u32[]{:S(2)}) collective-permute-start(f32[4,2,128]{2,1,0:T(2,128)S(1)} %get-tuple-element.234), channel_id=1, source_target_pairs={{0,4},{4,8},{8,12},{1,5},{5,9},{9,13},{2,6},{6,10},{10,14},{3,7},{... | collective-permute-start | bytes 12296 | tf_op jit(solution)/shard_map/ppermute | solution.py:28
  6.5 33.2 %collective-permute-start.1 = (f32[4,2,128]{2,1,0:T(2,128)S(1)}, f32[4,2,128]{2,1,0:T(2,128)S(1)}, u32[]{:S(2)}, u32[]{:S(2)}) collective-permute-start(f32[4,2,128]{2,1,0:T(2,128)S(1)} %get-tuple-element.235), channel_id=1, source_target_pairs={{4,0},{8,4},{12,8},{5,1},{9,5},{13,9},{6,2},{10,6},{14,10},{7,3},{... | collective-permute-start | bytes 12296 | tf_op jit(solution)/shard_map/ppermute | solution.py:29
  8.6 28.5 %copy-start.10 = (s32[1,1,4]{2,1,0:T(1,128)S(1)}, s32[1,1,4]{2,1,0:T(1,128)}, u32[]{:S(2)}) copy-start(s32[1,1,4]{2,1,0:T(1,128)} %param.50) | copy-start | bytes 52
  8.7 28.5 %copy-start.11 = (s32[4]{0:T(128)S(1)}, s32[4]{0:T(128)}, u32[]{:S(2)}) copy-start(s32[4]{0:T(128)} %constant.470.clone) | copy-start | bytes 52
  9.3 46.5 %all-to-all-start = ((s32[4,1,1]{2,1,0:T(1,128)}), s32[4,1,1]{2,1,0:T(1,128)S(1)}, u32[]{:S(2)}, u32[]{:S(2)}) async-start(s32[4,1,1]{2,1,0:T(1,128)} %copy.190), calls=%async_computation | async-start | bytes 4096 | tf_op jit(solution)/shard_map/all_to_all | solution.py:150
  12.6 25.3 %copy-start.3 = (f32[1,1,5,16384]{3,1,2,0:T(1,128)S(1)}, f32[1,1,5,16384]{3,1,2,0:T(1,128)}, u32[]{:S(2)}) copy-start(f32[1,1,5,16384]{3,1,2,0:T(1,128)} %param.52) | copy-start | bytes 983044
  12.6 25.3 %copy-start.4 = (f32[1,1,5,16384]{3,1,2,0:T(1,128)S(1)}, f32[1,1,5,16384]{3,1,2,0:T(1,128)}, u32[]{:S(2)}) copy-start(f32[1,1,5,16384]{3,1,2,0:T(1,128)} %param.51) | copy-start | bytes 983044
  39.0 0.9 copy-start.1
  40.1 8.6 %collective-permute-start.2 = (f32[4,68,2]{2,1,0:T(8,128)S(1)}, f32[4,68,2]{2,1,0:T(8,128)S(1)}, u32[]{:S(2)}, u32[]{:S(2)}) collective-permute-start(f32[4,68,2]{2,1,0:T(8,128)S(1)} %get-tuple-element.220), channel_id=1, source_target_pairs={{0,1},{1,2},{2,3},{4,5},{5,6},{6,7},{8,9},{9,10},{10,11},{12,13},{... | collective-permute-start | bytes 6536 | tf_op jit(solution)/shard_map/ppermute | solution.py:28
  42.3 6.4 %collective-permute-start.3 = (f32[4,68,2]{2,1,0:T(8,128)S(1)}, f32[4,68,2]{2,1,0:T(8,128)S(1)}, u32[]{:S(2)}, u32[]{:S(2)}) collective-permute-start(f32[4,68,2]{2,1,0:T(8,128)S(1)} %get-tuple-element.221), channel_id=1, source_target_pairs={{1,0},{2,1},{3,2},{5,4},{6,5},{7,6},{9,8},{10,9},{11,10},{13,12},{... | collective-permute-start | bytes 6536 | tf_op jit(solution)/shard_map/ppermute | solution.py:29
  43.8 0.8 copy-start.5
  48.9 0.8 copy-start.8
  49.7 0.8 copy-start.6
  55.8 11.0 %all-to-all-start.1 = ((bf16[4,2,24576]{2,1,0:T(2,128)(2,1)}), bf16[4,2,24576]{2,1,0:T(2,128)(2,1)S(1)}, u32[]{:S(2)}, u32[]{:S(2)}) async-start(bf16[4,2,24576]{2,1,0:T(2,128)(2,1)} %reshape.1402), calls=%async_computation.1 | async-start | bytes 786432 | tf_op jit(solution)/shard_map/all_to_all | solution.py:149
  67.7 0.9 copy-start.2
  67.7 1.0 copy-start.7
  142.4 10.9 %all-to-all-start.2 = ((bf16[4,2,24576]{2,1,0:T(2,128)(2,1)}), bf16[4,2,24576]{2,1,0:T(2,128)(2,1)S(1)}, u32[]{:S(2)}, u32[]{:S(2)}) async-start(bf16[4,2,24576]{2,1,0:T(2,128)(2,1)} %reshape.1404), calls=%async_computation.2 | async-start | bytes 786432 | tf_op jit(solution)/shard_map/all_to_all | solution.py:191
where the time goes:
time: 158 us; the launch traced here: 157 us
  blocking collectives  77.7 us (49%)
  local copies, waits for them, and re-layouts  34.1 us (22%)
  starting transfers between devices  20.1 us (13%)
  waiting for transfers between devices  13.9 us (9%)
  other arithmetic  8.44 us (5%)
    all_gather x4, blocking collectives, shards(): lax.all_gather(rim_edges.reshape(block_count, 8 * block_side), ('tile', '...  77.7 us
    unnamed x32, local copies, waits for them, and re-layouts  7.74 us
    ppermute x2, starting transfers between devices, extended(): before = lax.ppermute(last, axis, up)  7.3 us
    all_to_all x1, waiting for transfers between devices, shards(): lax.all_to_all(outgoing, ('sub', 'lev'), split_axis=0, concat_axis=0, til...  7.23 us
    scatter x4, local copies, waits for them, and re-layouts, with_halo(): padded = padded.at[:, :, 0, 1:-1].set(rim_halos[:, 1])  7.02 us
    all_to_all x1, waiting for transfers between devices, shards(): lax.all_to_all(replies.reshape(group_count, capacity, item_width), ('sub'...  6.61 us
    scatter x4, local copies, waits for them, and re-layouts, with_halo(): padded = padded.at[:, :, 1:-1, -1].set(rim_halos[:, 2])  4.06 us
    all_to_all x1, starting transfers between devices, shards(): lax.all_to_all(outgoing, ('sub', 'lev'), split_axis=0, concat_axis=0, til...  3.52 us
  transfers between devices with their start and end apart: 7, of which 2 were waited for; matrix products, arithmetic and copies ran while one was open for 11% of the time, Pallas kernels for 0%

commit v1 on v0

--- a/solution.py
+++ b/solution.py
@@ -170,10 +170,12 @@
     current_ice = forcing[:, 1:]
     for subcycle_index in range(SUBCYCLES):
         rim_edges = block_edges(velocity)
-        everything = lax.all_gather(
-            rim_edges.reshape(block_count, 8 * block_side),
+        sent_rims = rim_edges.reshape(1, block_count, 8 * block_side)
+        everything = lax.all_to_all(
+            jnp.broadcast_to(sent_rims, (device_count, block_count, 8 * block_side)),
             ("tile", "sub", "lev"),
-            axis=0,
+            split_axis=0,
+            concat_axis=0,
             tiled=True,
         )
         rim_halos = everything.reshape(device_count * block_count * 4, 2, block_side)[

time: 158 us -> 125 us (0.79)
  blocking collectives: 77.7 us -> 0 us
  starting transfers between devices: 20.1 us -> 41.7 us
  waiting for transfers between devices: 13.9 us -> 29.3 us
  local copies, waits for them, and re-layouts: 34.1 us -> 38.6 us
  other arithmetic: 8.44 us -> 11.5 us
    all_gather x4 -> x0, blocking collectives: 77.7 us -> none  [shards(): lax.all_gather(rim_edges.reshape(block_count, 8 * block_side), ('tile', '...]
    all_to_all x0 -> x4, starting transfers between devices: none -> 21.7 us  [shards(): lax.all_to_all(jnp.broadcast_to(sent_rims, (device_count, block_count, 8...]
    all_to_all x0 -> x4, waiting for transfers between devices: none -> 20.1 us  [shards(): lax.all_to_all(jnp.broadcast_to(sent_rims, (device_count, block_count, 8...]
    all_to_all x1, waiting for transfers between devices: 7.23 us -> 2.57 us  [shards(): lax.all_to_all(outgoing, ('sub', 'lev'), split_axis=0, concat_axis=0, til...]
    broadcast_in_dim x0 -> x4, local copies, waits for them, and re-layouts: none -> 2.66 us  [shards(): jnp.broadcast_to(sent_rims, (device_count, block_count, 8 * block_side))]
    unnamed x32 -> x28, local copies, waits for them, and re-layouts: 7.74 us -> 9.5 us
  transfers between devices with their start and end apart: 7 -> 11, of which waited for: 2 -> 5; matrix products, arithmetic and copies ran while one was open for 11% -> 17% of each run, Pallas kernels for 0% -> 0%
where the time goes in v1:
time: 125 us; the launch traced here: 124 us
  starting transfers between devices  41.7 us (33%)
  local copies, waits for them, and re-layouts  38.6 us (31%)
  waiting for transfers between devices  29.3 us (23%)
  other arithmetic  11.5 us (9%)
  between operations  1.45 us (1%)
    all_to_all x4, starting transfers between devices, shards(): lax.all_to_all(jnp.broadcast_to(sent_rims, (device_count, block_count, 8...  21.7 us
    all_to_all x4, waiting for transfers between devices, shards(): lax.all_to_all(jnp.broadcast_to(sent_rims, (device_count, block_count, 8...  20.1 us
    unnamed x28, local copies, waits for them, and re-layouts  9.5 us
    ppermute x2, starting transfers between devices, extended(): before = lax.ppermute(last, axis, up)  7.29 us
    scatter x4, local copies, waits for them, and re-layouts, with_halo(): padded = padded.at[:, :, 0, 1:-1].set(rim_halos[:, 1])  7.02 us
    all_to_all x1, waiting for transfers between devices, shards(): lax.all_to_all(replies.reshape(group_count, capacity, item_width), ('sub'...  6.61 us
    scatter x4, local copies, waits for them, and re-layouts, with_halo(): padded = padded.at[:, :, 1:-1, -1].set(rim_halos[:, 2])  4.06 us
    all_to_all x1, starting transfers between devices, shards(): lax.all_to_all(outgoing, ('sub', 'lev'), split_axis=0, concat_axis=0, til...  3.46 us
  transfers between devices with their start and end apart: 11, of which 5 were waited for; matrix products, arithmetic and copies ran while one was open for 17% of the time, Pallas kernels for 0%

profile of v1, /device:TPU:0, one launch (start us, length us, event | category | flops | bytes accessed | tf_op | source)
XLA Modules:
  0.0 123.7 jit_solution(6919100968196293674)
XLA Ops:
  0.7 0.8 fusion.91
  1.5 4.9 %collective-permute-start = (f32[4,2,128]{2,1,0:T(2,128)S(1)}, f32[4,2,128]{2,1,0:T(2,128)S(1)}, u32[]{:S(2)}, u32[]{:S(2)}) collective-permute-start(f32[4,2,128]{2,1,0:T(2,128)S(1)} %get-tuple-element.234), channel_id=1, source_target_pairs={{0,4},{4,8},{8,12},{1,5},{5,9},{9,13},{2,6},{6,10},{10,14},{3,7},{... | collective-permute-start | bytes 12296 | tf_op jit(solution)/shard_map/ppermute | solution.py:28
  6.4 1.3 %collective-permute-start.1 = (f32[4,2,128]{2,1,0:T(2,128)S(1)}, f32[4,2,128]{2,1,0:T(2,128)S(1)}, u32[]{:S(2)}, u32[]{:S(2)}) collective-permute-start(f32[4,2,128]{2,1,0:T(2,128)S(1)} %get-tuple-element.235), channel_id=1, source_target_pairs={{4,0},{8,4},{12,8},{5,1},{9,5},{13,9},{6,2},{10,6},{14,10},{7,3},{... | collective-permute-start | bytes 12296 | tf_op jit(solution)/shard_map/ppermute | solution.py:29
  7.7 0.7 and_select_fusion.2
  8.3 0.7 fusion.69
  9.2 0.7 fusion.75
  9.9 0.6 scatter_custom_fusion
  10.5 0.7 copy.190
  11.1 3.2 %all-to-all-start = ((s32[4,1,1]{2,1,0:T(1,128)}), s32[4,1,1]{2,1,0:T(1,128)S(1)}, u32[]{:S(2)}, u32[]{:S(2)}) async-start(s32[4,1,1]{2,1,0:T(1,128)} %copy.190), calls=%async_computation | async-start | bytes 4096 | tf_op jit(solution)/shard_map/all_to_all | solution.py:150
  14.4 0.9 copy.250
  15.5 0.6 copy-done.8
  16.2 0.6 copy-done.9
  16.9 0.6 fusion.92
  17.5 2.2 %fusion.10 = (f32[16384]{0:T(1024)S(1)}, f32[16384]{0:T(1024)S(1)}, f32[16384]{0:T(1024)S(1)}) fusion(f32[1,1,5,16384]{3,1,2,0:T(1,128)S(1)} %copy-done.3, f32[1,1,5,16384]{3,1,2,0:T(1,128)} %param.51), kind=kLoop, calls=%fused_computation.23 | loop fusion | flops 442368 | bytes 851968 | tf_op jit(solution)/shard_map/reduce_sum | solution.py:65
  19.7 0.8 copy-done.4
  20.6 0.7 copy-done.1
  21.5 2.4 %collective-permute-start.2 = (f32[4,68,2]{2,1,0:T(8,128)S(1)}, f32[4,68,2]{2,1,0:T(8,128)S(1)}, u32[]{:S(2)}, u32[]{:S(2)}) collective-permute-start(f32[4,68,2]{2,1,0:T(8,128)S(1)} %get-tuple-element.220), channel_id=1, source_target_pairs={{0,1},{1,2},{2,3},{4,5},{5,6},{6,7},{8,9},{9,10},{10,11},{12,13},{... | collective-permute-start | bytes 6536 | tf_op jit(solution)/shard_map/ppermute | solution.py:28
  23.9 1.3 %collective-permute-start.3 = (f32[4,68,2]{2,1,0:T(8,128)S(1)}, f32[4,68,2]{2,1,0:T(8,128)S(1)}, u32[]{:S(2)}, u32[]{:S(2)}) collective-permute-start(f32[4,68,2]{2,1,0:T(8,128)S(1)} %get-tuple-element.221), channel_id=1, source_target_pairs={{1,0},{2,1},{3,2},{5,4},{6,5},{7,6},{9,8},{10,9},{11,10},{13,12},{... | collective-permute-start | bytes 6536 | tf_op jit(solution)/shard_map/ppermute | solution.py:29
  25.2 0.7 broadcast_in_dim.25
  25.9 9.4 %all-to-all-start.2 = ((f32[16,1,1024]{2,1,0:T(1,128)}), f32[16,1,1024]{2,1,0:T(1,128)S(1)}, u32[]{:S(2)}, u32[]{:S(2)}) async-start(f32[16,1,1024]{2,1,0:T(1,128)} %broadcast_in_dim.25), calls=%async_computation.2 | async-start | bytes 131072 | tf_op jit(solution)/shard_map/all_to_all | solution.py:174
  36.6 0.6 copy-done.5
  37.2 0.5 convolution_convert_fusion
  37.7 1.9 %scatter_custom_fusion.1 = bf16[4,49152]{1,0:T(4,128)(2,1)S(1)} fusion(s32[4]{0:T(128)S(1)} %fusion.77, bf16[1,4,384,128]{3,2,1,0:T(8,128)(2,1)S(1)} %bitcast.259, bf16[]{:T(256)} %constant.462.clone.1), kind=kCustom, calls=%fused_computation.16 | custom fusion | bytes 786434 | tf_op jit(solution)/shard_map/scatter | solution.py:143
  39.7 0.6 broadcast.771
  40.3 1.2 reduce.57
  41.5 1.2 reshape.1386
  42.6 3.5 %all-to-all-start.1 = ((bf16[4,2,24576]{2,1,0:T(2,128)(2,1)}), bf16[4,2,24576]{2,1,0:T(2,128)(2,1)S(1)}, u32[]{:S(2)}, u32[]{:S(2)}) async-start(bf16[4,2,24576]{2,1,0:T(2,128)(2,1)} %reshape.1386), calls=%async_computation.1 | async-start | bytes 786432 | tf_op jit(solution)/shard_map/all_to_all | solution.py:149
  46.1 0.6 gather_fusion
  47.5 1.8 %scatter.71 = f32[1,2,130,130]{3,2,1,0:T(8,128)S(1)} dynamic-update-slice(f32[1,2,130,130]{3,2,1,0:T(8,128)S(1)} %scatter.70, f32[1,2,1,128]{3,2,1,0:T(1,128)S(1)} %bitcast.292, s32[]{:T(128)} %constant.453.clone.1, s32[]{:T(128)} %constant.453.clone.1, s32[]{:T(128)} %bitcast.37, s32[]{:T(128)} %bitcast.38) | dynamic-update-slice | bytes 2052 | tf_op jit(solution)/shard_map/scatter | solution.py:54
  49.3 1.0 scatter.74
  50.3 0.6 scatter.75
  50.9 2.6 %all-to-all-done.1 = bf16[4,2,24576]{2,1,0:T(2,128)(2,1)S(1)} async-done(((bf16[4,2,24576]{2,1,0:T(2,128)(2,1)}), bf16[4,2,24576]{2,1,0:T(2,128)(2,1)S(1)}, u32[]{:S(2)}, u32[]{:S(2)}) %all-to-all-start.1) | async-done | bytes 393248 | tf_op jit(solution)/shard_map/all_to_all | solution.py:149
  53.9 0.5 copy.225
  54.8 0.5 copy-done.2
  55.9 0.7 broadcast_in_dim.28
  56.6 5.1 %all-to-all-start.3 = ((f32[16,1,1024]{2,1,0:T(1,128)}), f32[16,1,1024]{2,1,0:T(1,128)S(1)}, u32[]{:S(2)}, u32[]{:S(2)}) async-start(f32[16,1,1024]{2,1,0:T(1,128)} %broadcast_in_dim.28), calls=%async_computation.3 | async-start | bytes 131072 | tf_op jit(solution)/shard_map/all_to_all | solution.py:174
  61.8 6.8 %all-to-all-done.3 = f32[16,1,1024]{2,1,0:T(1,128)S(1)} async-done(((f32[16,1,1024]{2,1,0:T(1,128)}), f32[16,1,1024]{2,1,0:T(1,128)S(1)}, u32[]{:S(2)}, u32[]{:S(2)}) %all-to-all-start.3) | async-done | bytes 65568 | tf_op jit(solution)/shard_map/all_to_all | solution.py:174
  68.6 0.6 gather_fusion.1
  70.0 1.8 %scatter.79 = f32[1,2,130,130]{3,2,1,0:T(8,128)S(1)} dynamic-update-slice(f32[1,2,130,130]{3,2,1,0:T(8,128)S(1)} %scatter.76, f32[1,2,1,128]{3,2,1,0:T(1,128)S(1)} %bitcast.293, s32[]{:T(128)} %constant.453.clone.1, s32[]{:T(128)} %constant.453.clone.1, s32[]{:T(128)} %bitcast.37, s32[]{:T(128)} %bitcast.38) | dynamic-update-slice | bytes 2052 | tf_op jit(solution)/shard_map/scatter | solution.py:54
  71.8 1.0 scatter.80
  72.8 0.6 scatter.81
  73.9 0.7 broadcast_in_dim.30
  74.6 3.7 %all-to-all-start.4 = ((f32[16,1,1024]{2,1,0:T(1,128)}), f32[16,1,1024]{2,1,0:T(1,128)S(1)}, u32[]{:S(2)}, u32[]{:S(2)}) async-start(f32[16,1,1024]{2,1,0:T(1,128)} %broadcast_in_dim.30), calls=%async_computation.4 | async-start | bytes 131072 | tf_op jit(solution)/shard_map/all_to_all | solution.py:174
  78.5 6.7 %all-to-all-done.4 = f32[16,1,1024]{2,1,0:T(1,128)S(1)} async-done(((f32[16,1,1024]{2,1,0:T(1,128)}), f32[16,1,1024]{2,1,0:T(1,128)S(1)}, u32[]{:S(2)}, u32[]{:S(2)}) %all-to-all-start.4) | async-done | bytes 65568 | tf_op jit(solution)/shard_map/all_to_all | solution.py:174
  85.2 0.6 gather_fusion.2
  86.6 1.8 %scatter.85 = f32[1,2,130,130]{3,2,1,0:T(8,128)S(1)} dynamic-update-slice(f32[1,2,130,130]{3,2,1,0:T(8,128)S(1)} %scatter.84, f32[1,2,1,128]{3,2,1,0:T(1,128)S(1)} %bitcast.294, s32[]{:T(128)} %constant.453.clone.1, s32[]{:T(128)} %constant.453.clone.1, s32[]{:T(128)} %bitcast.37, s32[]{:T(128)} %bitcast.38) | dynamic-update-slice | bytes 2052 | tf_op jit(solution)/shard_map/scatter | solution.py:54
  88.3 1.0 scatter.86
  89.3 0.6 scatter.89
  90.5 0.7 broadcast_in_dim.32
  91.2 3.5 %all-to-all-start.5 = ((f32[16,1,1024]{2,1,0:T(1,128)}), f32[16,1,1024]{2,1,0:T(1,128)S(1)}, u32[]{:S(2)}, u32[]{:S(2)}) async-start(f32[16,1,1024]{2,1,0:T(1,128)} %broadcast_in_dim.32), calls=%async_computation.5 | async-start | bytes 131072 | tf_op jit(solution)/shard_map/all_to_all | solution.py:174
  94.8 6.7 %all-to-all-done.5 = f32[16,1,1024]{2,1,0:T(1,128)S(1)} async-done(((f32[16,1,1024]{2,1,0:T(1,128)}), f32[16,1,1024]{2,1,0:T(1,128)S(1)}, u32[]{:S(2)}, u32[]{:S(2)}) %all-to-all-start.5) | async-done | bytes 65568 | tf_op jit(solution)/shard_map/all_to_all | solution.py:174
  101.5 0.6 gather_fusion.3
  102.9 1.8 %scatter.109 = f32[1,2,130,130]{3,2,1,0:T(8,128)S(1)} dynamic-update-slice(f32[1,2,130,130]{3,2,1,0:T(8,128)S(1)} %scatter.108, f32[1,2,1,128]{3,2,1,0:T(1,128)S(1)} %bitcast.291, s32[]{:T(128)} %constant.453.clone.1, s32[]{:T(128)} %constant.453.clone.1, s32[]{:T(128)} %bitcast.37, s32[]{:T(128)} %bitcast.38) | dynamic-update-slice | bytes 2052 | tf_op jit(solution)/shard_map/scatter | solution.py:54
  104.7 1.0 scatter.110
  105.7 0.6 scatter.111
  106.9 1.2 reduce.58
  108.1 1.2 reshape.1388
  109.2 3.5 %all-to-all-start.6 = ((bf16[4,2,24576]{2,1,0:T(2,128)(2,1)}), bf16[4,2,24576]{2,1,0:T(2,128)(2,1)S(1)}, u32[]{:S(2)}, u32[]{:S(2)}) async-start(bf16[4,2,24576]{2,1,0:T(2,128)(2,1)} %reshape.1388), calls=%async_computation.6 | async-start | bytes 786432 | tf_op jit(solution)/shard_map/all_to_all | solution.py:193
  112.7 0.8 maximum_divide_fusion.4
  113.5 6.6 %all-to-all-done.6 = bf16[4,2,24576]{2,1,0:T(2,128)(2,1)S(1)} async-done(((bf16[4,2,24576]{2,1,0:T(2,128)(2,1)}), bf16[4,2,24576]{2,1,0:T(2,128)(2,1)S(1)}, u32[]{:S(2)}, u32[]{:S(2)}) %all-to-all-start.6) | async-done | bytes 393248 | tf_op jit(solution)/shard_map/all_to_all | solution.py:193
  120.5 0.5 copy.249
  121.1 0.9 gather_fusion.4
  122.4 0.6 fusion.41
  123.1 0.7 broadcast_add_fusion
  (96 shorter events, 9.4 us)
Async XLA Ops:
  0.6 36.0 %copy-start = (bf16[1,4,128,128]{3,2,1,0:T(8,128)(2,1)S(1)}, bf16[1,4,128,128]{3,2,1,0:T(8,128)(2,1)}, u32[]{:S(2)}) copy-start(bf16[1,4,128,128]{3,2,1,0:T(8,128)(2,1)} %param.49) | copy-start | bytes 393220
  0.6 16.8 %copy-start.3 = (f32[1,1,5,16384]{3,1,2,0:T(1,128)S(1)}, f32[1,1,5,16384]{3,1,2,0:T(1,128)}, u32[]{:S(2)}) copy-start(f32[1,1,5,16384]{3,1,2,0:T(1,128)} %param.52) | copy-start | bytes 983044
  1.5 19.2 %collective-permute-start = (f32[4,2,128]{2,1,0:T(2,128)S(1)}, f32[4,2,128]{2,1,0:T(2,128)S(1)}, u32[]{:S(2)}, u32[]{:S(2)}) collective-permute-start(f32[4,2,128]{2,1,0:T(2,128)S(1)} %get-tuple-element.234), channel_id=1, source_target_pairs={{0,4},{4,8},{8,12},{1,5},{5,9},{9,13},{2,6},{6,10},{10,14},{3,7},{... | collective-permute-start | bytes 12296 | tf_op jit(solution)/shard_map/ppermute | solution.py:28
  6.4 14.3 %collective-permute-start.1 = (f32[4,2,128]{2,1,0:T(2,128)S(1)}, f32[4,2,128]{2,1,0:T(2,128)S(1)}, u32[]{:S(2)}, u32[]{:S(2)}) collective-permute-start(f32[4,2,128]{2,1,0:T(2,128)S(1)} %get-tuple-element.235), channel_id=1, source_target_pairs={{4,0},{8,4},{12,8},{5,1},{9,5},{13,9},{6,2},{10,6},{14,10},{7,3},{... | collective-permute-start | bytes 12296 | tf_op jit(solution)/shard_map/ppermute | solution.py:29
  11.1 14.0 %all-to-all-start = ((s32[4,1,1]{2,1,0:T(1,128)}), s32[4,1,1]{2,1,0:T(1,128)S(1)}, u32[]{:S(2)}, u32[]{:S(2)}) async-start(s32[4,1,1]{2,1,0:T(1,128)} %copy.190), calls=%async_computation | async-start | bytes 4096 | tf_op jit(solution)/shard_map/all_to_all | solution.py:150
  15.5 0.7 copy-start.8
  16.2 0.7 copy-start.9
  19.6 0.8 copy-start.4
  20.5 0.9 copy-start.1
  21.5 13.9 %collective-permute-start.2 = (f32[4,68,2]{2,1,0:T(8,128)S(1)}, f32[4,68,2]{2,1,0:T(8,128)S(1)}, u32[]{:S(2)}, u32[]{:S(2)}) collective-permute-start(f32[4,68,2]{2,1,0:T(8,128)S(1)} %get-tuple-element.220), channel_id=1, source_target_pairs={{0,1},{1,2},{2,3},{4,5},{5,6},{6,7},{8,9},{9,10},{10,11},{12,13},{... | collective-permute-start | bytes 6536 | tf_op jit(solution)/shard_map/ppermute | solution.py:28
  23.9 11.5 %collective-permute-start.3 = (f32[4,68,2]{2,1,0:T(8,128)S(1)}, f32[4,68,2]{2,1,0:T(8,128)S(1)}, u32[]{:S(2)}, u32[]{:S(2)}) collective-permute-start(f32[4,68,2]{2,1,0:T(8,128)S(1)} %get-tuple-element.221), channel_id=1, source_target_pairs={{1,0},{2,1},{3,2},{5,4},{6,5},{7,6},{9,8},{10,9},{11,10},{13,12},{... | collective-permute-start | bytes 6536 | tf_op jit(solution)/shard_map/ppermute | solution.py:29
  25.9 16.8 %all-to-all-start.2 = ((f32[16,1,1024]{2,1,0:T(1,128)}), f32[16,1,1024]{2,1,0:T(1,128)S(1)}, u32[]{:S(2)}, u32[]{:S(2)}) async-start(f32[16,1,1024]{2,1,0:T(1,128)} %broadcast_in_dim.25), calls=%async_computation.2 | async-start | bytes 131072 | tf_op jit(solution)/shard_map/all_to_all | solution.py:174
  35.6 0.8 copy-start.7
  36.4 0.8 copy-start.5
  42.6 10.9 %all-to-all-start.1 = ((bf16[4,2,24576]{2,1,0:T(2,128)(2,1)}), bf16[4,2,24576]{2,1,0:T(2,128)(2,1)S(1)}, u32[]{:S(2)}, u32[]{:S(2)}) async-start(bf16[4,2,24576]{2,1,0:T(2,128)(2,1)} %reshape.1386), calls=%async_computation.1 | async-start | bytes 786432 | tf_op jit(solution)/shard_map/all_to_all | solution.py:149
  54.4 0.9 copy-start.2
  54.4 1.0 copy-start.6
  56.6 12.0 %all-to-all-start.3 = ((f32[16,1,1024]{2,1,0:T(1,128)}), f32[16,1,1024]{2,1,0:T(1,128)S(1)}, u32[]{:S(2)}, u32[]{:S(2)}) async-start(f32[16,1,1024]{2,1,0:T(1,128)} %broadcast_in_dim.28), calls=%async_computation.3 | async-start | bytes 131072 | tf_op jit(solution)/shard_map/all_to_all | solution.py:174
  74.6 10.6 %all-to-all-start.4 = ((f32[16,1,1024]{2,1,0:T(1,128)}), f32[16,1,1024]{2,1,0:T(1,128)S(1)}, u32[]{:S(2)}, u32[]{:S(2)}) async-start(f32[16,1,1024]{2,1,0:T(1,128)} %broadcast_in_dim.30), calls=%async_computation.4 | async-start | bytes 131072 | tf_op jit(solution)/shard_map/all_to_all | solution.py:174
  91.2 10.4 %all-to-all-start.5 = ((f32[16,1,1024]{2,1,0:T(1,128)}), f32[16,1,1024]{2,1,0:T(1,128)S(1)}, u32[]{:S(2)}, u32[]{:S(2)}) async-start(f32[16,1,1024]{2,1,0:T(1,128)} %broadcast_in_dim.32), calls=%async_computation.5 | async-start | bytes 131072 | tf_op jit(solution)/shard_map/all_to_all | solution.py:174
  109.2 10.9 %all-to-all-start.6 = ((bf16[4,2,24576]{2,1,0:T(2,128)(2,1)}), bf16[4,2,24576]{2,1,0:T(2,128)(2,1)S(1)}, u32[]{:S(2)}, u32[]{:S(2)}) async-start(bf16[4,2,24576]{2,1,0:T(2,128)(2,1)} %reshape.1388), calls=%async_computation.6 | async-start | bytes 786432 | tf_op jit(solution)/shard_map/all_to_all | solution.py:193

commit v2 on v0

v2 whole, which is shorter than its diff:
```python
import functools

import jax
import jax.numpy as jnp
from jax import lax
from jax.experimental import pallas as pl
from jax.experimental.pallas import tpu as pltpu
from jax.sharding import PartitionSpec as P

SUBCYCLES = 4
STRENGTH_DECAY = 5.0
VISCOUS_STEP = 0.24
SUBCYCLE_STEP = 0.5
CORIOLIS_TURN = 0.1
BASE_MASS = 0.5
HEAT_RATE = 0.2
THIN_ICE = 0.1
THERMAL_DIFFUSE = 0.5
STRESS_MIXING = 0.5

OPPOSITE = (1, 0, 3, 2)
LATERAL = ((2, 3), (2, 3), (0, 1), (0, 1))
DEPTH = SUBCYCLES
TILE_ROWS = 16
F32 = jnp.float32
BF16 = jnp.bfloat16
VMEM_LIMIT = 16 * 1024 * 1024


def call(kernel, outs, args, scratch=(), smem=(), flops=1_000_000):
    specs = [
        pl.BlockSpec(memory_space=pltpu.SMEM if i in smem else pltpu.VMEM) for i in range(len(args))
    ]
    size = sum(a.size * a.dtype.itemsize for a in args)
    return pl.pallas_call(
        kernel,
        out_shape=outs,
        in_specs=specs,
        out_specs=jax.tree.map(lambda _: pl.BlockSpec(memory_space=pltpu.VMEM), outs),
        scratch_shapes=list(scratch),
        compiler_params=pltpu.CompilerParams(vmem_limit_bytes=VMEM_LIMIT),
        cost_estimate=pl.CostEstimate(flops=flops, bytes_accessed=size, transcendentals=0),
    )(*args)


def iota(shape, axis):
    return lax.broadcasted_iota(jnp.int32, shape, axis)


def roll(x, shift, axis):
    return pltpu.roll(x, shift % x.shape[axis], axis)


def flag(condition):
    return jnp.where(condition, 1.0, 0.0).astype(F32)


def forward_kernel(group, blocks, rows, cols, currents, *outs):
    side = rows.shape[1]
    depth = cols.shape[1]
    devices = group[0]
    members = group[1]
    me = group[2]()
    fields = [currents[c].astype(BF16) for c in range(2)]
    pairs = rows.shape[0]
    for k, out in enumerate(outs):
        partner = me ^ k
        pair = jnp.int32(0)
        found = jnp.int32(0)
        for m in range(pairs):
            owner = lax.rem(lax.rem(blocks[0, m], devices), members)
            pair = jnp.where(owner == partner, m, pair)
            found = jnp.where(owner == partner, 1, found)
        if pairs == members:
            out[0:side] = rows[pair]
            out[side : side + depth] = cols[pair]
        else:
            out[0:side] = jnp.where(found > 0, rows[pair].astype(F32), 0.0).astype(BF16)
            out[side : side + depth] = jnp.where(found > 0, cols[pair].astype(F32), 0.0).astype(BF16)
        for c in range(2):
            out[side + depth + c * side : side + depth + (c + 1) * side] = fields[c]


def put_side_rims(store, planes, at):
    size = planes[0].shape[0]
    lane = iota((size, size), 1)
    mixed = jnp.zeros((size, size), F32)
    for i, plane in enumerate(planes):
        turned = roll(plane, DEPTH + 2 * DEPTH * i, 1)
        mixed = jnp.where(lane // (2 * DEPTH) == i, turned, mixed)
    across = mixed.T
    for i, plane in enumerate(planes):
        for k in range(DEPTH):
            base = i * DEPTH + k
            store[at(0) + base : at(0) + base + 1] = plane[size - 1 - k : size - k]
            store[at(1) + base : at(1) + base + 1] = plane[k : k + 1]
            east = 2 * DEPTH * i + DEPTH - 1 - k
            west = 2 * DEPTH * i + DEPTH + k
            store[at(2) + base : at(2) + base + 1] = across[east : east + 1]
            store[at(3) + base : at(3) + base + 1] = across[west : west + 1]


def rims_kernel(
    where_am_i, links, thick, conc, ice, water, out, viscous_o, gain_o, mass_o, drag_o, conduct_o,
    speed_o, store,
):
    tile_count, sub_count, lev_count, place = where_am_i
    my_tile, my_sub, my_lev = place()
    size = thick.shape[1]
    cover = jnp.zeros((size, size), F32)
    volume = jnp.zeros((size, size), F32)
    conduct = jnp.zeros((size, size), F32)
    for c in range(thick.shape[0]):
        h, a = thick[c], conc[c]
        cover = cover + a
        volume = volume + a * h
        conduct = conduct + a / (h + THIN_ICE)
    mass = volume + BASE_MASS
    viscous = VISCOUS_STEP * (volume * jnp.exp(-STRENGTH_DECAY * (1.0 - cover))) / mass
    step_mass = SUBCYCLE_STEP / mass
    gain = 1.0 / (1.0 + step_mass * cover)
    speed_x = ice[pl.ds(0, size, stride=2), :]
    speed_y = ice[pl.ds(1, size, stride=2), :]
    viscous_o[...] = viscous
    gain_o[...] = gain
    mass_o[...] = step_mass
    drag_o[...] = cover
    conduct_o[...] = -HEAT_RATE * conduct
    speed_o[0] = speed_x
    speed_o[1] = speed_y
    side_rows = 4 * 4 * DEPTH
    put_side_rims(store, [speed_x, speed_y, viscous, gain], lambda side: side * 4 * DEPTH)
    rim_rows = store[0:side_rows].astype(BF16)
    for d in range(out.shape[0]):
        out[d, 0:side_rows] = rim_rows
    levels, rows, width = water.shape
    lane = iota((rows, width), 1)
    mixed = jnp.zeros((rows, width), F32)
    for l in range(levels):
        mixed = jnp.where(lane // 4 == l, roll(water[l], 2 + 4 * l, 1), mixed)
    across = jnp.concatenate([mixed, jnp.zeros((width - rows, width), F32)], axis=0).T
    row_lane = iota((1, width), 1)
    names = jnp.zeros((1, width), F32)
    for q in range(4):
        high = links[0, 0, q] >> 7
        low = links[0, 0, q] & 127
        names = jnp.where(row_lane == q, high.astype(F32), names)
        names = jnp.where(row_lane == 4 + q, low.astype(F32), names)
    spare = out.shape[1] - side_rows
    blank = jnp.concatenate(
        [jnp.zeros((2 * levels, width), F32), names, jnp.zeros((spare - 2 * levels - 1, width), F32)]
    )
    empty = blank.astype(BF16)
    for d in range(out.shape[0]):
        out[d, side_rows:] = empty
    tail = blank[2 * levels :]
    for dt in (-1, 0, 1):
        for ds in (-1, 0, 1):
            if dt == 0 and ds == 0:
                continue
            strip = []
            for l in range(levels):
                for j in range(2):
                    r = rows - 1 - j if dt > 0 else j
                    if ds == 0:
                        strip.append(water[l, r : r + 1])
                    elif dt == 0:
                        at = 4 * l + (1 - j if ds > 0 else 2 + j)
                        strip.append(across[at : at + 1])
                    else:
                        line = water[l, r : r + 1]
                        strip.append(roll(line, 1, 1) if ds > 0 else line)
            message = jnp.concatenate(strip + [tail], axis=0).astype(BF16)
            to_tile, to_sub = my_tile + dt, my_sub + ds
            inside = (to_tile >= 0) & (to_tile < tile_count) & (to_sub >= 0) & (to_sub < sub_count)

            @pl.when(inside)
            def _():
                out[(to_tile * sub_count + to_sub) * lev_count + my_lev, side_rows:] = message


def remap_forward(chunks, field_rows, side, depth):
    total = None
    for chunk, fields in zip(chunks, field_rows):
        down = chunk[0:side]
        right = chunk[side : side + depth]
        wide = jnp.concatenate(fields, axis=1) if len(fields) > 1 else fields[0]
        part = lax.dot_general(down, wide, (((0,), (0,)), ((), ())), preferred_element_type=F32)
        part = part.astype(BF16)
        width = fields[0].shape[1]
        if len(fields) > 1:
            part = jnp.concatenate(
                [part[:, c * width : (c + 1) * width] for c in range(len(fields))], axis=0
            )
        piece = lax.dot_general(part, right, (((1,), (1,)), ((), ())), preferred_element_type=F32)
        piece = piece.astype(BF16).astype(F32)
        total = piece if total is None else total + piece
    return total


def forcing_kernel(group, side, mass, drag, wind, *refs):
    chunks = refs[:group]
    out, current_o, push_o, store = refs[group:]
    size = mass.shape[0]
    depth = chunks[0].shape[0] - 3 * side
    fields = [
        [c[side + depth : 2 * side + depth], c[2 * side + depth : 3 * side + depth]] for c in chunks
    ]
    total = remap_forward(chunks, fields, side, depth)
    pushes = []
    for c in range(2):
        current = total[c * size : (c + 1) * size]
        current_o[c] = current
        force = wind[pl.ds(c, size, stride=2), :]
        push = mass[...] * (force + drag[...] * current)
        push_o[c] = push
        pushes.append(push)
    put_side_rims(store, pushes, lambda q: q * 2 * DEPTH)
    message = store[...].astype(BF16)
    for d in range(out.shape[0]):
        out[d] = message


def ocean_kernel(where_am_i, strip_at, water, mixing, rims, warm_o, top_o):
    tile_count, sub_count, lev_count, place = where_am_i
    my_tile, my_sub, my_lev = place()
    levels, rows, width = water.shape
    halo = {}
    for dt in (-1, 0, 1):
        for ds in (-1, 0, 1):
            if dt == 0 and ds == 0:
                continue
            t, s = my_tile + dt, my_sub + ds
            inside = (t >= 0) & (t < tile_count) & (s >= 0) & (s < sub_count)
            device = jnp.where(inside, (t * sub_count + s) * lev_count + my_lev, 0)
            strip = rims[device, strip_at : strip_at + TILE_ROWS].astype(F32)[: 2 * levels]
            halo[dt, ds] = strip * flag(inside)
    left_cols = halo[0, -1].T
    right_cols = halo[0, 1].T
    row = iota((rows, width), 0)
    lane = iota((rows, width), 1)
    line = iota((1, width), 1)
    total = None

    def laplacian(x, top, bottom, left, right):
        up = jnp.where(row == 0, top, roll(x, 1, 0))
        down = jnp.where(row == rows - 1, bottom, roll(x, -1, 0))
        west = jnp.where(lane == 0, left, roll(x, 1, 1))
        east = jnp.where(lane == width - 1, right, roll(x, -1, 1))
        return up + down + west + east - 4.0 * x

    for l in range(levels):
        x = water[l]
        near, far = 2 * l, 2 * l + 1
        top, top_far = halo[-1, 0][near : near + 1], halo[-1, 0][far : far + 1]
        bottom, bottom_far = halo[1, 0][near : near + 1], halo[1, 0][far : far + 1]
        left, left_far = left_cols[0:rows, near : near + 1], left_cols[0:rows, far : far + 1]
        right, right_far = right_cols[0:rows, near : near + 1], right_cols[0:rows, far : far + 1]
        corner = {}
        for dt in (-1, 1):
            for ds in (-1, 1):
                corner[dt, ds] = halo[dt, ds][near : near + 1, 0:1]

        def ring_row(mid, out_row, in_row, dt):
            west = jnp.where(line == 0, corner[dt, -1], roll(mid, 1, 1))
            east = jnp.where(line == width - 1, corner[dt, 1], roll(mid, -1, 1))
            return west + east + out_row + in_row - 4.0 * mid

        def ring_col(mid, out_col, in_col, ds):
            up = jnp.concatenate([corner[-1, ds], mid[:-1]], axis=0)
            down = jnp.concatenate([mid[1:], corner[1, ds]], axis=0)
            return up + down + out_col + in_col - 4.0 * mid

        once = laplacian(x, top, bottom, left, right)
        twice = laplacian(
            once,
            ring_row(top, top_far, x[0:1], -1),
            ring_row(bottom, bottom_far, x[rows - 1 :], 1),
            ring_col(left, left_far, x[:, 0:1], -1),
            ring_col(right, right_far, x[:, width - 1 :], 1),
        )
        warm = x - mixing[...] * twice
        warm_o[l] = warm
        total = warm if total is None else total + warm
    top_o[...] = (total / (levels * lev_count)).astype(top_o.dtype)


def subcycles_kernel(me, table, viscous, gain, speed, push, rims, push_rims, out, flat_o):
    size = viscous.shape[0]
    half = DEPTH
    high = 2 * DEPTH
    sub = iota((high, size), 0)
    lane = iota((high, size), 1)
    edge = (sub & (half - 1)) == 0
    turn = jnp.where(sub < half, CORIOLIS_TURN, -CORIOLIS_TURN).astype(F32)
    first, last = lane == 0, lane == size - 1

    def load(device, side, mask, with_push=True):
        block = rims[device, side * 2 * high : (side + 1) * 2 * high].astype(F32)
        velocity, both = block[:high] * mask, block[high:]
        if not with_push:
            return velocity
        other = roll(both, half, 0)
        visc = jnp.where(sub < half, both, other)
        scale = jnp.where(sub < half, other, both) * mask
        start = side // 2 * 2 * high
        pushed = push_rims[device, start : start + 2 * high].astype(F32)
        pushed = pushed[:high] if side % 2 == 0 else pushed[high:]
        return [velocity, visc, scale, pushed]

    def follow(device, side):
        name = table[device, side]
        return jnp.where(name >= 0, name, 0), name >= 0

    def step(state, left, right, inner, outer):
        c, visc, scale, pushed = state
        spread = left + right + inner + outer - 4.0 * c
        return scale * (c + visc * spread + pushed + turn * roll(c, half, 0))

    strips = []
    for q in range(4):
        x, has_x = follow(me(), q)
        strip = load(x, OPPOSITE[q], flag(has_x))
        sides = []
        for s in LATERAL[q]:
            y, has_y = follow(x, s)
            z, has_z = follow(y, OPPOSITE[q])
            w, has_w = follow(z, OPPOSITE[s])
            sides.append(
                [
                    load(y, OPPOSITE[q], flag(has_y)),
                    load(z, q, flag(has_z)),
                    load(w, q, flag(has_w), with_push=False),
                ]
            )
        strips.append((strip, sides))

    row = iota((size, size), 0)
    col = iota((size, size), 1)
    vx, vy = speed[0], speed[1]
    visc, scale, push_x, push_y = viscous[...], gain[...], push[0], push[1]

    def spread_of(v, north, south, east, west):
        up = jnp.where(row == size - 1, north, roll(v, -1, 0))
        down = jnp.where(row == 0, south, roll(v, 1, 0))
        right = jnp.where(col == size - 1, east, roll(v, -1, 1))
        left = jnp.where(col == 0, west, roll(v, 1, 1))
        return up + down + right + left - 4.0 * v

    for t in range(SUBCYCLES):
        cells = [strip[0] for strip, _ in strips]
        if t < SUBCYCLES - 1:
            mixed = jnp.where(col < half, roll(vx, 1, 1), roll(vy, 1 + half, 1))
            across = mixed.T[0:high]
            own = [
                jnp.where(sub < half, vx[size - 1 :], vy[size - 1 :]),
                jnp.where(sub < half, vx[0:1], vy[0:1]),
                across,
                roll(across, -1, 0),
            ]
            for q in range(4):
                strip, (beyond, before) = strips[q]
                c, y_hi, y_lo = strip[0], beyond[0][0], before[0][0]
                left = jnp.where(first, roll(y_lo, 1, 1), roll(c, 1, 1))
                right = jnp.where(last, roll(y_hi, -1, 1), roll(c, -1, 1))
                inner = jnp.where(edge, own[q], roll(c, 1, 0))
                new_strip = step(strip, left, right, inner, roll(c, -1, 0))
                if t < SUBCYCLES - 2:
                    new_sides = []
                    for i, (y, z, w) in enumerate((beyond, before)):
                        away = 1 if i == 0 else -1
                        boundary = first if i == 0 else last
                        yc, zc = y[0], z[0]
                        toward = jnp.where(boundary, roll(c, away, 1), roll(yc, away, 1))
                        inner = jnp.where(edge, zc, roll(yc, 1, 0))
                        new_y = step(y, toward, roll(yc, -away, 1), inner, roll(yc, -1, 0))
                        new_z = zc
                        if t < SUBCYCLES - 3:
                            toward = jnp.where(boundary, roll(w, away, 1), roll(zc, away, 1))
                            inner = jnp.where(edge, yc, roll(zc, 1, 0))
                            new_z = step(z, toward, roll(zc, -away, 1), inner, roll(zc, -1, 0))
                        new_sides.append((new_y, new_z))
                    for item, (new_y, new_z) in zip((beyond, before), new_sides):
                        item[0][0] = new_y
                        item[1][0] = new_z
                strip[0] = new_strip
        north, south = cells[0], cells[1]
        sides = jnp.where(edge, cells[2], roll(cells[3], 1, 0)).T
        east_x, west_x = sides[:, 0:1], sides[:, 1:2]
        east_y, west_y = sides[:, half : half + 1], sides[:, half + 1 : half + 2]
        spread_x = spread_of(vx, north[0:1], south[0:1], east_x, west_x)
        spread_y = spread_of(
            vy, north[half : half + 1], south[half : half + 1], east_y, west_y
        )
        new_x = scale * (vx + visc * spread_x + push_x + CORIOLIS_TURN * vy)
        new_y = scale * (vy + visc * spread_y + push_y - CORIOLIS_TURN * vx)
        vx, vy = new_x, new_y
    out[0] = vx
    out[1] = vy
    flat_o[pl.ds(0, size, stride=2), :] = vx
    flat_o[pl.ds(1, size, stride=2), :] = vy


def back_kernel(group, side, drag, conduct, current, speed, *refs):
    chunks = refs[:group]
    tops = refs[group : 2 * group]
    outs = refs[2 * group :]
    size = drag.shape[0]
    depth = chunks[0].shape[0] - 3 * side
    warm = remap_forward(chunks, [[t[...]] for t in tops], side, depth)
    heat = conduct[...] * warm
    fluxes = [heat.astype(BF16)]
    for c in range(2):
        fluxes.append((drag[...] * (speed[c] - current[c])).astype(BF16))
    wide = jnp.concatenate(fluxes, axis=1)
    for chunk, out in zip(chunks, outs):
        part = jnp.dot(chunk[0:side], wide, preferred_element_type=F32).astype(BF16)
        part = jnp.concatenate([part[:, c * size : (c + 1) * size] for c in range(3)], axis=0)
        reply = jnp.dot(part, chunk[side : side + depth], preferred_element_type=F32)
        out[...] = reply.astype(BF16)


def finish_kernel(warm, currents, *refs):
    replies, (heat_o, current_o) = refs[:-2], refs[-2:]
    total = replies[0][...].astype(F32)
    for reply in replies[1:]:
        total = total + reply[...].astype(F32)
    side = currents.shape[1]
    heat = THERMAL_DIFFUSE * total[0:side]
    for l in range(warm.shape[0]):
        heat_o[l] = warm[l] + heat
    for c in range(2):
        current_o[c] = currents[c] + STRESS_MIXING * total[(c + 1) * side : (c + 2) * side]


def shards(
    water_heat_state,
    diffusion_coefficient,
    upper_current_vector,
    remap_blocks,
    remap_rows,
    remap_cols,
    neighbors,
    thickness,
    concentration,
    ice_velocity,
    wind_stress,
):
    tile_count, sub_count, lev_count = (lax.axis_size(a) for a in ("tile", "sub", "lev"))
    group = sub_count * lev_count
    devices = tile_count * group
    group_axes = ("sub", "lev")
    member_axes = ("tile", "sub", "lev")
    levels, side, width = water_heat_state.shape
    pairs, size = remap_rows.shape[1:3]
    categories = thickness.shape[2]

    def place():
        return tuple(lax.axis_index(a) for a in member_axes)

    def group_place():
        return lax.axis_index("sub") * lev_count + lax.axis_index("lev")

    def device_place():
        return lax.axis_index("tile") * group + group_place()

    def swap(value, k):
        return lax.ppermute(value, group_axes, [(i, i ^ k) for i in range(group)])

    def shape(*dims, dtype=F32):
        return jax.ShapeDtypeStruct(dims, dtype)

    def interleaved(value):
        return value.reshape(2, size, size).transpose(1, 0, 2).reshape(2 * size, size)

    grid = (tile_count, sub_count, lev_count, place)
    plane = shape(size, size)
    planes = shape(2, size, size)
    wind = interleaved(wind_stress)

    chunk_rows = 3 * side + width
    sent = call(
        functools.partial(forward_kernel, (devices, group, group_place)),
        [shape(chunk_rows, width, dtype=BF16)] * group,
        (remap_blocks, remap_rows[0].swapaxes(1, 2), remap_cols[0], upper_current_vector),
        smem=(0,),
    )
    chunks = [sent[0]] + [swap(sent[k], k) for k in range(1, group)]

    side_rows = 16 * DEPTH
    message_rows = side_rows + -(-(2 * levels + 1) // TILE_ROWS) * TILE_ROWS
    message, viscous, gain, step_mass, drag, conduct, speed = call(
        functools.partial(rims_kernel, grid),
        [shape(devices, message_rows, size, dtype=BF16)] + [plane] * 5 + [planes],
        (
            neighbors,
            thickness.reshape(categories, size, size),
            concentration.reshape(categories, size, size),
            interleaved(ice_velocity),
            water_heat_state,
        ),
        scratch=[pltpu.VMEM((side_rows, size), F32)],
        smem=(0,),
    )
    rims = lax.all_to_all(message, member_axes, split_axis=0, concat_axis=0, tiled=True)

    push_message, current_ice, push = call(
        functools.partial(forcing_kernel, group, side),
        [shape(devices, 8 * DEPTH, size, dtype=BF16), planes, planes],
        (step_mass, drag, wind, *chunks),
        scratch=[pltpu.VMEM((8 * DEPTH, size), F32)],
    )
    push_rims = lax.all_to_all(push_message, member_axes, split_axis=0, concat_axis=0, tiled=True)

    warm, top = call(
        functools.partial(ocean_kernel, grid, side_rows),
        [shape(levels, side, width), shape(side, width, dtype=BF16 if lev_count == 1 else F32)],
        (water_heat_state, diffusion_coefficient, rims),
    )
    if lev_count > 1:
        top = lax.psum(top, "lev").astype(BF16)
    tops = [top] + [swap(top, k) for k in range(1, group)]

    names = rims[:, side_rows + 2 * levels, 0:8].astype(jnp.int32)
    table = names[:, 0:4] * 128 + names[:, 4:8]
    speed, flat = call(
        functools.partial(subcycles_kernel, device_place),
        [planes, shape(2 * size, size)],
        (table, viscous, gain, speed, push, rims, push_rims),
        smem=(0,),
    )

    replies = call(
        functools.partial(back_kernel, group, side),
        [shape(3 * side, width, dtype=BF16)] * group,
        (drag, conduct, current_ice, speed, *chunks, *tops),
    )
    replies = [replies[0]] + [swap(replies[k], k) for k in range(1, group)]
    if lev_count > 1:
        replies = [lax.psum(sum(r.astype(F32) for r in replies), "lev")]
    heat, current = call(
        finish_kernel,
        [shape(levels, side, width), shape(2, side, width)],
        (warm, upper_current_vector, *replies),
    )
    velocity = flat.reshape(size, 2, size).transpose(1, 0, 2).reshape(1, 1, 2, size * size)
    return heat, current, velocity


def solution(mesh):
    member = ("tile", "sub", "lev")
    whole = ("copies",) + member
    ice = P(None, whole, None, None)
    water = P("lev", ("copies", "tile"), "sub")
    current = P(None, ("copies", "tile"), "sub")
    return jax.shard_map(
        shards,
        mesh=mesh,
        in_specs=(
            water,
            P("tile", "sub"),
            current,
            P(member, None),
            P(member, None, None, None),
            P(member, None, None, None),
            P(None, member, None),
            ice,
            ice,
            ice,
            ice,
        ),
        out_specs=(water, current, ice),
        check_vma=False,
    )
```

time: 158 us -> 48.7 us (0.31)
  blocking collectives: 77.7 us -> 0 us
  local copies, waits for them, and re-layouts: 34.1 us -> 5.04 us
  Pallas kernels: 0 us -> 9.12 us
  other arithmetic: 8.44 us -> 0.08 us
    all_gather x4 -> x0, blocking collectives: 77.7 us -> none  [shards(): lax.all_gather(rim_edges.reshape(block_count, 8 * block_side), ('tile', '...]
    scatter x19 -> x0, local copies, waits for them, and re-layouts: 18.5 us -> none  [the longest x4 7.02 us: with_halo(): padded = padded.at[:, :, 0, 1:-1].set(rim_halos[:, 1])]
    pallas_call x0 -> x7, Pallas kernels: none -> 9.12 us  [call(): pl.pallas_call(kernel, out_shape=outs, in_specs=specs, out_specs=jax.tree...]
    ppermute x4 -> x9, waiting for transfers between devices: 0.01 us -> 9.07 us  [swap(): return lax.ppermute(value, group_axes, [(i, i ^ k) for i in range(group)])]
    all_to_all x3 -> x2, waiting for transfers between devices: 13.8 us -> 5.01 us  [the longest x1 4.73 us: shards(): lax.all_to_all(push_message, member_axes, split_axis=0, concat_axis=0, ti...]
    ppermute x4 -> x9, starting transfers between devices: 9.89 us -> 6.17 us  [swap(): return lax.ppermute(value, group_axes, [(i, i ^ k) for i in range(group)])]
    gather x5 -> x0, local copies, waits for them, and re-layouts: 3.21 us -> none  [the longest x4 2.28 us: shards(): everything.reshape(device_count * block_count * 4, 2, block_side)]
    all_to_all x3 -> x2, starting transfers between devices: 10.2 us -> 13 us  [the longest x1 7.49 us: shards(): lax.all_to_all(message, member_axes, split_axis=0, concat_axis=0, tiled=T...]
  transfers between devices with their start and end apart: 7 -> 11, of which waited for: 2 -> 6; matrix products, arithmetic and copies ran while one was open for 11% -> 0% of each run, Pallas kernels for 0% -> 11%
where the time goes in v2:
time: 48.7 us; the launch traced here: 48.3 us
  starting transfers between devices  19.2 us (39%)
  waiting for transfers between devices  14.1 us (29%)
  Pallas kernels  9.12 us (19%)
  local copies, waits for them, and re-layouts  5.04 us (10%)
  between operations  0.76 us (2%)
    pallas_call x7, Pallas kernels, call(): pl.pallas_call(kernel, out_shape=outs, in_specs=specs, out_specs=jax.tree...  9.12 us
    ppermute x9, waiting for transfers between devices, swap(): return lax.ppermute(value, group_axes, [(i, i ^ k) for i in range(group)])  9.07 us
    all_to_all x1, starting transfers between devices, shards(): lax.all_to_all(message, member_axes, split_axis=0, concat_axis=0, tiled=T...  7.49 us
    ppermute x9, starting transfers between devices, swap(): return lax.ppermute(value, group_axes, [(i, i ^ k) for i in range(group)])  6.17 us
    all_to_all x1, starting transfers between devices, shards(): lax.all_to_all(push_message, member_axes, split_axis=0, concat_axis=0, ti...  5.53 us
    unnamed x24, local copies, waits for them, and re-layouts  5.04 us
    all_to_all x1, waiting for transfers between devices, shards(): lax.all_to_all(push_message, member_axes, split_axis=0, concat_axis=0, ti...  4.73 us
  transfers between devices with their start and end apart: 11, of which 6 were waited for; matrix products, arithmetic and copies ran while one was open for 0% of the time, Pallas kernels for 11%

profile of v2, /device:TPU:0, one launch (start us, length us, event | category | flops | bytes accessed | tf_op | source)
XLA Modules:
  0.0 48.3 jit_solution(8680580501984076933)
XLA Ops:
  0.6 0.0 copy-start.10
  0.6 0.6 %copy-done.10 = s32[1,1,4]{2,1,0:T(1,128)S(1)} copy-done((s32[1,1,4]{2,1,0:T(1,128)S(1)}, s32[1,1,4]{2,1,0:T(1,128)}, u32[]{:S(2)}) %copy-start.10) | copy-done | bytes 40
  1.3 0.0 copy-start
  1.3 0.9 %copy-done = f32[4,64,128]{2,1,0:T(8,128)S(1)} copy-done((f32[4,64,128]{2,1,0:T(8,128)S(1)}, f32[4,64,128]{2,1,0:T(8,128)}, u32[]{:S(2)}) %copy-start) | copy-done | bytes 131096
  2.2 0.0 copy-start.2
  2.2 1.0 %copy-done.2 = f32[1,1,5,16384]{3,1,2,0:T(1,128)S(1)} copy-done((f32[1,1,5,16384]{3,1,2,0:T(1,128)S(1)}, f32[1,1,5,16384]{3,1,2,0:T(1,128)}, u32[]{:S(2)}) %copy-start.2) | copy-done | bytes 327704
  3.2 0.0 copy-start.3
  3.2 1.0 %copy-done.3 = f32[1,1,5,16384]{3,1,2,0:T(1,128)S(1)} copy-done((f32[1,1,5,16384]{3,1,2,0:T(1,128)S(1)}, f32[1,1,5,16384]{3,1,2,0:T(1,128)}, u32[]{:S(2)}) %copy-start.3) | copy-done | bytes 327704
  4.1 0.0 copy-start.5
  4.1 0.9 %copy-done.5 = f32[1,1,2,16384]{3,2,1,0:T(2,128)S(1)} copy-done((f32[1,1,2,16384]{3,2,1,0:T(2,128)S(1)}, f32[1,1,2,16384]{3,2,1,0:T(2,128)}, u32[]{:S(2)}) %copy-start.5) | copy-done | bytes 131096
  5.0 1.8 %shard_map.130 = (bf16[16,80,128]{2,1,0:T(8,128)(2,1)}, f32[128,128]{1,0:T(8,128)S(1)}, f32[128,128]{1,0:T(8,128)S(1)}, f32[128,128]{1,0:T(8,128)S(1)}, f32[128,...) custom-call(s32[1,1,4]{2,1,0:T(1,128)S(1)} %copy-done.10, f32[5,128,128]{2,1,0:T(8,128)S(1)} %bitcast.22, ...), custom_call_target="tpu_custom_call" | custom-call | flops 1000000 | bytes 917520 | tf_op jit(solution)/shard_map/pallas_call | solution.py:35
  6.9 0.0 copy-start.4
  6.9 0.0 copy-start.6
  6.9 0.0 copy-start.8
  6.9 7.5 %all-to-all-start = ((bf16[16,80,128]{2,1,0:T(8,128)(2,1)}), bf16[16,80,128]{2,1,0:T(8,128)(2,1)S(1)}, u32[]{:S(2)}, u32[]{:S(2)}) async-start(bf16[16,80,128]{2,1,0:T(8,128)(2,1)} %get-tuple-element.27), calls=%async_computation | async-start | bytes 655360 | tf_op jit(solution)/shard_map/all_to_all | solution.py:505
  14.4 0.0 copy-start.11
  14.4 0.0 copy-done.4
  14.4 0.0 copy-done.6
  14.4 0.0 copy-done.8
  14.4 0.6 %copy-done.11 = s32[1,4]{1,0:T(1,128)S(1)} copy-done((s32[1,4]{1,0:T(1,128)S(1)}, s32[1,4]{1,0:T(1,128)}, u32[]{:S(2)}) %copy-start.11) | copy-done | bytes 40
  15.0 0.0 copy-start.7
  15.0 0.6 %shard_map.132 = (bf16[320,128]{1,0:T(8,128)(2,1)S(1)}, bf16[320,128]{1,0:T(8,128)(2,1)S(1)}, bf16[320,128]{1,0:T(8,128)(2,1)S(1)}, bf16[320,128]{1,0:T(8,128)(2,1)S(1)}) custom-call(s32[1,4]{1,0:T(1,128)S(1)} %copy-done.11, bf16[4,64,128]{2,1,0:T(8,128)(2,1)S(1)} %bitcast.27, bf16[4,128,128]{2,1,0:T(8,128)(2,1)S(1)} %bitcast.25, f32[2,64,128]{2,1,0:T(8,128)S(1)} %copy-done.4), custom_call_target="tpu_custom_call" | custom-call | flops 1000000 | bytes 262160 | tf_op jit(solution)/shard_map/pallas_call | solution.py:35
  15.6 0.5 collective-permute-start
  16.1 1.7 %collective-permute-start.1 = (bf16[320,128]{1,0:T(8,128)(2,1)S(1)}, bf16[320,128]{1,0:T(8,128)(2,1)S(1)}, u32[]{:S(2)}, u32[]{:S(2)}) collective-permute-start(bf16[320,128]{1,0:T(8,128)(2,1)S(1)} %get-tuple-element.34), channel_id=1, source_target_pairs={{0,2},{1,3},{2,0},{3,1},{4,6},{5,7},{6,4},{7,5},{8,10},{9,11},{10,... | collective-permute-start | bytes 245768 | tf_op jit(solution)/shard_map/ppermute | solution.py:468
  17.8 0.0 collective-permute-start.2
  17.8 0.0 collective-permute-done.refs_1_
  17.8 4.1 %collective-permute-done.1.refs_2_ = bf16[320,128]{1,0:T(8,128)(2,1)S(1)} collective-permute-done((bf16[320,128]{1,0:T(8,128)(2,1)S(1)}, bf16[320,128]{1,0:T(8,128)(2,1)S(1)}, u32[]{:S(2)}, u32[]{:S(2)}) %collective-permute-start.1) | collective-permute-done | bytes 81952 | tf_op jit(solution)/shard_map/ppermute | solution.py:468
  21.8 2.1 %collective-permute-done.2.refs_3_ = bf16[320,128]{1,0:T(8,128)(2,1)S(1)} collective-permute-done((bf16[320,128]{1,0:T(8,128)(2,1)S(1)}, bf16[320,128]{1,0:T(8,128)(2,1)S(1)}, u32[]{:S(2)}, u32[]{:S(2)}) %collective-permute-start.2) | collective-permute-done | bytes 81952 | tf_op jit(solution)/shard_map/ppermute | solution.py:468
  23.9 0.0 copy-done.7
  23.9 1.2 %shard_map.133 = (bf16[16,32,128]{2,1,0:T(8,128)(2,1)}, f32[2,128,128]{2,1,0:T(8,128)S(1)}, f32[2,128,128]{2,1,0:T(8,128)S(1)}) custom-call(f32[128,128]{1,0:T(8,128)S(1)} %get-tuple-element.31.mass, f32[128,128]{1,0:T(8,128)S(1)} %get-tuple-element.29.drag, f32[256,128]{1,0:T(8,128)S(1)} %bitcast.26, bf16[320,128]{1,0:T(8,128)(2,1)S(1)} %get-tuple-element.32.refs_0_, ...), custom_call_target="tpu_custom_call" | custom-call | flops 1000000 | bytes 589824 | tf_op jit(solution)/shard_map/pallas_call | solution.py:35
  25.2 0.3 all-to-all-done.rims
  25.5 0.0 copy-start.1
  25.5 0.0 copy-start.9
  25.5 5.5 %all-to-all-start.1 = ((bf16[16,32,128]{2,1,0:T(8,128)(2,1)}), bf16[16,32,128]{2,1,0:T(8,128)(2,1)S(1)}, u32[]{:S(2)}, u32[]{:S(2)}) async-start(bf16[16,32,128]{2,1,0:T(8,128)(2,1)} %get-tuple-element.41), calls=%async_computation.1 | async-start | bytes 262144 | tf_op jit(solution)/shard_map/all_to_all | solution.py:513
  31.0 0.0 copy-done.1
  31.0 0.0 copy-done.9
  31.0 0.9 %shard_map.131 = (f32[4,64,128]{2,1,0:T(8,128)S(1)}, bf16[64,128]{1,0:T(8,128)(2,1)S(1)}) custom-call(f32[4,64,128]{2,1,0:T(8,128)S(1)} %copy-done.1, f32[64,128]{1,0:T(8,128)S(1)} %copy-done.9, bf16[16,80,128]{2,1,0:T(8,128)(2,1)S(1)} %all-to-all-done.rims), custom_call_target="tpu_custom_call" | custom-call | flops 1000000 | bytes 491520 | tf_op jit(solution)/shard_map/pallas_call | solution.py:35
  32.0 0.5 collective-permute-start.3
  32.4 1.7 %collective-permute-start.4 = (bf16[64,128]{1,0:T(8,128)(2,1)S(1)}, bf16[64,128]{1,0:T(8,128)(2,1)S(1)}, u32[]{:S(2)}, u32[]{:S(2)}) collective-permute-start(bf16[64,128]{1,0:T(8,128)(2,1)S(1)} %get-tuple-element.43.refs_4_), channel_id=1, source_target_pairs={{0,2},{1,3},{2,0},{3,1},{4,6},{5,7},{6,4},{7,5},{8,10},{9,11},{10,... | collective-permute-start | bytes 49160 | tf_op jit(solution)/shard_map/ppermute | solution.py:468
  34.1 0.0 collective-permute-start.5
  34.1 0.1 slice_add_fusion.table
  34.2 4.7 %all-to-all-done.1.push_rims = bf16[16,32,128]{2,1,0:T(8,128)(2,1)S(1)} async-done(((bf16[16,32,128]{2,1,0:T(8,128)(2,1)}), bf16[16,32,128]{2,1,0:T(8,128)(2,1)S(1)}, u32[]{:S(2)}, u32[]{:S(2)}) %all-to-all-start.1) | async-done | bytes 131104 | tf_op jit(solution)/shard_map/all_to_all | solution.py:513
  38.9 2.8 %shard_map.134 = (f32[2,128,128]{2,1,0:T(8,128)S(1)}, f32[256,128]{1,0:T(8,128)}) custom-call(s32[16,4]{1,0:T(8,128)S(1)} %slice_add_fusion.table, f32[128,128]{1,0:T(8,128)S(1)} %get-tuple-element.37.viscous, f32[128,128]{1,0:T(8,128)S(1)} %get-tuple-element.38.gain, f32[2,128,128]{2,1,0:T(8,128)S(1)} %get-tuple-element.39.speed, ...), custom_call_target="tpu_custom_call" | custom-call | flops 1000000 | bytes 852224 | tf_op jit(solution)/shard_map/pallas_call | solution.py:35
  41.7 0.0 collective-permute-done.3.refs_5_
  41.7 0.0 collective-permute-done.4.refs_6_
  41.7 0.0 collective-permute-done.5.refs_7_
  41.7 1.1 %shard_map.135 = (bf16[192,128]{1,0:T(8,128)(2,1)S(1)}, bf16[192,128]{1,0:T(8,128)(2,1)S(1)}, bf16[192,128]{1,0:T(8,128)(2,1)S(1)}, bf16[192,128]{1,0:T(8,128)(2,1)S(1)}) custom-call(f32[128,128]{1,0:T(8,128)S(1)} %get-tuple-element.29.drag, f32[128,128]{1,0:T(8,128)S(1)} %get-tuple-element.30.conduct, f32[2,128,128]{2,1,0:T(8,128)S(1)} %get-tuple-element.36.current, ...), custom_call_target="tpu_custom_call" | custom-call | flops 1000000 | bytes 786432 | tf_op jit(solution)/shard_map/pallas_call | solution.py:35
  42.8 0.0 collective-permute-start.6
  42.8 0.1 collective-permute-start.7
  42.9 1.8 %collective-permute-start.8 = (bf16[192,128]{1,0:T(8,128)(2,1)S(1)}, bf16[192,128]{1,0:T(8,128)(2,1)S(1)}, u32[]{:S(2)}, u32[]{:S(2)}) collective-permute-start(bf16[192,128]{1,0:T(8,128)(2,1)S(1)} %get-tuple-element.47), channel_id=1, source_target_pairs={{0,3},{1,2},{2,1},{3,0},{4,7},{5,6},{6,5},{7,4},{8,11},{9,10},{10,... | collective-permute-start | bytes 147464 | tf_op jit(solution)/shard_map/ppermute | solution.py:468
  44.7 0.0 collective-permute-done.6.refs_1_
  44.7 2.8 %collective-permute-done.7.refs_2_ = bf16[192,128]{1,0:T(8,128)(2,1)S(1)} collective-permute-done((bf16[192,128]{1,0:T(8,128)(2,1)S(1)}, bf16[192,128]{1,0:T(8,128)(2,1)S(1)}, u32[]{:S(2)}, u32[]{:S(2)}) %collective-permute-start.7) | collective-permute-done | bytes 49184 | tf_op jit(solution)/shard_map/ppermute | solution.py:468
  47.4 0.1 collective-permute-done.8.refs_3_
  47.6 0.7 %shard_map.136 = (f32[4,64,128]{2,1,0:T(8,128)}, f32[2,64,128]{2,1,0:T(8,128)}) custom-call(f32[4,64,128]{2,1,0:T(8,128)S(1)} %get-tuple-element.28.warm, f32[2,64,128]{2,1,0:T(8,128)S(1)} %copy-done.4, bf16[192,128]{1,0:T(8,128)(2,1)S(1)} %get-tuple-element.44.refs_0_, bf16[192,128]{1,0:T(8,128)(2,1)S(1)} %collective-permute-done.6.refs_1_, ...), custom_call_target="tpu_custom_call" | custom-call | flops 1000000 | bytes 393216 | tf_op jit(solution)/shard_map/pallas_call | solution.py:35
  (1 shorter events, 0.0 us)
Async XLA Ops:
  0.6 0.7 %copy-start.10 = (s32[1,1,4]{2,1,0:T(1,128)S(1)}, s32[1,1,4]{2,1,0:T(1,128)}, u32[]{:S(2)}) copy-start(s32[1,1,4]{2,1,0:T(1,128)} %links.1) | copy-start | bytes 52
  1.3 0.9 %copy-start = (f32[4,64,128]{2,1,0:T(8,128)S(1)}, f32[4,64,128]{2,1,0:T(8,128)}, u32[]{:S(2)}) copy-start(f32[4,64,128]{2,1,0:T(8,128)} %water.3) | copy-start | bytes 393220
  2.2 1.0 %copy-start.2 = (f32[1,1,5,16384]{3,1,2,0:T(1,128)S(1)}, f32[1,1,5,16384]{3,1,2,0:T(1,128)}, u32[]{:S(2)}) copy-start(f32[1,1,5,16384]{3,1,2,0:T(1,128)} %param.18) | copy-start | bytes 983044
  3.2 1.0 %copy-start.3 = (f32[1,1,5,16384]{3,1,2,0:T(1,128)S(1)}, f32[1,1,5,16384]{3,1,2,0:T(1,128)}, u32[]{:S(2)}) copy-start(f32[1,1,5,16384]{3,1,2,0:T(1,128)} %param.19) | copy-start | bytes 983044
  4.1 0.9 %copy-start.5 = (f32[1,1,2,16384]{3,2,1,0:T(2,128)S(1)}, f32[1,1,2,16384]{3,2,1,0:T(2,128)}, u32[]{:S(2)}) copy-start(f32[1,1,2,16384]{3,2,1,0:T(2,128)} %param.20) | copy-start | bytes 393220
  6.9 7.5 %copy-start.4 = (f32[2,64,128]{2,1,0:T(8,128)S(1)}, f32[2,64,128]{2,1,0:T(8,128)}, u32[]{:S(2)}) copy-start(f32[2,64,128]{2,1,0:T(8,128)} %currents.3) | copy-start | bytes 196612
  6.9 7.5 %copy-start.6 = (bf16[1,4,128,128]{3,2,1,0:T(8,128)(2,1)S(1)}, bf16[1,4,128,128]{3,2,1,0:T(8,128)(2,1)}, u32[]{:S(2)}) copy-start(bf16[1,4,128,128]{3,2,1,0:T(8,128)(2,1)} %param.16) | copy-start | bytes 393220
  6.9 7.5 %copy-start.8 = (bf16[1,4,128,64]{2,3,1,0:T(8,128)(2,1)S(1)}, bf16[1,4,128,64]{2,3,1,0:T(8,128)(2,1)}, u32[]{:S(2)}) copy-start(bf16[1,4,128,64]{2,3,1,0:T(8,128)(2,1)} %param.15) | copy-start | bytes 196612
  6.9 18.6 %all-to-all-start = ((bf16[16,80,128]{2,1,0:T(8,128)(2,1)}), bf16[16,80,128]{2,1,0:T(8,128)(2,1)S(1)}, u32[]{:S(2)}, u32[]{:S(2)}) async-start(bf16[16,80,128]{2,1,0:T(8,128)(2,1)} %get-tuple-element.27), calls=%async_computation | async-start | bytes 655360 | tf_op jit(solution)/shard_map/all_to_all | solution.py:505
  14.4 0.7 %copy-start.11 = (s32[1,4]{1,0:T(1,128)S(1)}, s32[1,4]{1,0:T(1,128)}, u32[]{:S(2)}) copy-start(s32[1,4]{1,0:T(1,128)} %blocks.1) | copy-start | bytes 52
  15.0 8.9 %copy-start.7 = (f32[1,1,2,16384]{3,2,1,0:T(2,128)S(1)}, f32[1,1,2,16384]{3,2,1,0:T(2,128)}, u32[]{:S(2)}) copy-start(f32[1,1,2,16384]{3,2,1,0:T(2,128)} %param.21) | copy-start | bytes 393220
  15.6 2.2 %collective-permute-start = (bf16[320,128]{1,0:T(8,128)(2,1)S(1)}, bf16[320,128]{1,0:T(8,128)(2,1)S(1)}, u32[]{:S(2)}, u32[]{:S(2)}) collective-permute-start(bf16[320,128]{1,0:T(8,128)(2,1)S(1)} %get-tuple-element.33), channel_id=1, source_target_pairs={{0,1},{1,0},{2,3},{3,2},{4,5},{5,4},{6,7},{7,6},{8,9},{9,8},{10,11... | collective-permute-start | bytes 245768 | tf_op jit(solution)/shard_map/ppermute | solution.py:468
  16.1 5.8 %collective-permute-start.1 = (bf16[320,128]{1,0:T(8,128)(2,1)S(1)}, bf16[320,128]{1,0:T(8,128)(2,1)S(1)}, u32[]{:S(2)}, u32[]{:S(2)}) collective-permute-start(bf16[320,128]{1,0:T(8,128)(2,1)S(1)} %get-tuple-element.34), channel_id=1, source_target_pairs={{0,2},{1,3},{2,0},{3,1},{4,6},{5,7},{6,4},{7,5},{8,10},{9,11},{10,... | collective-permute-start | bytes 245768 | tf_op jit(solution)/shard_map/ppermute | solution.py:468
  17.8 6.2 %collective-permute-start.2 = (bf16[320,128]{1,0:T(8,128)(2,1)S(1)}, bf16[320,128]{1,0:T(8,128)(2,1)S(1)}, u32[]{:S(2)}, u32[]{:S(2)}) collective-permute-start(bf16[320,128]{1,0:T(8,128)(2,1)S(1)} %get-tuple-element.35), channel_id=1, source_target_pairs={{0,3},{1,2},{2,1},{3,0},{4,7},{5,6},{6,5},{7,4},{8,11},{9,10},{10,... | collective-permute-start | bytes 245768 | tf_op jit(solution)/shard_map/ppermute | solution.py:468
  25.5 5.5 %copy-start.1 = (f32[4,64,128]{2,1,0:T(8,128)S(1)}, f32[4,64,128]{2,1,0:T(8,128)}, u32[]{:S(2)}) copy-start(f32[4,64,128]{2,1,0:T(8,128)} %water.3) | copy-start | bytes 393220
  25.5 5.5 %copy-start.9 = (f32[64,128]{1,0:T(8,128)S(1)}, f32[64,128]{1,0:T(8,128)}, u32[]{:S(2)}) copy-start(f32[64,128]{1,0:T(8,128)} %mixing.1) | copy-start | bytes 98308
  25.5 13.5 %all-to-all-start.1 = ((bf16[16,32,128]{2,1,0:T(8,128)(2,1)}), bf16[16,32,128]{2,1,0:T(8,128)(2,1)S(1)}, u32[]{:S(2)}, u32[]{:S(2)}) async-start(bf16[16,32,128]{2,1,0:T(8,128)(2,1)} %get-tuple-element.41), calls=%async_computation.1 | async-start | bytes 262144 | tf_op jit(solution)/shard_map/all_to_all | solution.py:513
  32.0 9.7 %collective-permute-start.3 = (bf16[64,128]{1,0:T(8,128)(2,1)S(1)}, bf16[64,128]{1,0:T(8,128)(2,1)S(1)}, u32[]{:S(2)}, u32[]{:S(2)}) collective-permute-start(bf16[64,128]{1,0:T(8,128)(2,1)S(1)} %get-tuple-element.43.refs_4_), channel_id=1, source_target_pairs={{0,1},{1,0},{2,3},{3,2},{4,5},{5,4},{6,7},{7,6},{8,9},{9,8},{10,11... | collective-permute-start | bytes 49160 | tf_op jit(solution)/shard_map/ppermute | solution.py:468
  32.4 9.3 %collective-permute-start.4 = (bf16[64,128]{1,0:T(8,128)(2,1)S(1)}, bf16[64,128]{1,0:T(8,128)(2,1)S(1)}, u32[]{:S(2)}, u32[]{:S(2)}) collective-permute-start(bf16[64,128]{1,0:T(8,128)(2,1)S(1)} %get-tuple-element.43.refs_4_), channel_id=1, source_target_pairs={{0,2},{1,3},{2,0},{3,1},{4,6},{5,7},{6,4},{7,5},{8,10},{9,11},{10,... | collective-permute-start | bytes 49160 | tf_op jit(solution)/shard_map/ppermute | solution.py:468
  34.1 7.6 %collective-permute-start.5 = (bf16[64,128]{1,0:T(8,128)(2,1)S(1)}, bf16[64,128]{1,0:T(8,128)(2,1)S(1)}, u32[]{:S(2)}, u32[]{:S(2)}) collective-permute-start(bf16[64,128]{1,0:T(8,128)(2,1)S(1)} %get-tuple-element.43.refs_4_), channel_id=1, source_target_pairs={{0,3},{1,2},{2,1},{3,0},{4,7},{5,6},{6,5},{7,4},{8,11},{9,10},{10,... | collective-permute-start | bytes 49160 | tf_op jit(solution)/shard_map/ppermute | solution.py:468
  42.8 1.9 %collective-permute-start.6 = (bf16[192,128]{1,0:T(8,128)(2,1)S(1)}, bf16[192,128]{1,0:T(8,128)(2,1)S(1)}, u32[]{:S(2)}, u32[]{:S(2)}) collective-permute-start(bf16[192,128]{1,0:T(8,128)(2,1)S(1)} %get-tuple-element.45), channel_id=1, source_target_pairs={{0,1},{1,0},{2,3},{3,2},{4,5},{5,4},{6,7},{7,6},{8,9},{9,8},{10,11... | collective-permute-start | bytes 147464 | tf_op jit(solution)/shard_map/ppermute | solution.py:468
  42.8 4.6 %collective-permute-start.7 = (bf16[192,128]{1,0:T(8,128)(2,1)S(1)}, bf16[192,128]{1,0:T(8,128)(2,1)S(1)}, u32[]{:S(2)}, u32[]{:S(2)}) collective-permute-start(bf16[192,128]{1,0:T(8,128)(2,1)S(1)} %get-tuple-element.46), channel_id=1, source_target_pairs={{0,2},{1,3},{2,0},{3,1},{4,6},{5,7},{6,4},{7,5},{8,10},{9,11},{10,... | collective-permute-start | bytes 147464 | tf_op jit(solution)/shard_map/ppermute | solution.py:468
  42.9 4.7 %collective-permute-start.8 = (bf16[192,128]{1,0:T(8,128)(2,1)S(1)}, bf16[192,128]{1,0:T(8,128)(2,1)S(1)}, u32[]{:S(2)}, u32[]{:S(2)}) collective-permute-start(bf16[192,128]{1,0:T(8,128)(2,1)S(1)} %get-tuple-element.47), channel_id=1, source_target_pairs={{0,3},{1,2},{2,1},{3,0},{4,7},{5,6},{6,5},{7,4},{8,11},{9,10},{10,... | collective-permute-start | bytes 147464 | tf_op jit(solution)/shard_map/ppermute | solution.py:468

commit v3 on v2

--- a/solution.py
+++ b/solution.py
@@ -21,25 +21,32 @@
 OPPOSITE = (1, 0, 3, 2)
 LATERAL = ((2, 3), (2, 3), (0, 1), (0, 1))
 DEPTH = SUBCYCLES
+SIDE_ROWS = 16 * DEPTH
+PUSH_ROWS = 8 * DEPTH
+NAMES_ROW = 4 * DEPTH - 1
 TILE_ROWS = 16
 F32 = jnp.float32
 BF16 = jnp.bfloat16
 VMEM_LIMIT = 16 * 1024 * 1024
-
-
-def call(kernel, outs, args, scratch=(), smem=(), flops=1_000_000):
-    specs = [
-        pl.BlockSpec(memory_space=pltpu.SMEM if i in smem else pltpu.VMEM) for i in range(len(args))
-    ]
+FLOPS_PER_MICRO = 1.15e9
+
+
+def call(kernel, outs, args, scratch=(), smem=(), hbm=(), out_space=pltpu.VMEM, grant=VMEM_LIMIT, micros=0.01):
+    def space(i):
+        return pltpu.SMEM if i in smem else pltpu.HBM if i in hbm else pltpu.VMEM
+
+    specs = [pl.BlockSpec(memory_space=space(i)) for i in range(len(args))]
     size = sum(a.size * a.dtype.itemsize for a in args)
     return pl.pallas_call(
         kernel,
         out_shape=outs,
         in_specs=specs,
-        out_specs=jax.tree.map(lambda _: pl.BlockSpec(memory_space=pltpu.VMEM), outs),
+        out_specs=jax.tree.map(lambda _: pl.BlockSpec(memory_space=out_space), outs),
         scratch_shapes=list(scratch),
-        compiler_params=pltpu.CompilerParams(vmem_limit_bytes=VMEM_LIMIT),
-        cost_estimate=pl.CostEstimate(flops=flops, bytes_accessed=size, transcendentals=0),
+        compiler_params=pltpu.CompilerParams(vmem_limit_bytes=grant),
+        cost_estimate=pl.CostEstimate(
+            flops=int(micros * FLOPS_PER_MICRO), bytes_accessed=size, transcendentals=0
+        ),
     )(*args)
 
 
@@ -55,30 +62,53 @@
     return jnp.where(condition, 1.0, 0.0).astype(F32)
 
 
-def forward_kernel(group, blocks, rows, cols, currents, *outs):
-    side = rows.shape[1]
-    depth = cols.shape[1]
-    devices = group[0]
-    members = group[1]
-    me = group[2]()
-    fields = [currents[c].astype(BF16) for c in range(2)]
-    pairs = rows.shape[0]
+def forward_kernel(group, blocks_h, rows_h, cols_h, currents_h, *refs):
+    devices, members, place = group
+    outs, (blocks, currents, fields, arrived, left) = refs[:members], refs[members:]
+    pairs, side, width = rows_h.shape
+    depth = cols_h.shape[1]
+    names = pltpu.make_async_copy(blocks_h, blocks, arrived.at[0])
+    water = pltpu.make_async_copy(currents_h, currents, arrived.at[1])
+    names.start()
+    water.start()
+    names.wait()
+    me = place()
+    owners = [lax.rem(lax.rem(blocks[0, m], devices), members) for m in range(pairs)]
+    copies = []
     for k, out in enumerate(outs):
         partner = me ^ k
-        pair = jnp.int32(0)
-        found = jnp.int32(0)
+        pair, found = jnp.int32(0), jnp.int32(0)
         for m in range(pairs):
-            owner = lax.rem(lax.rem(blocks[0, m], devices), members)
-            pair = jnp.where(owner == partner, m, pair)
-            found = jnp.where(owner == partner, 1, found)
-        if pairs == members:
-            out[0:side] = rows[pair]
-            out[side : side + depth] = cols[pair]
+            pair = jnp.where(owners[m] == partner, m, pair)
+            found = jnp.where(owners[m] == partner, 1, found)
+        copies.append(
+            pltpu.make_async_copy(rows_h.at[pair], out.at[pl.ds(0, side)], left.at[3 * k])
+        )
+        copies.append(
+            pltpu.make_async_copy(cols_h.at[pair], out.at[pl.ds(side, depth)], left.at[3 * k + 1])
+        )
+        if pairs < members:
+            keep = jnp.where(found > 0, 1.0, 0.0).astype(F32)
         else:
-            out[0:side] = jnp.where(found > 0, rows[pair].astype(F32), 0.0).astype(BF16)
-            out[side : side + depth] = jnp.where(found > 0, cols[pair].astype(F32), 0.0).astype(BF16)
-        for c in range(2):
-            out[side + depth + c * side : side + depth + (c + 1) * side] = fields[c]
+            keep = None
+        copies[-2].start()
+        copies[-1].start()
+        if k == 0:
+            water.wait()
+        if k == 0 or keep is not None:
+            for c in range(2):
+                field = currents[c] if keep is None else currents[c] * keep
+                fields[0 if keep is None else k, c * side : (c + 1) * side] = field.astype(BF16)
+        copies.append(
+            pltpu.make_async_copy(
+                fields.at[0 if keep is None else k],
+                out.at[pl.ds(side + depth, 2 * side)],
+                left.at[3 * k + 2],
+            )
+        )
+        copies[-1].start()
+    for copy in copies:
+        copy.wait()
 
 
 def put_side_rims(store, planes, at):
@@ -101,11 +131,9 @@
 
 
 def rims_kernel(
-    where_am_i, links, thick, conc, ice, water, out, viscous_o, gain_o, mass_o, drag_o, conduct_o,
+    links, thick, conc, ice, water, out, cols_o, viscous_o, gain_o, mass_o, drag_o, conduct_o,
     speed_o, store,
 ):
-    tile_count, sub_count, lev_count, place = where_am_i
-    my_tile, my_sub, my_lev = place()
     size = thick.shape[1]
     cover = jnp.zeros((size, size), F32)
     volume = jnp.zeros((size, size), F32)
@@ -128,55 +156,54 @@
     conduct_o[...] = -HEAT_RATE * conduct
     speed_o[0] = speed_x
     speed_o[1] = speed_y
-    side_rows = 4 * 4 * DEPTH
     put_side_rims(store, [speed_x, speed_y, viscous, gain], lambda side: side * 4 * DEPTH)
-    rim_rows = store[0:side_rows].astype(BF16)
-    for d in range(out.shape[0]):
-        out[d, 0:side_rows] = rim_rows
+    line = iota((1, size), 1)
+    names = jnp.zeros((1, size), F32)
+    for q in range(4):
+        names = jnp.where(line == q, (links[0, 0, q] >> 7).astype(F32), names)
+        names = jnp.where(line == 4 + q, (links[0, 0, q] & 127).astype(F32), names)
+    store[NAMES_ROW : NAMES_ROW + 1] = names
     levels, rows, width = water.shape
+    start = SIDE_ROWS
+    for l in range(levels):
+        for j in range(2):
+            at = start + 2 * l + j
+            store[at : at + 1] = water[l, rows - 1 - j : rows - j]
+            store[at + 2 * levels : at + 2 * levels + 1] = water[l, j : j + 1]
+    out[...] = store[...].astype(BF16)
     lane = iota((rows, width), 1)
     mixed = jnp.zeros((rows, width), F32)
     for l in range(levels):
         mixed = jnp.where(lane // 4 == l, roll(water[l], 2 + 4 * l, 1), mixed)
     across = jnp.concatenate([mixed, jnp.zeros((width - rows, width), F32)], axis=0).T
-    row_lane = iota((1, width), 1)
-    names = jnp.zeros((1, width), F32)
-    for q in range(4):
-        high = links[0, 0, q] >> 7
-        low = links[0, 0, q] & 127
-        names = jnp.where(row_lane == q, high.astype(F32), names)
-        names = jnp.where(row_lane == 4 + q, low.astype(F32), names)
-    spare = out.shape[1] - side_rows
-    blank = jnp.concatenate(
-        [jnp.zeros((2 * levels, width), F32), names, jnp.zeros((spare - 2 * levels - 1, width), F32)]
-    )
-    empty = blank.astype(BF16)
-    for d in range(out.shape[0]):
-        out[d, side_rows:] = empty
-    tail = blank[2 * levels :]
-    for dt in (-1, 0, 1):
-        for ds in (-1, 0, 1):
-            if dt == 0 and ds == 0:
-                continue
-            strip = []
-            for l in range(levels):
-                for j in range(2):
-                    r = rows - 1 - j if dt > 0 else j
-                    if ds == 0:
-                        strip.append(water[l, r : r + 1])
-                    elif dt == 0:
-                        at = 4 * l + (1 - j if ds > 0 else 2 + j)
-                        strip.append(across[at : at + 1])
-                    else:
-                        line = water[l, r : r + 1]
-                        strip.append(roll(line, 1, 1) if ds > 0 else line)
-            message = jnp.concatenate(strip + [tail], axis=0).astype(BF16)
-            to_tile, to_sub = my_tile + dt, my_sub + ds
-            inside = (to_tile >= 0) & (to_tile < tile_count) & (to_sub >= 0) & (to_sub < sub_count)
-
-            @pl.when(inside)
-            def _():
-                out[(to_tile * sub_count + to_sub) * lev_count + my_lev, side_rows:] = message
+    beside = []
+    for l in range(levels):
+        for j in range(2):
+            last = across[4 * l + 1 - j : 4 * l + 2 - j]
+            lead = across[4 * l + 2 + j : 4 * l + 3 + j]
+            beside.append(jnp.where(line < rows, last, roll(lead, rows, 1)))
+    cols_o[...] = jnp.concatenate(beside, axis=0)
+
+
+def relay_kernel(tiles, place, cols, *refs):
+    messages, out = refs[:tiles], refs[tiles]
+    for k, message in enumerate(messages):
+        out[k * SIDE_ROWS : (k + 1) * SIDE_ROWS] = message[0:SIDE_ROWS]
+    levels = cols.shape[0] // 2
+    before, after = around(place(), tiles, messages, levels)
+    rows = []
+    for strip in (before, after):
+        rows += [strip[2 * l : 2 * l + 1] for l in range(levels)]
+    out[tiles * SIDE_ROWS :] = jnp.concatenate([cols[...]] + rows, axis=0).astype(BF16)
+
+
+def around(me, tiles, messages, levels):
+    before, after = 0.0, 0.0
+    for k in range(1, tiles):
+        strips = messages[k][SIDE_ROWS : SIDE_ROWS + 4 * levels].astype(F32)
+        before = before + strips[: 2 * levels] * flag((me > 0) & ((me ^ k) == me - 1))
+        after = after + strips[2 * levels :] * flag((me < tiles - 1) & ((me ^ k) == me + 1))
+    return before, after
 
 
 def remap_forward(chunks, field_rows, side, depth):
@@ -216,25 +243,42 @@
         push_o[c] = push
         pushes.append(push)
     put_side_rims(store, pushes, lambda q: q * 2 * DEPTH)
-    message = store[...].astype(BF16)
-    for d in range(out.shape[0]):
-        out[d] = message
-
-
-def ocean_kernel(where_am_i, strip_at, water, mixing, rims, warm_o, top_o):
-    tile_count, sub_count, lev_count, place = where_am_i
-    my_tile, my_sub, my_lev = place()
+    out[...] = store[...].astype(BF16)
+
+
+def ocean_kernel(counts, tile_place, member_place, water, mixing, *refs):
+    tiles, subs, levs = counts
+    members = subs * levs
+    messages, relays = refs[:tiles], refs[tiles : tiles + members]
+    warm_o, top_o, table_o = refs[tiles + members :]
     levels, rows, width = water.shape
+    my_tile, me = tile_place(), member_place()
     halo = {}
-    for dt in (-1, 0, 1):
-        for ds in (-1, 0, 1):
-            if dt == 0 and ds == 0:
-                continue
-            t, s = my_tile + dt, my_sub + ds
-            inside = (t >= 0) & (t < tile_count) & (s >= 0) & (s < sub_count)
-            device = jnp.where(inside, (t * sub_count + s) * lev_count + my_lev, 0)
-            strip = rims[device, strip_at : strip_at + TILE_ROWS].astype(F32)[: 2 * levels]
-            halo[dt, ds] = strip * flag(inside)
+    halo[-1, 0], halo[1, 0] = around(my_tile, tiles, messages, levels)
+    for ds in (-1, 1):
+        beyond = me + ds * levs
+        inside = (beyond >= 0) & (beyond < members)
+        found = 0.0
+        for k in range(1, members):
+            strip = relays[k][tiles * SIDE_ROWS : tiles * SIDE_ROWS + 4 * levels].astype(F32)
+            found = found + strip * flag(inside & ((me ^ k) == beyond))
+        beside, corners = found[: 2 * levels], found[2 * levels :]
+        if ds > 0:
+            beside = roll(beside, -rows, 1)
+        halo[0, ds] = beside
+        at = width - 1 if ds < 0 else 0
+        halo[-1, ds] = corners[:levels, at : at + 1]
+        halo[1, ds] = corners[levels:, at : at + 1]
+    mine = my_tile * members + me
+    column = iota((table_o.shape[0], width), 1)
+    names = []
+    for k in range(tiles):
+        for m in range(members):
+            at = k * SIDE_ROWS
+            names.append(relays[m][at : at + TILE_ROWS].astype(F32)[NAMES_ROW : NAMES_ROW + 1])
+    names = jnp.concatenate(names, axis=0)
+    table = (128.0 * names + roll(names, -4, 1)).astype(jnp.int32)
+    table_o[...] = jnp.where((table >= 0) & (column < 4), table ^ mine, -1)
     left_cols = halo[0, -1].T
     right_cols = halo[0, 1].T
     row = iota((rows, width), 0)
@@ -259,7 +303,7 @@
         corner = {}
         for dt in (-1, 1):
             for ds in (-1, 1):
-                corner[dt, ds] = halo[dt, ds][near : near + 1, 0:1]
+                corner[dt, ds] = halo[dt, ds][l : l + 1]
 
         def ring_row(mid, out_row, in_row, dt):
             west = jnp.where(line == 0, corner[dt, -1], roll(mid, 1, 1))
@@ -282,11 +326,17 @@
         warm = x - mixing[...] * twice
         warm_o[l] = warm
         total = warm if total is None else total + warm
-    top_o[...] = (total / (levels * lev_count)).astype(top_o.dtype)
-
-
-def subcycles_kernel(me, table, viscous, gain, speed, push, rims, push_rims, out, flat_o):
+    top_o[...] = (total / (levels * levs)).astype(top_o.dtype)
+
+
+def subcycles_kernel(tiles, members, table, viscous, gain, speed, push, *refs):
+    relays, push_relays = refs[:members], refs[members : 2 * members]
+    out, rims, push_rims = refs[2 * members :]
     size = viscous.shape[0]
+    for k in range(tiles):
+        for m in range(members):
+            rims[k * members + m] = relays[m][k * SIDE_ROWS : (k + 1) * SIDE_ROWS]
+            push_rims[k * members + m] = push_relays[m][k * PUSH_ROWS : (k + 1) * PUSH_ROWS]
     half = DEPTH
     high = 2 * DEPTH
     sub = iota((high, size), 0)
@@ -319,7 +369,7 @@
 
     strips = []
     for q in range(4):
-        x, has_x = follow(me(), q)
+        x, has_x = follow(0, q)
         strip = load(x, OPPOSITE[q], flag(has_x))
         sides = []
         for s in LATERAL[q]:
@@ -397,8 +447,6 @@
         vx, vy = new_x, new_y
     out[0] = vx
     out[1] = vy
-    flat_o[pl.ds(0, size, stride=2), :] = vx
-    flat_o[pl.ds(1, size, stride=2), :] = vy
 
 
 def back_kernel(group, side, drag, conduct, current, speed, *refs):
@@ -420,17 +468,33 @@
         out[...] = reply.astype(BF16)
 
 
-def finish_kernel(warm, currents, *refs):
-    replies, (heat_o, current_o) = refs[:-2], refs[-2:]
+def finish_kernel(warm, currents, speed, *refs):
+    outs, (flat, heat_v, current_v, left) = refs[-7:-4], refs[-4:]
+    replies = refs[:-7]
+    flat_o, heat_o, current_o = outs
+    size = speed.shape[1]
+    copies = [
+        pltpu.make_async_copy(source, target, left.at[i])
+        for i, (source, target) in enumerate(
+            ((flat, flat_o), (heat_v, heat_o), (current_v, current_o))
+        )
+    ]
+    for c in range(2):
+        flat[pl.ds(c, size, stride=2), :] = speed[c]
+    copies[0].start()
     total = replies[0][...].astype(F32)
     for reply in replies[1:]:
         total = total + reply[...].astype(F32)
     side = currents.shape[1]
     heat = THERMAL_DIFFUSE * total[0:side]
     for l in range(warm.shape[0]):
-        heat_o[l] = warm[l] + heat
+        heat_v[l] = warm[l] + heat
+    copies[1].start()
     for c in range(2):
-        current_o[c] = currents[c] + STRESS_MIXING * total[(c + 1) * side : (c + 2) * side]
+        current_v[c] = currents[c] + STRESS_MIXING * total[(c + 1) * side : (c + 2) * side]
+    copies[2].start()
+    for copy in copies:
+        copy.wait()
 
 
 def shards(
@@ -455,17 +519,22 @@
     pairs, size = remap_rows.shape[1:3]
     categories = thickness.shape[2]
 
-    def place():
-        return tuple(lax.axis_index(a) for a in member_axes)
-
-    def group_place():
+    def tile_place():
+        return lax.axis_index("tile")
+
+    def member_place():
         return lax.axis_index("sub") * lev_count + lax.axis_index("lev")
 
-    def device_place():
-        return lax.axis_index("tile") * group + group_place()
-
-    def swap(value, k):
-        return lax.ppermute(value, group_axes, [(i, i ^ k) for i in range(group)])
+    def swap(value, axes, count):
+        return [value] + [
+            lax.ppermute(value, axes, [(i, i ^ k) for i in range(count)]) for k in range(1, count)
+        ]
+
+    def swap_each(values):
+        return [values[0]] + [
+            lax.ppermute(values[k], group_axes, [(i, i ^ k) for i in range(group)])
+            for k in range(1, group)
+        ]
 
     def shape(*dims, dtype=F32):
         return jax.ShapeDtypeStruct(dims, dtype)
@@ -473,60 +542,86 @@
     def interleaved(value):
         return value.reshape(2, size, size).transpose(1, 0, 2).reshape(2 * size, size)
 
-    grid = (tile_count, sub_count, lev_count, place)
     plane = shape(size, size)
     planes = shape(2, size, size)
     wind = interleaved(wind_stress)
 
     chunk_rows = 3 * side + width
     sent = call(
-        functools.partial(forward_kernel, (devices, group, group_place)),
+        functools.partial(forward_kernel, (devices, group, member_place)),
         [shape(chunk_rows, width, dtype=BF16)] * group,
         (remap_blocks, remap_rows[0].swapaxes(1, 2), remap_cols[0], upper_current_vector),
-        smem=(0,),
-    )
-    chunks = [sent[0]] + [swap(sent[k], k) for k in range(1, group)]
-
-    side_rows = 16 * DEPTH
-    message_rows = side_rows + -(-(2 * levels + 1) // TILE_ROWS) * TILE_ROWS
-    message, viscous, gain, step_mass, drag, conduct, speed = call(
-        functools.partial(rims_kernel, grid),
-        [shape(devices, message_rows, size, dtype=BF16)] + [plane] * 5 + [planes],
+        scratch=[
+            pltpu.SMEM((1, pairs), jnp.int32),
+            pltpu.VMEM((2, side, width), F32),
+            pltpu.VMEM((1 if pairs == group else group, 2 * side, width), BF16),
+            pltpu.SemaphoreType.DMA((2,)),
+            pltpu.SemaphoreType.DMA((3 * group,)),
+        ],
+        hbm=(0, 1, 2, 3),
+        grant=60 * 2**20,
+        micros=2,
+    )
+    chunks = swap_each(sent)
+
+    links, sent = lax.optimization_barrier((neighbors, sent))
+    message, cols, viscous, gain, step_mass, drag, conduct, speed = call(
+        rims_kernel,
+        [shape(SIDE_ROWS + 4 * levels, size, dtype=BF16), shape(2 * levels, width)]
+        + [plane] * 5
+        + [planes],
         (
-            neighbors,
+            links,
             thickness.reshape(categories, size, size),
             concentration.reshape(categories, size, size),
             interleaved(ice_velocity),
             water_heat_state,
         ),
-        scratch=[pltpu.VMEM((side_rows, size), F32)],
+        scratch=[pltpu.VMEM((SIDE_ROWS + 4 * levels, size), F32)],
         smem=(0,),
     )
-    rims = lax.all_to_all(message, member_axes, split_axis=0, concat_axis=0, tiled=True)
+    messages = swap(message, "tile", tile_count)
 
     push_message, current_ice, push = call(
         functools.partial(forcing_kernel, group, side),
-        [shape(devices, 8 * DEPTH, size, dtype=BF16), planes, planes],
+        [shape(PUSH_ROWS, size, dtype=BF16), planes, planes],
         (step_mass, drag, wind, *chunks),
-        scratch=[pltpu.VMEM((8 * DEPTH, size), F32)],
-    )
-    push_rims = lax.all_to_all(push_message, member_axes, split_axis=0, concat_axis=0, tiled=True)
-
-    warm, top = call(
-        functools.partial(ocean_kernel, grid, side_rows),
-        [shape(levels, side, width), shape(side, width, dtype=BF16 if lev_count == 1 else F32)],
-        (water_heat_state, diffusion_coefficient, rims),
+        scratch=[pltpu.VMEM((PUSH_ROWS, size), F32)],
+    )
+    cols, push_message = lax.optimization_barrier((cols, push_message))
+    push_messages = swap(push_message, "tile", tile_count)
+
+    relay = call(
+        functools.partial(relay_kernel, tile_count, tile_place),
+        shape(tile_count * SIDE_ROWS + 4 * levels, size, dtype=BF16),
+        (cols, *messages),
+    )
+    relays = swap(relay, group_axes, group)
+    push_relays = swap(jnp.concatenate(push_messages, axis=0), group_axes, group)
+
+    warm, top, table = call(
+        functools.partial(
+            ocean_kernel, (tile_count, sub_count, lev_count), tile_place, member_place
+        ),
+        [
+            shape(levels, side, width),
+            shape(side, width, dtype=BF16 if lev_count == 1 else F32),
+            shape(devices, width, dtype=jnp.int32),
+        ],
+        (water_heat_state, diffusion_coefficient, *messages, *relays),
     )
     if lev_count > 1:
         top = lax.psum(top, "lev").astype(BF16)
-    tops = [top] + [swap(top, k) for k in range(1, group)]
-
-    names = rims[:, side_rows + 2 * levels, 0:8].astype(jnp.int32)
-    table = names[:, 0:4] * 128 + names[:, 4:8]
-    speed, flat = call(
-        functools.partial(subcycles_kernel, device_place),
-        [planes, shape(2 * size, size)],
-        (table, viscous, gain, speed, push, rims, push_rims),
+    tops = swap(top, group_axes, group)
+
+    speed = call(
+        functools.partial(subcycles_kernel, tile_count, group),
+        planes,
+        (table, viscous, gain, speed, push, *relays, *push_relays),
+        scratch=[
+            pltpu.VMEM((devices, SIDE_ROWS, size), BF16),
+            pltpu.VMEM((devices, PUSH_ROWS, size), BF16),
+        ],
         smem=(0,),
     )
 
@@ -535,13 +630,20 @@
         [shape(3 * side, width, dtype=BF16)] * group,
         (drag, conduct, current_ice, speed, *chunks, *tops),
     )
-    replies = [replies[0]] + [swap(replies[k], k) for k in range(1, group)]
+    replies = swap_each(replies)
     if lev_count > 1:
         replies = [lax.psum(sum(r.astype(F32) for r in replies), "lev")]
-    heat, current = call(
+    flat, heat, current = call(
         finish_kernel,
-        [shape(levels, side, width), shape(2, side, width)],
-        (warm, upper_current_vector, *replies),
+        [shape(2 * size, size), shape(levels, side, width), shape(2, side, width)],
+        (warm, upper_current_vector, speed, *replies),
+        scratch=[
+            pltpu.VMEM((2 * size, size), F32),
+            pltpu.VMEM((levels, side, width), F32),
+            pltpu.VMEM((2, side, width), F32),
+            pltpu.SemaphoreType.DMA((3,)),
+        ],
+        out_space=pltpu.HBM,
     )
     velocity = flat.reshape(size, 2, size).transpose(1, 0, 2).reshape(1, 1, 2, size * size)
     return heat, current, velocity

time: 48.7 us -> 36.6 us (0.75)
  waiting for transfers between devices: 14.1 us -> 6.08 us
  local copies, waits for them, and re-layouts: 5.04 us -> 0.69 us
    ppermute x9 -> x21, starting transfers between devices: 6.17 us -> 19.6 us  [the longest x15 14.6 us: swap(): lax.ppermute(value, axes, [(i, i ^ k) for i in range(count)])]
    all_to_all x2 -> x0, starting transfers between devices: 13 us -> none  [the longest x1 7.49 us: shards(): lax.all_to_all(message, member_axes, split_axis=0, concat_axis=0, tiled=T...]
    all_to_all x2 -> x0, waiting for transfers between devices: 5.01 us -> none  [the longest x1 4.73 us: shards(): lax.all_to_all(push_message, member_axes, split_axis=0, concat_axis=0, ti...]
    unnamed x24 -> x21, local copies, waits for them, and re-layouts: 5.04 us -> 0.68 us
    ppermute x9 -> x21, waiting for transfers between devices: 9.07 us -> 6.08 us  [the longest x6 3.08 us: swap_each(): lax.ppermute(values[k], group_axes, [(i, i ^ k) for i in range(group)])]
    pallas_call x7 -> x8, Pallas kernels: 9.12 us -> 9.22 us  [call(): pl.pallas_call(kernel, out_shape=outs, in_specs=specs, out_specs=jax.tree...]
  transfers between devices with their start and end apart: 11 -> 21, of which waited for: 6 -> 6; matrix products, arithmetic and copies ran while one was open for 0% -> 0% of each run, Pallas kernels for 11% -> 13%
where the time goes in v3:
time: 36.6 us; the launch traced here: 36.4 us
  starting transfers between devices  19.6 us (54%)
  Pallas kernels  9.22 us (25%)
  waiting for transfers between devices  6.08 us (17%)
  between operations  0.78 us (2%)
  local copies, waits for them, and re-layouts  0.69 us (2%)
    ppermute x15, starting transfers between devices, swap(): lax.ppermute(value, axes, [(i, i ^ k) for i in range(count)])  14.6 us
    pallas_call x8, Pallas kernels, call(): pl.pallas_call(kernel, out_shape=outs, in_specs=specs, out_specs=jax.tree...  9.22 us
    ppermute x6, starting transfers between devices, swap_each(): lax.ppermute(values[k], group_axes, [(i, i ^ k) for i in range(group)])  5.01 us
    ppermute x6, waiting for transfers between devices, swap_each(): lax.ppermute(values[k], group_axes, [(i, i ^ k) for i in range(group)])  3.08 us
    ppermute x15, waiting for transfers between devices, swap(): lax.ppermute(value, axes, [(i, i ^ k) for i in range(count)])  3 us
  transfers between devices with their start and end apart: 21, of which 6 were waited for; matrix products, arithmetic and copies ran while one was open for 0% of the time, Pallas kernels for 13%

profile of v3, /device:TPU:0, one launch (start us, length us, event | category | flops | bytes accessed | tf_op | source)
XLA Modules:
  0.0 36.4 jit_solution(8054405847413850978)
XLA Ops:
  0.6 0.0 copy-start
  0.6 0.0 copy-start.1
  0.7 0.0 copy-start.2
  0.7 0.0 copy-start.4
  0.7 2.7 %shard_map.130 = (bf16[320,128]{1,0:T(8,128)(2,1)}, bf16[320,128]{1,0:T(8,128)(2,1)}, bf16[320,128]{1,0:T(8,128)(2,1)}, bf16[320,128]{1,0:T(8,128)(2,1)}) custom-call(s32[1,4]{1,0:T(1,128)} %blocks_h.1, bf16[4,64,128]{2,1,0:T(8,128)(2,1)} %bitcast.27, bf16[4,128,128]{2,1,0:T(8,128)(2,1)} %bitcast.25, f32[2,64,128]{2,1,0:T(8,128)} %currents.1), custom_call_target="tpu_custom_call" | custom-call | flops 2300000000 | bytes 262160 | tf_op jit(solution)/shard_map/pallas_call | solution.py:40
  3.3 0.5 %collective-permute-start.3 = (bf16[320,128]{1,0:T(8,128)(2,1)}, bf16[320,128]{1,0:T(8,128)(2,1)S(1)}, u32[]{:S(2)}, u32[]{:S(2)}) collective-permute-start(bf16[320,128]{1,0:T(8,128)(2,1)} %get-tuple-element.32), channel_id=1, source_target_pairs={{0,1},{1,0},{2,3},{3,2},{4,5},{5,4},{6,7},{7,6},{8,9},{9,8},{10,11... | collective-permute-start | bytes 245768 | tf_op jit(solution)/shard_map/ppermute | solution.py:535
  3.9 2.6 %collective-permute-start.4 = (bf16[320,128]{1,0:T(8,128)(2,1)}, bf16[320,128]{1,0:T(8,128)(2,1)S(1)}, u32[]{:S(2)}, u32[]{:S(2)}) collective-permute-start(bf16[320,128]{1,0:T(8,128)(2,1)} %get-tuple-element.33), channel_id=1, source_target_pairs={{0,2},{1,3},{2,0},{3,1},{4,6},{5,7},{6,4},{7,5},{8,10},{9,11},{10,... | collective-permute-start | bytes 245768 | tf_op jit(solution)/shard_map/ppermute | solution.py:535
  6.4 0.1 collective-permute-start.5
  6.5 0.0 copy-start.8
  6.5 0.0 copy-done
  6.5 0.0 copy-done.1
  6.5 0.0 copy-done.2
  6.5 0.0 copy-done.4
  6.5 0.6 %copy-done.8 = s32[1,1,4]{2,1,0:T(1,128)S(1)} copy-done((s32[1,1,4]{2,1,0:T(1,128)S(1)}, s32[1,1,4]{2,1,0:T(1,128)}, u32[]{:S(2)}) %copy-start.8) | copy-done | bytes 40
  7.2 0.9 %shard_map.131 = (bf16[80,128]{1,0:T(8,128)(2,1)S(1)}, f32[8,128]{1,0:T(8,128)S(1)}, f32[128,128]{1,0:T(8,128)S(1)}, f32[128,128]{1,0:T(8,128)S(1)}, f32[128,128...) custom-call(s32[1,1,4]{2,1,0:T(1,128)S(1)} %copy-done.8, ...), custom_call_target="tpu_custom_call" | custom-call | flops 11500000 | bytes 917520 | tf_op jit(solution)/shard_map/pallas_call | solution.py:40
  8.1 3.9 %collective-permute-start.2 = (bf16[80,128]{1,0:T(8,128)(2,1)S(1)}, bf16[80,128]{1,0:T(8,128)(2,1)S(1)}, u32[]{:S(2)}, u32[]{:S(2)}) collective-permute-start(bf16[80,128]{1,0:T(8,128)(2,1)S(1)} %get-tuple-element.36.refs_0_), channel_id=1, source_target_pairs={{0,12},{4,8},{8,4},{12,0},{1,13},{5,9},{9,5},{13,1},{2,14},{6,10},... | collective-permute-start | bytes 61448 | tf_op jit(solution)/shard_map/ppermute | solution.py:530
  12.0 0.0 collective-permute-start.1
  12.0 0.0 collective-permute-done.3.refs_1_
  12.0 0.6 %collective-permute-start = (bf16[80,128]{1,0:T(8,128)(2,1)S(1)}, bf16[80,128]{1,0:T(8,128)(2,1)S(1)}, u32[]{:S(2)}, u32[]{:S(2)}) collective-permute-start(bf16[80,128]{1,0:T(8,128)(2,1)S(1)} %get-tuple-element.36.refs_0_), channel_id=1, source_target_pairs={{0,4},{4,0},{8,12},{12,8},{1,5},{5,1},{9,13},{13,9},{2,6},{6,2},{1... | collective-permute-start | bytes 61448 | tf_op jit(solution)/shard_map/ppermute | solution.py:530
  12.6 0.0 collective-permute-done.4.refs_2_
  12.6 0.0 collective-permute-done.5.refs_3_
  12.6 0.0 copy-done.3
  12.7 0.0 copy-done.5
  12.7 0.6 %shard_map.132 = (bf16[32,128]{1,0:T(8,128)(2,1)S(1)}, f32[2,128,128]{2,1,0:T(8,128)S(1)}, f32[2,128,128]{2,1,0:T(8,128)S(1)}) custom-call(f32[128,128]{1,0:T(8,128)S(1)} %get-tuple-element.38.mass, f32[128,128]{1,0:T(8,128)S(1)} %get-tuple-element.39.drag, f32[256,128]{1,0:T(8,128)S(1)} %bitcast.24, bf16[320,128]{1,0:T(8,128)(2,1)S(1)} %copy-done.3, ...), custom_call_target="tpu_custom_call" | custom-call | flops 11500000 | bytes 589824 | tf_op jit(solution)/shard_map/pallas_call | solution.py:40
  13.2 3.8 %collective-permute-start.11 = (bf16[32,128]{1,0:T(8,128)(2,1)S(1)}, bf16[32,128]{1,0:T(8,128)(2,1)S(1)}, u32[]{:S(2)}, u32[]{:S(2)}) collective-permute-start(bf16[32,128]{1,0:T(8,128)(2,1)S(1)} %get-tuple-element.48), channel_id=1, source_target_pairs={{0,12},{4,8},{8,4},{12,0},{1,13},{5,9},{9,5},{13,1},{2,14},{6,10},... | collective-permute-start | bytes 24584 | tf_op jit(solution)/shard_map/ppermute | solution.py:530
  17.0 0.0 collective-permute-start.9
  17.0 0.0 collective-permute-done.2.refs_3_
  17.0 0.6 %collective-permute-start.10 = (bf16[32,128]{1,0:T(8,128)(2,1)S(1)}, bf16[32,128]{1,0:T(8,128)(2,1)S(1)}, u32[]{:S(2)}, u32[]{:S(2)}) collective-permute-start(bf16[32,128]{1,0:T(8,128)(2,1)S(1)} %get-tuple-element.48), channel_id=1, source_target_pairs={{0,8},{4,12},{8,0},{12,4},{1,9},{5,13},{9,1},{13,5},{2,10},{6,14},... | collective-permute-start | bytes 24584 | tf_op jit(solution)/shard_map/ppermute | solution.py:530
  17.7 0.0 collective-permute-done.1.refs_2_
  17.7 0.0 collective-permute-done.refs_1_
  17.7 0.0 copy-start.7
  17.7 0.1 collective-permute-start.8
  17.8 1.7 %collective-permute-start.7 = (bf16[272,128]{1,0:T(8,128)(2,1)S(1)}, bf16[272,128]{1,0:T(8,128)(2,1)S(1)}, u32[]{:S(2)}, u32[]{:S(2)}) collective-permute-start(bf16[272,128]{1,0:T(8,128)(2,1)S(1)} %shard_map.133.refs_4_.refs_0_), channel_id=1, source_target_pairs={{0,2},{1,3},{2,0},{3,1},{4,6},{5,7},{6,4},{7,5},{8,10},{9,11},{10,... | collective-permute-start | bytes 208904 | tf_op jit(solution)/shard_map/ppermute | solution.py:530
  19.5 1.2 %collective-permute-done.9 = bf16[32,128]{1,0:T(8,128)(2,1)S(1)} collective-permute-done((bf16[32,128]{1,0:T(8,128)(2,1)S(1)}, bf16[32,128]{1,0:T(8,128)(2,1)S(1)}, u32[]{:S(2)}, u32[]{:S(2)}) %collective-permute-start.9) | collective-permute-done | bytes 8224 | tf_op jit(solution)/shard_map/ppermute | solution.py:530
  20.7 0.0 collective-permute-start.6
  20.7 1.0 %collective-permute-done.10 = bf16[32,128]{1,0:T(8,128)(2,1)S(1)} collective-permute-done((bf16[32,128]{1,0:T(8,128)(2,1)S(1)}, bf16[32,128]{1,0:T(8,128)(2,1)S(1)}, u32[]{:S(2)}, u32[]{:S(2)}) %collective-permute-start.10) | collective-permute-done | bytes 8224 | tf_op jit(solution)/shard_map/ppermute | solution.py:530
  21.7 0.0 collective-permute-done.11
  21.7 0.7 %collective-permute-start.14 = (bf16[128,128]{1,0:T(8,128)(2,1)S(1)}, bf16[128,128]{1,0:T(8,128)(2,1)S(1)}, u32[]{:S(2)}, u32[]{:S(2)}) collective-permute-start(bf16[128,128]{1,0:T(8,128)(2,1)S(1)} %constant_dynamic-update-slice_fusion.refs_4_), channel_id=1, source_target_pairs={{0,3},{1,2},{2,1},{3,0},{4,7},{5,6},{6,5},{7,4},{8,11},{9,10},{10,... | collective-permute-start | bytes 98312 | tf_op jit(solution)/shard_map/ppermute | solution.py:530
  22.4 0.9 %collective-permute-start.13 = (bf16[128,128]{1,0:T(8,128)(2,1)S(1)}, bf16[128,128]{1,0:T(8,128)(2,1)S(1)}, u32[]{:S(2)}, u32[]{:S(2)}) collective-permute-start(bf16[128,128]{1,0:T(8,128)(2,1)S(1)} %constant_dynamic-update-slice_fusion.refs_4_), channel_id=1, source_target_pairs={{0,2},{1,3},{2,0},{3,1},{4,6},{5,7},{6,4},{7,5},{8,10},{9,11},{10,... | collective-permute-start | bytes 98312 | tf_op jit(solution)/shard_map/ppermute | solution.py:530
  23.3 0.0 collective-permute-done.8.refs_7_.refs_3_
  23.3 0.3 collective-permute-start.12
  23.6 0.2 collective-permute-done.7.refs_6_.refs_2_
  23.8 0.0 collective-permute-done.6.refs_5_.refs_1_
  23.8 0.0 copy-done.7
  23.8 1.0 %shard_map.134 = (f32[4,64,128]{2,1,0:T(8,128)S(1)}, bf16[64,128]{1,0:T(8,128)(2,1)S(1)}, s32[16,128]{1,0:T(8,128)S(1)}) custom-call(f32[4,64,128]{2,1,0:T(8,128)S(1)} %copy-done, f32[64,128]{1,0:T(8,128)S(1)} %copy-done.7, bf16[80,128]{1,0:T(8,128)(2,1)S(1)} %get-tuple-element.36.refs_0_, bf16[80,128]{1,0:T(8,128)(2,1)S(1)} %collective-permute-done.refs_1_, ...), custom_call_target="tpu_custom_call" | custom-call | flops 11500000 | bytes 524288 | tf_op jit(solution)/shard_map/pallas_call | solution.py:40
  24.8 1.0 %collective-permute-start.17 = (bf16[64,128]{1,0:T(8,128)(2,1)S(1)}, bf16[64,128]{1,0:T(8,128)(2,1)S(1)}, u32[]{:S(2)}, u32[]{:S(2)}) collective-permute-start(bf16[64,128]{1,0:T(8,128)(2,1)S(1)} %get-tuple-element.51.refs_4_), channel_id=1, source_target_pairs={{0,3},{1,2},{2,1},{3,0},{4,7},{5,6},{6,5},{7,4},{8,11},{9,10},{10,... | collective-permute-start | bytes 49160 | tf_op jit(solution)/shard_map/ppermute | solution.py:530
  25.8 0.7 %collective-permute-start.16 = (bf16[64,128]{1,0:T(8,128)(2,1)S(1)}, bf16[64,128]{1,0:T(8,128)(2,1)S(1)}, u32[]{:S(2)}, u32[]{:S(2)}) collective-permute-start(bf16[64,128]{1,0:T(8,128)(2,1)S(1)} %get-tuple-element.51.refs_4_), channel_id=1, source_target_pairs={{0,2},{1,3},{2,0},{3,1},{4,6},{5,7},{6,4},{7,5},{8,10},{9,11},{10,... | collective-permute-start | bytes 49160 | tf_op jit(solution)/shard_map/ppermute | solution.py:530
  26.6 0.0 collective-permute-done.14.refs_7_
  26.6 0.2 collective-permute-start.15
  26.7 0.0 collective-permute-done.13.refs_6_
  26.7 0.0 collective-permute-done.12.refs_5_
  26.7 2.1 %shard_map.135.speed = f32[2,128,128]{2,1,0:T(8,128)S(1)} custom-call(s32[16,128]{1,0:T(8,128)S(1)} %get-tuple-element.43.table, f32[128,128]{1,0:T(8,128)S(1)} %get-tuple-element.44.viscous, f32[128,128]{1,0:T(8,128)S(1)} %get-tuple-element.45.gain, f32[2,128,128]{2,1,0:T(8,128)S(1)} %get-tuple-element.46.speed, f32[2,128,128]{2,1,0:T(8,128)S(1)} %get-tuple-element.47.push, ...), custom_call_target="tpu_custom_call" | custom-call | flops 11500000 | bytes 811008 | tf_op jit(solution)/shard_map/pallas_call | solution.py:40
  28.9 0.0 collective-permute-done.17.refs_7_
  28.9 0.7 %collective-permute-done.16.refs_6_ = bf16[64,128]{1,0:T(8,128)(2,1)S(1)} collective-permute-done((bf16[64,128]{1,0:T(8,128)(2,1)S(1)}, bf16[64,128]{1,0:T(8,128)(2,1)S(1)}, u32[]{:S(2)}, u32[]{:S(2)}) %collective-permute-start.16) | collective-permute-done | bytes 16416 | tf_op jit(solution)/shard_map/ppermute | solution.py:530
  29.6 0.0 collective-permute-done.15.refs_5_
  29.6 1.1 %shard_map.136 = (bf16[192,128]{1,0:T(8,128)(2,1)S(1)}, bf16[192,128]{1,0:T(8,128)(2,1)S(1)}, bf16[192,128]{1,0:T(8,128)(2,1)S(1)}, bf16[192,128]{1,0:T(8,128)(2,1)S(1)}) custom-call(f32[128,128]{1,0:T(8,128)S(1)} %get-tuple-element.39.drag, f32[128,128]{1,0:T(8,128)S(1)} %get-tuple-element.49.conduct, f32[2,128,128]{2,1,0:T(8,128)S(1)} %get-tuple-element.50.current, ...), custom_call_target="tpu_custom_call" | custom-call | flops 11500000 | bytes 786432 | tf_op jit(solution)/shard_map/pallas_call | solution.py:40
  30.7 0.0 collective-permute-start.18
  30.7 1.0 %collective-permute-start.19 = (bf16[192,128]{1,0:T(8,128)(2,1)S(1)}, bf16[192,128]{1,0:T(8,128)(2,1)S(1)}, u32[]{:S(2)}, u32[]{:S(2)}) collective-permute-start(bf16[192,128]{1,0:T(8,128)(2,1)S(1)} %get-tuple-element.54), channel_id=1, source_target_pairs={{0,2},{1,3},{2,0},{3,1},{4,6},{5,7},{6,4},{7,5},{8,10},{9,11},{10,... | collective-permute-start | bytes 147464 | tf_op jit(solution)/shard_map/ppermute | solution.py:535
  31.7 0.9 %collective-permute-start.20 = (bf16[192,128]{1,0:T(8,128)(2,1)S(1)}, bf16[192,128]{1,0:T(8,128)(2,1)S(1)}, u32[]{:S(2)}, u32[]{:S(2)}) collective-permute-start(bf16[192,128]{1,0:T(8,128)(2,1)S(1)} %get-tuple-element.55), channel_id=1, source_target_pairs={{0,3},{1,2},{2,1},{3,0},{4,7},{5,6},{6,5},{7,4},{8,11},{9,10},{10,... | collective-permute-start | bytes 147464 | tf_op jit(solution)/shard_map/ppermute | solution.py:535
  32.5 0.0 collective-permute-done.18.refs_1_
  32.6 2.6 %collective-permute-done.19.refs_2_ = bf16[192,128]{1,0:T(8,128)(2,1)S(1)} collective-permute-done((bf16[192,128]{1,0:T(8,128)(2,1)S(1)}, bf16[192,128]{1,0:T(8,128)(2,1)S(1)}, u32[]{:S(2)}, u32[]{:S(2)}) %collective-permute-start.19) | collective-permute-done | bytes 49184 | tf_op jit(solution)/shard_map/ppermute | solution.py:535
  35.1 0.5 %collective-permute-done.20.refs_3_ = bf16[192,128]{1,0:T(8,128)(2,1)S(1)} collective-permute-done((bf16[192,128]{1,0:T(8,128)(2,1)S(1)}, bf16[192,128]{1,0:T(8,128)(2,1)S(1)}, u32[]{:S(2)}, u32[]{:S(2)}) %collective-permute-start.20) | collective-permute-done | bytes 49184 | tf_op jit(solution)/shard_map/ppermute | solution.py:535
  35.6 0.0 copy-done.6
  35.6 0.7 %shard_map.137 = (f32[256,128]{1,0:T(8,128)}, f32[4,64,128]{2,1,0:T(8,128)}, f32[2,64,128]{2,1,0:T(8,128)}) custom-call(f32[4,64,128]{2,1,0:T(8,128)S(1)} %get-tuple-element.42.warm, f32[2,64,128]{2,1,0:T(8,128)S(1)} %copy-done.6, f32[2,128,128]{2,1,0:T(8,128)S(1)} %shard_map.135.speed, bf16[192,128]{1,0:T(8,128)(2,1)S(1)} %get-tuple-element.52.refs_0_, ...), custom_call_target="tpu_custom_call" | custom-call | flops 11500000 | bytes 524288 | tf_op jit(solution)/shard_map/pallas_call | solution.py:40
  (8 shorter events, 0.1 us)
Async XLA Ops:
  0.6 5.9 %copy-start = (f32[4,64,128]{2,1,0:T(8,128)S(1)}, f32[4,64,128]{2,1,0:T(8,128)}, u32[]{:S(2)}) copy-start(f32[4,64,128]{2,1,0:T(8,128)} %water.3) | copy-start | bytes 393220
  0.6 5.9 %copy-start.1 = (f32[1,1,5,16384]{3,1,2,0:T(1,128)S(1)}, f32[1,1,5,16384]{3,1,2,0:T(1,128)}, u32[]{:S(2)}) copy-start(f32[1,1,5,16384]{3,1,2,0:T(1,128)} %param.18) | copy-start | bytes 983044
  0.7 5.9 %copy-start.2 = (f32[1,1,5,16384]{3,1,2,0:T(1,128)S(1)}, f32[1,1,5,16384]{3,1,2,0:T(1,128)}, u32[]{:S(2)}) copy-start(f32[1,1,5,16384]{3,1,2,0:T(1,128)} %param.19) | copy-start | bytes 983044
  0.7 5.9 %copy-start.4 = (f32[1,1,2,16384]{3,2,1,0:T(2,128)S(1)}, f32[1,1,2,16384]{3,2,1,0:T(2,128)}, u32[]{:S(2)}) copy-start(f32[1,1,2,16384]{3,2,1,0:T(2,128)} %param.20) | copy-start | bytes 393220
  3.3 8.6 %collective-permute-start.3 = (bf16[320,128]{1,0:T(8,128)(2,1)}, bf16[320,128]{1,0:T(8,128)(2,1)S(1)}, u32[]{:S(2)}, u32[]{:S(2)}) collective-permute-start(bf16[320,128]{1,0:T(8,128)(2,1)} %get-tuple-element.32), channel_id=1, source_target_pairs={{0,1},{1,0},{2,3},{3,2},{4,5},{5,4},{6,7},{7,6},{8,9},{9,8},{10,11... | collective-permute-start | bytes 245768 | tf_op jit(solution)/shard_map/ppermute | solution.py:535
  3.9 8.8 %collective-permute-start.4 = (bf16[320,128]{1,0:T(8,128)(2,1)}, bf16[320,128]{1,0:T(8,128)(2,1)S(1)}, u32[]{:S(2)}, u32[]{:S(2)}) collective-permute-start(bf16[320,128]{1,0:T(8,128)(2,1)} %get-tuple-element.33), channel_id=1, source_target_pairs={{0,2},{1,3},{2,0},{3,1},{4,6},{5,7},{6,4},{7,5},{8,10},{9,11},{10,... | collective-permute-start | bytes 245768 | tf_op jit(solution)/shard_map/ppermute | solution.py:535
  6.4 6.2 %collective-permute-start.5 = (bf16[320,128]{1,0:T(8,128)(2,1)}, bf16[320,128]{1,0:T(8,128)(2,1)S(1)}, u32[]{:S(2)}, u32[]{:S(2)}) collective-permute-start(bf16[320,128]{1,0:T(8,128)(2,1)} %get-tuple-element.34), channel_id=1, source_target_pairs={{0,3},{1,2},{2,1},{3,0},{4,7},{5,6},{6,5},{7,4},{8,11},{9,10},{10,... | collective-permute-start | bytes 245768 | tf_op jit(solution)/shard_map/ppermute | solution.py:535
  6.5 0.7 %copy-start.8 = (s32[1,1,4]{2,1,0:T(1,128)S(1)}, s32[1,1,4]{2,1,0:T(1,128)}, u32[]{:S(2)}) copy-start(s32[1,1,4]{2,1,0:T(1,128)} %links) | copy-start | bytes 52
  7.2 5.5 %copy-start.3 = (bf16[320,128]{1,0:T(8,128)(2,1)S(1)}, bf16[320,128]{1,0:T(8,128)(2,1)}, u32[]{:S(2)}) copy-start(bf16[320,128]{1,0:T(8,128)(2,1)} %get-tuple-element.31.refs_0_) | copy-start | bytes 245764
  7.2 5.5 %copy-start.5 = (f32[1,1,2,16384]{3,2,1,0:T(2,128)S(1)}, f32[1,1,2,16384]{3,2,1,0:T(2,128)}, u32[]{:S(2)}) copy-start(f32[1,1,2,16384]{3,2,1,0:T(2,128)} %param.21) | copy-start | bytes 393220
  8.1 8.9 %collective-permute-start.2 = (bf16[80,128]{1,0:T(8,128)(2,1)S(1)}, bf16[80,128]{1,0:T(8,128)(2,1)S(1)}, u32[]{:S(2)}, u32[]{:S(2)}) collective-permute-start(bf16[80,128]{1,0:T(8,128)(2,1)S(1)} %get-tuple-element.36.refs_0_), channel_id=1, source_target_pairs={{0,12},{4,8},{8,4},{12,0},{1,13},{5,9},{9,5},{13,1},{2,14},{6,10},... | collective-permute-start | bytes 61448 | tf_op jit(solution)/shard_map/ppermute | solution.py:530
  12.0 5.7 %collective-permute-start.1 = (bf16[80,128]{1,0:T(8,128)(2,1)S(1)}, bf16[80,128]{1,0:T(8,128)(2,1)S(1)}, u32[]{:S(2)}, u32[]{:S(2)}) collective-permute-start(bf16[80,128]{1,0:T(8,128)(2,1)S(1)} %get-tuple-element.36.refs_0_), channel_id=1, source_target_pairs={{0,8},{4,12},{8,0},{12,4},{1,9},{5,13},{9,1},{13,5},{2,10},{6,14},... | collective-permute-start | bytes 61448 | tf_op jit(solution)/shard_map/ppermute | solution.py:530
  12.0 5.7 %collective-permute-start = (bf16[80,128]{1,0:T(8,128)(2,1)S(1)}, bf16[80,128]{1,0:T(8,128)(2,1)S(1)}, u32[]{:S(2)}, u32[]{:S(2)}) collective-permute-start(bf16[80,128]{1,0:T(8,128)(2,1)S(1)} %get-tuple-element.36.refs_0_), channel_id=1, source_target_pairs={{0,4},{4,0},{8,12},{12,8},{1,5},{5,1},{9,13},{13,9},{2,6},{6,2},{1... | collective-permute-start | bytes 61448 | tf_op jit(solution)/shard_map/ppermute | solution.py:530
  13.2 8.4 %collective-permute-start.11 = (bf16[32,128]{1,0:T(8,128)(2,1)S(1)}, bf16[32,128]{1,0:T(8,128)(2,1)S(1)}, u32[]{:S(2)}, u32[]{:S(2)}) collective-permute-start(bf16[32,128]{1,0:T(8,128)(2,1)S(1)} %get-tuple-element.48), channel_id=1, source_target_pairs={{0,12},{4,8},{8,4},{12,0},{1,13},{5,9},{9,5},{13,1},{2,14},{6,10},... | collective-permute-start | bytes 24584 | tf_op jit(solution)/shard_map/ppermute | solution.py:530
  17.0 3.7 %collective-permute-start.9 = (bf16[32,128]{1,0:T(8,128)(2,1)S(1)}, bf16[32,128]{1,0:T(8,128)(2,1)S(1)}, u32[]{:S(2)}, u32[]{:S(2)}) collective-permute-start(bf16[32,128]{1,0:T(8,128)(2,1)S(1)} %get-tuple-element.48), channel_id=1, source_target_pairs={{0,4},{4,0},{8,12},{12,8},{1,5},{5,1},{9,13},{13,9},{2,6},{6,2},{1... | collective-permute-start | bytes 24584 | tf_op jit(solution)/shard_map/ppermute | solution.py:530
  17.0 4.6 %collective-permute-start.10 = (bf16[32,128]{1,0:T(8,128)(2,1)S(1)}, bf16[32,128]{1,0:T(8,128)(2,1)S(1)}, u32[]{:S(2)}, u32[]{:S(2)}) collective-permute-start(bf16[32,128]{1,0:T(8,128)(2,1)S(1)} %get-tuple-element.48), channel_id=1, source_target_pairs={{0,8},{4,12},{8,0},{12,4},{1,9},{5,13},{9,1},{13,5},{2,10},{6,14},... | collective-permute-start | bytes 24584 | tf_op jit(solution)/shard_map/ppermute | solution.py:530
  17.7 6.1 %copy-start.7 = (f32[64,128]{1,0:T(8,128)S(1)}, f32[64,128]{1,0:T(8,128)}, u32[]{:S(2)}) copy-start(f32[64,128]{1,0:T(8,128)} %mixing.1) | copy-start | bytes 98308
  17.7 5.6 %collective-permute-start.8 = (bf16[272,128]{1,0:T(8,128)(2,1)S(1)}, bf16[272,128]{1,0:T(8,128)(2,1)S(1)}, u32[]{:S(2)}, u32[]{:S(2)}) collective-permute-start(bf16[272,128]{1,0:T(8,128)(2,1)S(1)} %shard_map.133.refs_4_.refs_0_), channel_id=1, source_target_pairs={{0,3},{1,2},{2,1},{3,0},{4,7},{5,6},{6,5},{7,4},{8,11},{9,10},{10,... | collective-permute-start | bytes 208904 | tf_op jit(solution)/shard_map/ppermute | solution.py:530
  17.8 5.9 %collective-permute-start.7 = (bf16[272,128]{1,0:T(8,128)(2,1)S(1)}, bf16[272,128]{1,0:T(8,128)(2,1)S(1)}, u32[]{:S(2)}, u32[]{:S(2)}) collective-permute-start(bf16[272,128]{1,0:T(8,128)(2,1)S(1)} %shard_map.133.refs_4_.refs_0_), channel_id=1, source_target_pairs={{0,2},{1,3},{2,0},{3,1},{4,6},{5,7},{6,4},{7,5},{8,10},{9,11},{10,... | collective-permute-start | bytes 208904 | tf_op jit(solution)/shard_map/ppermute | solution.py:530
  20.7 3.1 %collective-permute-start.6 = (bf16[272,128]{1,0:T(8,128)(2,1)S(1)}, bf16[272,128]{1,0:T(8,128)(2,1)S(1)}, u32[]{:S(2)}, u32[]{:S(2)}) collective-permute-start(bf16[272,128]{1,0:T(8,128)(2,1)S(1)} %shard_map.133.refs_4_.refs_0_), channel_id=1, source_target_pairs={{0,1},{1,0},{2,3},{3,2},{4,5},{5,4},{6,7},{7,6},{8,9},{9,8},{10,11... | collective-permute-start | bytes 208904 | tf_op jit(solution)/shard_map/ppermute | solution.py:530
  21.7 4.9 %collective-permute-start.14 = (bf16[128,128]{1,0:T(8,128)(2,1)S(1)}, bf16[128,128]{1,0:T(8,128)(2,1)S(1)}, u32[]{:S(2)}, u32[]{:S(2)}) collective-permute-start(bf16[128,128]{1,0:T(8,128)(2,1)S(1)} %constant_dynamic-update-slice_fusion.refs_4_), channel_id=1, source_target_pairs={{0,3},{1,2},{2,1},{3,0},{4,7},{5,6},{6,5},{7,4},{8,11},{9,10},{10,... | collective-permute-start | bytes 98312 | tf_op jit(solution)/shard_map/ppermute | solution.py:530
  22.4 4.4 %collective-permute-start.13 = (bf16[128,128]{1,0:T(8,128)(2,1)S(1)}, bf16[128,128]{1,0:T(8,128)(2,1)S(1)}, u32[]{:S(2)}, u32[]{:S(2)}) collective-permute-start(bf16[128,128]{1,0:T(8,128)(2,1)S(1)} %constant_dynamic-update-slice_fusion.refs_4_), channel_id=1, source_target_pairs={{0,2},{1,3},{2,0},{3,1},{4,6},{5,7},{6,4},{7,5},{8,10},{9,11},{10,... | collective-permute-start | bytes 98312 | tf_op jit(solution)/shard_map/ppermute | solution.py:530
  23.3 3.5 %collective-permute-start.12 = (bf16[128,128]{1,0:T(8,128)(2,1)S(1)}, bf16[128,128]{1,0:T(8,128)(2,1)S(1)}, u32[]{:S(2)}, u32[]{:S(2)}) collective-permute-start(bf16[128,128]{1,0:T(8,128)(2,1)S(1)} %constant_dynamic-update-slice_fusion.refs_4_), channel_id=1, source_target_pairs={{0,1},{1,0},{2,3},{3,2},{4,5},{5,4},{6,7},{7,6},{8,9},{9,8},{10,11... | collective-permute-start | bytes 98312 | tf_op jit(solution)/shard_map/ppermute | solution.py:530
  24.8 4.1 %collective-permute-start.17 = (bf16[64,128]{1,0:T(8,128)(2,1)S(1)}, bf16[64,128]{1,0:T(8,128)(2,1)S(1)}, u32[]{:S(2)}, u32[]{:S(2)}) collective-permute-start(bf16[64,128]{1,0:T(8,128)(2,1)S(1)} %get-tuple-element.51.refs_4_), channel_id=1, source_target_pairs={{0,3},{1,2},{2,1},{3,0},{4,7},{5,6},{6,5},{7,4},{8,11},{9,10},{10,... | collective-permute-start | bytes 49160 | tf_op jit(solution)/shard_map/ppermute | solution.py:530
  25.8 3.7 %collective-permute-start.16 = (bf16[64,128]{1,0:T(8,128)(2,1)S(1)}, bf16[64,128]{1,0:T(8,128)(2,1)S(1)}, u32[]{:S(2)}, u32[]{:S(2)}) collective-permute-start(bf16[64,128]{1,0:T(8,128)(2,1)S(1)} %get-tuple-element.51.refs_4_), channel_id=1, source_target_pairs={{0,2},{1,3},{2,0},{3,1},{4,6},{5,7},{6,4},{7,5},{8,10},{9,11},{10,... | collective-permute-start | bytes 49160 | tf_op jit(solution)/shard_map/ppermute | solution.py:530
  26.6 3.0 %collective-permute-start.15 = (bf16[64,128]{1,0:T(8,128)(2,1)S(1)}, bf16[64,128]{1,0:T(8,128)(2,1)S(1)}, u32[]{:S(2)}, u32[]{:S(2)}) collective-permute-start(bf16[64,128]{1,0:T(8,128)(2,1)S(1)} %get-tuple-element.51.refs_4_), channel_id=1, source_target_pairs={{0,1},{1,0},{2,3},{3,2},{4,5},{5,4},{6,7},{7,6},{8,9},{9,8},{10,11... | collective-permute-start | bytes 49160 | tf_op jit(solution)/shard_map/ppermute | solution.py:530
  29.6 6.1 %copy-start.6 = (f32[2,64,128]{2,1,0:T(8,128)S(1)}, f32[2,64,128]{2,1,0:T(8,128)}, u32[]{:S(2)}) copy-start(f32[2,64,128]{2,1,0:T(8,128)} %currents.1) | copy-start | bytes 196612
  30.7 1.9 %collective-permute-start.18 = (bf16[192,128]{1,0:T(8,128)(2,1)S(1)}, bf16[192,128]{1,0:T(8,128)(2,1)S(1)}, u32[]{:S(2)}, u32[]{:S(2)}) collective-permute-start(bf16[192,128]{1,0:T(8,128)(2,1)S(1)} %get-tuple-element.53), channel_id=1, source_target_pairs={{0,1},{1,0},{2,3},{3,2},{4,5},{5,4},{6,7},{7,6},{8,9},{9,8},{10,11... | collective-permute-start | bytes 147464 | tf_op jit(solution)/shard_map/ppermute | solution.py:535
  30.7 4.4 %collective-permute-start.19 = (bf16[192,128]{1,0:T(8,128)(2,1)S(1)}, bf16[192,128]{1,0:T(8,128)(2,1)S(1)}, u32[]{:S(2)}, u32[]{:S(2)}) collective-permute-start(bf16[192,128]{1,0:T(8,128)(2,1)S(1)} %get-tuple-element.54), channel_id=1, source_target_pairs={{0,2},{1,3},{2,0},{3,1},{4,6},{5,7},{6,4},{7,5},{8,10},{9,11},{10,... | collective-permute-start | bytes 147464 | tf_op jit(solution)/shard_map/ppermute | solution.py:535
  31.7 3.9 %collective-permute-start.20 = (bf16[192,128]{1,0:T(8,128)(2,1)S(1)}, bf16[192,128]{1,0:T(8,128)(2,1)S(1)}, u32[]{:S(2)}, u32[]{:S(2)}) collective-permute-start(bf16[192,128]{1,0:T(8,128)(2,1)S(1)} %get-tuple-element.55), channel_id=1, source_target_pairs={{0,3},{1,2},{2,1},{3,0},{4,7},{5,6},{6,5},{7,4},{8,11},{9,10},{10,... | collective-permute-start | bytes 147464 | tf_op jit(solution)/shard_map/ppermute | solution.py:535

commit v4 on v2

--- a/solution.py
+++ b/solution.py
@@ -21,25 +21,31 @@
 OPPOSITE = (1, 0, 3, 2)
 LATERAL = ((2, 3), (2, 3), (0, 1), (0, 1))
 DEPTH = SUBCYCLES
+SIDE_ROWS = 16 * DEPTH
+PUSH_ROWS = 8 * DEPTH
 TILE_ROWS = 16
 F32 = jnp.float32
 BF16 = jnp.bfloat16
 VMEM_LIMIT = 16 * 1024 * 1024
-
-
-def call(kernel, outs, args, scratch=(), smem=(), flops=1_000_000):
-    specs = [
-        pl.BlockSpec(memory_space=pltpu.SMEM if i in smem else pltpu.VMEM) for i in range(len(args))
-    ]
+FLOPS_PER_MICRO = 1.15e9
+
+
+def call(kernel, outs, args, scratch=(), smem=(), hbm=(), out_space=pltpu.VMEM, grant=VMEM_LIMIT, micros=0.01):
+    def space(i):
+        return pltpu.SMEM if i in smem else pltpu.HBM if i in hbm else pltpu.VMEM
+
+    specs = [pl.BlockSpec(memory_space=space(i)) for i in range(len(args))]
     size = sum(a.size * a.dtype.itemsize for a in args)
     return pl.pallas_call(
         kernel,
         out_shape=outs,
         in_specs=specs,
-        out_specs=jax.tree.map(lambda _: pl.BlockSpec(memory_space=pltpu.VMEM), outs),
+        out_specs=jax.tree.map(lambda _: pl.BlockSpec(memory_space=out_space), outs),
         scratch_shapes=list(scratch),
-        compiler_params=pltpu.CompilerParams(vmem_limit_bytes=VMEM_LIMIT),
-        cost_estimate=pl.CostEstimate(flops=flops, bytes_accessed=size, transcendentals=0),
+        compiler_params=pltpu.CompilerParams(vmem_limit_bytes=grant),
+        cost_estimate=pl.CostEstimate(
+            flops=int(micros * FLOPS_PER_MICRO), bytes_accessed=size, transcendentals=0
+        ),
     )(*args)
 
 
@@ -55,30 +61,56 @@
     return jnp.where(condition, 1.0, 0.0).astype(F32)
 
 
-def forward_kernel(group, blocks, rows, cols, currents, *outs):
-    side = rows.shape[1]
-    depth = cols.shape[1]
-    devices = group[0]
-    members = group[1]
-    me = group[2]()
-    fields = [currents[c].astype(BF16) for c in range(2)]
-    pairs = rows.shape[0]
+def forward_kernel(group, blocks_h, rows_h, cols_h, currents_h, *refs):
+    devices, members, place = group
+    outs, (blocks, currents, rows, cols, fields, arrived, left) = refs[:members], refs[members:]
+    pairs, side, width = rows_h.shape
+    depth = cols_h.shape[1]
+    loads = [
+        pltpu.make_async_copy(source, target, arrived.at[i])
+        for i, (source, target) in enumerate(
+            ((blocks_h, blocks), (currents_h, currents), (rows_h, rows), (cols_h, cols))
+        )
+    ]
+    for load in loads:
+        load.start()
+    for load in loads:
+        load.wait()
+    me = place()
+    owners = [lax.rem(lax.rem(blocks[0, m], devices), members) for m in range(pairs)]
+    copies = []
     for k, out in enumerate(outs):
         partner = me ^ k
-        pair = jnp.int32(0)
-        found = jnp.int32(0)
+        pair, found = jnp.int32(0), jnp.int32(0)
         for m in range(pairs):
-            owner = lax.rem(lax.rem(blocks[0, m], devices), members)
-            pair = jnp.where(owner == partner, m, pair)
-            found = jnp.where(owner == partner, 1, found)
-        if pairs == members:
-            out[0:side] = rows[pair]
-            out[side : side + depth] = cols[pair]
+            pair = jnp.where(owners[m] == partner, m, pair)
+            found = jnp.where(owners[m] == partner, 1, found)
+        copies.append(
+            pltpu.make_async_copy(rows.at[pair], out.at[pl.ds(0, side)], left.at[3 * k])
+        )
+        copies.append(
+            pltpu.make_async_copy(cols.at[pair], out.at[pl.ds(side, depth)], left.at[3 * k + 1])
+        )
+        if pairs < members:
+            keep = jnp.where(found > 0, 1.0, 0.0).astype(F32)
         else:
-            out[0:side] = jnp.where(found > 0, rows[pair].astype(F32), 0.0).astype(BF16)
-            out[side : side + depth] = jnp.where(found > 0, cols[pair].astype(F32), 0.0).astype(BF16)
-        for c in range(2):
-            out[side + depth + c * side : side + depth + (c + 1) * side] = fields[c]
+            keep = None
+        copies[-2].start()
+        copies[-1].start()
+        if k == 0 or keep is not None:
+            for c in range(2):
+                field = currents[c] if keep is None else currents[c] * keep
+                fields[0 if keep is None else k, c * side : (c + 1) * side] = field.astype(BF16)
+        copies.append(
+            pltpu.make_async_copy(
+                fields.at[0 if keep is None else k],
+                out.at[pl.ds(side + depth, 2 * side)],
+                left.at[3 * k + 2],
+            )
+        )
+        copies[-1].start()
+    for copy in copies:
+        copy.wait()
 
 
 def put_side_rims(store, planes, at):
@@ -128,7 +160,7 @@
     conduct_o[...] = -HEAT_RATE * conduct
     speed_o[0] = speed_x
     speed_o[1] = speed_y
-    side_rows = 4 * 4 * DEPTH
+    side_rows = SIDE_ROWS
     put_side_rims(store, [speed_x, speed_y, viscous, gain], lambda side: side * 4 * DEPTH)
     rim_rows = store[0:side_rows].astype(BF16)
     for d in range(out.shape[0]):
@@ -216,9 +248,7 @@
         push_o[c] = push
         pushes.append(push)
     put_side_rims(store, pushes, lambda q: q * 2 * DEPTH)
-    message = store[...].astype(BF16)
-    for d in range(out.shape[0]):
-        out[d] = message
+    out[...] = store[...].astype(BF16)
 
 
 def ocean_kernel(where_am_i, strip_at, water, mixing, rims, warm_o, top_o):
@@ -285,8 +315,14 @@
     top_o[...] = (total / (levels * lev_count)).astype(top_o.dtype)
 
 
-def subcycles_kernel(me, table, viscous, gain, speed, push, rims, push_rims, out, flat_o):
+def subcycles_kernel(tiles, members, place, table, viscous, gain, speed, push, rims, *refs):
+    push_relays, (out, push_rims) = refs[:members], refs[members:]
     size = viscous.shape[0]
+    me = place()
+    for k in range(tiles):
+        for m in range(members):
+            device = me ^ (k * members + m)
+            push_rims[device] = push_relays[m][k * PUSH_ROWS : (k + 1) * PUSH_ROWS]
     half = DEPTH
     high = 2 * DEPTH
     sub = iota((high, size), 0)
@@ -319,7 +355,7 @@
 
     strips = []
     for q in range(4):
-        x, has_x = follow(me(), q)
+        x, has_x = follow(me, q)
         strip = load(x, OPPOSITE[q], flag(has_x))
         sides = []
         for s in LATERAL[q]:
@@ -397,8 +433,6 @@
         vx, vy = new_x, new_y
     out[0] = vx
     out[1] = vy
-    flat_o[pl.ds(0, size, stride=2), :] = vx
-    flat_o[pl.ds(1, size, stride=2), :] = vy
 
 
 def back_kernel(group, side, drag, conduct, current, speed, *refs):
@@ -420,17 +454,33 @@
         out[...] = reply.astype(BF16)
 
 
-def finish_kernel(warm, currents, *refs):
-    replies, (heat_o, current_o) = refs[:-2], refs[-2:]
+def finish_kernel(warm, currents, speed, *refs):
+    outs, (flat, heat_v, current_v, left) = refs[-7:-4], refs[-4:]
+    replies = refs[:-7]
+    flat_o, heat_o, current_o = outs
+    size = speed.shape[1]
+    copies = [
+        pltpu.make_async_copy(source, target, left.at[i])
+        for i, (source, target) in enumerate(
+            ((flat, flat_o), (heat_v, heat_o), (current_v, current_o))
+        )
+    ]
+    for c in range(2):
+        flat[pl.ds(c, size, stride=2), :] = speed[c]
+    copies[0].start()
     total = replies[0][...].astype(F32)
     for reply in replies[1:]:
         total = total + reply[...].astype(F32)
     side = currents.shape[1]
     heat = THERMAL_DIFFUSE * total[0:side]
     for l in range(warm.shape[0]):
-        heat_o[l] = warm[l] + heat
+        heat_v[l] = warm[l] + heat
+    copies[1].start()
     for c in range(2):
-        current_o[c] = currents[c] + STRESS_MIXING * total[(c + 1) * side : (c + 2) * side]
+        current_v[c] = currents[c] + STRESS_MIXING * total[(c + 1) * side : (c + 2) * side]
+    copies[2].start()
+    for copy in copies:
+        copy.wait()
 
 
 def shards(
@@ -458,14 +508,22 @@
     def place():
         return tuple(lax.axis_index(a) for a in member_axes)
 
-    def group_place():
+    def member_place():
         return lax.axis_index("sub") * lev_count + lax.axis_index("lev")
 
     def device_place():
-        return lax.axis_index("tile") * group + group_place()
-
-    def swap(value, k):
-        return lax.ppermute(value, group_axes, [(i, i ^ k) for i in range(group)])
+        return lax.axis_index("tile") * group + member_place()
+
+    def swap(value, axes, count):
+        return [value] + [
+            lax.ppermute(value, axes, [(i, i ^ k) for i in range(count)]) for k in range(1, count)
+        ]
+
+    def swap_each(values):
+        return [values[0]] + [
+            lax.ppermute(values[k], group_axes, [(i, i ^ k) for i in range(group)])
+            for k in range(1, group)
+        ]
 
     def shape(*dims, dtype=F32):
         return jax.ShapeDtypeStruct(dims, dtype)
@@ -480,15 +538,25 @@
 
     chunk_rows = 3 * side + width
     sent = call(
-        functools.partial(forward_kernel, (devices, group, group_place)),
+        functools.partial(forward_kernel, (devices, group, member_place)),
         [shape(chunk_rows, width, dtype=BF16)] * group,
         (remap_blocks, remap_rows[0].swapaxes(1, 2), remap_cols[0], upper_current_vector),
-        smem=(0,),
-    )
-    chunks = [sent[0]] + [swap(sent[k], k) for k in range(1, group)]
-
-    side_rows = 16 * DEPTH
-    message_rows = side_rows + -(-(2 * levels + 1) // TILE_ROWS) * TILE_ROWS
+        scratch=[
+            pltpu.SMEM((1, pairs), jnp.int32),
+            pltpu.VMEM((2, side, width), F32),
+            pltpu.VMEM((pairs, side, size), BF16),
+            pltpu.VMEM((pairs, size, width), BF16),
+            pltpu.VMEM((1 if pairs == group else group, 2 * side, width), BF16),
+            pltpu.SemaphoreType.DMA((4,)),
+            pltpu.SemaphoreType.DMA((3 * group,)),
+        ],
+        hbm=(0, 1, 2, 3),
+        grant=60 * 2**20,
+        micros=2,
+    )
+    chunks = swap_each(sent)
+
+    message_rows = SIDE_ROWS + -(-(2 * levels + 1) // TILE_ROWS) * TILE_ROWS
     message, viscous, gain, step_mass, drag, conduct, speed = call(
         functools.partial(rims_kernel, grid),
         [shape(devices, message_rows, size, dtype=BF16)] + [plane] * 5 + [planes],
@@ -499,34 +567,37 @@
             interleaved(ice_velocity),
             water_heat_state,
         ),
-        scratch=[pltpu.VMEM((side_rows, size), F32)],
+        scratch=[pltpu.VMEM((SIDE_ROWS, size), F32)],
         smem=(0,),
     )
     rims = lax.all_to_all(message, member_axes, split_axis=0, concat_axis=0, tiled=True)
 
     push_message, current_ice, push = call(
         functools.partial(forcing_kernel, group, side),
-        [shape(devices, 8 * DEPTH, size, dtype=BF16), planes, planes],
+        [shape(PUSH_ROWS, size, dtype=BF16), planes, planes],
         (step_mass, drag, wind, *chunks),
-        scratch=[pltpu.VMEM((8 * DEPTH, size), F32)],
-    )
-    push_rims = lax.all_to_all(push_message, member_axes, split_axis=0, concat_axis=0, tiled=True)
+        scratch=[pltpu.VMEM((PUSH_ROWS, size), F32)],
+    )
+    push_messages = swap(push_message, "tile", tile_count)
+    push_relay, rims = lax.optimization_barrier((jnp.concatenate(push_messages, axis=0), rims))
+    push_relays = swap(push_relay, group_axes, group)
 
     warm, top = call(
-        functools.partial(ocean_kernel, grid, side_rows),
+        functools.partial(ocean_kernel, grid, SIDE_ROWS),
         [shape(levels, side, width), shape(side, width, dtype=BF16 if lev_count == 1 else F32)],
         (water_heat_state, diffusion_coefficient, rims),
     )
     if lev_count > 1:
         top = lax.psum(top, "lev").astype(BF16)
-    tops = [top] + [swap(top, k) for k in range(1, group)]
-
-    names = rims[:, side_rows + 2 * levels, 0:8].astype(jnp.int32)
+    tops = swap(top, group_axes, group)
+
+    names = rims[:, SIDE_ROWS + 2 * levels, 0:8].astype(jnp.int32)
     table = names[:, 0:4] * 128 + names[:, 4:8]
-    speed, flat = call(
-        functools.partial(subcycles_kernel, device_place),
-        [planes, shape(2 * size, size)],
-        (table, viscous, gain, speed, push, rims, push_rims),
+    speed = call(
+        functools.partial(subcycles_kernel, tile_count, group, device_place),
+        planes,
+        (table, viscous, gain, speed, push, rims, *push_relays),
+        scratch=[pltpu.VMEM((devices, PUSH_ROWS, size), BF16)],
         smem=(0,),
     )
 
@@ -535,13 +606,20 @@
         [shape(3 * side, width, dtype=BF16)] * group,
         (drag, conduct, current_ice, speed, *chunks, *tops),
     )
-    replies = [replies[0]] + [swap(replies[k], k) for k in range(1, group)]
+    replies = swap_each(replies)
     if lev_count > 1:
         replies = [lax.psum(sum(r.astype(F32) for r in replies), "lev")]
-    heat, current = call(
+    flat, heat, current = call(
         finish_kernel,
-        [shape(levels, side, width), shape(2, side, width)],
-        (warm, upper_current_vector, *replies),
+        [shape(2 * size, size), shape(levels, side, width), shape(2, side, width)],
+        (warm, upper_current_vector, speed, *replies),
+        scratch=[
+            pltpu.VMEM((2 * size, size), F32),
+            pltpu.VMEM((levels, side, width), F32),
+            pltpu.VMEM((2, side, width), F32),
+            pltpu.SemaphoreType.DMA((3,)),
+        ],
+        out_space=pltpu.HBM,
     )
     velocity = flat.reshape(size, 2, size).transpose(1, 0, 2).reshape(1, 1, 2, size * size)
     return heat, current, velocity

time: 48.7 us -> 48.8 us (level)
  waiting for transfers between devices: 14.1 us -> 13.1 us
  starting transfers between devices: 19.2 us -> 19.7 us
    ppermute x9 -> x15, starting transfers between devices: 6.17 us -> 12.3 us  [the longest x9 8.29 us: swap(): lax.ppermute(value, axes, [(i, i ^ k) for i in range(count)])]
    all_to_all x1 -> x0, starting transfers between devices: 5.53 us -> none  [shards(): lax.all_to_all(push_message, member_axes, split_axis=0, concat_axis=0, ti...]
    all_to_all x1 -> x0, waiting for transfers between devices: 4.73 us -> none  [shards(): lax.all_to_all(push_message, member_axes, split_axis=0, concat_axis=0, ti...]
    ppermute x9 -> x15, waiting for transfers between devices: 9.07 us -> 13.1 us  [the longest x6 8.8 us: swap_each(): lax.ppermute(values[k], group_axes, [(i, i ^ k) for i in range(group)])]
    unnamed x24 -> x22, local copies, waits for them, and re-layouts: 5.04 us -> 5.31 us
  transfers between devices with their start and end apart: 11 -> 16, of which waited for: 6 -> 7; matrix products, arithmetic and copies ran while one was open for 0% -> 0% of each run, Pallas kernels for 11% -> 12%
where the time goes in v4:
time: 48.8 us; the launch traced here: 48.5 us
  starting transfers between devices  19.7 us (40%)
  waiting for transfers between devices  13.1 us (27%)
  Pallas kernels  9.59 us (20%)
  local copies, waits for them, and re-layouts  5.31 us (11%)
  between operations  0.76 us (2%)
    pallas_call x7, Pallas kernels, call(): pl.pallas_call(kernel, out_shape=outs, in_specs=specs, out_specs=jax.tree...  9.59 us
    ppermute x6, waiting for transfers between devices, swap_each(): lax.ppermute(values[k], group_axes, [(i, i ^ k) for i in range(group)])  8.8 us
    ppermute x9, starting transfers between devices, swap(): lax.ppermute(value, axes, [(i, i ^ k) for i in range(count)])  8.29 us
    all_to_all x1, starting transfers between devices, shards(): lax.all_to_all(message, member_axes, split_axis=0, concat_axis=0, tiled=T...  7.36 us
    unnamed x22, local copies, waits for them, and re-layouts  5.31 us
    ppermute x9, waiting for transfers between devices, swap(): lax.ppermute(value, axes, [(i, i ^ k) for i in range(count)])  4.26 us
    ppermute x6, starting transfers between devices, swap_each(): lax.ppermute(values[k], group_axes, [(i, i ^ k) for i in range(group)])  4.02 us
  transfers between devices with their start and end apart: 16, of which 7 were waited for; matrix products, arithmetic and copies ran while one was open for 0% of the time, Pallas kernels for 12%

profile of v4, /device:TPU:0, one launch (start us, length us, event | category | flops | bytes accessed | tf_op | source)
XLA Modules:
  0.0 48.5 jit_solution(5820658909090370230)
XLA Ops:
  0.6 0.0 copy-start.10
  0.6 0.6 %copy-done.10 = s32[1,1,4]{2,1,0:T(1,128)S(1)} copy-done((s32[1,1,4]{2,1,0:T(1,128)S(1)}, s32[1,1,4]{2,1,0:T(1,128)}, u32[]{:S(2)}) %copy-start.10) | copy-done | bytes 40
  1.3 0.0 copy-start
  1.3 0.9 %copy-done = f32[4,64,128]{2,1,0:T(8,128)S(1)} copy-done((f32[4,64,128]{2,1,0:T(8,128)S(1)}, f32[4,64,128]{2,1,0:T(8,128)}, u32[]{:S(2)}) %copy-start) | copy-done | bytes 131096
  2.2 0.0 copy-start.2
  2.2 1.0 %copy-done.2 = f32[1,1,5,16384]{3,1,2,0:T(1,128)S(1)} copy-done((f32[1,1,5,16384]{3,1,2,0:T(1,128)S(1)}, f32[1,1,5,16384]{3,1,2,0:T(1,128)}, u32[]{:S(2)}) %copy-start.2) | copy-done | bytes 327704
  3.2 0.0 copy-start.3
  3.2 1.0 %copy-done.3 = f32[1,1,5,16384]{3,1,2,0:T(1,128)S(1)} copy-done((f32[1,1,5,16384]{3,1,2,0:T(1,128)S(1)}, f32[1,1,5,16384]{3,1,2,0:T(1,128)}, u32[]{:S(2)}) %copy-start.3) | copy-done | bytes 327704
  4.1 0.0 copy-start.6
  4.1 0.9 %copy-done.6 = f32[1,1,2,16384]{3,2,1,0:T(2,128)S(1)} copy-done((f32[1,1,2,16384]{3,2,1,0:T(2,128)S(1)}, f32[1,1,2,16384]{3,2,1,0:T(2,128)}, u32[]{:S(2)}) %copy-start.6) | copy-done | bytes 131096
  5.0 1.8 %shard_map.130 = (bf16[16,80,128]{2,1,0:T(8,128)(2,1)}, f32[128,128]{1,0:T(8,128)S(1)}, f32[128,128]{1,0:T(8,128)S(1)}, f32[128,128]{1,0:T(8,128)S(1)}, f32[128,...) custom-call(s32[1,1,4]{2,1,0:T(1,128)S(1)} %copy-done.10, f32[5,128,128]{2,1,0:T(8,128)S(1)} %bitcast.22, ...), custom_call_target="tpu_custom_call" | custom-call | flops 11500000 | bytes 917520 | tf_op jit(solution)/shard_map/pallas_call | solution.py:39
  6.9 7.4 %all-to-all-start = ((bf16[16,80,128]{2,1,0:T(8,128)(2,1)}), bf16[16,80,128]{2,1,0:T(8,128)(2,1)S(1)}, u32[]{:S(2)}, u32[]{:S(2)}) async-start(bf16[16,80,128]{2,1,0:T(8,128)(2,1)} %get-tuple-element.35), calls=%async_computation | async-start | bytes 655360 | tf_op jit(solution)/shard_map/all_to_all | solution.py:573
  14.2 0.0 copy-start.7
  14.2 2.3 %shard_map.131 = (bf16[320,128]{1,0:T(8,128)(2,1)}, bf16[320,128]{1,0:T(8,128)(2,1)}, bf16[320,128]{1,0:T(8,128)(2,1)}, bf16[320,128]{1,0:T(8,128)(2,1)}) custom-call(s32[1,4]{1,0:T(1,128)} %blocks_h.1, bf16[4,64,128]{2,1,0:T(8,128)(2,1)} %bitcast.29, bf16[4,128,128]{2,1,0:T(8,128)(2,1)} %bitcast.27, f32[2,64,128]{2,1,0:T(8,128)} %currents.1), custom_call_target="tpu_custom_call" | custom-call | flops 2300000000 | bytes 262160 | tf_op jit(solution)/shard_map/pallas_call | solution.py:39
  16.5 0.5 collective-permute-start
  17.0 1.7 %collective-permute-start.1 = (bf16[320,128]{1,0:T(8,128)(2,1)}, bf16[320,128]{1,0:T(8,128)(2,1)S(1)}, u32[]{:S(2)}, u32[]{:S(2)}) collective-permute-start(bf16[320,128]{1,0:T(8,128)(2,1)} %get-tuple-element.32), channel_id=1, source_target_pairs={{0,2},{1,3},{2,0},{3,1},{4,6},{5,7},{6,4},{7,5},{8,10},{9,11},{10,... | collective-permute-start | bytes 245768 | tf_op jit(solution)/shard_map/ppermute | solution.py:524
  18.7 0.0 collective-permute-start.2
  18.7 0.0 collective-permute-done.refs_1_
  18.7 4.1 %collective-permute-done.1.refs_2_ = bf16[320,128]{1,0:T(8,128)(2,1)S(1)} collective-permute-done((bf16[320,128]{1,0:T(8,128)(2,1)}, bf16[320,128]{1,0:T(8,128)(2,1)S(1)}, u32[]{:S(2)}, u32[]{:S(2)}) %collective-permute-start.1) | collective-permute-done | bytes 81952 | tf_op jit(solution)/shard_map/ppermute | solution.py:524
  22.8 1.6 %collective-permute-done.2.refs_3_ = bf16[320,128]{1,0:T(8,128)(2,1)S(1)} collective-permute-done((bf16[320,128]{1,0:T(8,128)(2,1)}, bf16[320,128]{1,0:T(8,128)(2,1)S(1)}, u32[]{:S(2)}, u32[]{:S(2)}) %collective-permute-start.2) | collective-permute-done | bytes 81952 | tf_op jit(solution)/shard_map/ppermute | solution.py:524
  24.4 0.0 copy-done.7
  24.4 0.0 copy-start.4
  24.4 0.9 %copy-done.4 = bf16[320,128]{1,0:T(8,128)(2,1)S(1)} copy-done((bf16[320,128]{1,0:T(8,128)(2,1)S(1)}, bf16[320,128]{1,0:T(8,128)(2,1)}, u32[]{:S(2)}) %copy-start.4) | copy-done | bytes 81944
  25.3 0.0 copy-start.1
  25.3 0.6 %shard_map.132 = (bf16[32,128]{1,0:T(8,128)(2,1)S(1)}, f32[2,128,128]{2,1,0:T(8,128)S(1)}, f32[2,128,128]{2,1,0:T(8,128)S(1)}) custom-call(f32[128,128]{1,0:T(8,128)S(1)} %get-tuple-element.28.mass, f32[128,128]{1,0:T(8,128)S(1)} %get-tuple-element.29.drag, f32[256,128]{1,0:T(8,128)S(1)} %bitcast.25, bf16[320,128]{1,0:T(8,128)(2,1)S(1)} %copy-done.4, ...), custom_call_target="tpu_custom_call" | custom-call | flops 11500000 | bytes 589824 | tf_op jit(solution)/shard_map/pallas_call | solution.py:39
  25.8 0.0 copy-start.9
  25.8 3.7 %collective-permute-start.5 = (bf16[32,128]{1,0:T(8,128)(2,1)S(1)}, bf16[32,128]{1,0:T(8,128)(2,1)S(1)}, u32[]{:S(2)}, u32[]{:S(2)}) collective-permute-start(bf16[32,128]{1,0:T(8,128)(2,1)S(1)} %get-tuple-element.34), channel_id=1, source_target_pairs={{0,12},{4,8},{8,4},{12,0},{1,13},{5,9},{9,5},{13,1},{2,14},{6,10},... | collective-permute-start | bytes 24584 | tf_op jit(solution)/shard_map/ppermute | solution.py:519
  29.5 0.0 collective-permute-start.4
  29.6 0.7 %collective-permute-start.3 = (bf16[32,128]{1,0:T(8,128)(2,1)S(1)}, bf16[32,128]{1,0:T(8,128)(2,1)S(1)}, u32[]{:S(2)}, u32[]{:S(2)}) collective-permute-start(bf16[32,128]{1,0:T(8,128)(2,1)S(1)} %get-tuple-element.34), channel_id=1, source_target_pairs={{0,4},{4,0},{8,12},{12,8},{1,5},{5,1},{9,13},{13,9},{2,6},{6,2},{1... | collective-permute-start | bytes 24584 | tf_op jit(solution)/shard_map/ppermute | solution.py:519
  30.3 1.1 %collective-permute-done.5 = bf16[32,128]{1,0:T(8,128)(2,1)S(1)} collective-permute-done((bf16[32,128]{1,0:T(8,128)(2,1)S(1)}, bf16[32,128]{1,0:T(8,128)(2,1)S(1)}, u32[]{:S(2)}, u32[]{:S(2)}) %collective-permute-start.5) | collective-permute-done | bytes 8224 | tf_op jit(solution)/shard_map/ppermute | solution.py:519
  31.3 2.8 %collective-permute-done.4 = bf16[32,128]{1,0:T(8,128)(2,1)S(1)} collective-permute-done((bf16[32,128]{1,0:T(8,128)(2,1)S(1)}, bf16[32,128]{1,0:T(8,128)(2,1)S(1)}, u32[]{:S(2)}, u32[]{:S(2)}) %collective-permute-start.4) | collective-permute-done | bytes 8224 | tf_op jit(solution)/shard_map/ppermute | solution.py:519
  34.1 0.0 collective-permute-done.3
  34.1 0.0 all-to-all-done.rims
  34.1 0.1 collective-permute-start.8
  34.2 1.2 %collective-permute-start.7 = (bf16[128,128]{1,0:T(8,128)(2,1)S(1)}, bf16[128,128]{1,0:T(8,128)(2,1)S(1)}, u32[]{:S(2)}, u32[]{:S(2)}) collective-permute-start(bf16[128,128]{1,0:T(8,128)(2,1)S(1)} %pad_maximum_fusion.refs_0_), channel_id=1, source_target_pairs={{0,2},{1,3},{2,0},{3,1},{4,6},{5,7},{6,4},{7,5},{8,10},{9,11},{10,... | collective-permute-start | bytes 98312 | tf_op jit(solution)/shard_map/ppermute | solution.py:519
  35.4 0.6 %collective-permute-start.6 = (bf16[128,128]{1,0:T(8,128)(2,1)S(1)}, bf16[128,128]{1,0:T(8,128)(2,1)S(1)}, u32[]{:S(2)}, u32[]{:S(2)}) collective-permute-start(bf16[128,128]{1,0:T(8,128)(2,1)S(1)} %pad_maximum_fusion.refs_0_), channel_id=1, source_target_pairs={{0,1},{1,0},{2,3},{3,2},{4,5},{5,4},{6,7},{7,6},{8,9},{9,8},{10,11... | collective-permute-start | bytes 98312 | tf_op jit(solution)/shard_map/ppermute | solution.py:519
  36.1 0.0 copy-done.1
  36.1 0.0 copy-done.9
  36.1 0.9 %shard_map.133 = (f32[4,64,128]{2,1,0:T(8,128)S(1)}, bf16[64,128]{1,0:T(8,128)(2,1)S(1)}) custom-call(f32[4,64,128]{2,1,0:T(8,128)S(1)} %copy-done.1, f32[64,128]{1,0:T(8,128)S(1)} %copy-done.9, bf16[16,80,128]{2,1,0:T(8,128)(2,1)S(1)} %all-to-all-done.rims), custom_call_target="tpu_custom_call" | custom-call | flops 11500000 | bytes 491520 | tf_op jit(solution)/shard_map/pallas_call | solution.py:39
  37.0 0.8 %collective-permute-start.11 = (bf16[64,128]{1,0:T(8,128)(2,1)S(1)}, bf16[64,128]{1,0:T(8,128)(2,1)S(1)}, u32[]{:S(2)}, u32[]{:S(2)}) collective-permute-start(bf16[64,128]{1,0:T(8,128)(2,1)S(1)} %get-tuple-element.45.refs_4_), channel_id=1, source_target_pairs={{0,3},{1,2},{2,1},{3,0},{4,7},{5,6},{6,5},{7,4},{8,11},{9,10},{10,... | collective-permute-start | bytes 49160 | tf_op jit(solution)/shard_map/ppermute | solution.py:519
  37.8 0.9 %collective-permute-start.10 = (bf16[64,128]{1,0:T(8,128)(2,1)S(1)}, bf16[64,128]{1,0:T(8,128)(2,1)S(1)}, u32[]{:S(2)}, u32[]{:S(2)}) collective-permute-start(bf16[64,128]{1,0:T(8,128)(2,1)S(1)} %get-tuple-element.45.refs_4_), channel_id=1, source_target_pairs={{0,2},{1,3},{2,0},{3,1},{4,6},{5,7},{6,4},{7,5},{8,10},{9,11},{10,... | collective-permute-start | bytes 49160 | tf_op jit(solution)/shard_map/ppermute | solution.py:519
  38.7 0.0 collective-permute-done.8.refs_3_
  38.7 0.2 collective-permute-start.9
  38.9 0.1 slice_add_fusion.table
  39.0 0.0 collective-permute-done.7.refs_2_
  39.0 0.0 collective-permute-done.6.refs_1_
  39.0 0.0 copy-start.5
  39.0 2.1 %shard_map.134.speed = f32[2,128,128]{2,1,0:T(8,128)S(1)} custom-call(s32[16,4]{1,0:T(8,128)S(1)} %slice_add_fusion.table, f32[128,128]{1,0:T(8,128)S(1)} %get-tuple-element.38.viscous, f32[128,128]{1,0:T(8,128)S(1)} %get-tuple-element.39.gain, f32[2,128,128]{2,1,0:T(8,128)S(1)} %get-tuple-element.40.speed, f32[2,128,128]{2,1,0:T(8,128)S(1)} %get-tuple-element.41.push, ...), custom_call_target="tpu_custom_call" | custom-call | flops 11500000 | bytes 852224 | tf_op jit(solution)/shard_map/pallas_call | solution.py:39
  41.1 0.0 collective-permute-done.11.refs_7_
  41.1 0.4 collective-permute-done.10.refs_6_
  41.6 0.0 collective-permute-done.9.refs_5_
  41.6 0.0 copy-done.5
  41.6 0.0 copy-start.8
  41.6 1.1 %shard_map.135 = (bf16[192,128]{1,0:T(8,128)(2,1)S(1)}, bf16[192,128]{1,0:T(8,128)(2,1)S(1)}, bf16[192,128]{1,0:T(8,128)(2,1)S(1)}, bf16[192,128]{1,0:T(8,128)(2,1)S(1)}) custom-call(f32[128,128]{1,0:T(8,128)S(1)} %get-tuple-element.29.drag, f32[128,128]{1,0:T(8,128)S(1)} %get-tuple-element.43.conduct, f32[2,128,128]{2,1,0:T(8,128)S(1)} %get-tuple-element.44.current, ...), custom_call_target="tpu_custom_call" | custom-call | flops 11500000 | bytes 786432 | tf_op jit(solution)/shard_map/pallas_call | solution.py:39
  42.7 0.0 collective-permute-start.12
  42.7 1.0 %collective-permute-start.13 = (bf16[192,128]{1,0:T(8,128)(2,1)S(1)}, bf16[192,128]{1,0:T(8,128)(2,1)S(1)}, u32[]{:S(2)}, u32[]{:S(2)}) collective-permute-start(bf16[192,128]{1,0:T(8,128)(2,1)S(1)} %get-tuple-element.48), channel_id=1, source_target_pairs={{0,2},{1,3},{2,0},{3,1},{4,6},{5,7},{6,4},{7,5},{8,10},{9,11},{10,... | collective-permute-start | bytes 147464 | tf_op jit(solution)/shard_map/ppermute | solution.py:524
  43.8 0.8 %collective-permute-start.14 = (bf16[192,128]{1,0:T(8,128)(2,1)S(1)}, bf16[192,128]{1,0:T(8,128)(2,1)S(1)}, u32[]{:S(2)}, u32[]{:S(2)}) collective-permute-start(bf16[192,128]{1,0:T(8,128)(2,1)S(1)} %get-tuple-element.49), channel_id=1, source_target_pairs={{0,3},{1,2},{2,1},{3,0},{4,7},{5,6},{6,5},{7,4},{8,11},{9,10},{10,... | collective-permute-start | bytes 147464 | tf_op jit(solution)/shard_map/ppermute | solution.py:524
  44.6 0.0 collective-permute-done.12.refs_1_
  44.6 2.5 %collective-permute-done.13.refs_2_ = bf16[192,128]{1,0:T(8,128)(2,1)S(1)} collective-permute-done((bf16[192,128]{1,0:T(8,128)(2,1)S(1)}, bf16[192,128]{1,0:T(8,128)(2,1)S(1)}, u32[]{:S(2)}, u32[]{:S(2)}) %collective-permute-start.13) | collective-permute-done | bytes 49184 | tf_op jit(solution)/shard_map/ppermute | solution.py:524
  47.1 0.6 %collective-permute-done.14.refs_3_ = bf16[192,128]{1,0:T(8,128)(2,1)S(1)} collective-permute-done((bf16[192,128]{1,0:T(8,128)(2,1)S(1)}, bf16[192,128]{1,0:T(8,128)(2,1)S(1)}, u32[]{:S(2)}, u32[]{:S(2)}) %collective-permute-start.14) | collective-permute-done | bytes 49184 | tf_op jit(solution)/shard_map/ppermute | solution.py:524
  47.7 0.0 copy-done.8
  47.7 0.7 %shard_map.136 = (f32[256,128]{1,0:T(8,128)}, f32[4,64,128]{2,1,0:T(8,128)}, f32[2,64,128]{2,1,0:T(8,128)}) custom-call(f32[4,64,128]{2,1,0:T(8,128)S(1)} %get-tuple-element.37.warm, f32[2,64,128]{2,1,0:T(8,128)S(1)} %copy-done.8, f32[2,128,128]{2,1,0:T(8,128)S(1)} %shard_map.134.speed, bf16[192,128]{1,0:T(8,128)(2,1)S(1)} %get-tuple-element.46.refs_0_, ...), custom_call_target="tpu_custom_call" | custom-call | flops 11500000 | bytes 524288 | tf_op jit(solution)/shard_map/pallas_call | solution.py:39
  (2 shorter events, 0.0 us)
Async XLA Ops:
  0.6 0.7 %copy-start.10 = (s32[1,1,4]{2,1,0:T(1,128)S(1)}, s32[1,1,4]{2,1,0:T(1,128)}, u32[]{:S(2)}) copy-start(s32[1,1,4]{2,1,0:T(1,128)} %links.1) | copy-start | bytes 52
  1.3 0.9 %copy-start = (f32[4,64,128]{2,1,0:T(8,128)S(1)}, f32[4,64,128]{2,1,0:T(8,128)}, u32[]{:S(2)}) copy-start(f32[4,64,128]{2,1,0:T(8,128)} %water.3) | copy-start | bytes 393220
  2.2 1.0 %copy-start.2 = (f32[1,1,5,16384]{3,1,2,0:T(1,128)S(1)}, f32[1,1,5,16384]{3,1,2,0:T(1,128)}, u32[]{:S(2)}) copy-start(f32[1,1,5,16384]{3,1,2,0:T(1,128)} %param.18) | copy-start | bytes 983044
  3.2 1.0 %copy-start.3 = (f32[1,1,5,16384]{3,1,2,0:T(1,128)S(1)}, f32[1,1,5,16384]{3,1,2,0:T(1,128)}, u32[]{:S(2)}) copy-start(f32[1,1,5,16384]{3,1,2,0:T(1,128)} %param.19) | copy-start | bytes 983044
  4.1 0.9 %copy-start.6 = (f32[1,1,2,16384]{3,2,1,0:T(2,128)S(1)}, f32[1,1,2,16384]{3,2,1,0:T(2,128)}, u32[]{:S(2)}) copy-start(f32[1,1,2,16384]{3,2,1,0:T(2,128)} %param.20) | copy-start | bytes 393220
  6.9 27.2 %all-to-all-start = ((bf16[16,80,128]{2,1,0:T(8,128)(2,1)}), bf16[16,80,128]{2,1,0:T(8,128)(2,1)S(1)}, u32[]{:S(2)}, u32[]{:S(2)}) async-start(bf16[16,80,128]{2,1,0:T(8,128)(2,1)} %get-tuple-element.35), calls=%async_computation | async-start | bytes 655360 | tf_op jit(solution)/shard_map/all_to_all | solution.py:573
  14.2 10.2 %copy-start.7 = (f32[1,1,2,16384]{3,2,1,0:T(2,128)S(1)}, f32[1,1,2,16384]{3,2,1,0:T(2,128)}, u32[]{:S(2)}) copy-start(f32[1,1,2,16384]{3,2,1,0:T(2,128)} %param.21) | copy-start | bytes 393220
  16.5 2.2 %collective-permute-start = (bf16[320,128]{1,0:T(8,128)(2,1)}, bf16[320,128]{1,0:T(8,128)(2,1)S(1)}, u32[]{:S(2)}, u32[]{:S(2)}) collective-permute-start(bf16[320,128]{1,0:T(8,128)(2,1)} %get-tuple-element.31), channel_id=1, source_target_pairs={{0,1},{1,0},{2,3},{3,2},{4,5},{5,4},{6,7},{7,6},{8,9},{9,8},{10,11... | collective-permute-start | bytes 245768 | tf_op jit(solution)/shard_map/ppermute | solution.py:524
  17.0 5.8 %collective-permute-start.1 = (bf16[320,128]{1,0:T(8,128)(2,1)}, bf16[320,128]{1,0:T(8,128)(2,1)S(1)}, u32[]{:S(2)}, u32[]{:S(2)}) collective-permute-start(bf16[320,128]{1,0:T(8,128)(2,1)} %get-tuple-element.32), channel_id=1, source_target_pairs={{0,2},{1,3},{2,0},{3,1},{4,6},{5,7},{6,4},{7,5},{8,10},{9,11},{10,... | collective-permute-start | bytes 245768 | tf_op jit(solution)/shard_map/ppermute | solution.py:524
  18.7 5.7 %collective-permute-start.2 = (bf16[320,128]{1,0:T(8,128)(2,1)}, bf16[320,128]{1,0:T(8,128)(2,1)S(1)}, u32[]{:S(2)}, u32[]{:S(2)}) collective-permute-start(bf16[320,128]{1,0:T(8,128)(2,1)} %get-tuple-element.33), channel_id=1, source_target_pairs={{0,3},{1,2},{2,1},{3,0},{4,7},{5,6},{6,5},{7,4},{8,11},{9,10},{10,... | collective-permute-start | bytes 245768 | tf_op jit(solution)/shard_map/ppermute | solution.py:524
  24.4 0.9 %copy-start.4 = (bf16[320,128]{1,0:T(8,128)(2,1)S(1)}, bf16[320,128]{1,0:T(8,128)(2,1)}, u32[]{:S(2)}) copy-start(bf16[320,128]{1,0:T(8,128)(2,1)} %get-tuple-element.30.refs_0_) | copy-start | bytes 245764
  25.3 10.8 %copy-start.1 = (f32[4,64,128]{2,1,0:T(8,128)S(1)}, f32[4,64,128]{2,1,0:T(8,128)}, u32[]{:S(2)}) copy-start(f32[4,64,128]{2,1,0:T(8,128)} %water.3) | copy-start | bytes 393220
  25.8 10.2 %copy-start.9 = (f32[64,128]{1,0:T(8,128)S(1)}, f32[64,128]{1,0:T(8,128)}, u32[]{:S(2)}) copy-start(f32[64,128]{1,0:T(8,128)} %mixing.1) | copy-start | bytes 98308
  25.8 5.5 %collective-permute-start.5 = (bf16[32,128]{1,0:T(8,128)(2,1)S(1)}, bf16[32,128]{1,0:T(8,128)(2,1)S(1)}, u32[]{:S(2)}, u32[]{:S(2)}) collective-permute-start(bf16[32,128]{1,0:T(8,128)(2,1)S(1)} %get-tuple-element.34), channel_id=1, source_target_pairs={{0,12},{4,8},{8,4},{12,0},{1,13},{5,9},{9,5},{13,1},{2,14},{6,10},... | collective-permute-start | bytes 24584 | tf_op jit(solution)/shard_map/ppermute | solution.py:519
  29.5 4.5 %collective-permute-start.4 = (bf16[32,128]{1,0:T(8,128)(2,1)S(1)}, bf16[32,128]{1,0:T(8,128)(2,1)S(1)}, u32[]{:S(2)}, u32[]{:S(2)}) collective-permute-start(bf16[32,128]{1,0:T(8,128)(2,1)S(1)} %get-tuple-element.34), channel_id=1, source_target_pairs={{0,8},{4,12},{8,0},{12,4},{1,9},{5,13},{9,1},{13,5},{2,10},{6,14},... | collective-permute-start | bytes 24584 | tf_op jit(solution)/shard_map/ppermute | solution.py:519
  29.6 4.5 %collective-permute-start.3 = (bf16[32,128]{1,0:T(8,128)(2,1)S(1)}, bf16[32,128]{1,0:T(8,128)(2,1)S(1)}, u32[]{:S(2)}, u32[]{:S(2)}) collective-permute-start(bf16[32,128]{1,0:T(8,128)(2,1)S(1)} %get-tuple-element.34), channel_id=1, source_target_pairs={{0,4},{4,0},{8,12},{12,8},{1,5},{5,1},{9,13},{13,9},{2,6},{6,2},{1... | collective-permute-start | bytes 24584 | tf_op jit(solution)/shard_map/ppermute | solution.py:519
  34.1 4.6 %collective-permute-start.8 = (bf16[128,128]{1,0:T(8,128)(2,1)S(1)}, bf16[128,128]{1,0:T(8,128)(2,1)S(1)}, u32[]{:S(2)}, u32[]{:S(2)}) collective-permute-start(bf16[128,128]{1,0:T(8,128)(2,1)S(1)} %pad_maximum_fusion.refs_0_), channel_id=1, source_target_pairs={{0,3},{1,2},{2,1},{3,0},{4,7},{5,6},{6,5},{7,4},{8,11},{9,10},{10,... | collective-permute-start | bytes 98312 | tf_op jit(solution)/shard_map/ppermute | solution.py:519
  34.2 4.8 %collective-permute-start.7 = (bf16[128,128]{1,0:T(8,128)(2,1)S(1)}, bf16[128,128]{1,0:T(8,128)(2,1)S(1)}, u32[]{:S(2)}, u32[]{:S(2)}) collective-permute-start(bf16[128,128]{1,0:T(8,128)(2,1)S(1)} %pad_maximum_fusion.refs_0_), channel_id=1, source_target_pairs={{0,2},{1,3},{2,0},{3,1},{4,6},{5,7},{6,4},{7,5},{8,10},{9,11},{10,... | collective-permute-start | bytes 98312 | tf_op jit(solution)/shard_map/ppermute | solution.py:519
  35.4 3.6 %collective-permute-start.6 = (bf16[128,128]{1,0:T(8,128)(2,1)S(1)}, bf16[128,128]{1,0:T(8,128)(2,1)S(1)}, u32[]{:S(2)}, u32[]{:S(2)}) collective-permute-start(bf16[128,128]{1,0:T(8,128)(2,1)S(1)} %pad_maximum_fusion.refs_0_), channel_id=1, source_target_pairs={{0,1},{1,0},{2,3},{3,2},{4,5},{5,4},{6,7},{7,6},{8,9},{9,8},{10,11... | collective-permute-start | bytes 98312 | tf_op jit(solution)/shard_map/ppermute | solution.py:519
  37.0 4.1 %collective-permute-start.11 = (bf16[64,128]{1,0:T(8,128)(2,1)S(1)}, bf16[64,128]{1,0:T(8,128)(2,1)S(1)}, u32[]{:S(2)}, u32[]{:S(2)}) collective-permute-start(bf16[64,128]{1,0:T(8,128)(2,1)S(1)} %get-tuple-element.45.refs_4_), channel_id=1, source_target_pairs={{0,3},{1,2},{2,1},{3,0},{4,7},{5,6},{6,5},{7,4},{8,11},{9,10},{10,... | collective-permute-start | bytes 49160 | tf_op jit(solution)/shard_map/ppermute | solution.py:519
  37.8 3.7 %collective-permute-start.10 = (bf16[64,128]{1,0:T(8,128)(2,1)S(1)}, bf16[64,128]{1,0:T(8,128)(2,1)S(1)}, u32[]{:S(2)}, u32[]{:S(2)}) collective-permute-start(bf16[64,128]{1,0:T(8,128)(2,1)S(1)} %get-tuple-element.45.refs_4_), channel_id=1, source_target_pairs={{0,2},{1,3},{2,0},{3,1},{4,6},{5,7},{6,4},{7,5},{8,10},{9,11},{10,... | collective-permute-start | bytes 49160 | tf_op jit(solution)/shard_map/ppermute | solution.py:519
  38.7 2.9 %collective-permute-start.9 = (bf16[64,128]{1,0:T(8,128)(2,1)S(1)}, bf16[64,128]{1,0:T(8,128)(2,1)S(1)}, u32[]{:S(2)}, u32[]{:S(2)}) collective-permute-start(bf16[64,128]{1,0:T(8,128)(2,1)S(1)} %get-tuple-element.45.refs_4_), channel_id=1, source_target_pairs={{0,1},{1,0},{2,3},{3,2},{4,5},{5,4},{6,7},{7,6},{8,9},{9,8},{10,11... | collective-permute-start | bytes 49160 | tf_op jit(solution)/shard_map/ppermute | solution.py:519
  39.0 2.6 %copy-start.5 = (bf16[320,128]{1,0:T(8,128)(2,1)S(1)}, bf16[320,128]{1,0:T(8,128)(2,1)}, u32[]{:S(2)}) copy-start(bf16[320,128]{1,0:T(8,128)(2,1)} %get-tuple-element.30.refs_0_) | copy-start | bytes 245764
  41.6 6.1 %copy-start.8 = (f32[2,64,128]{2,1,0:T(8,128)S(1)}, f32[2,64,128]{2,1,0:T(8,128)}, u32[]{:S(2)}) copy-start(f32[2,64,128]{2,1,0:T(8,128)} %currents.1) | copy-start | bytes 196612
  42.7 1.9 %collective-permute-start.12 = (bf16[192,128]{1,0:T(8,128)(2,1)S(1)}, bf16[192,128]{1,0:T(8,128)(2,1)S(1)}, u32[]{:S(2)}, u32[]{:S(2)}) collective-permute-start(bf16[192,128]{1,0:T(8,128)(2,1)S(1)} %get-tuple-element.47), channel_id=1, source_target_pairs={{0,1},{1,0},{2,3},{3,2},{4,5},{5,4},{6,7},{7,6},{8,9},{9,8},{10,11... | collective-permute-start | bytes 147464 | tf_op jit(solution)/shard_map/ppermute | solution.py:524
  42.7 4.4 %collective-permute-start.13 = (bf16[192,128]{1,0:T(8,128)(2,1)S(1)}, bf16[192,128]{1,0:T(8,128)(2,1)S(1)}, u32[]{:S(2)}, u32[]{:S(2)}) collective-permute-start(bf16[192,128]{1,0:T(8,128)(2,1)S(1)} %get-tuple-element.48), channel_id=1, source_target_pairs={{0,2},{1,3},{2,0},{3,1},{4,6},{5,7},{6,4},{7,5},{8,10},{9,11},{10,... | collective-permute-start | bytes 147464 | tf_op jit(solution)/shard_map/ppermute | solution.py:524
  43.8 4.0 %collective-permute-start.14 = (bf16[192,128]{1,0:T(8,128)(2,1)S(1)}, bf16[192,128]{1,0:T(8,128)(2,1)S(1)}, u32[]{:S(2)}, u32[]{:S(2)}) collective-permute-start(bf16[192,128]{1,0:T(8,128)(2,1)S(1)} %get-tuple-element.49), channel_id=1, source_target_pairs={{0,3},{1,2},{2,1},{3,0},{4,7},{5,6},{6,5},{7,4},{8,11},{9,10},{10,... | collective-permute-start | bytes 147464 | tf_op jit(solution)/shard_map/ppermute | solution.py:524

commit v5 on v3

--- a/solution.py
+++ b/solution.py
@@ -1,4 +1,5 @@
 import functools
+import math
 
 import jax
 import jax.numpy as jnp
@@ -64,14 +65,19 @@
 
 def forward_kernel(group, blocks_h, rows_h, cols_h, currents_h, *refs):
     devices, members, place = group
-    outs, (blocks, currents, fields, arrived, left) = refs[:members], refs[members:]
+    outs, (blocks, currents, rows, cols, fields, arrived, left) = refs[:members], refs[members:]
     pairs, side, width = rows_h.shape
     depth = cols_h.shape[1]
-    names = pltpu.make_async_copy(blocks_h, blocks, arrived.at[0])
-    water = pltpu.make_async_copy(currents_h, currents, arrived.at[1])
-    names.start()
-    water.start()
-    names.wait()
+    loads = [
+        pltpu.make_async_copy(source, target, arrived.at[i])
+        for i, (source, target) in enumerate(
+            ((blocks_h, blocks), (currents_h, currents), (rows_h, rows), (cols_h, cols))
+        )
+    ]
+    for load in loads:
+        load.start()
+    for load in loads:
+        load.wait()
     me = place()
     owners = [lax.rem(lax.rem(blocks[0, m], devices), members) for m in range(pairs)]
     copies = []
@@ -82,10 +88,10 @@
             pair = jnp.where(owners[m] == partner, m, pair)
             found = jnp.where(owners[m] == partner, 1, found)
         copies.append(
-            pltpu.make_async_copy(rows_h.at[pair], out.at[pl.ds(0, side)], left.at[3 * k])
+            pltpu.make_async_copy(rows.at[pair], out.at[pl.ds(0, side)], left.at[3 * k])
         )
         copies.append(
-            pltpu.make_async_copy(cols_h.at[pair], out.at[pl.ds(side, depth)], left.at[3 * k + 1])
+            pltpu.make_async_copy(cols.at[pair], out.at[pl.ds(side, depth)], left.at[3 * k + 1])
         )
         if pairs < members:
             keep = jnp.where(found > 0, 1.0, 0.0).astype(F32)
@@ -93,8 +99,6 @@
             keep = None
         copies[-2].start()
         copies[-1].start()
-        if k == 0:
-            water.wait()
         if k == 0 or keep is not None:
             for c in range(2):
                 field = currents[c] if keep is None else currents[c] * keep
@@ -185,10 +189,10 @@
     cols_o[...] = jnp.concatenate(beside, axis=0)
 
 
-def relay_kernel(tiles, place, cols, *refs):
-    messages, out = refs[:tiles], refs[tiles]
-    for k, message in enumerate(messages):
-        out[k * SIDE_ROWS : (k + 1) * SIDE_ROWS] = message[0:SIDE_ROWS]
+def relay_kernel(tiles, place, cols, messages, out):
+    step = messages.shape[0] // tiles
+    for k in range(tiles):
+        out[k * SIDE_ROWS : (k + 1) * SIDE_ROWS] = messages[k * step : k * step + SIDE_ROWS]
     levels = cols.shape[0] // 2
     before, after = around(place(), tiles, messages, levels)
     rows = []
@@ -199,8 +203,10 @@
 
 def around(me, tiles, messages, levels):
     before, after = 0.0, 0.0
+    step = messages.shape[0] // tiles
     for k in range(1, tiles):
-        strips = messages[k][SIDE_ROWS : SIDE_ROWS + 4 * levels].astype(F32)
+        at = k * step + SIDE_ROWS
+        strips = messages[at : at + 4 * levels].astype(F32)
         before = before + strips[: 2 * levels] * flag((me > 0) & ((me ^ k) == me - 1))
         after = after + strips[2 * levels :] * flag((me < tiles - 1) & ((me ^ k) == me + 1))
     return before, after
@@ -246,11 +252,12 @@
     out[...] = store[...].astype(BF16)
 
 
-def ocean_kernel(counts, tile_place, member_place, water, mixing, *refs):
+def ocean_kernel(
+    counts, tile_place, member_place, water, mixing, messages, relays, warm_o, top_o, table_o
+):
     tiles, subs, levs = counts
     members = subs * levs
-    messages, relays = refs[:tiles], refs[tiles : tiles + members]
-    warm_o, top_o, table_o = refs[tiles + members :]
+    step = relays.shape[0] // members
     levels, rows, width = water.shape
     my_tile, me = tile_place(), member_place()
     halo = {}
@@ -260,7 +267,8 @@
         inside = (beyond >= 0) & (beyond < members)
         found = 0.0
         for k in range(1, members):
-            strip = relays[k][tiles * SIDE_ROWS : tiles * SIDE_ROWS + 4 * levels].astype(F32)
+            at = k * step + tiles * SIDE_ROWS
+            strip = relays[at : at + 4 * levels].astype(F32)
             found = found + strip * flag(inside & ((me ^ k) == beyond))
         beside, corners = found[: 2 * levels], found[2 * levels :]
         if ds > 0:
@@ -274,8 +282,8 @@
     names = []
     for k in range(tiles):
         for m in range(members):
-            at = k * SIDE_ROWS
-            names.append(relays[m][at : at + TILE_ROWS].astype(F32)[NAMES_ROW : NAMES_ROW + 1])
+            at = m * step + k * SIDE_ROWS
+            names.append(relays[at : at + TILE_ROWS].astype(F32)[NAMES_ROW : NAMES_ROW + 1])
     names = jnp.concatenate(names, axis=0)
     table = (128.0 * names + roll(names, -4, 1)).astype(jnp.int32)
     table_o[...] = jnp.where((table >= 0) & (column < 4), table ^ mine, -1)
@@ -330,13 +338,15 @@
 
 
 def subcycles_kernel(tiles, members, table, viscous, gain, speed, push, *refs):
-    relays, push_relays = refs[:members], refs[members : 2 * members]
-    out, rims, push_rims = refs[2 * members :]
+    relays, push_relays, out, rims, push_rims = refs
+    step = relays.shape[0] // members
     size = viscous.shape[0]
     for k in range(tiles):
         for m in range(members):
-            rims[k * members + m] = relays[m][k * SIDE_ROWS : (k + 1) * SIDE_ROWS]
-            push_rims[k * members + m] = push_relays[m][k * PUSH_ROWS : (k + 1) * PUSH_ROWS]
+            at = m * step + k * SIDE_ROWS
+            rims[k * members + m] = relays[at : at + SIDE_ROWS]
+            at = (m * tiles + k) * PUSH_ROWS
+            push_rims[k * members + m] = push_relays[at : at + PUSH_ROWS]
     half = DEPTH
     high = 2 * DEPTH
     sub = iota((high, size), 0)
@@ -450,12 +460,10 @@
 
 
 def back_kernel(group, side, drag, conduct, current, speed, *refs):
-    chunks = refs[:group]
-    tops = refs[group : 2 * group]
-    outs = refs[2 * group :]
+    chunks, tops, outs = refs[:group], refs[group], refs[group + 1 :]
     size = drag.shape[0]
     depth = chunks[0].shape[0] - 3 * side
-    warm = remap_forward(chunks, [[t[...]] for t in tops], side, depth)
+    warm = remap_forward(chunks, [[tops[k * side : (k + 1) * side]] for k in range(group)], side, depth)
     heat = conduct[...] * warm
     fluxes = [heat.astype(BF16)]
     for c in range(2):
@@ -525,10 +533,22 @@
     def member_place():
         return lax.axis_index("sub") * lev_count + lax.axis_index("lev")
 
-    def swap(value, axes, count):
-        return [value] + [
-            lax.ppermute(value, axes, [(i, i ^ k) for i in range(count)]) for k in range(1, count)
-        ]
+    def swap(value, axes, count, k):
+        return lax.ppermute(value, axes, [(i, i ^ k) for i in range(count)])
+
+    def gather(value, axes, steps):
+        count = math.prod(lax.axis_size(a) for a in axes)
+        for k in steps:
+            value = jnp.concatenate([value, swap(value, axes, count, k)], axis=0)
+        return value
+
+    def doublings(count):
+        return [1 << i for i in range(count.bit_length() - 1)]
+
+    def gather_members(value):
+        for k in reversed(doublings(group)):
+            value = jnp.stack([value, swap(value, group_axes, group, k)], axis=-3)
+        return value.reshape(group * value.shape[-2], value.shape[-1])
 
     def swap_each(values):
         return [values[0]] + [
@@ -554,8 +574,10 @@
         scratch=[
             pltpu.SMEM((1, pairs), jnp.int32),
             pltpu.VMEM((2, side, width), F32),
+            pltpu.VMEM((pairs, side, size), BF16),
+            pltpu.VMEM((pairs, size, width), BF16),
             pltpu.VMEM((1 if pairs == group else group, 2 * side, width), BF16),
-            pltpu.SemaphoreType.DMA((2,)),
+            pltpu.SemaphoreType.DMA((4,)),
             pltpu.SemaphoreType.DMA((3 * group,)),
         ],
         hbm=(0, 1, 2, 3),
@@ -580,7 +602,7 @@
         scratch=[pltpu.VMEM((SIDE_ROWS + 4 * levels, size), F32)],
         smem=(0,),
     )
-    messages = swap(message, "tile", tile_count)
+    messages = gather(message, ("tile",), doublings(tile_count))
 
     push_message, current_ice, push = call(
         functools.partial(forcing_kernel, group, side),
@@ -589,15 +611,15 @@
         scratch=[pltpu.VMEM((PUSH_ROWS, size), F32)],
     )
     cols, push_message = lax.optimization_barrier((cols, push_message))
-    push_messages = swap(push_message, "tile", tile_count)
+    push_messages = gather(push_message, ("tile",), doublings(tile_count))
 
     relay = call(
         functools.partial(relay_kernel, tile_count, tile_place),
         shape(tile_count * SIDE_ROWS + 4 * levels, size, dtype=BF16),
-        (cols, *messages),
-    )
-    relays = swap(relay, group_axes, group)
-    push_relays = swap(jnp.concatenate(push_messages, axis=0), group_axes, group)
+        (cols, messages),
+    )
+    relays = gather_members(relay)
+    push_relays = gather_members(push_messages)
 
     warm, top, table = call(
         functools.partial(
@@ -608,16 +630,16 @@
             shape(side, width, dtype=BF16 if lev_count == 1 else F32),
             shape(devices, width, dtype=jnp.int32),
         ],
-        (water_heat_state, diffusion_coefficient, *messages, *relays),
+        (water_heat_state, diffusion_coefficient, messages, relays),
     )
     if lev_count > 1:
         top = lax.psum(top, "lev").astype(BF16)
-    tops = swap(top, group_axes, group)
+    tops = gather_members(top)
 
     speed = call(
         functools.partial(subcycles_kernel, tile_count, group),
         planes,
-        (table, viscous, gain, speed, push, *relays, *push_relays),
+        (table, viscous, gain, speed, push, relays, push_relays),
         scratch=[
             pltpu.VMEM((devices, SIDE_ROWS, size), BF16),
             pltpu.VMEM((devices, PUSH_ROWS, size), BF16),
@@ -628,7 +650,7 @@
     replies = call(
         functools.partial(back_kernel, group, side),
         [shape(3 * side, width, dtype=BF16)] * group,
-        (drag, conduct, current_ice, speed, *chunks, *tops),
+        (drag, conduct, current_ice, speed, *chunks, tops),
     )
     replies = swap_each(replies)
     if lev_count > 1:

time: 36.6 us -> 42 us (1.15)
  waiting for transfers between devices: 6.08 us -> 12.3 us
  starting transfers between devices: 19.6 us -> 18.2 us
  local copies, waits for them, and re-layouts: 0.69 us -> 1.47 us
    ppermute x15 -> x10, waiting for transfers between devices: 3 us -> 9.34 us  [swap(): return lax.ppermute(value, axes, [(i, i ^ k) for i in range(count)])]
    ppermute x15 -> x10, starting transfers between devices: 14.6 us -> 13.2 us  [swap(): return lax.ppermute(value, axes, [(i, i ^ k) for i in range(count)])]
    unnamed x21 -> x22, local copies, waits for them, and re-layouts: 0.68 us -> 1.41 us
  transfers between devices with their start and end apart: 21 -> 16, of which waited for: 6 -> 6; matrix products, arithmetic and copies ran while one was open for 0% -> 0% of each run, Pallas kernels for 13% -> 10%
where the time goes in v5:
time: 42 us; the launch traced here: 41.8 us
  starting transfers between devices  18.2 us (43%)
  waiting for transfers between devices  12.3 us (29%)
  Pallas kernels  8.86 us (21%)
  local copies, waits for them, and re-layouts  1.47 us (4%)
  between operations  0.88 us (2%)
    ppermute x10, starting transfers between devices, swap(): return lax.ppermute(value, axes, [(i, i ^ k) for i in range(count)])  13.2 us
    ppermute x10, waiting for transfers between devices, swap(): return lax.ppermute(value, axes, [(i, i ^ k) for i in range(count)])  9.34 us
    pallas_call x8, Pallas kernels, call(): pl.pallas_call(kernel, out_shape=outs, in_specs=specs, out_specs=jax.tree...  8.86 us
    ppermute x6, starting transfers between devices, swap_each(): lax.ppermute(values[k], group_axes, [(i, i ^ k) for i in range(group)])  5.07 us
    ppermute x6, waiting for transfers between devices, swap_each(): lax.ppermute(values[k], group_axes, [(i, i ^ k) for i in range(group)])  2.95 us
    unnamed x22, local copies, waits for them, and re-layouts  1.41 us
  transfers between devices with their start and end apart: 16, of which 6 were waited for; matrix products, arithmetic and copies ran while one was open for 0% of the time, Pallas kernels for 10%

profile of v5, /device:TPU:0, one launch (start us, length us, event | category | flops | bytes accessed | tf_op | source)
XLA Modules:
  0.0 41.8 jit_solution(12092988193947051627)
XLA Ops:
  0.6 0.0 copy-start
  0.6 0.0 copy-start.1
  0.7 0.0 copy-start.2
  0.7 0.0 copy-start.4
  0.7 2.3 %shard_map.130 = (bf16[320,128]{1,0:T(8,128)(2,1)}, bf16[320,128]{1,0:T(8,128)(2,1)}, bf16[320,128]{1,0:T(8,128)(2,1)}, bf16[320,128]{1,0:T(8,128)(2,1)}) custom-call(s32[1,4]{1,0:T(1,128)} %blocks_h.1, bf16[4,64,128]{2,1,0:T(8,128)(2,1)} %bitcast.58, bf16[4,128,128]{2,1,0:T(8,128)(2,1)} %bitcast.56, f32[2,64,128]{2,1,0:T(8,128)} %currents.1), custom_call_target="tpu_custom_call" | custom-call | flops 2300000000 | bytes 262160 | tf_op jit(solution)/shard_map/pallas_call | solution.py:41
  3.0 0.5 %collective-permute-start.2 = (bf16[320,128]{1,0:T(8,128)(2,1)}, bf16[320,128]{1,0:T(8,128)(2,1)S(1)}, u32[]{:S(2)}, u32[]{:S(2)}) collective-permute-start(bf16[320,128]{1,0:T(8,128)(2,1)} %get-tuple-element.32), channel_id=1, source_target_pairs={{0,1},{1,0},{2,3},{3,2},{4,5},{5,4},{6,7},{7,6},{8,9},{9,8},{10,11... | collective-permute-start | bytes 245768 | tf_op jit(solution)/shard_map/ppermute | solution.py:555
  3.5 2.6 %collective-permute-start.3 = (bf16[320,128]{1,0:T(8,128)(2,1)}, bf16[320,128]{1,0:T(8,128)(2,1)S(1)}, u32[]{:S(2)}, u32[]{:S(2)}) collective-permute-start(bf16[320,128]{1,0:T(8,128)(2,1)} %get-tuple-element.33), channel_id=1, source_target_pairs={{0,2},{1,3},{2,0},{3,1},{4,6},{5,7},{6,4},{7,5},{8,10},{9,11},{10,... | collective-permute-start | bytes 245768 | tf_op jit(solution)/shard_map/ppermute | solution.py:555
  6.1 0.1 collective-permute-start.4
  6.1 0.0 copy-start.8
  6.2 0.0 copy-done
  6.2 0.0 copy-done.1
  6.2 0.0 copy-done.2
  6.2 0.0 copy-done.4
  6.2 0.6 %copy-done.8 = s32[1,1,4]{2,1,0:T(1,128)S(1)} copy-done((s32[1,1,4]{2,1,0:T(1,128)S(1)}, s32[1,1,4]{2,1,0:T(1,128)}, u32[]{:S(2)}) %copy-start.8) | copy-done | bytes 40
  6.8 0.9 %shard_map.131 = (bf16[80,128]{1,0:T(8,128)(2,1)S(1)}, f32[8,128]{1,0:T(8,128)S(1)}, f32[128,128]{1,0:T(8,128)S(1)}, f32[128,128]{1,0:T(8,128)S(1)}, f32[128,128...) custom-call(s32[1,1,4]{2,1,0:T(1,128)S(1)} %copy-done.8, ...), custom_call_target="tpu_custom_call" | custom-call | flops 11500000 | bytes 917520 | tf_op jit(solution)/shard_map/pallas_call | solution.py:41
  7.7 0.0 copy-start.5
  7.7 1.9 %collective-permute-start = (bf16[80,128]{1,0:T(8,128)(2,1)S(1)}, bf16[80,128]{1,0:T(8,128)(2,1)S(1)}, u32[]{:S(2)}, u32[]{:S(2)}) collective-permute-start(bf16[80,128]{1,0:T(8,128)(2,1)S(1)} %get-tuple-element.36), channel_id=1, source_target_pairs={{0,4},{4,0},{8,12},{12,8},{1,5},{5,1},{9,13},{13,9},{2,6},{6,2},{1... | collective-permute-start | bytes 61448 | tf_op jit(solution)/shard_map/ppermute | solution.py:537
  9.6 2.0 %collective-permute-done = bf16[80,128]{1,0:T(8,128)(2,1)S(1)} collective-permute-done((bf16[80,128]{1,0:T(8,128)(2,1)S(1)}, bf16[80,128]{1,0:T(8,128)(2,1)S(1)}, u32[]{:S(2)}, u32[]{:S(2)}) %collective-permute-start) | collective-permute-done | bytes 20512 | tf_op jit(solution)/shard_map/ppermute | solution.py:537
  11.6 0.0 copy-start.3
  11.6 2.8 %collective-permute-start.1 = (bf16[160,128]{1,0:T(8,128)(2,1)S(1)}, bf16[160,128]{1,0:T(8,128)(2,1)S(1)}, u32[]{:S(2)}, u32[]{:S(2)}) collective-permute-start(bf16[160,128]{1,0:T(8,128)(2,1)S(1)} %pad_maximum_fusion.5), channel_id=1, source_target_pairs={{0,8},{4,12},{8,0},{12,4},{1,9},{5,13},{9,1},{13,5},{2,10},{6,14},... | collective-permute-start | bytes 122888 | tf_op jit(solution)/shard_map/ppermute | solution.py:537
  14.4 2.1 %collective-permute-done.1 = bf16[160,128]{1,0:T(8,128)(2,1)S(1)} collective-permute-done((bf16[160,128]{1,0:T(8,128)(2,1)S(1)}, bf16[160,128]{1,0:T(8,128)(2,1)S(1)}, u32[]{:S(2)}, u32[]{:S(2)}) %collective-permute-start.1) | collective-permute-done | bytes 40992 | tf_op jit(solution)/shard_map/ppermute | solution.py:537
  16.5 0.0 collective-permute-done.2.refs_1_
  16.5 0.0 collective-permute-done.3.refs_2_
  16.5 0.0 collective-permute-done.4.refs_3_
  16.6 0.0 copy-done.5
  16.6 0.0 copy-done.3
  16.6 0.6 %shard_map.132 = (bf16[32,128]{1,0:T(8,128)(2,1)S(1)}, f32[2,128,128]{2,1,0:T(8,128)S(1)}, f32[2,128,128]{2,1,0:T(8,128)S(1)}) custom-call(f32[128,128]{1,0:T(8,128)S(1)} %get-tuple-element.38.mass, f32[128,128]{1,0:T(8,128)S(1)} %get-tuple-element.39.drag, f32[256,128]{1,0:T(8,128)S(1)} %bitcast.47, bf16[320,128]{1,0:T(8,128)(2,1)S(1)} %copy-done.3, ...), custom_call_target="tpu_custom_call" | custom-call | flops 11500000 | bytes 589824 | tf_op jit(solution)/shard_map/pallas_call | solution.py:41
  17.1 1.8 %collective-permute-start.7 = (bf16[32,128]{1,0:T(8,128)(2,1)S(1)}, bf16[32,128]{1,0:T(8,128)(2,1)S(1)}, u32[]{:S(2)}, u32[]{:S(2)}) collective-permute-start(bf16[32,128]{1,0:T(8,128)(2,1)S(1)} %get-tuple-element.48), channel_id=1, source_target_pairs={{0,4},{4,0},{8,12},{12,8},{1,5},{5,1},{9,13},{13,9},{2,6},{6,2},{1... | collective-permute-start | bytes 24584 | tf_op jit(solution)/shard_map/ppermute | solution.py:537
  19.0 1.6 %collective-permute-start.5 = (bf16[272,128]{1,0:T(8,128)(2,1)S(1)}, bf16[272,128]{1,0:T(8,128)(2,1)S(1)}, u32[]{:S(2)}, u32[]{:S(2)}) collective-permute-start(bf16[272,128]{1,0:T(8,128)(2,1)S(1)} %shard_map.133), channel_id=1, source_target_pairs={{0,2},{1,3},{2,0},{3,1},{4,6},{5,7},{6,4},{7,5},{8,10},{9,11},{10,... | collective-permute-start | bytes 208904 | tf_op jit(solution)/shard_map/ppermute | solution.py:537
  20.6 0.3 collective-permute-done.7
  20.8 2.8 %collective-permute-start.8 = (bf16[64,128]{1,0:T(8,128)(2,1)S(1)}, bf16[64,128]{1,0:T(8,128)(2,1)S(1)}, u32[]{:S(2)}, u32[]{:S(2)}) collective-permute-start(bf16[64,128]{1,0:T(8,128)(2,1)S(1)} %pad_maximum_fusion.7), channel_id=1, source_target_pairs={{0,8},{4,12},{8,0},{12,4},{1,9},{5,13},{9,1},{13,5},{2,10},{6,14},... | collective-permute-start | bytes 49160 | tf_op jit(solution)/shard_map/ppermute | solution.py:537
  23.7 0.0 collective-permute-done.5
  23.7 0.1 collective-permute-start.6
  23.8 1.7 %collective-permute-done.8 = bf16[64,128]{1,0:T(8,128)(2,1)S(1)} collective-permute-done((bf16[64,128]{1,0:T(8,128)(2,1)S(1)}, bf16[64,128]{1,0:T(8,128)(2,1)S(1)}, u32[]{:S(2)}, u32[]{:S(2)}) %collective-permute-start.8) | collective-permute-done | bytes 16416 | tf_op jit(solution)/shard_map/ppermute | solution.py:537
  25.5 1.7 %collective-permute-start.9 = (bf16[128,128]{1,0:T(8,128)(2,1)S(1)}, bf16[128,128]{1,0:T(8,128)(2,1)S(1)}, u32[]{:S(2)}, u32[]{:S(2)}) collective-permute-start(bf16[128,128]{1,0:T(8,128)(2,1)S(1)} %constant_dynamic-update-slice_fusion.3), channel_id=1, source_target_pairs={{0,2},{1,3},{2,0},{3,1},{4,6},{5,7},{6,4},{7,5},{8,10},{9,11},{10,... | collective-permute-start | bytes 98312 | tf_op jit(solution)/shard_map/ppermute | solution.py:537
  27.2 0.0 collective-permute-done.6
  27.2 0.0 copy-start.7
  27.3 0.7 %copy-done.7 = f32[64,128]{1,0:T(8,128)S(1)} copy-done((f32[64,128]{1,0:T(8,128)S(1)}, f32[64,128]{1,0:T(8,128)}, u32[]{:S(2)}) %copy-start.7) | copy-done | bytes 32792
  28.0 1.0 %shard_map.134 = (f32[4,64,128]{2,1,0:T(8,128)S(1)}, bf16[64,128]{1,0:T(8,128)(2,1)S(1)}, s32[16,128]{1,0:T(8,128)S(1)}) custom-call(f32[4,64,128]{2,1,0:T(8,128)S(1)} %copy-done, f32[64,128]{1,0:T(8,128)S(1)} %copy-done.7, bf16[320,128]{1,0:T(8,128)(2,1)S(1)} %constant_dynamic-update-slice_fusion.messages, bf16[1088,128]{1,0:T(8,128)(2,1)S(1)} %bitcast.39), custom_call_target="tpu_custom_call" | custom-call | flops 11500000 | bytes 524288 | tf_op jit(solution)/shard_map/pallas_call | solution.py:41
  29.0 0.4 collective-permute-start.11
  29.4 0.0 collective-permute-done.9
  29.4 0.1 collective-permute-start.10
  29.5 3.3 %collective-permute-done.11 = bf16[64,128]{1,0:T(8,128)(2,1)S(1)} collective-permute-done((bf16[64,128]{1,0:T(8,128)(2,1)S(1)}, bf16[64,128]{1,0:T(8,128)(2,1)S(1)}, u32[]{:S(2)}, u32[]{:S(2)}) %collective-permute-start.11) | collective-permute-done | bytes 16416 | tf_op jit(solution)/shard_map/ppermute | solution.py:537
  32.8 0.0 collective-permute-start.12
  32.9 0.0 collective-permute-done.10
  32.9 2.1 %shard_map.135.speed = f32[2,128,128]{2,1,0:T(8,128)S(1)} custom-call(s32[16,128]{1,0:T(8,128)S(1)} %get-tuple-element.43.table, f32[128,128]{1,0:T(8,128)S(1)} %get-tuple-element.44.viscous, f32[128,128]{1,0:T(8,128)S(1)} %get-tuple-element.45.gain, f32[2,128,128]{2,1,0:T(8,128)S(1)} %get-tuple-element.46.speed, f32[2,128,128]{2,1,0:T(8,128)S(1)} %get-tuple-element.47.push, ...), custom_call_target="tpu_custom_call" | custom-call | flops 11500000 | bytes 811008 | tf_op jit(solution)/shard_map/pallas_call | solution.py:41
  35.0 0.0 collective-permute-done.12
  35.1 0.0 copy-start.6
  35.1 1.1 %shard_map.136 = (bf16[192,128]{1,0:T(8,128)(2,1)S(1)}, bf16[192,128]{1,0:T(8,128)(2,1)S(1)}, bf16[192,128]{1,0:T(8,128)(2,1)S(1)}, bf16[192,128]{1,0:T(8,128)(2,1)S(1)}) custom-call(f32[128,128]{1,0:T(8,128)S(1)} %get-tuple-element.39.drag, f32[128,128]{1,0:T(8,128)S(1)} %get-tuple-element.49.conduct, f32[2,128,128]{2,1,0:T(8,128)S(1)} %get-tuple-element.50.current, ...), custom_call_target="tpu_custom_call" | custom-call | flops 11500000 | bytes 786432 | tf_op jit(solution)/shard_map/pallas_call | solution.py:41
  36.2 0.5 %collective-permute-start.13 = (bf16[192,128]{1,0:T(8,128)(2,1)S(1)}, bf16[192,128]{1,0:T(8,128)(2,1)S(1)}, u32[]{:S(2)}, u32[]{:S(2)}) collective-permute-start(bf16[192,128]{1,0:T(8,128)(2,1)S(1)} %get-tuple-element.53), channel_id=1, source_target_pairs={{0,1},{1,0},{2,3},{3,2},{4,5},{5,4},{6,7},{7,6},{8,9},{9,8},{10,11... | collective-permute-start | bytes 147464 | tf_op jit(solution)/shard_map/ppermute | solution.py:555
  36.7 0.3 collective-permute-start.14
  37.0 1.1 %collective-permute-start.15 = (bf16[192,128]{1,0:T(8,128)(2,1)S(1)}, bf16[192,128]{1,0:T(8,128)(2,1)S(1)}, u32[]{:S(2)}, u32[]{:S(2)}) collective-permute-start(bf16[192,128]{1,0:T(8,128)(2,1)S(1)} %get-tuple-element.55), channel_id=1, source_target_pairs={{0,3},{1,2},{2,1},{3,0},{4,7},{5,6},{6,5},{7,4},{8,11},{9,10},{10,... | collective-permute-start | bytes 147464 | tf_op jit(solution)/shard_map/ppermute | solution.py:555
  38.1 0.0 collective-permute-done.13.refs_1_
  38.1 2.9 %collective-permute-done.14.refs_2_ = bf16[192,128]{1,0:T(8,128)(2,1)S(1)} collective-permute-done((bf16[192,128]{1,0:T(8,128)(2,1)S(1)}, bf16[192,128]{1,0:T(8,128)(2,1)S(1)}, u32[]{:S(2)}, u32[]{:S(2)}) %collective-permute-start.14) | collective-permute-done | bytes 49184 | tf_op jit(solution)/shard_map/ppermute | solution.py:555
  41.1 0.0 collective-permute-done.15.refs_3_
  41.1 0.0 copy-done.6
  41.1 0.8 %shard_map.137 = (f32[256,128]{1,0:T(8,128)}, f32[4,64,128]{2,1,0:T(8,128)}, f32[2,64,128]{2,1,0:T(8,128)}) custom-call(f32[4,64,128]{2,1,0:T(8,128)S(1)} %get-tuple-element.42.warm, f32[2,64,128]{2,1,0:T(8,128)S(1)} %copy-done.6, f32[2,128,128]{2,1,0:T(8,128)S(1)} %shard_map.135.speed, bf16[192,128]{1,0:T(8,128)(2,1)S(1)} %get-tuple-element.52.refs_0_, ...), custom_call_target="tpu_custom_call" | custom-call | flops 11500000 | bytes 524288 | tf_op jit(solution)/shard_map/pallas_call | solution.py:41
  (18 shorter events, 0.2 us)
Async XLA Ops:
  0.6 5.5 %copy-start = (f32[4,64,128]{2,1,0:T(8,128)S(1)}, f32[4,64,128]{2,1,0:T(8,128)}, u32[]{:S(2)}) copy-start(f32[4,64,128]{2,1,0:T(8,128)} %water.3) | copy-start | bytes 393220
  0.6 5.5 %copy-start.1 = (f32[1,1,5,16384]{3,1,2,0:T(1,128)S(1)}, f32[1,1,5,16384]{3,1,2,0:T(1,128)}, u32[]{:S(2)}) copy-start(f32[1,1,5,16384]{3,1,2,0:T(1,128)} %param.18) | copy-start | bytes 983044
  0.7 5.5 %copy-start.2 = (f32[1,1,5,16384]{3,1,2,0:T(1,128)S(1)}, f32[1,1,5,16384]{3,1,2,0:T(1,128)}, u32[]{:S(2)}) copy-start(f32[1,1,5,16384]{3,1,2,0:T(1,128)} %param.19) | copy-start | bytes 983044
  0.7 5.5 %copy-start.4 = (f32[1,1,2,16384]{3,2,1,0:T(2,128)S(1)}, f32[1,1,2,16384]{3,2,1,0:T(2,128)}, u32[]{:S(2)}) copy-start(f32[1,1,2,16384]{3,2,1,0:T(2,128)} %param.20) | copy-start | bytes 393220
  3.0 13.5 %collective-permute-start.2 = (bf16[320,128]{1,0:T(8,128)(2,1)}, bf16[320,128]{1,0:T(8,128)(2,1)S(1)}, u32[]{:S(2)}, u32[]{:S(2)}) collective-permute-start(bf16[320,128]{1,0:T(8,128)(2,1)} %get-tuple-element.32), channel_id=1, source_target_pairs={{0,1},{1,0},{2,3},{3,2},{4,5},{5,4},{6,7},{7,6},{8,9},{9,8},{10,11... | collective-permute-start | bytes 245768 | tf_op jit(solution)/shard_map/ppermute | solution.py:555
  3.5 13.0 %collective-permute-start.3 = (bf16[320,128]{1,0:T(8,128)(2,1)}, bf16[320,128]{1,0:T(8,128)(2,1)S(1)}, u32[]{:S(2)}, u32[]{:S(2)}) collective-permute-start(bf16[320,128]{1,0:T(8,128)(2,1)} %get-tuple-element.33), channel_id=1, source_target_pairs={{0,2},{1,3},{2,0},{3,1},{4,6},{5,7},{6,4},{7,5},{8,10},{9,11},{10,... | collective-permute-start | bytes 245768 | tf_op jit(solution)/shard_map/ppermute | solution.py:555
  6.1 10.5 %collective-permute-start.4 = (bf16[320,128]{1,0:T(8,128)(2,1)}, bf16[320,128]{1,0:T(8,128)(2,1)S(1)}, u32[]{:S(2)}, u32[]{:S(2)}) collective-permute-start(bf16[320,128]{1,0:T(8,128)(2,1)} %get-tuple-element.34), channel_id=1, source_target_pairs={{0,3},{1,2},{2,1},{3,0},{4,7},{5,6},{6,5},{7,4},{8,11},{9,10},{10,... | collective-permute-start | bytes 245768 | tf_op jit(solution)/shard_map/ppermute | solution.py:555
  6.1 0.7 %copy-start.8 = (s32[1,1,4]{2,1,0:T(1,128)S(1)}, s32[1,1,4]{2,1,0:T(1,128)}, u32[]{:S(2)}) copy-start(s32[1,1,4]{2,1,0:T(1,128)} %links) | copy-start | bytes 52
  7.7 8.8 %copy-start.5 = (f32[1,1,2,16384]{3,2,1,0:T(2,128)S(1)}, f32[1,1,2,16384]{3,2,1,0:T(2,128)}, u32[]{:S(2)}) copy-start(f32[1,1,2,16384]{3,2,1,0:T(2,128)} %param.21) | copy-start | bytes 393220
  7.7 3.8 %collective-permute-start = (bf16[80,128]{1,0:T(8,128)(2,1)S(1)}, bf16[80,128]{1,0:T(8,128)(2,1)S(1)}, u32[]{:S(2)}, u32[]{:S(2)}) collective-permute-start(bf16[80,128]{1,0:T(8,128)(2,1)S(1)} %get-tuple-element.36), channel_id=1, source_target_pairs={{0,4},{4,0},{8,12},{12,8},{1,5},{5,1},{9,13},{13,9},{2,6},{6,2},{1... | collective-permute-start | bytes 61448 | tf_op jit(solution)/shard_map/ppermute | solution.py:537
  11.6 5.0 %copy-start.3 = (bf16[320,128]{1,0:T(8,128)(2,1)S(1)}, bf16[320,128]{1,0:T(8,128)(2,1)}, u32[]{:S(2)}) copy-start(bf16[320,128]{1,0:T(8,128)(2,1)} %get-tuple-element.31.refs_0_) | copy-start | bytes 245764
  11.6 4.9 %collective-permute-start.1 = (bf16[160,128]{1,0:T(8,128)(2,1)S(1)}, bf16[160,128]{1,0:T(8,128)(2,1)S(1)}, u32[]{:S(2)}, u32[]{:S(2)}) collective-permute-start(bf16[160,128]{1,0:T(8,128)(2,1)S(1)} %pad_maximum_fusion.5), channel_id=1, source_target_pairs={{0,8},{4,12},{8,0},{12,4},{1,9},{5,13},{9,1},{13,5},{2,10},{6,14},... | collective-permute-start | bytes 122888 | tf_op jit(solution)/shard_map/ppermute | solution.py:537
  17.1 3.7 %collective-permute-start.7 = (bf16[32,128]{1,0:T(8,128)(2,1)S(1)}, bf16[32,128]{1,0:T(8,128)(2,1)S(1)}, u32[]{:S(2)}, u32[]{:S(2)}) collective-permute-start(bf16[32,128]{1,0:T(8,128)(2,1)S(1)} %get-tuple-element.48), channel_id=1, source_target_pairs={{0,4},{4,0},{8,12},{12,8},{1,5},{5,1},{9,13},{13,9},{2,6},{6,2},{1... | collective-permute-start | bytes 24584 | tf_op jit(solution)/shard_map/ppermute | solution.py:537
  19.0 4.7 %collective-permute-start.5 = (bf16[272,128]{1,0:T(8,128)(2,1)S(1)}, bf16[272,128]{1,0:T(8,128)(2,1)S(1)}, u32[]{:S(2)}, u32[]{:S(2)}) collective-permute-start(bf16[272,128]{1,0:T(8,128)(2,1)S(1)} %shard_map.133), channel_id=1, source_target_pairs={{0,2},{1,3},{2,0},{3,1},{4,6},{5,7},{6,4},{7,5},{8,10},{9,11},{10,... | collective-permute-start | bytes 208904 | tf_op jit(solution)/shard_map/ppermute | solution.py:537
  20.8 4.6 %collective-permute-start.8 = (bf16[64,128]{1,0:T(8,128)(2,1)S(1)}, bf16[64,128]{1,0:T(8,128)(2,1)S(1)}, u32[]{:S(2)}, u32[]{:S(2)}) collective-permute-start(bf16[64,128]{1,0:T(8,128)(2,1)S(1)} %pad_maximum_fusion.7), channel_id=1, source_target_pairs={{0,8},{4,12},{8,0},{12,4},{1,9},{5,13},{9,1},{13,5},{2,10},{6,14},... | collective-permute-start | bytes 49160 | tf_op jit(solution)/shard_map/ppermute | solution.py:537
  23.7 3.5 %collective-permute-start.6 = (bf16[2,272,128]{2,1,0:T(8,128)(2,1)S(1)}, bf16[2,272,128]{2,1,0:T(8,128)(2,1)S(1)}, u32[]{:S(2)}, u32[]{:S(2)}) collective-permute-start(bf16[2,272,128]{2,1,0:T(8,128)(2,1)S(1)} %get-tuple-element.60), channel_id=1, source_target_pairs={{0,1},{1,0},{2,3},{3,2},{4,5},{5,4},{6,7},{7,6},{8,9},{9,8},{10,11... | collective-permute-start | bytes 417800 | tf_op jit(solution)/shard_map/ppermute | solution.py:537
  25.5 3.9 %collective-permute-start.9 = (bf16[128,128]{1,0:T(8,128)(2,1)S(1)}, bf16[128,128]{1,0:T(8,128)(2,1)S(1)}, u32[]{:S(2)}, u32[]{:S(2)}) collective-permute-start(bf16[128,128]{1,0:T(8,128)(2,1)S(1)} %constant_dynamic-update-slice_fusion.3), channel_id=1, source_target_pairs={{0,2},{1,3},{2,0},{3,1},{4,6},{5,7},{6,4},{7,5},{8,10},{9,11},{10,... | collective-permute-start | bytes 98312 | tf_op jit(solution)/shard_map/ppermute | solution.py:537
  27.2 0.8 %copy-start.7 = (f32[64,128]{1,0:T(8,128)S(1)}, f32[64,128]{1,0:T(8,128)}, u32[]{:S(2)}) copy-start(f32[64,128]{1,0:T(8,128)} %mixing.1) | copy-start | bytes 98308
  29.0 3.8 %collective-permute-start.11 = (bf16[64,128]{1,0:T(8,128)(2,1)S(1)}, bf16[64,128]{1,0:T(8,128)(2,1)S(1)}, u32[]{:S(2)}, u32[]{:S(2)}) collective-permute-start(bf16[64,128]{1,0:T(8,128)(2,1)S(1)} %get-tuple-element.51), channel_id=1, source_target_pairs={{0,2},{1,3},{2,0},{3,1},{4,6},{5,7},{6,4},{7,5},{8,10},{9,11},{10,... | collective-permute-start | bytes 49160 | tf_op jit(solution)/shard_map/ppermute | solution.py:537
  29.4 3.4 %collective-permute-start.10 = (bf16[2,128,128]{2,1,0:T(8,128)(2,1)S(1)}, bf16[2,128,128]{2,1,0:T(8,128)(2,1)S(1)}, u32[]{:S(2)}, u32[]{:S(2)}) collective-permute-start(bf16[2,128,128]{2,1,0:T(8,128)(2,1)S(1)} %get-tuple-element.62), channel_id=1, source_target_pairs={{0,1},{1,0},{2,3},{3,2},{4,5},{5,4},{6,7},{7,6},{8,9},{9,8},{10,11... | collective-permute-start | bytes 196616 | tf_op jit(solution)/shard_map/ppermute | solution.py:537
  32.8 2.2 %collective-permute-start.12 = (bf16[2,64,128]{2,1,0:T(8,128)(2,1)S(1)}, bf16[2,64,128]{2,1,0:T(8,128)(2,1)S(1)}, u32[]{:S(2)}, u32[]{:S(2)}) collective-permute-start(bf16[2,64,128]{2,1,0:T(8,128)(2,1)S(1)} %get-tuple-element.64), channel_id=1, source_target_pairs={{0,1},{1,0},{2,3},{3,2},{4,5},{5,4},{6,7},{7,6},{8,9},{9,8},{10,11... | collective-permute-start | bytes 98312 | tf_op jit(solution)/shard_map/ppermute | solution.py:537
  35.1 6.0 %copy-start.6 = (f32[2,64,128]{2,1,0:T(8,128)S(1)}, f32[2,64,128]{2,1,0:T(8,128)}, u32[]{:S(2)}) copy-start(f32[2,64,128]{2,1,0:T(8,128)} %currents.1) | copy-start | bytes 196612
  36.2 1.9 %collective-permute-start.13 = (bf16[192,128]{1,0:T(8,128)(2,1)S(1)}, bf16[192,128]{1,0:T(8,128)(2,1)S(1)}, u32[]{:S(2)}, u32[]{:S(2)}) collective-permute-start(bf16[192,128]{1,0:T(8,128)(2,1)S(1)} %get-tuple-element.53), channel_id=1, source_target_pairs={{0,1},{1,0},{2,3},{3,2},{4,5},{5,4},{6,7},{7,6},{8,9},{9,8},{10,11... | collective-permute-start | bytes 147464 | tf_op jit(solution)/shard_map/ppermute | solution.py:555
  36.7 4.4 %collective-permute-start.14 = (bf16[192,128]{1,0:T(8,128)(2,1)S(1)}, bf16[192,128]{1,0:T(8,128)(2,1)S(1)}, u32[]{:S(2)}, u32[]{:S(2)}) collective-permute-start(bf16[192,128]{1,0:T(8,128)(2,1)S(1)} %get-tuple-element.54), channel_id=1, source_target_pairs={{0,2},{1,3},{2,0},{3,1},{4,6},{5,7},{6,4},{7,5},{8,10},{9,11},{10,... | collective-permute-start | bytes 147464 | tf_op jit(solution)/shard_map/ppermute | solution.py:555
  37.0 4.0 %collective-permute-start.15 = (bf16[192,128]{1,0:T(8,128)(2,1)S(1)}, bf16[192,128]{1,0:T(8,128)(2,1)S(1)}, u32[]{:S(2)}, u32[]{:S(2)}) collective-permute-start(bf16[192,128]{1,0:T(8,128)(2,1)S(1)} %get-tuple-element.55), channel_id=1, source_target_pairs={{0,3},{1,2},{2,1},{3,0},{4,7},{5,6},{6,5},{7,4},{8,11},{9,10},{10,... | collective-permute-start | bytes 147464 | tf_op jit(solution)/shard_map/ppermute | solution.py:555

commit v6 on v3

--- a/solution.py
+++ b/solution.py
@@ -23,7 +23,7 @@
 DEPTH = SUBCYCLES
 SIDE_ROWS = 16 * DEPTH
 PUSH_ROWS = 8 * DEPTH
-NAMES_ROW = 4 * DEPTH - 1
+NAMES_ROW = 2 * DEPTH - 1
 TILE_ROWS = 16
 F32 = jnp.float32
 BF16 = jnp.bfloat16
@@ -62,19 +62,42 @@
     return jnp.where(condition, 1.0, 0.0).astype(F32)
 
 
-def forward_kernel(group, blocks_h, rows_h, cols_h, currents_h, *refs):
+def forward_kernel(group, links_h, blocks_h, rows_h, cols_h, currents_h, *refs):
     devices, members, place = group
-    outs, (blocks, currents, fields, arrived, left) = refs[:members], refs[members:]
+    outs, scratch = refs[:members], refs[members:]
+    links, blocks, currents, rows, cols, fields, names, arrived, left = scratch
     pairs, side, width = rows_h.shape
     depth = cols_h.shape[1]
-    names = pltpu.make_async_copy(blocks_h, blocks, arrived.at[0])
-    water = pltpu.make_async_copy(currents_h, currents, arrived.at[1])
-    names.start()
-    water.start()
-    names.wait()
+    loads = [
+        pltpu.make_async_copy(source, target, arrived.at[i])
+        for i, (source, target) in enumerate(
+            (
+                (links_h, links),
+                (blocks_h, blocks),
+                (currents_h, currents),
+                (rows_h, rows),
+                (cols_h, cols),
+            )
+        )
+    ]
+    for load in loads:
+        load.start()
+    for load in loads:
+        load.wait()
     me = place()
     owners = [lax.rem(lax.rem(blocks[0, m], devices), members) for m in range(pairs)]
-    copies = []
+    lane = iota((TILE_ROWS, width), 1)
+    numbers = jnp.zeros((TILE_ROWS, width), F32)
+    for q in range(4):
+        numbers = jnp.where(lane == q, (links[0, 0, q] >> 7).astype(F32), numbers)
+        numbers = jnp.where(lane == 4 + q, (links[0, 0, q] & 127).astype(F32), numbers)
+    names[...] = numbers.astype(BF16)
+    copies = [
+        pltpu.make_async_copy(
+            names, outs[0].at[pl.ds(3 * side + depth, TILE_ROWS)], left.at[3 * members]
+        )
+    ]
+    copies[0].start()
     for k, out in enumerate(outs):
         partner = me ^ k
         pair, found = jnp.int32(0), jnp.int32(0)
@@ -82,10 +105,10 @@
             pair = jnp.where(owners[m] == partner, m, pair)
             found = jnp.where(owners[m] == partner, 1, found)
         copies.append(
-            pltpu.make_async_copy(rows_h.at[pair], out.at[pl.ds(0, side)], left.at[3 * k])
+            pltpu.make_async_copy(rows.at[pair], out.at[pl.ds(0, side)], left.at[3 * k])
         )
         copies.append(
-            pltpu.make_async_copy(cols_h.at[pair], out.at[pl.ds(side, depth)], left.at[3 * k + 1])
+            pltpu.make_async_copy(cols.at[pair], out.at[pl.ds(side, depth)], left.at[3 * k + 1])
         )
         if pairs < members:
             keep = jnp.where(found > 0, 1.0, 0.0).astype(F32)
@@ -93,8 +116,6 @@
             keep = None
         copies[-2].start()
         copies[-1].start()
-        if k == 0:
-            water.wait()
         if k == 0 or keep is not None:
             for c in range(2):
                 field = currents[c] if keep is None else currents[c] * keep
@@ -131,7 +152,7 @@
 
 
 def rims_kernel(
-    links, thick, conc, ice, water, out, cols_o, viscous_o, gain_o, mass_o, drag_o, conduct_o,
+    thick, conc, ice, water, out, cols_o, viscous_o, gain_o, mass_o, drag_o, conduct_o,
     speed_o, store,
 ):
     size = thick.shape[1]
@@ -158,11 +179,6 @@
     speed_o[1] = speed_y
     put_side_rims(store, [speed_x, speed_y, viscous, gain], lambda side: side * 4 * DEPTH)
     line = iota((1, size), 1)
-    names = jnp.zeros((1, size), F32)
-    for q in range(4):
-        names = jnp.where(line == q, (links[0, 0, q] >> 7).astype(F32), names)
-        names = jnp.where(line == 4 + q, (links[0, 0, q] & 127).astype(F32), names)
-    store[NAMES_ROW : NAMES_ROW + 1] = names
     levels, rows, width = water.shape
     start = SIDE_ROWS
     for l in range(levels):
@@ -229,7 +245,7 @@
     chunks = refs[:group]
     out, current_o, push_o, store = refs[group:]
     size = mass.shape[0]
-    depth = chunks[0].shape[0] - 3 * side
+    depth = chunks[-1].shape[0] - 3 * side
     fields = [
         [c[side + depth : 2 * side + depth], c[2 * side + depth : 3 * side + depth]] for c in chunks
     ]
@@ -243,14 +259,18 @@
         push_o[c] = push
         pushes.append(push)
     put_side_rims(store, pushes, lambda q: q * 2 * DEPTH)
-    out[...] = store[...].astype(BF16)
+    names = chunks[0][3 * side + depth :].astype(F32)
+    store[NAMES_ROW : NAMES_ROW + 1] = names[0:1]
+    message = store[...].astype(BF16)
+    for d in range(out.shape[0]):
+        out[d] = message
 
 
 def ocean_kernel(counts, tile_place, member_place, water, mixing, *refs):
     tiles, subs, levs = counts
     members = subs * levs
     messages, relays = refs[:tiles], refs[tiles : tiles + members]
-    warm_o, top_o, table_o = refs[tiles + members :]
+    warm_o, top_o = refs[tiles + members :]
     levels, rows, width = water.shape
     my_tile, me = tile_place(), member_place()
     halo = {}
@@ -269,16 +289,6 @@
         at = width - 1 if ds < 0 else 0
         halo[-1, ds] = corners[:levels, at : at + 1]
         halo[1, ds] = corners[levels:, at : at + 1]
-    mine = my_tile * members + me
-    column = iota((table_o.shape[0], width), 1)
-    names = []
-    for k in range(tiles):
-        for m in range(members):
-            at = k * SIDE_ROWS
-            names.append(relays[m][at : at + TILE_ROWS].astype(F32)[NAMES_ROW : NAMES_ROW + 1])
-    names = jnp.concatenate(names, axis=0)
-    table = (128.0 * names + roll(names, -4, 1)).astype(jnp.int32)
-    table_o[...] = jnp.where((table >= 0) & (column < 4), table ^ mine, -1)
     left_cols = halo[0, -1].T
     right_cols = halo[0, 1].T
     row = iota((rows, width), 0)
@@ -329,14 +339,13 @@
     top_o[...] = (total / (levels * levs)).astype(top_o.dtype)
 
 
-def subcycles_kernel(tiles, members, table, viscous, gain, speed, push, *refs):
-    relays, push_relays = refs[:members], refs[members : 2 * members]
-    out, rims, push_rims = refs[2 * members :]
+def subcycles_kernel(tiles, members, place, table, viscous, gain, speed, push, push_rims, *refs):
+    relays, (out, rims) = refs[:members], refs[members:]
     size = viscous.shape[0]
+    me = place()
     for k in range(tiles):
         for m in range(members):
-            rims[k * members + m] = relays[m][k * SIDE_ROWS : (k + 1) * SIDE_ROWS]
-            push_rims[k * members + m] = push_relays[m][k * PUSH_ROWS : (k + 1) * PUSH_ROWS]
+            rims[me ^ (k * members + m)] = relays[m][k * SIDE_ROWS : (k + 1) * SIDE_ROWS]
     half = DEPTH
     high = 2 * DEPTH
     sub = iota((high, size), 0)
@@ -369,7 +378,7 @@
 
     strips = []
     for q in range(4):
-        x, has_x = follow(0, q)
+        x, has_x = follow(me, q)
         strip = load(x, OPPOSITE[q], flag(has_x))
         sides = []
         for s in LATERAL[q]:
@@ -454,7 +463,7 @@
     tops = refs[group : 2 * group]
     outs = refs[2 * group :]
     size = drag.shape[0]
-    depth = chunks[0].shape[0] - 3 * side
+    depth = chunks[-1].shape[0] - 3 * side
     warm = remap_forward(chunks, [[t[...]] for t in tops], side, depth)
     heat = conduct[...] * warm
     fluxes = [heat.astype(BF16)]
@@ -525,6 +534,9 @@
     def member_place():
         return lax.axis_index("sub") * lev_count + lax.axis_index("lev")
 
+    def device_place():
+        return lax.axis_index("tile") * group + member_place()
+
     def swap(value, axes, count):
         return [value] + [
             lax.ppermute(value, axes, [(i, i ^ k) for i in range(count)]) for k in range(1, count)
@@ -549,47 +561,49 @@
     chunk_rows = 3 * side + width
     sent = call(
         functools.partial(forward_kernel, (devices, group, member_place)),
-        [shape(chunk_rows, width, dtype=BF16)] * group,
-        (remap_blocks, remap_rows[0].swapaxes(1, 2), remap_cols[0], upper_current_vector),
+        [shape(chunk_rows + TILE_ROWS, width, dtype=BF16)]
+        + [shape(chunk_rows, width, dtype=BF16)] * (group - 1),
+        (neighbors, remap_blocks, remap_rows[0].swapaxes(1, 2), remap_cols[0], upper_current_vector),
         scratch=[
+            pltpu.SMEM(neighbors.shape, jnp.int32),
             pltpu.SMEM((1, pairs), jnp.int32),
             pltpu.VMEM((2, side, width), F32),
+            pltpu.VMEM((pairs, side, size), BF16),
+            pltpu.VMEM((pairs, size, width), BF16),
             pltpu.VMEM((1 if pairs == group else group, 2 * side, width), BF16),
-            pltpu.SemaphoreType.DMA((2,)),
-            pltpu.SemaphoreType.DMA((3 * group,)),
+            pltpu.VMEM((TILE_ROWS, width), BF16),
+            pltpu.SemaphoreType.DMA((5,)),
+            pltpu.SemaphoreType.DMA((3 * group + 1,)),
         ],
-        hbm=(0, 1, 2, 3),
+        hbm=(0, 1, 2, 3, 4),
         grant=60 * 2**20,
-        micros=2,
+        micros=10,
     )
     chunks = swap_each(sent)
 
-    links, sent = lax.optimization_barrier((neighbors, sent))
     message, cols, viscous, gain, step_mass, drag, conduct, speed = call(
         rims_kernel,
         [shape(SIDE_ROWS + 4 * levels, size, dtype=BF16), shape(2 * levels, width)]
         + [plane] * 5
         + [planes],
         (
-            links,
             thickness.reshape(categories, size, size),
             concentration.reshape(categories, size, size),
             interleaved(ice_velocity),
             water_heat_state,
         ),
         scratch=[pltpu.VMEM((SIDE_ROWS + 4 * levels, size), F32)],
-        smem=(0,),
     )
     messages = swap(message, "tile", tile_count)
 
     push_message, current_ice, push = call(
         functools.partial(forcing_kernel, group, side),
-        [shape(PUSH_ROWS, size, dtype=BF16), planes, planes],
+        [shape(devices, PUSH_ROWS, size, dtype=BF16), planes, planes],
         (step_mass, drag, wind, *chunks),
         scratch=[pltpu.VMEM((PUSH_ROWS, size), F32)],
     )
     cols, push_message = lax.optimization_barrier((cols, push_message))
-    push_messages = swap(push_message, "tile", tile_count)
+    push_rims = lax.all_to_all(push_message, member_axes, split_axis=0, concat_axis=0, tiled=True)
 
     relay = call(
         functools.partial(relay_kernel, tile_count, tile_place),
@@ -597,16 +611,14 @@
         (cols, *messages),
     )
     relays = swap(relay, group_axes, group)
-    push_relays = swap(jnp.concatenate(push_messages, axis=0), group_axes, group)
-
-    warm, top, table = call(
+
+    warm, top = call(
         functools.partial(
             ocean_kernel, (tile_count, sub_count, lev_count), tile_place, member_place
         ),
         [
             shape(levels, side, width),
             shape(side, width, dtype=BF16 if lev_count == 1 else F32),
-            shape(devices, width, dtype=jnp.int32),
         ],
         (water_heat_state, diffusion_coefficient, *messages, *relays),
     )
@@ -614,14 +626,14 @@
         top = lax.psum(top, "lev").astype(BF16)
     tops = swap(top, group_axes, group)
 
+    push_rims, _ = lax.optimization_barrier((push_rims, top))
+    names = push_rims[:, NAMES_ROW, 0:8].astype(jnp.int32)
+    table = names[:, 0:4] * 128 + names[:, 4:8]
     speed = call(
-        functools.partial(subcycles_kernel, tile_count, group),
+        functools.partial(subcycles_kernel, tile_count, group, device_place),
         planes,
-        (table, viscous, gain, speed, push, *relays, *push_relays),
-        scratch=[
-            pltpu.VMEM((devices, SIDE_ROWS, size), BF16),
-            pltpu.VMEM((devices, PUSH_ROWS, size), BF16),
-        ],
+        (table, viscous, gain, speed, push, push_rims, *relays),
+        scratch=[pltpu.VMEM((devices, SIDE_ROWS, size), BF16)],
         smem=(0,),
     )
 

time: 36.6 us -> 45.5 us (1.24)
  waiting for transfers between devices: 6.08 us -> 15.9 us
  local copies, waits for them, and re-layouts: 0.69 us -> 0.04 us
    ppermute x15 -> x9, starting transfers between devices: 14.6 us -> 8.32 us  [swap(): lax.ppermute(value, axes, [(i, i ^ k) for i in range(count)])]
    all_to_all x0 -> x1, starting transfers between devices: none -> 6.02 us  [shards(): lax.all_to_all(push_message, member_axes, split_axis=0, concat_axis=0, ti...]
    ppermute x15 -> x9, waiting for transfers between devices: 3 us -> 8.5 us  [swap(): lax.ppermute(value, axes, [(i, i ^ k) for i in range(count)])]
    ppermute x6, waiting for transfers between devices: 3.08 us -> 7.39 us  [swap_each(): lax.ppermute(values[k], group_axes, [(i, i ^ k) for i in range(group)])]
    unnamed x21 -> x16, local copies, waits for them, and re-layouts: 0.68 us -> 0.04 us
  transfers between devices with their start and end apart: 21 -> 16, of which waited for: 6 -> 9; matrix products, arithmetic and copies ran while one was open for 0% -> 0% of each run, Pallas kernels for 13% -> 8%
where the time goes in v6:
time: 45.5 us; the launch traced here: 45.3 us
  starting transfers between devices  19.4 us (43%)
  waiting for transfers between devices  15.9 us (35%)
  Pallas kernels  9.12 us (20%)
  between operations  0.78 us (2%)
    pallas_call x8, Pallas kernels, call(): pl.pallas_call(kernel, out_shape=outs, in_specs=specs, out_specs=jax.tree...  9.12 us
    ppermute x9, waiting for transfers between devices, swap(): lax.ppermute(value, axes, [(i, i ^ k) for i in range(count)])  8.5 us
    ppermute x9, starting transfers between devices, swap(): lax.ppermute(value, axes, [(i, i ^ k) for i in range(count)])  8.32 us
    ppermute x6, waiting for transfers between devices, swap_each(): lax.ppermute(values[k], group_axes, [(i, i ^ k) for i in range(group)])  7.39 us
    all_to_all x1, starting transfers between devices, shards(): lax.all_to_all(push_message, member_axes, split_axis=0, concat_axis=0, ti...  6.02 us
    ppermute x6, starting transfers between devices, swap_each(): lax.ppermute(values[k], group_axes, [(i, i ^ k) for i in range(group)])  5.02 us
  transfers between devices with their start and end apart: 16, of which 9 were waited for; matrix products, arithmetic and copies ran while one was open for 0% of the time, Pallas kernels for 8%

profile of v6, /device:TPU:0, one launch (start us, length us, event | category | flops | bytes accessed | tf_op | source)
XLA Modules:
  0.0 45.3 jit_solution(17023480037623801332)
XLA Ops:
  0.6 0.0 copy-start
  0.6 0.0 copy-start.2
  0.7 0.0 copy-start.3
  0.7 0.0 copy-start.4
  0.7 2.4 %shard_map.131 = (bf16[336,128]{1,0:T(8,128)(2,1)}, bf16[320,128]{1,0:T(8,128)(2,1)}, bf16[320,128]{1,0:T(8,128)(2,1)}, bf16[320,128]{1,0:T(8,128)(2,1)}) custom-call(s32[1,1,4]{2,1,0:T(1,128)} %links_h.1, s32[1,4]{1,0:T(1,128)} %blocks_h.1, bf16[4,64,128]{2,1,0:T(8,128)(2,1)} %bitcast.29, bf16[4,128,128]{2,1,0:T(8,128)(2,1)} %bitcast.27, f32[2,64,128]{2,1,0:T(8,128)} %currents.1), custom_call_target="tpu_custom_call" | custom-call | flops 11500000256 | bytes 262176 | tf_op jit(solution)/shard_map/pallas_call | solution.py:40
  3.1 0.5 %collective-permute-start.3 = (bf16[320,128]{1,0:T(8,128)(2,1)}, bf16[320,128]{1,0:T(8,128)(2,1)S(1)}, u32[]{:S(2)}, u32[]{:S(2)}) collective-permute-start(bf16[320,128]{1,0:T(8,128)(2,1)} %get-tuple-element.35), channel_id=1, source_target_pairs={{0,1},{1,0},{2,3},{3,2},{4,5},{5,4},{6,7},{7,6},{8,9},{9,8},{10,11... | collective-permute-start | bytes 245768 | tf_op jit(solution)/shard_map/ppermute | solution.py:547
  3.6 2.6 %collective-permute-start.4 = (bf16[320,128]{1,0:T(8,128)(2,1)}, bf16[320,128]{1,0:T(8,128)(2,1)S(1)}, u32[]{:S(2)}, u32[]{:S(2)}) collective-permute-start(bf16[320,128]{1,0:T(8,128)(2,1)} %get-tuple-element.36), channel_id=1, source_target_pairs={{0,2},{1,3},{2,0},{3,1},{4,6},{5,7},{6,4},{7,5},{8,10},{9,11},{10,... | collective-permute-start | bytes 245768 | tf_op jit(solution)/shard_map/ppermute | solution.py:547
  6.2 0.1 collective-permute-start.5
  6.2 0.0 copy-done
  6.2 0.0 copy-done.2
  6.2 0.0 copy-done.3
  6.2 0.0 copy-done.4
  6.2 0.0 copy-start.1
  6.3 0.0 copy-start.5
  6.3 0.4 shard_map.130
  6.7 0.0 collective-permute-done.3.refs_1_
  6.7 2.7 %collective-permute-done.4.refs_2_ = bf16[320,128]{1,0:T(8,128)(2,1)S(1)} collective-permute-done((bf16[320,128]{1,0:T(8,128)(2,1)}, bf16[320,128]{1,0:T(8,128)(2,1)S(1)}, u32[]{:S(2)}, u32[]{:S(2)}) %collective-permute-start.4) | collective-permute-done | bytes 81952 | tf_op jit(solution)/shard_map/ppermute | solution.py:547
  9.4 1.5 %collective-permute-done.5.refs_3_ = bf16[320,128]{1,0:T(8,128)(2,1)S(1)} collective-permute-done((bf16[320,128]{1,0:T(8,128)(2,1)}, bf16[320,128]{1,0:T(8,128)(2,1)S(1)}, u32[]{:S(2)}, u32[]{:S(2)}) %collective-permute-start.5) | collective-permute-done | bytes 81952 | tf_op jit(solution)/shard_map/ppermute | solution.py:547
  10.9 0.0 copy-done.1
  10.9 0.0 copy-done.5
  10.9 1.2 %shard_map.132 = (bf16[16,32,128]{2,1,0:T(8,128)(2,1)}, f32[2,128,128]{2,1,0:T(8,128)S(1)}, f32[2,128,128]{2,1,0:T(8,128)S(1)}) custom-call(f32[128,128]{1,0:T(8,128)S(1)} %get-tuple-element.32.mass, f32[128,128]{1,0:T(8,128)S(1)} %get-tuple-element.33.drag, f32[256,128]{1,0:T(8,128)S(1)} %bitcast.25, bf16[336,128]{1,0:T(8,128)(2,1)S(1)} %copy-done.1, ...), custom_call_target="tpu_custom_call" | custom-call | flops 11500000 | bytes 593920 | tf_op jit(solution)/shard_map/pallas_call | solution.py:40
  12.1 6.0 %all-to-all-start = ((bf16[16,32,128]{2,1,0:T(8,128)(2,1)}), bf16[16,32,128]{2,1,0:T(8,128)(2,1)S(1)}, u32[]{:S(2)}, u32[]{:S(2)}) async-start(bf16[16,32,128]{2,1,0:T(8,128)(2,1)} %get-tuple-element.41), calls=%async_computation | async-start | bytes 262144 | tf_op jit(solution)/shard_map/all_to_all | solution.py:606
  18.1 0.0 copy-start.7
  18.1 3.8 %collective-permute-start.2 = (bf16[80,128]{1,0:T(8,128)(2,1)S(1)}, bf16[80,128]{1,0:T(8,128)(2,1)S(1)}, u32[]{:S(2)}, u32[]{:S(2)}) collective-permute-start(bf16[80,128]{1,0:T(8,128)(2,1)S(1)} %get-tuple-element.30.refs_0_), channel_id=1, source_target_pairs={{0,12},{4,8},{8,4},{12,0},{1,13},{5,9},{9,5},{13,1},{2,14},{6,10},... | collective-permute-start | bytes 61448 | tf_op jit(solution)/shard_map/ppermute | solution.py:542
  21.9 0.0 collective-permute-start.1
  21.9 0.7 %collective-permute-start = (bf16[80,128]{1,0:T(8,128)(2,1)S(1)}, bf16[80,128]{1,0:T(8,128)(2,1)S(1)}, u32[]{:S(2)}, u32[]{:S(2)}) collective-permute-start(bf16[80,128]{1,0:T(8,128)(2,1)S(1)} %get-tuple-element.30.refs_0_), channel_id=1, source_target_pairs={{0,4},{4,0},{8,12},{12,8},{1,5},{5,1},{9,13},{13,9},{2,6},{6,2},{1... | collective-permute-start | bytes 61448 | tf_op jit(solution)/shard_map/ppermute | solution.py:542
  22.6 3.3 %collective-permute-done.2.refs_3_ = bf16[80,128]{1,0:T(8,128)(2,1)S(1)} collective-permute-done((bf16[80,128]{1,0:T(8,128)(2,1)S(1)}, bf16[80,128]{1,0:T(8,128)(2,1)S(1)}, u32[]{:S(2)}, u32[]{:S(2)}) %collective-permute-start.2) | collective-permute-done | bytes 20512 | tf_op jit(solution)/shard_map/ppermute | solution.py:542
  25.9 0.9 %collective-permute-done.1.refs_2_ = bf16[80,128]{1,0:T(8,128)(2,1)S(1)} collective-permute-done((bf16[80,128]{1,0:T(8,128)(2,1)S(1)}, bf16[80,128]{1,0:T(8,128)(2,1)S(1)}, u32[]{:S(2)}, u32[]{:S(2)}) %collective-permute-start.1) | collective-permute-done | bytes 20512 | tf_op jit(solution)/shard_map/ppermute | solution.py:542
  26.7 0.0 collective-permute-done.refs_1_
  26.8 0.7 %collective-permute-start.8 = (bf16[272,128]{1,0:T(8,128)(2,1)S(1)}, bf16[272,128]{1,0:T(8,128)(2,1)S(1)}, u32[]{:S(2)}, u32[]{:S(2)}) collective-permute-start(bf16[272,128]{1,0:T(8,128)(2,1)S(1)} %shard_map.133.refs_4_.refs_0_), channel_id=1, source_target_pairs={{0,3},{1,2},{2,1},{3,0},{4,7},{5,6},{6,5},{7,4},{8,11},{9,10},{10,... | collective-permute-start | bytes 208904 | tf_op jit(solution)/shard_map/ppermute | solution.py:542
  27.5 0.9 %collective-permute-start.7 = (bf16[272,128]{1,0:T(8,128)(2,1)S(1)}, bf16[272,128]{1,0:T(8,128)(2,1)S(1)}, u32[]{:S(2)}, u32[]{:S(2)}) collective-permute-start(bf16[272,128]{1,0:T(8,128)(2,1)S(1)} %shard_map.133.refs_4_.refs_0_), channel_id=1, source_target_pairs={{0,2},{1,3},{2,0},{3,1},{4,6},{5,7},{6,4},{7,5},{8,10},{9,11},{10,... | collective-permute-start | bytes 208904 | tf_op jit(solution)/shard_map/ppermute | solution.py:542
  28.4 0.3 collective-permute-start.6
  28.7 2.6 %collective-permute-done.8.refs_7_.refs_3_ = bf16[272,128]{1,0:T(8,128)(2,1)S(1)} collective-permute-done((bf16[272,128]{1,0:T(8,128)(2,1)S(1)}, bf16[272,128]{1,0:T(8,128)(2,1)S(1)}, u32[]{:S(2)}, u32[]{:S(2)}) %collective-permute-start.8) | collective-permute-done | bytes 69664 | tf_op jit(solution)/shard_map/ppermute | solution.py:542
  31.3 1.5 %collective-permute-done.7.refs_6_.refs_2_ = bf16[272,128]{1,0:T(8,128)(2,1)S(1)} collective-permute-done((bf16[272,128]{1,0:T(8,128)(2,1)S(1)}, bf16[272,128]{1,0:T(8,128)(2,1)S(1)}, u32[]{:S(2)}, u32[]{:S(2)}) %collective-permute-start.7) | collective-permute-done | bytes 69664 | tf_op jit(solution)/shard_map/ppermute | solution.py:542
  32.8 0.0 collective-permute-done.6.refs_5_.refs_1_
  32.8 0.0 copy-done.7
  32.8 1.1 %shard_map.134 = (f32[4,64,128]{2,1,0:T(8,128)S(1)}, bf16[64,128]{1,0:T(8,128)(2,1)S(1)}) custom-call(f32[4,64,128]{2,1,0:T(8,128)S(1)} %copy-done, f32[64,128]{1,0:T(8,128)S(1)} %copy-done.7, bf16[80,128]{1,0:T(8,128)(2,1)S(1)} %get-tuple-element.30.refs_0_, bf16[80,128]{1,0:T(8,128)(2,1)S(1)} %collective-permute-done.refs_1_, ...), custom_call_target="tpu_custom_call" | custom-call | flops 11500000 | bytes 524288 | tf_op jit(solution)/shard_map/pallas_call | solution.py:40
  33.9 0.7 %collective-permute-start.11 = (bf16[64,128]{1,0:T(8,128)(2,1)S(1)}, bf16[64,128]{1,0:T(8,128)(2,1)S(1)}, u32[]{:S(2)}, u32[]{:S(2)}) collective-permute-start(bf16[64,128]{1,0:T(8,128)(2,1)S(1)} %get-tuple-element.42.refs_4_), channel_id=1, source_target_pairs={{0,3},{1,2},{2,1},{3,0},{4,7},{5,6},{6,5},{7,4},{8,11},{9,10},{10,... | collective-permute-start | bytes 49160 | tf_op jit(solution)/shard_map/ppermute | solution.py:542
  34.6 1.1 %collective-permute-start.10 = (bf16[64,128]{1,0:T(8,128)(2,1)S(1)}, bf16[64,128]{1,0:T(8,128)(2,1)S(1)}, u32[]{:S(2)}, u32[]{:S(2)}) collective-permute-start(bf16[64,128]{1,0:T(8,128)(2,1)S(1)} %get-tuple-element.42.refs_4_), channel_id=1, source_target_pairs={{0,2},{1,3},{2,0},{3,1},{4,6},{5,7},{6,4},{7,5},{8,10},{9,11},{10,... | collective-permute-start | bytes 49160 | tf_op jit(solution)/shard_map/ppermute | solution.py:542
  35.7 0.2 collective-permute-start.9
  35.8 0.0 all-to-all-done.push_rims
  35.9 0.1 slice_add_fusion.table
  35.9 2.1 %shard_map.135.speed = f32[2,128,128]{2,1,0:T(8,128)S(1)} custom-call(s32[16,4]{1,0:T(8,128)S(1)} %slice_add_fusion.table, f32[128,128]{1,0:T(8,128)S(1)} %get-tuple-element.44.viscous, f32[128,128]{1,0:T(8,128)S(1)} %get-tuple-element.45.gain, f32[2,128,128]{2,1,0:T(8,128)S(1)} %get-tuple-element.46.speed, f32[2,128,128]{2,1,0:T(8,128)S(1)} %get-tuple-element.47.push, ...), custom_call_target="tpu_custom_call" | custom-call | flops 11500000 | bytes 803072 | tf_op jit(solution)/shard_map/pallas_call | solution.py:40
  38.1 0.0 collective-permute-done.11.refs_7_
  38.1 0.3 collective-permute-done.10.refs_6_
  38.3 0.0 collective-permute-done.9.refs_5_
  38.3 0.0 copy-start.6
  38.4 1.1 %shard_map.136 = (bf16[192,128]{1,0:T(8,128)(2,1)S(1)}, bf16[192,128]{1,0:T(8,128)(2,1)S(1)}, bf16[192,128]{1,0:T(8,128)(2,1)S(1)}, bf16[192,128]{1,0:T(8,128)(2,1)S(1)}) custom-call(f32[128,128]{1,0:T(8,128)S(1)} %get-tuple-element.33.drag, f32[128,128]{1,0:T(8,128)S(1)} %get-tuple-element.48.conduct, f32[2,128,128]{2,1,0:T(8,128)S(1)} %get-tuple-element.49.current, ...), custom_call_target="tpu_custom_call" | custom-call | flops 11500000 | bytes 790528 | tf_op jit(solution)/shard_map/pallas_call | solution.py:40
  39.5 0.1 collective-permute-start.12
  39.6 1.0 %collective-permute-start.13 = (bf16[192,128]{1,0:T(8,128)(2,1)S(1)}, bf16[192,128]{1,0:T(8,128)(2,1)S(1)}, u32[]{:S(2)}, u32[]{:S(2)}) collective-permute-start(bf16[192,128]{1,0:T(8,128)(2,1)S(1)} %get-tuple-element.52), channel_id=1, source_target_pairs={{0,2},{1,3},{2,0},{3,1},{4,6},{5,7},{6,4},{7,5},{8,10},{9,11},{10,... | collective-permute-start | bytes 147464 | tf_op jit(solution)/shard_map/ppermute | solution.py:547
  40.6 0.7 %collective-permute-start.14 = (bf16[192,128]{1,0:T(8,128)(2,1)S(1)}, bf16[192,128]{1,0:T(8,128)(2,1)S(1)}, u32[]{:S(2)}, u32[]{:S(2)}) collective-permute-start(bf16[192,128]{1,0:T(8,128)(2,1)S(1)} %get-tuple-element.53), channel_id=1, source_target_pairs={{0,3},{1,2},{2,1},{3,0},{4,7},{5,6},{6,5},{7,4},{8,11},{9,10},{10,... | collective-permute-start | bytes 147464 | tf_op jit(solution)/shard_map/ppermute | solution.py:547
  41.3 0.0 collective-permute-done.12.refs_1_
  41.3 2.6 %collective-permute-done.13.refs_2_ = bf16[192,128]{1,0:T(8,128)(2,1)S(1)} collective-permute-done((bf16[192,128]{1,0:T(8,128)(2,1)S(1)}, bf16[192,128]{1,0:T(8,128)(2,1)S(1)}, u32[]{:S(2)}, u32[]{:S(2)}) %collective-permute-start.13) | collective-permute-done | bytes 49184 | tf_op jit(solution)/shard_map/ppermute | solution.py:547
  43.9 0.6 %collective-permute-done.14.refs_3_ = bf16[192,128]{1,0:T(8,128)(2,1)S(1)} collective-permute-done((bf16[192,128]{1,0:T(8,128)(2,1)S(1)}, bf16[192,128]{1,0:T(8,128)(2,1)S(1)}, u32[]{:S(2)}, u32[]{:S(2)}) %collective-permute-start.14) | collective-permute-done | bytes 49184 | tf_op jit(solution)/shard_map/ppermute | solution.py:547
  44.5 0.0 copy-done.6
  44.5 0.7 %shard_map.137 = (f32[256,128]{1,0:T(8,128)}, f32[4,64,128]{2,1,0:T(8,128)}, f32[2,64,128]{2,1,0:T(8,128)}) custom-call(f32[4,64,128]{2,1,0:T(8,128)S(1)} %get-tuple-element.40.warm, f32[2,64,128]{2,1,0:T(8,128)S(1)} %copy-done.6, f32[2,128,128]{2,1,0:T(8,128)S(1)} %shard_map.135.speed, bf16[192,128]{1,0:T(8,128)(2,1)S(1)} %get-tuple-element.50.refs_0_, ...), custom_call_target="tpu_custom_call" | custom-call | flops 11500000 | bytes 524288 | tf_op jit(solution)/shard_map/pallas_call | solution.py:40
  (2 shorter events, 0.0 us)
Async XLA Ops:
  0.6 5.6 %copy-start = (f32[4,64,128]{2,1,0:T(8,128)S(1)}, f32[4,64,128]{2,1,0:T(8,128)}, u32[]{:S(2)}) copy-start(f32[4,64,128]{2,1,0:T(8,128)} %water.3) | copy-start | bytes 393220
  0.6 5.6 %copy-start.2 = (f32[1,1,5,16384]{3,1,2,0:T(1,128)S(1)}, f32[1,1,5,16384]{3,1,2,0:T(1,128)}, u32[]{:S(2)}) copy-start(f32[1,1,5,16384]{3,1,2,0:T(1,128)} %param.18) | copy-start | bytes 983044
  0.7 5.6 %copy-start.3 = (f32[1,1,5,16384]{3,1,2,0:T(1,128)S(1)}, f32[1,1,5,16384]{3,1,2,0:T(1,128)}, u32[]{:S(2)}) copy-start(f32[1,1,5,16384]{3,1,2,0:T(1,128)} %param.19) | copy-start | bytes 983044
  0.7 5.6 %copy-start.4 = (f32[1,1,2,16384]{3,2,1,0:T(2,128)S(1)}, f32[1,1,2,16384]{3,2,1,0:T(2,128)}, u32[]{:S(2)}) copy-start(f32[1,1,2,16384]{3,2,1,0:T(2,128)} %param.20) | copy-start | bytes 393220
  3.1 3.6 %collective-permute-start.3 = (bf16[320,128]{1,0:T(8,128)(2,1)}, bf16[320,128]{1,0:T(8,128)(2,1)S(1)}, u32[]{:S(2)}, u32[]{:S(2)}) collective-permute-start(bf16[320,128]{1,0:T(8,128)(2,1)} %get-tuple-element.35), channel_id=1, source_target_pairs={{0,1},{1,0},{2,3},{3,2},{4,5},{5,4},{6,7},{7,6},{8,9},{9,8},{10,11... | collective-permute-start | bytes 245768 | tf_op jit(solution)/shard_map/ppermute | solution.py:547
  3.6 5.8 %collective-permute-start.4 = (bf16[320,128]{1,0:T(8,128)(2,1)}, bf16[320,128]{1,0:T(8,128)(2,1)S(1)}, u32[]{:S(2)}, u32[]{:S(2)}) collective-permute-start(bf16[320,128]{1,0:T(8,128)(2,1)} %get-tuple-element.36), channel_id=1, source_target_pairs={{0,2},{1,3},{2,0},{3,1},{4,6},{5,7},{6,4},{7,5},{8,10},{9,11},{10,... | collective-permute-start | bytes 245768 | tf_op jit(solution)/shard_map/ppermute | solution.py:547
  6.2 4.7 %collective-permute-start.5 = (bf16[320,128]{1,0:T(8,128)(2,1)}, bf16[320,128]{1,0:T(8,128)(2,1)S(1)}, u32[]{:S(2)}, u32[]{:S(2)}) collective-permute-start(bf16[320,128]{1,0:T(8,128)(2,1)} %get-tuple-element.37), channel_id=1, source_target_pairs={{0,3},{1,2},{2,1},{3,0},{4,7},{5,6},{6,5},{7,4},{8,11},{9,10},{10,... | collective-permute-start | bytes 245768 | tf_op jit(solution)/shard_map/ppermute | solution.py:547
  6.2 4.6 %copy-start.1 = (bf16[336,128]{1,0:T(8,128)(2,1)S(1)}, bf16[336,128]{1,0:T(8,128)(2,1)}, u32[]{:S(2)}) copy-start(bf16[336,128]{1,0:T(8,128)(2,1)} %get-tuple-element.34.refs_0_) | copy-start | bytes 258052
  6.3 4.6 %copy-start.5 = (f32[1,1,2,16384]{3,2,1,0:T(2,128)S(1)}, f32[1,1,2,16384]{3,2,1,0:T(2,128)}, u32[]{:S(2)}) copy-start(f32[1,1,2,16384]{3,2,1,0:T(2,128)} %param.21) | copy-start | bytes 393220
  12.1 23.7 %all-to-all-start = ((bf16[16,32,128]{2,1,0:T(8,128)(2,1)}), bf16[16,32,128]{2,1,0:T(8,128)(2,1)S(1)}, u32[]{:S(2)}, u32[]{:S(2)}) async-start(bf16[16,32,128]{2,1,0:T(8,128)(2,1)} %get-tuple-element.41), calls=%async_computation | async-start | bytes 262144 | tf_op jit(solution)/shard_map/all_to_all | solution.py:606
  18.1 14.7 %copy-start.7 = (f32[64,128]{1,0:T(8,128)S(1)}, f32[64,128]{1,0:T(8,128)}, u32[]{:S(2)}) copy-start(f32[64,128]{1,0:T(8,128)} %mixing.1) | copy-start | bytes 98308
  18.1 7.7 %collective-permute-start.2 = (bf16[80,128]{1,0:T(8,128)(2,1)S(1)}, bf16[80,128]{1,0:T(8,128)(2,1)S(1)}, u32[]{:S(2)}, u32[]{:S(2)}) collective-permute-start(bf16[80,128]{1,0:T(8,128)(2,1)S(1)} %get-tuple-element.30.refs_0_), channel_id=1, source_target_pairs={{0,12},{4,8},{8,4},{12,0},{1,13},{5,9},{9,5},{13,1},{2,14},{6,10},... | collective-permute-start | bytes 61448 | tf_op jit(solution)/shard_map/ppermute | solution.py:542
  21.9 4.8 %collective-permute-start.1 = (bf16[80,128]{1,0:T(8,128)(2,1)S(1)}, bf16[80,128]{1,0:T(8,128)(2,1)S(1)}, u32[]{:S(2)}, u32[]{:S(2)}) collective-permute-start(bf16[80,128]{1,0:T(8,128)(2,1)S(1)} %get-tuple-element.30.refs_0_), channel_id=1, source_target_pairs={{0,8},{4,12},{8,0},{12,4},{1,9},{5,13},{9,1},{13,5},{2,10},{6,14},... | collective-permute-start | bytes 61448 | tf_op jit(solution)/shard_map/ppermute | solution.py:542
  21.9 4.8 %collective-permute-start = (bf16[80,128]{1,0:T(8,128)(2,1)S(1)}, bf16[80,128]{1,0:T(8,128)(2,1)S(1)}, u32[]{:S(2)}, u32[]{:S(2)}) collective-permute-start(bf16[80,128]{1,0:T(8,128)(2,1)S(1)} %get-tuple-element.30.refs_0_), channel_id=1, source_target_pairs={{0,4},{4,0},{8,12},{12,8},{1,5},{5,1},{9,13},{13,9},{2,6},{6,2},{1... | collective-permute-start | bytes 61448 | tf_op jit(solution)/shard_map/ppermute | solution.py:542
  26.8 4.5 %collective-permute-start.8 = (bf16[272,128]{1,0:T(8,128)(2,1)S(1)}, bf16[272,128]{1,0:T(8,128)(2,1)S(1)}, u32[]{:S(2)}, u32[]{:S(2)}) collective-permute-start(bf16[272,128]{1,0:T(8,128)(2,1)S(1)} %shard_map.133.refs_4_.refs_0_), channel_id=1, source_target_pairs={{0,3},{1,2},{2,1},{3,0},{4,7},{5,6},{6,5},{7,4},{8,11},{9,10},{10,... | collective-permute-start | bytes 208904 | tf_op jit(solution)/shard_map/ppermute | solution.py:542
  27.5 5.3 %collective-permute-start.7 = (bf16[272,128]{1,0:T(8,128)(2,1)S(1)}, bf16[272,128]{1,0:T(8,128)(2,1)S(1)}, u32[]{:S(2)}, u32[]{:S(2)}) collective-permute-start(bf16[272,128]{1,0:T(8,128)(2,1)S(1)} %shard_map.133.refs_4_.refs_0_), channel_id=1, source_target_pairs={{0,2},{1,3},{2,0},{3,1},{4,6},{5,7},{6,4},{7,5},{8,10},{9,11},{10,... | collective-permute-start | bytes 208904 | tf_op jit(solution)/shard_map/ppermute | solution.py:542
  28.4 4.4 %collective-permute-start.6 = (bf16[272,128]{1,0:T(8,128)(2,1)S(1)}, bf16[272,128]{1,0:T(8,128)(2,1)S(1)}, u32[]{:S(2)}, u32[]{:S(2)}) collective-permute-start(bf16[272,128]{1,0:T(8,128)(2,1)S(1)} %shard_map.133.refs_4_.refs_0_), channel_id=1, source_target_pairs={{0,1},{1,0},{2,3},{3,2},{4,5},{5,4},{6,7},{7,6},{8,9},{9,8},{10,11... | collective-permute-start | bytes 208904 | tf_op jit(solution)/shard_map/ppermute | solution.py:542
  33.9 4.2 %collective-permute-start.11 = (bf16[64,128]{1,0:T(8,128)(2,1)S(1)}, bf16[64,128]{1,0:T(8,128)(2,1)S(1)}, u32[]{:S(2)}, u32[]{:S(2)}) collective-permute-start(bf16[64,128]{1,0:T(8,128)(2,1)S(1)} %get-tuple-element.42.refs_4_), channel_id=1, source_target_pairs={{0,3},{1,2},{2,1},{3,0},{4,7},{5,6},{6,5},{7,4},{8,11},{9,10},{10,... | collective-permute-start | bytes 49160 | tf_op jit(solution)/shard_map/ppermute | solution.py:542
  34.6 3.7 %collective-permute-start.10 = (bf16[64,128]{1,0:T(8,128)(2,1)S(1)}, bf16[64,128]{1,0:T(8,128)(2,1)S(1)}, u32[]{:S(2)}, u32[]{:S(2)}) collective-permute-start(bf16[64,128]{1,0:T(8,128)(2,1)S(1)} %get-tuple-element.42.refs_4_), channel_id=1, source_target_pairs={{0,2},{1,3},{2,0},{3,1},{4,6},{5,7},{6,4},{7,5},{8,10},{9,11},{10,... | collective-permute-start | bytes 49160 | tf_op jit(solution)/shard_map/ppermute | solution.py:542
  35.7 2.7 %collective-permute-start.9 = (bf16[64,128]{1,0:T(8,128)(2,1)S(1)}, bf16[64,128]{1,0:T(8,128)(2,1)S(1)}, u32[]{:S(2)}, u32[]{:S(2)}) collective-permute-start(bf16[64,128]{1,0:T(8,128)(2,1)S(1)} %get-tuple-element.42.refs_4_), channel_id=1, source_target_pairs={{0,1},{1,0},{2,3},{3,2},{4,5},{5,4},{6,7},{7,6},{8,9},{9,8},{10,11... | collective-permute-start | bytes 49160 | tf_op jit(solution)/shard_map/ppermute | solution.py:542
  38.3 6.2 %copy-start.6 = (f32[2,64,128]{2,1,0:T(8,128)S(1)}, f32[2,64,128]{2,1,0:T(8,128)}, u32[]{:S(2)}) copy-start(f32[2,64,128]{2,1,0:T(8,128)} %currents.1) | copy-start | bytes 196612
  39.5 1.9 %collective-permute-start.12 = (bf16[192,128]{1,0:T(8,128)(2,1)S(1)}, bf16[192,128]{1,0:T(8,128)(2,1)S(1)}, u32[]{:S(2)}, u32[]{:S(2)}) collective-permute-start(bf16[192,128]{1,0:T(8,128)(2,1)S(1)} %get-tuple-element.51), channel_id=1, source_target_pairs={{0,1},{1,0},{2,3},{3,2},{4,5},{5,4},{6,7},{7,6},{8,9},{9,8},{10,11... | collective-permute-start | bytes 147464 | tf_op jit(solution)/shard_map/ppermute | solution.py:547
  39.6 4.3 %collective-permute-start.13 = (bf16[192,128]{1,0:T(8,128)(2,1)S(1)}, bf16[192,128]{1,0:T(8,128)(2,1)S(1)}, u32[]{:S(2)}, u32[]{:S(2)}) collective-permute-start(bf16[192,128]{1,0:T(8,128)(2,1)S(1)} %get-tuple-element.52), channel_id=1, source_target_pairs={{0,2},{1,3},{2,0},{3,1},{4,6},{5,7},{6,4},{7,5},{8,10},{9,11},{10,... | collective-permute-start | bytes 147464 | tf_op jit(solution)/shard_map/ppermute | solution.py:547
  40.6 3.9 %collective-permute-start.14 = (bf16[192,128]{1,0:T(8,128)(2,1)S(1)}, bf16[192,128]{1,0:T(8,128)(2,1)S(1)}, u32[]{:S(2)}, u32[]{:S(2)}) collective-permute-start(bf16[192,128]{1,0:T(8,128)(2,1)S(1)} %get-tuple-element.53), channel_id=1, source_target_pairs={{0,3},{1,2},{2,1},{3,0},{4,7},{5,6},{6,5},{7,4},{8,11},{9,10},{10,... | collective-permute-start | bytes 147464 | tf_op jit(solution)/shard_map/ppermute | solution.py:547

commit v7 on v6

--- a/solution.py
+++ b/solution.py
@@ -23,7 +23,9 @@
 DEPTH = SUBCYCLES
 SIDE_ROWS = 16 * DEPTH
 PUSH_ROWS = 8 * DEPTH
+BLOCK_ROWS = SIDE_ROWS + PUSH_ROWS
 NAMES_ROW = 2 * DEPTH - 1
+CORNER_ROWS = tuple(DEPTH * i - 1 for i in (1, 3, 4, 5, 6, 7, 8))
 TILE_ROWS = 16
 F32 = jnp.float32
 BF16 = jnp.bfloat16
@@ -62,10 +64,27 @@
     return jnp.where(condition, 1.0, 0.0).astype(F32)
 
 
-def forward_kernel(group, links_h, blocks_h, rows_h, cols_h, currents_h, *refs):
+def ocean_columns(water):
+    levels, rows, width = water.shape
+    lane = iota((rows, width), 1)
+    line = iota((1, width), 1)
+    mixed = jnp.zeros((rows, width), F32)
+    for l in range(levels):
+        mixed = jnp.where(lane // 4 == l, roll(water[l], 2 + 4 * l, 1), mixed)
+    across = jnp.concatenate([mixed, jnp.zeros((width - rows, width), F32)], axis=0).T
+    beside = []
+    for l in range(levels):
+        for j in range(2):
+            last = across[4 * l + 1 - j : 4 * l + 2 - j]
+            lead = across[4 * l + 2 + j : 4 * l + 3 + j]
+            beside.append(jnp.where(line < rows, last, roll(lead, rows, 1)))
+    return beside
+
+
+def forward_kernel(group, links_h, blocks_h, rows_h, cols_h, currents_h, water_h, *refs):
     devices, members, place = group
     outs, scratch = refs[:members], refs[members:]
-    links, blocks, currents, rows, cols, fields, names, arrived, left = scratch
+    links, blocks, currents, rows, cols, water, fields, tail, arrived, left = scratch
     pairs, side, width = rows_h.shape
     depth = cols_h.shape[1]
     loads = [
@@ -77,6 +96,7 @@
                 (currents_h, currents),
                 (rows_h, rows),
                 (cols_h, cols),
+                (water_h, water),
             )
         )
     ]
@@ -86,18 +106,15 @@
         load.wait()
     me = place()
     owners = [lax.rem(lax.rem(blocks[0, m], devices), members) for m in range(pairs)]
-    lane = iota((TILE_ROWS, width), 1)
-    numbers = jnp.zeros((TILE_ROWS, width), F32)
+    lane = iota((1, width), 1)
+    numbers = jnp.zeros((1, width), F32)
     for q in range(4):
         numbers = jnp.where(lane == q, (links[0, 0, q] >> 7).astype(F32), numbers)
         numbers = jnp.where(lane == 4 + q, (links[0, 0, q] & 127).astype(F32), numbers)
-    names[...] = numbers.astype(BF16)
-    copies = [
-        pltpu.make_async_copy(
-            names, outs[0].at[pl.ds(3 * side + depth, TILE_ROWS)], left.at[3 * members]
-        )
-    ]
-    copies[0].start()
+    ends = ocean_columns(water) + [numbers]
+    blank = jnp.zeros((tail.shape[0] - len(ends), width), F32)
+    tail[...] = jnp.concatenate(ends + [blank], axis=0).astype(BF16)
+    copies = []
     for k, out in enumerate(outs):
         partner = me ^ k
         pair, found = jnp.int32(0), jnp.int32(0)
@@ -114,8 +131,13 @@
             keep = jnp.where(found > 0, 1.0, 0.0).astype(F32)
         else:
             keep = None
-        copies[-2].start()
-        copies[-1].start()
+        copies.append(
+            pltpu.make_async_copy(
+                tail, out.at[pl.ds(3 * side + depth, tail.shape[0])], left.at[3 * members + k]
+            )
+        )
+        for copy in copies[-3:]:
+            copy.start()
         if k == 0 or keep is not None:
             for c in range(2):
                 field = currents[c] if keep is None else currents[c] * keep
@@ -152,7 +174,7 @@
 
 
 def rims_kernel(
-    thick, conc, ice, water, out, cols_o, viscous_o, gain_o, mass_o, drag_o, conduct_o,
+    thick, conc, ice, water, out, viscous_o, gain_o, mass_o, drag_o, conduct_o,
     speed_o, store,
 ):
     size = thick.shape[1]
@@ -178,7 +200,6 @@
     speed_o[0] = speed_x
     speed_o[1] = speed_y
     put_side_rims(store, [speed_x, speed_y, viscous, gain], lambda side: side * 4 * DEPTH)
-    line = iota((1, size), 1)
     levels, rows, width = water.shape
     start = SIDE_ROWS
     for l in range(levels):
@@ -187,39 +208,23 @@
             store[at : at + 1] = water[l, rows - 1 - j : rows - j]
             store[at + 2 * levels : at + 2 * levels + 1] = water[l, j : j + 1]
     out[...] = store[...].astype(BF16)
-    lane = iota((rows, width), 1)
-    mixed = jnp.zeros((rows, width), F32)
-    for l in range(levels):
-        mixed = jnp.where(lane // 4 == l, roll(water[l], 2 + 4 * l, 1), mixed)
-    across = jnp.concatenate([mixed, jnp.zeros((width - rows, width), F32)], axis=0).T
-    beside = []
-    for l in range(levels):
-        for j in range(2):
-            last = across[4 * l + 1 - j : 4 * l + 2 - j]
-            lead = across[4 * l + 2 + j : 4 * l + 3 + j]
-            beside.append(jnp.where(line < rows, last, roll(lead, rows, 1)))
-    cols_o[...] = jnp.concatenate(beside, axis=0)
-
-
-def relay_kernel(tiles, place, cols, *refs):
-    messages, out = refs[:tiles], refs[tiles]
-    for k, message in enumerate(messages):
-        out[k * SIDE_ROWS : (k + 1) * SIDE_ROWS] = message[0:SIDE_ROWS]
-    levels = cols.shape[0] // 2
-    before, after = around(place(), tiles, messages, levels)
-    rows = []
-    for strip in (before, after):
-        rows += [strip[2 * l : 2 * l + 1] for l in range(levels)]
-    out[tiles * SIDE_ROWS :] = jnp.concatenate([cols[...]] + rows, axis=0).astype(BF16)
-
-
-def around(me, tiles, messages, levels):
-    before, after = 0.0, 0.0
-    for k in range(1, tiles):
-        strips = messages[k][SIDE_ROWS : SIDE_ROWS + 4 * levels].astype(F32)
-        before = before + strips[: 2 * levels] * flag((me > 0) & ((me ^ k) == me - 1))
-        after = after + strips[2 * levels :] * flag((me < tiles - 1) & ((me ^ k) == me + 1))
-    return before, after
+
+
+def relay_kernel(tiles, *refs):
+    messages, pushes, out = refs[:tiles], refs[tiles : 2 * tiles], refs[2 * tiles]
+    for k in range(tiles):
+        at = k * BLOCK_ROWS
+        out[at : at + SIDE_ROWS] = messages[k][0:SIDE_ROWS]
+        out[at + SIDE_ROWS : at + BLOCK_ROWS] = pushes[k][...]
+
+
+def nearby(me, members, distance, arrays):
+    at = me + distance
+    inside = (at >= 0) & (at < members)
+    found = 0.0
+    for k in range(1, members):
+        found = found + arrays[k].astype(F32) * flag(inside & ((me ^ k) == at))
+    return found
 
 
 def remap_forward(chunks, field_rows, side, depth):
@@ -241,11 +246,11 @@
     return total
 
 
-def forcing_kernel(group, side, mass, drag, wind, *refs):
-    chunks = refs[:group]
+def forcing_kernel(group, side, levels, subs, place, mass, drag, wind, *refs):
+    chunks = refs[:group][::-1]
     out, current_o, push_o, store = refs[group:]
     size = mass.shape[0]
-    depth = chunks[-1].shape[0] - 3 * side
+    depth = chunks[0].shape[1]
     fields = [
         [c[side + depth : 2 * side + depth], c[2 * side + depth : 3 * side + depth]] for c in chunks
     ]
@@ -259,36 +264,42 @@
         push_o[c] = push
         pushes.append(push)
     put_side_rims(store, pushes, lambda q: q * 2 * DEPTH)
-    names = chunks[0][3 * side + depth :].astype(F32)
-    store[NAMES_ROW : NAMES_ROW + 1] = names[0:1]
-    message = store[...].astype(BF16)
-    for d in range(out.shape[0]):
-        out[d] = message
+    tail = [c[3 * side + depth :] for c in chunks]
+    store[NAMES_ROW : NAMES_ROW + 1] = tail[0].astype(F32)[2 * levels : 2 * levels + 1]
+    me, step = place(), group // subs
+    left, right = (nearby(me, group, d * step, tail) for d in (-1, 1))
+    line = iota((1, size), 1)
+    for l in range(levels):
+        near = slice(2 * l, 2 * l + 1)
+        store[CORNER_ROWS[l] : CORNER_ROWS[l] + 1] = jnp.where(line < side, left[near], right[near])
+    out[...] = store[...].astype(BF16)
 
 
 def ocean_kernel(counts, tile_place, member_place, water, mixing, *refs):
     tiles, subs, levs = counts
     members = subs * levs
-    messages, relays = refs[:tiles], refs[tiles : tiles + members]
-    warm_o, top_o = refs[tiles + members :]
+    messages, pushes = refs[:tiles], refs[tiles : 2 * tiles]
+    chunks, (warm_o, top_o) = refs[2 * tiles : -2], refs[-2:]
     levels, rows, width = water.shape
     my_tile, me = tile_place(), member_place()
     halo = {}
-    halo[-1, 0], halo[1, 0] = around(my_tile, tiles, messages, levels)
+    strips = [m[SIDE_ROWS : SIDE_ROWS + 4 * levels] for m in messages]
+    rims = [p[...] for p in pushes]
+    tails = [c[3 * rows + width :] for c in chunks]
+    for dt in (-1, 1):
+        beyond = nearby(my_tile, tiles, dt, strips)
+        halo[dt, 0] = beyond[: 2 * levels] if dt < 0 else beyond[2 * levels :]
+        corners = nearby(my_tile, tiles, dt, rims)
+        at = rows - 1 if dt < 0 else 0
+        for ds in (-1, 1):
+            lane_at = at if ds < 0 else rows + at
+            halo[dt, ds] = [
+                corners[CORNER_ROWS[l] : CORNER_ROWS[l] + 1, lane_at : lane_at + 1]
+                for l in range(levels)
+            ]
     for ds in (-1, 1):
-        beyond = me + ds * levs
-        inside = (beyond >= 0) & (beyond < members)
-        found = 0.0
-        for k in range(1, members):
-            strip = relays[k][tiles * SIDE_ROWS : tiles * SIDE_ROWS + 4 * levels].astype(F32)
-            found = found + strip * flag(inside & ((me ^ k) == beyond))
-        beside, corners = found[: 2 * levels], found[2 * levels :]
-        if ds > 0:
-            beside = roll(beside, -rows, 1)
-        halo[0, ds] = beside
-        at = width - 1 if ds < 0 else 0
-        halo[-1, ds] = corners[:levels, at : at + 1]
-        halo[1, ds] = corners[levels:, at : at + 1]
+        beside = nearby(me, members, ds * levs, tails)[: 2 * levels]
+        halo[0, ds] = roll(beside, -rows, 1) if ds > 0 else beside
     left_cols = halo[0, -1].T
     right_cols = halo[0, 1].T
     row = iota((rows, width), 0)
@@ -313,7 +324,7 @@
         corner = {}
         for dt in (-1, 1):
             for ds in (-1, 1):
-                corner[dt, ds] = halo[dt, ds][l : l + 1]
+                corner[dt, ds] = halo[dt, ds][l]
 
         def ring_row(mid, out_row, in_row, dt):
             west = jnp.where(line == 0, corner[dt, -1], roll(mid, 1, 1))
@@ -339,13 +350,12 @@
     top_o[...] = (total / (levels * levs)).astype(top_o.dtype)
 
 
-def subcycles_kernel(tiles, members, place, table, viscous, gain, speed, push, push_rims, *refs):
+def subcycles_kernel(tiles, members, table, viscous, gain, speed, push, *refs):
     relays, (out, rims) = refs[:members], refs[members:]
     size = viscous.shape[0]
-    me = place()
     for k in range(tiles):
         for m in range(members):
-            rims[me ^ (k * members + m)] = relays[m][k * SIDE_ROWS : (k + 1) * SIDE_ROWS]
+            rims[k * members + m] = relays[m][k * BLOCK_ROWS : (k + 1) * BLOCK_ROWS]
     half = DEPTH
     high = 2 * DEPTH
     sub = iota((high, size), 0)
@@ -362,8 +372,8 @@
         other = roll(both, half, 0)
         visc = jnp.where(sub < half, both, other)
         scale = jnp.where(sub < half, other, both) * mask
-        start = side // 2 * 2 * high
-        pushed = push_rims[device, start : start + 2 * high].astype(F32)
+        start = SIDE_ROWS + side // 2 * 2 * high
+        pushed = rims[device, start : start + 2 * high].astype(F32)
         pushed = pushed[:high] if side % 2 == 0 else pushed[high:]
         return [velocity, visc, scale, pushed]
 
@@ -378,7 +388,7 @@
 
     strips = []
     for q in range(4):
-        x, has_x = follow(me, q)
+        x, has_x = follow(0, q)
         strip = load(x, OPPOSITE[q], flag(has_x))
         sides = []
         for s in LATERAL[q]:
@@ -463,7 +473,7 @@
     tops = refs[group : 2 * group]
     outs = refs[2 * group :]
     size = drag.shape[0]
-    depth = chunks[-1].shape[0] - 3 * side
+    depth = chunks[0].shape[1]
     warm = remap_forward(chunks, [[t[...]] for t in tops], side, depth)
     heat = conduct[...] * warm
     fluxes = [heat.astype(BF16)]
@@ -537,16 +547,20 @@
     def device_place():
         return lax.axis_index("tile") * group + member_place()
 
+    def far_first(count):
+        return [*range(2, count), 1]
+
     def swap(value, axes, count):
-        return [value] + [
-            lax.ppermute(value, axes, [(i, i ^ k) for i in range(count)]) for k in range(1, count)
-        ]
+        got = {0: value}
+        for k in far_first(count):
+            got[k] = lax.ppermute(value, axes, [(i, i ^ k) for i in range(count)])
+        return [got[k] for k in range(count)]
 
     def swap_each(values):
-        return [values[0]] + [
-            lax.ppermute(values[k], group_axes, [(i, i ^ k) for i in range(group)])
-            for k in range(1, group)
-        ]
+        got = {0: values[0]}
+        for k in far_first(group):
+            got[k] = lax.ppermute(values[k], group_axes, [(i, i ^ k) for i in range(group)])
+        return [got[k] for k in range(group)]
 
     def shape(*dims, dtype=F32):
         return jax.ShapeDtypeStruct(dims, dtype)
@@ -558,34 +572,40 @@
     planes = shape(2, size, size)
     wind = interleaved(wind_stress)
 
-    chunk_rows = 3 * side + width
+    tail_rows = -(-(2 * levels + 1) // TILE_ROWS) * TILE_ROWS
+    chunk_rows = 3 * side + width + tail_rows
     sent = call(
         functools.partial(forward_kernel, (devices, group, member_place)),
-        [shape(chunk_rows + TILE_ROWS, width, dtype=BF16)]
-        + [shape(chunk_rows, width, dtype=BF16)] * (group - 1),
-        (neighbors, remap_blocks, remap_rows[0].swapaxes(1, 2), remap_cols[0], upper_current_vector),
+        [shape(chunk_rows, width, dtype=BF16)] * group,
+        (
+            neighbors,
+            remap_blocks,
+            remap_rows[0].swapaxes(1, 2),
+            remap_cols[0],
+            upper_current_vector,
+            water_heat_state,
+        ),
         scratch=[
             pltpu.SMEM(neighbors.shape, jnp.int32),
             pltpu.SMEM((1, pairs), jnp.int32),
             pltpu.VMEM((2, side, width), F32),
             pltpu.VMEM((pairs, side, size), BF16),
             pltpu.VMEM((pairs, size, width), BF16),
+            pltpu.VMEM((levels, side, width), F32),
             pltpu.VMEM((1 if pairs == group else group, 2 * side, width), BF16),
-            pltpu.VMEM((TILE_ROWS, width), BF16),
-            pltpu.SemaphoreType.DMA((5,)),
-            pltpu.SemaphoreType.DMA((3 * group + 1,)),
+            pltpu.VMEM((tail_rows, width), BF16),
+            pltpu.SemaphoreType.DMA((6,)),
+            pltpu.SemaphoreType.DMA((4 * group,)),
         ],
-        hbm=(0, 1, 2, 3, 4),
+        hbm=(0, 1, 2, 3, 4, 5),
         grant=60 * 2**20,
         micros=10,
     )
     chunks = swap_each(sent)
 
-    message, cols, viscous, gain, step_mass, drag, conduct, speed = call(
+    message, viscous, gain, step_mass, drag, conduct, speed = call(
         rims_kernel,
-        [shape(SIDE_ROWS + 4 * levels, size, dtype=BF16), shape(2 * levels, width)]
-        + [plane] * 5
-        + [planes],
+        [shape(SIDE_ROWS + 4 * levels, size, dtype=BF16)] + [plane] * 5 + [planes],
         (
             thickness.reshape(categories, size, size),
             concentration.reshape(categories, size, size),
@@ -596,44 +616,47 @@
     )
     messages = swap(message, "tile", tile_count)
 
+    forcing_drag, _ = lax.optimization_barrier((drag, messages[2:]))
     push_message, current_ice, push = call(
-        functools.partial(forcing_kernel, group, side),
-        [shape(devices, PUSH_ROWS, size, dtype=BF16), planes, planes],
-        (step_mass, drag, wind, *chunks),
+        functools.partial(forcing_kernel, group, side, levels, sub_count, member_place),
+        [shape(PUSH_ROWS, size, dtype=BF16), planes, planes],
+        (step_mass, forcing_drag, wind, *chunks[::-1]),
         scratch=[pltpu.VMEM((PUSH_ROWS, size), F32)],
     )
-    cols, push_message = lax.optimization_barrier((cols, push_message))
-    push_rims = lax.all_to_all(push_message, member_axes, split_axis=0, concat_axis=0, tiled=True)
+    push_messages = swap(push_message, "tile", tile_count)
 
     relay = call(
-        functools.partial(relay_kernel, tile_count, tile_place),
-        shape(tile_count * SIDE_ROWS + 4 * levels, size, dtype=BF16),
-        (cols, *messages),
+        functools.partial(relay_kernel, tile_count),
+        shape(tile_count * BLOCK_ROWS, size, dtype=BF16),
+        (*messages, *push_messages),
     )
     relays = swap(relay, group_axes, group)
 
+    mixing, _ = lax.optimization_barrier((diffusion_coefficient, relay))
     warm, top = call(
         functools.partial(
             ocean_kernel, (tile_count, sub_count, lev_count), tile_place, member_place
         ),
-        [
-            shape(levels, side, width),
-            shape(side, width, dtype=BF16 if lev_count == 1 else F32),
-        ],
-        (water_heat_state, diffusion_coefficient, *messages, *relays),
+        [shape(levels, side, width), shape(side, width, dtype=BF16 if lev_count == 1 else F32)],
+        (water_heat_state, mixing, *messages, *push_messages, *chunks),
     )
     if lev_count > 1:
         top = lax.psum(top, "lev").astype(BF16)
     tops = swap(top, group_axes, group)
 
-    push_rims, _ = lax.optimization_barrier((push_rims, top))
-    names = push_rims[:, NAMES_ROW, 0:8].astype(jnp.int32)
+    names = jnp.stack(
+        [r.reshape(tile_count, BLOCK_ROWS, size)[:, SIDE_ROWS + NAMES_ROW, 0:8] for r in relays],
+        axis=1,
+    )
+    names = names.reshape(devices, 8).astype(jnp.int32)
     table = names[:, 0:4] * 128 + names[:, 4:8]
+    table = jnp.where(table < 0, -1, table ^ device_place())
+    push, _ = lax.optimization_barrier((push, top))
     speed = call(
-        functools.partial(subcycles_kernel, tile_count, group, device_place),
+        functools.partial(subcycles_kernel, tile_count, group),
         planes,
-        (table, viscous, gain, speed, push, push_rims, *relays),
-        scratch=[pltpu.VMEM((devices, SIDE_ROWS, size), BF16)],
+        (table, viscous, gain, speed, push, *relays),
+        scratch=[pltpu.VMEM((devices, BLOCK_ROWS, size), BF16)],
         smem=(0,),
     )
 
@@ -648,7 +671,7 @@
     flat, heat, current = call(
         finish_kernel,
         [shape(2 * size, size), shape(levels, side, width), shape(2, side, width)],
-        (warm, upper_current_vector, speed, *replies),
+        (warm, upper_current_vector, speed, *replies[::-1]),
         scratch=[
             pltpu.VMEM((2 * size, size), F32),
             pltpu.VMEM((levels, side, width), F32),

time: 45.5 us -> 40.1 us (0.88)
  waiting for transfers between devices: 15.9 us -> 11.2 us
  Pallas kernels: 9.12 us -> 8.65 us
    all_to_all x1 -> x0, starting transfers between devices: 6.02 us -> none  [shards(): lax.all_to_all(push_message, member_axes, split_axis=0, concat_axis=0, ti...]
    ppermute x9 -> x12, starting transfers between devices: 8.32 us -> 14.1 us  [swap(): got[k] = lax.ppermute(value, axes, [(i, i ^ k) for i in range(count)])]
    ppermute x6, waiting for transfers between devices: 7.39 us -> 3.24 us  [swap_each(): lax.ppermute(values[k], group_axes, [(i, i ^ k) for i in range(group)])]
    ppermute x9 -> x12, waiting for transfers between devices: 8.5 us -> 7.96 us  [swap(): got[k] = lax.ppermute(value, axes, [(i, i ^ k) for i in range(count)])]
    pallas_call x8, Pallas kernels: 9.12 us -> 8.65 us  [call(): pl.pallas_call(kernel, out_shape=outs, in_specs=specs, out_specs=jax.tree...]
  transfers between devices with their start and end apart: 16 -> 18, of which waited for: 9 -> 8; matrix products, arithmetic and copies ran while one was open for 0% -> 0% of each run, Pallas kernels for 8% -> 10%
where the time goes in v7:
time: 40.1 us; the launch traced here: 39.9 us
  starting transfers between devices  19.1 us (48%)
  waiting for transfers between devices  11.2 us (28%)
  Pallas kernels  8.65 us (22%)
  between operations  0.84 us (2%)
    ppermute x12, starting transfers between devices, swap(): got[k] = lax.ppermute(value, axes, [(i, i ^ k) for i in range(count)])  14.1 us
    pallas_call x8, Pallas kernels, call(): pl.pallas_call(kernel, out_shape=outs, in_specs=specs, out_specs=jax.tree...  8.65 us
    ppermute x12, waiting for transfers between devices, swap(): got[k] = lax.ppermute(value, axes, [(i, i ^ k) for i in range(count)])  7.96 us
    ppermute x6, starting transfers between devices, swap_each(): lax.ppermute(values[k], group_axes, [(i, i ^ k) for i in range(group)])  4.98 us
    ppermute x6, waiting for transfers between devices, swap_each(): lax.ppermute(values[k], group_axes, [(i, i ^ k) for i in range(group)])  3.24 us
  transfers between devices with their start and end apart: 18, of which 8 were waited for; matrix products, arithmetic and copies ran while one was open for 0% of the time, Pallas kernels for 10%

profile of v7, /device:TPU:0, one launch (start us, length us, event | category | flops | bytes accessed | tf_op | source)
XLA Modules:
  0.0 39.9 jit_solution(14341974147682700736)
XLA Ops:
  0.6 0.0 copy-start.1
  0.6 0.0 copy-start.2
  0.7 0.0 copy-start.3
  0.7 0.0 copy-start.4
  0.7 2.7 %shard_map.131 = (bf16[336,128]{1,0:T(8,128)(2,1)}, bf16[336,128]{1,0:T(8,128)(2,1)}, bf16[336,128]{1,0:T(8,128)(2,1)}, bf16[336,128]{1,0:T(8,128)(2,1)}) custom-call(s32[1,1,4]{2,1,0:T(1,128)} %links_h.1, s32[1,4]{1,0:T(1,128)} %blocks_h.1, bf16[4,64,128]{2,1,0:T(8,128)(2,1)} %bitcast.38, bf16[4,128,128]{2,1,0:T(8,128)(2,1)} %bitcast.36, ...), custom_call_target="tpu_custom_call" | custom-call | flops 11500000256 | bytes 393248 | tf_op jit(solution)/shard_map/pallas_call | solution.py:42
  3.4 2.4 %collective-permute-start.3 = (bf16[336,128]{1,0:T(8,128)(2,1)}, bf16[336,128]{1,0:T(8,128)(2,1)S(1)}, u32[]{:S(2)}, u32[]{:S(2)}) collective-permute-start(bf16[336,128]{1,0:T(8,128)(2,1)} %get-tuple-element.33), channel_id=1, source_target_pairs={{0,3},{1,2},{2,1},{3,0},{4,7},{5,6},{6,5},{7,4},{8,11},{9,10},{10,... | collective-permute-start | bytes 258056 | tf_op jit(solution)/shard_map/ppermute | solution.py:562
  5.8 0.6 %collective-permute-start.4 = (bf16[336,128]{1,0:T(8,128)(2,1)}, bf16[336,128]{1,0:T(8,128)(2,1)S(1)}, u32[]{:S(2)}, u32[]{:S(2)}) collective-permute-start(bf16[336,128]{1,0:T(8,128)(2,1)} %get-tuple-element.34), channel_id=1, source_target_pairs={{0,2},{1,3},{2,0},{3,1},{4,6},{5,7},{6,4},{7,5},{8,10},{9,11},{10,... | collective-permute-start | bytes 258056 | tf_op jit(solution)/shard_map/ppermute | solution.py:562
  6.5 0.0 collective-permute-start.5
  6.5 0.0 copy-done.1
  6.5 0.0 copy-done.2
  6.5 0.0 copy-done.3
  6.5 0.0 copy-done.4
  6.5 0.0 copy-start
  6.5 0.0 copy-start.5
  6.6 0.2 shard_map.130
  6.8 2.9 %collective-permute-start.1 = (bf16[80,128]{1,0:T(8,128)(2,1)S(1)}, bf16[80,128]{1,0:T(8,128)(2,1)S(1)}, u32[]{:S(2)}, u32[]{:S(2)}) collective-permute-start(bf16[80,128]{1,0:T(8,128)(2,1)S(1)} %get-tuple-element.29.refs_0_), channel_id=1, source_target_pairs={{0,8},{4,12},{8,0},{12,4},{1,9},{5,13},{9,1},{13,5},{2,10},{6,14},... | collective-permute-start | bytes 61448 | tf_op jit(solution)/shard_map/ppermute | solution.py:556
  9.7 1.3 %collective-permute-start.2 = (bf16[80,128]{1,0:T(8,128)(2,1)S(1)}, bf16[80,128]{1,0:T(8,128)(2,1)S(1)}, u32[]{:S(2)}, u32[]{:S(2)}) collective-permute-start(bf16[80,128]{1,0:T(8,128)(2,1)S(1)} %get-tuple-element.29.refs_0_), channel_id=1, source_target_pairs={{0,12},{4,8},{8,4},{12,0},{1,13},{5,9},{9,5},{13,1},{2,14},{6,10},... | collective-permute-start | bytes 61448 | tf_op jit(solution)/shard_map/ppermute | solution.py:556
  11.1 0.5 %collective-permute-done.1.refs_2_ = bf16[80,128]{1,0:T(8,128)(2,1)S(1)} collective-permute-done((bf16[80,128]{1,0:T(8,128)(2,1)S(1)}, bf16[80,128]{1,0:T(8,128)(2,1)S(1)}, u32[]{:S(2)}, u32[]{:S(2)}) %collective-permute-start.1) | collective-permute-done | bytes 20512 | tf_op jit(solution)/shard_map/ppermute | solution.py:556
  11.6 1.8 %collective-permute-start = (bf16[80,128]{1,0:T(8,128)(2,1)S(1)}, bf16[80,128]{1,0:T(8,128)(2,1)S(1)}, u32[]{:S(2)}, u32[]{:S(2)}) collective-permute-start(bf16[80,128]{1,0:T(8,128)(2,1)S(1)} %get-tuple-element.29.refs_0_), channel_id=1, source_target_pairs={{0,4},{4,0},{8,12},{12,8},{1,5},{5,1},{9,13},{13,9},{2,6},{6,2},{1... | collective-permute-start | bytes 61448 | tf_op jit(solution)/shard_map/ppermute | solution.py:556
  13.4 1.9 %collective-permute-done.2.refs_3_ = bf16[80,128]{1,0:T(8,128)(2,1)S(1)} collective-permute-done((bf16[80,128]{1,0:T(8,128)(2,1)S(1)}, bf16[80,128]{1,0:T(8,128)(2,1)S(1)}, u32[]{:S(2)}, u32[]{:S(2)}) %collective-permute-start.2) | collective-permute-done | bytes 20512 | tf_op jit(solution)/shard_map/ppermute | solution.py:556
  15.3 0.0 collective-permute-done.3.refs_0_.refs_11_.refs_3_
  15.3 0.0 collective-permute-done.4.refs_1_.refs_10_.refs_2_
  15.3 0.0 collective-permute-done.5.refs_2_.refs_9_.refs_1_
  15.3 0.0 copy-done
  15.3 0.0 copy-done.5
  15.3 0.6 %shard_map.132 = (bf16[32,128]{1,0:T(8,128)(2,1)S(1)}, f32[2,128,128]{2,1,0:T(8,128)S(1)}, f32[2,128,128]{2,1,0:T(8,128)S(1)}) custom-call(f32[128,128]{1,0:T(8,128)S(1)} %get-tuple-element.30.mass, f32[128,128]{1,0:T(8,128)S(1)} %get-tuple-element.32.drag, f32[256,128]{1,0:T(8,128)S(1)} %bitcast.31, ...), custom_call_target="tpu_custom_call" | custom-call | flops 11500000 | bytes 606208 | tf_op jit(solution)/shard_map/pallas_call | solution.py:42
  15.9 0.1 collective-permute-start.6
  16.0 1.9 %collective-permute-start.7 = (bf16[32,128]{1,0:T(8,128)(2,1)S(1)}, bf16[32,128]{1,0:T(8,128)(2,1)S(1)}, u32[]{:S(2)}, u32[]{:S(2)}) collective-permute-start(bf16[32,128]{1,0:T(8,128)(2,1)S(1)} %get-tuple-element.37.refs_4_), channel_id=1, source_target_pairs={{0,8},{4,12},{8,0},{12,4},{1,9},{5,13},{9,1},{13,5},{2,10},{6,14},... | collective-permute-start | bytes 24584 | tf_op jit(solution)/shard_map/ppermute | solution.py:556
  17.9 2.5 %collective-permute-start.8 = (bf16[32,128]{1,0:T(8,128)(2,1)S(1)}, bf16[32,128]{1,0:T(8,128)(2,1)S(1)}, u32[]{:S(2)}, u32[]{:S(2)}) collective-permute-start(bf16[32,128]{1,0:T(8,128)(2,1)S(1)} %get-tuple-element.37.refs_4_), channel_id=1, source_target_pairs={{0,12},{4,8},{8,4},{12,0},{1,13},{5,9},{9,5},{13,1},{2,14},{6,10},... | collective-permute-start | bytes 24584 | tf_op jit(solution)/shard_map/ppermute | solution.py:556
  20.4 0.0 collective-permute-done.refs_1_
  20.4 0.0 collective-permute-done.6.refs_5_
  20.4 0.3 collective-permute-done.7.refs_6_
  20.7 2.6 %collective-permute-done.8.refs_7_ = bf16[32,128]{1,0:T(8,128)(2,1)S(1)} collective-permute-done((bf16[32,128]{1,0:T(8,128)(2,1)S(1)}, bf16[32,128]{1,0:T(8,128)(2,1)S(1)}, u32[]{:S(2)}, u32[]{:S(2)}) %collective-permute-start.8) | collective-permute-done | bytes 8224 | tf_op jit(solution)/shard_map/ppermute | solution.py:556
  23.3 0.0 copy-start.7
  23.3 0.1 collective-permute-start.11
  23.4 1.6 %collective-permute-start.10 = (bf16[384,128]{1,0:T(8,128)(2,1)S(1)}, bf16[384,128]{1,0:T(8,128)(2,1)S(1)}, u32[]{:S(2)}, u32[]{:S(2)}) collective-permute-start(bf16[384,128]{1,0:T(8,128)(2,1)S(1)} %shard_map.133.refs_0_), channel_id=1, source_target_pairs={{0,2},{1,3},{2,0},{3,1},{4,6},{5,7},{6,4},{7,5},{8,10},{9,11},{10,... | collective-permute-start | bytes 294920 | tf_op jit(solution)/shard_map/ppermute | solution.py:556
  25.0 0.3 collective-permute-start.9
  25.3 0.0 copy-done.7
  25.3 1.1 %shard_map.134 = (f32[4,64,128]{2,1,0:T(8,128)S(1)}, bf16[64,128]{1,0:T(8,128)(2,1)S(1)}) custom-call(f32[4,64,128]{2,1,0:T(8,128)S(1)} %copy-done.1, f32[64,128]{1,0:T(8,128)S(1)} %copy-done.7, bf16[80,128]{1,0:T(8,128)(2,1)S(1)} %get-tuple-element.29.refs_0_, bf16[80,128]{1,0:T(8,128)(2,1)S(1)} %collective-permute-done.refs_1_, ...), custom_call_target="tpu_custom_call" | custom-call | flops 11500000 | bytes 622592 | tf_op jit(solution)/shard_map/pallas_call | solution.py:42
  26.4 0.3 collective-permute-start.12
  26.7 1.4 %collective-permute-start.13 = (bf16[64,128]{1,0:T(8,128)(2,1)S(1)}, bf16[64,128]{1,0:T(8,128)(2,1)S(1)}, u32[]{:S(2)}, u32[]{:S(2)}) collective-permute-start(bf16[64,128]{1,0:T(8,128)(2,1)S(1)} %get-tuple-element.44.refs_4_), channel_id=1, source_target_pairs={{0,2},{1,3},{2,0},{3,1},{4,6},{5,7},{6,4},{7,5},{8,10},{9,11},{10,... | collective-permute-start | bytes 49160 | tf_op jit(solution)/shard_map/ppermute | solution.py:556
  28.1 0.4 collective-permute-done.11.refs_3_
  28.4 0.0 collective-permute-start.14
  28.5 2.2 %collective-permute-done.10.refs_2_ = bf16[384,128]{1,0:T(8,128)(2,1)S(1)} collective-permute-done((bf16[384,128]{1,0:T(8,128)(2,1)S(1)}, bf16[384,128]{1,0:T(8,128)(2,1)S(1)}, u32[]{:S(2)}, u32[]{:S(2)}) %collective-permute-start.10) | collective-permute-done | bytes 98336 | tf_op jit(solution)/shard_map/ppermute | solution.py:556
  30.6 0.0 collective-permute-done.9.refs_1_
  30.7 0.1 xor_select_fusion.table
  30.8 2.1 %shard_map.135.speed = f32[2,128,128]{2,1,0:T(8,128)S(1)} custom-call(s32[16,4]{1,0:T(8,128)S(1)} %xor_select_fusion.table, f32[128,128]{1,0:T(8,128)S(1)} %get-tuple-element.40.viscous, f32[128,128]{1,0:T(8,128)S(1)} %get-tuple-element.41.gain, f32[2,128,128]{2,1,0:T(8,128)S(1)} %get-tuple-element.42.speed, f32[2,128,128]{2,1,0:T(8,128)S(1)} %get-tuple-element.45.push, ...), custom_call_target="tpu_custom_call" | custom-call | flops 11500000 | bytes 786688 | tf_op jit(solution)/shard_map/pallas_call | solution.py:42
  32.9 0.0 collective-permute-done.12.refs_5_
  32.9 0.0 collective-permute-done.13.refs_6_
  32.9 0.0 collective-permute-done.14.refs_7_
  32.9 0.0 copy-start.6
  32.9 1.1 %shard_map.136 = (bf16[192,128]{1,0:T(8,128)(2,1)S(1)}, bf16[192,128]{1,0:T(8,128)(2,1)S(1)}, bf16[192,128]{1,0:T(8,128)(2,1)S(1)}, bf16[192,128]{1,0:T(8,128)(2,1)S(1)}) custom-call(f32[128,128]{1,0:T(8,128)S(1)} %get-tuple-element.32.drag, f32[128,128]{1,0:T(8,128)S(1)} %get-tuple-element.46.conduct, f32[2,128,128]{2,1,0:T(8,128)S(1)} %get-tuple-element.47.current, ...), custom_call_target="tpu_custom_call" | custom-call | flops 11500000 | bytes 802816 | tf_op jit(solution)/shard_map/pallas_call | solution.py:42
  34.0 0.0 collective-permute-start.15
  34.1 1.6 %collective-permute-start.16 = (bf16[192,128]{1,0:T(8,128)(2,1)S(1)}, bf16[192,128]{1,0:T(8,128)(2,1)S(1)}, u32[]{:S(2)}, u32[]{:S(2)}) collective-permute-start(bf16[192,128]{1,0:T(8,128)(2,1)S(1)} %get-tuple-element.49), channel_id=1, source_target_pairs={{0,2},{1,3},{2,0},{3,1},{4,6},{5,7},{6,4},{7,5},{8,10},{9,11},{10,... | collective-permute-start | bytes 147464 | tf_op jit(solution)/shard_map/ppermute | solution.py:562
  35.7 0.2 collective-permute-start.17
  35.9 2.0 %collective-permute-done.15.refs_0_ = bf16[192,128]{1,0:T(8,128)(2,1)S(1)} collective-permute-done((bf16[192,128]{1,0:T(8,128)(2,1)S(1)}, bf16[192,128]{1,0:T(8,128)(2,1)S(1)}, u32[]{:S(2)}, u32[]{:S(2)}) %collective-permute-start.15) | collective-permute-done | bytes 49184 | tf_op jit(solution)/shard_map/ppermute | solution.py:562
  37.9 1.3 %collective-permute-done.16.refs_1_ = bf16[192,128]{1,0:T(8,128)(2,1)S(1)} collective-permute-done((bf16[192,128]{1,0:T(8,128)(2,1)S(1)}, bf16[192,128]{1,0:T(8,128)(2,1)S(1)}, u32[]{:S(2)}, u32[]{:S(2)}) %collective-permute-start.16) | collective-permute-done | bytes 49184 | tf_op jit(solution)/shard_map/ppermute | solution.py:562
  39.2 0.0 collective-permute-done.17.refs_2_
  39.2 0.0 copy-done.6
  39.2 0.8 %shard_map.137 = (f32[256,128]{1,0:T(8,128)}, f32[4,64,128]{2,1,0:T(8,128)}, f32[2,64,128]{2,1,0:T(8,128)}) custom-call(f32[4,64,128]{2,1,0:T(8,128)S(1)} %get-tuple-element.39.warm, f32[2,64,128]{2,1,0:T(8,128)S(1)} %copy-done.6, f32[2,128,128]{2,1,0:T(8,128)S(1)} %shard_map.135.speed, bf16[192,128]{1,0:T(8,128)(2,1)S(1)} %collective-permute-done.15.refs_0_, ...), custom_call_target="tpu_custom_call" | custom-call | flops 11500000 | bytes 524288 | tf_op jit(solution)/shard_map/pallas_call | solution.py:42
  (7 shorter events, 0.1 us)
Async XLA Ops:
  0.6 5.9 %copy-start.1 = (f32[4,64,128]{2,1,0:T(8,128)S(1)}, f32[4,64,128]{2,1,0:T(8,128)}, u32[]{:S(2)}) copy-start(f32[4,64,128]{2,1,0:T(8,128)} %water.3) | copy-start | bytes 393220
  0.6 5.9 %copy-start.2 = (f32[1,1,5,16384]{3,1,2,0:T(1,128)S(1)}, f32[1,1,5,16384]{3,1,2,0:T(1,128)}, u32[]{:S(2)}) copy-start(f32[1,1,5,16384]{3,1,2,0:T(1,128)} %param.18) | copy-start | bytes 983044
  0.7 5.9 %copy-start.3 = (f32[1,1,5,16384]{3,1,2,0:T(1,128)S(1)}, f32[1,1,5,16384]{3,1,2,0:T(1,128)}, u32[]{:S(2)}) copy-start(f32[1,1,5,16384]{3,1,2,0:T(1,128)} %param.19) | copy-start | bytes 983044
  0.7 5.9 %copy-start.4 = (f32[1,1,2,16384]{3,2,1,0:T(2,128)S(1)}, f32[1,1,2,16384]{3,2,1,0:T(2,128)}, u32[]{:S(2)}) copy-start(f32[1,1,2,16384]{3,2,1,0:T(2,128)} %param.20) | copy-start | bytes 393220
  3.4 11.9 %collective-permute-start.3 = (bf16[336,128]{1,0:T(8,128)(2,1)}, bf16[336,128]{1,0:T(8,128)(2,1)S(1)}, u32[]{:S(2)}, u32[]{:S(2)}) collective-permute-start(bf16[336,128]{1,0:T(8,128)(2,1)} %get-tuple-element.33), channel_id=1, source_target_pairs={{0,3},{1,2},{2,1},{3,0},{4,7},{5,6},{6,5},{7,4},{8,11},{9,10},{10,... | collective-permute-start | bytes 258056 | tf_op jit(solution)/shard_map/ppermute | solution.py:562
  5.8 9.5 %collective-permute-start.4 = (bf16[336,128]{1,0:T(8,128)(2,1)}, bf16[336,128]{1,0:T(8,128)(2,1)S(1)}, u32[]{:S(2)}, u32[]{:S(2)}) collective-permute-start(bf16[336,128]{1,0:T(8,128)(2,1)} %get-tuple-element.34), channel_id=1, source_target_pairs={{0,2},{1,3},{2,0},{3,1},{4,6},{5,7},{6,4},{7,5},{8,10},{9,11},{10,... | collective-permute-start | bytes 258056 | tf_op jit(solution)/shard_map/ppermute | solution.py:562
  6.5 8.8 %collective-permute-start.5 = (bf16[336,128]{1,0:T(8,128)(2,1)}, bf16[336,128]{1,0:T(8,128)(2,1)S(1)}, u32[]{:S(2)}, u32[]{:S(2)}) collective-permute-start(bf16[336,128]{1,0:T(8,128)(2,1)} %get-tuple-element.35), channel_id=1, source_target_pairs={{0,1},{1,0},{2,3},{3,2},{4,5},{5,4},{6,7},{7,6},{8,9},{9,8},{10,11... | collective-permute-start | bytes 258056 | tf_op jit(solution)/shard_map/ppermute | solution.py:562
  6.5 8.8 %copy-start = (bf16[336,128]{1,0:T(8,128)(2,1)S(1)}, bf16[336,128]{1,0:T(8,128)(2,1)}, u32[]{:S(2)}) copy-start(bf16[336,128]{1,0:T(8,128)(2,1)} %get-tuple-element.36.refs_3_.refs_8_.refs_0_) | copy-start | bytes 258052
  6.5 8.8 %copy-start.5 = (f32[1,1,2,16384]{3,2,1,0:T(2,128)S(1)}, f32[1,1,2,16384]{3,2,1,0:T(2,128)}, u32[]{:S(2)}) copy-start(f32[1,1,2,16384]{3,2,1,0:T(2,128)} %param.21) | copy-start | bytes 393220
  6.8 4.7 %collective-permute-start.1 = (bf16[80,128]{1,0:T(8,128)(2,1)S(1)}, bf16[80,128]{1,0:T(8,128)(2,1)S(1)}, u32[]{:S(2)}, u32[]{:S(2)}) collective-permute-start(bf16[80,128]{1,0:T(8,128)(2,1)S(1)} %get-tuple-element.29.refs_0_), channel_id=1, source_target_pairs={{0,8},{4,12},{8,0},{12,4},{1,9},{5,13},{9,1},{13,5},{2,10},{6,14},... | collective-permute-start | bytes 61448 | tf_op jit(solution)/shard_map/ppermute | solution.py:556
  9.7 5.6 %collective-permute-start.2 = (bf16[80,128]{1,0:T(8,128)(2,1)S(1)}, bf16[80,128]{1,0:T(8,128)(2,1)S(1)}, u32[]{:S(2)}, u32[]{:S(2)}) collective-permute-start(bf16[80,128]{1,0:T(8,128)(2,1)S(1)} %get-tuple-element.29.refs_0_), channel_id=1, source_target_pairs={{0,12},{4,8},{8,4},{12,0},{1,13},{5,9},{9,5},{13,1},{2,14},{6,10},... | collective-permute-start | bytes 61448 | tf_op jit(solution)/shard_map/ppermute | solution.py:556
  11.6 8.8 %collective-permute-start = (bf16[80,128]{1,0:T(8,128)(2,1)S(1)}, bf16[80,128]{1,0:T(8,128)(2,1)S(1)}, u32[]{:S(2)}, u32[]{:S(2)}) collective-permute-start(bf16[80,128]{1,0:T(8,128)(2,1)S(1)} %get-tuple-element.29.refs_0_), channel_id=1, source_target_pairs={{0,4},{4,0},{8,12},{12,8},{1,5},{5,1},{9,13},{13,9},{2,6},{6,2},{1... | collective-permute-start | bytes 61448 | tf_op jit(solution)/shard_map/ppermute | solution.py:556
  15.9 4.4 %collective-permute-start.6 = (bf16[32,128]{1,0:T(8,128)(2,1)S(1)}, bf16[32,128]{1,0:T(8,128)(2,1)S(1)}, u32[]{:S(2)}, u32[]{:S(2)}) collective-permute-start(bf16[32,128]{1,0:T(8,128)(2,1)S(1)} %get-tuple-element.37.refs_4_), channel_id=1, source_target_pairs={{0,4},{4,0},{8,12},{12,8},{1,5},{5,1},{9,13},{13,9},{2,6},{6,2},{1... | collective-permute-start | bytes 24584 | tf_op jit(solution)/shard_map/ppermute | solution.py:556
  16.0 4.7 %collective-permute-start.7 = (bf16[32,128]{1,0:T(8,128)(2,1)S(1)}, bf16[32,128]{1,0:T(8,128)(2,1)S(1)}, u32[]{:S(2)}, u32[]{:S(2)}) collective-permute-start(bf16[32,128]{1,0:T(8,128)(2,1)S(1)} %get-tuple-element.37.refs_4_), channel_id=1, source_target_pairs={{0,8},{4,12},{8,0},{12,4},{1,9},{5,13},{9,1},{13,5},{2,10},{6,14},... | collective-permute-start | bytes 24584 | tf_op jit(solution)/shard_map/ppermute | solution.py:556
  17.9 5.4 %collective-permute-start.8 = (bf16[32,128]{1,0:T(8,128)(2,1)S(1)}, bf16[32,128]{1,0:T(8,128)(2,1)S(1)}, u32[]{:S(2)}, u32[]{:S(2)}) collective-permute-start(bf16[32,128]{1,0:T(8,128)(2,1)S(1)} %get-tuple-element.37.refs_4_), channel_id=1, source_target_pairs={{0,12},{4,8},{8,4},{12,0},{1,13},{5,9},{9,5},{13,1},{2,14},{6,10},... | collective-permute-start | bytes 24584 | tf_op jit(solution)/shard_map/ppermute | solution.py:556
  23.3 1.9 %copy-start.7 = (f32[64,128]{1,0:T(8,128)S(1)}, f32[64,128]{1,0:T(8,128)}, u32[]{:S(2)}) copy-start(f32[64,128]{1,0:T(8,128)} %mixing) | copy-start | bytes 98308
  23.3 5.1 %collective-permute-start.11 = (bf16[384,128]{1,0:T(8,128)(2,1)S(1)}, bf16[384,128]{1,0:T(8,128)(2,1)S(1)}, u32[]{:S(2)}, u32[]{:S(2)}) collective-permute-start(bf16[384,128]{1,0:T(8,128)(2,1)S(1)} %shard_map.133.refs_0_), channel_id=1, source_target_pairs={{0,3},{1,2},{2,1},{3,0},{4,7},{5,6},{6,5},{7,4},{8,11},{9,10},{10,... | collective-permute-start | bytes 294920 | tf_op jit(solution)/shard_map/ppermute | solution.py:556
  23.4 7.2 %collective-permute-start.10 = (bf16[384,128]{1,0:T(8,128)(2,1)S(1)}, bf16[384,128]{1,0:T(8,128)(2,1)S(1)}, u32[]{:S(2)}, u32[]{:S(2)}) collective-permute-start(bf16[384,128]{1,0:T(8,128)(2,1)S(1)} %shard_map.133.refs_0_), channel_id=1, source_target_pairs={{0,2},{1,3},{2,0},{3,1},{4,6},{5,7},{6,4},{7,5},{8,10},{9,11},{10,... | collective-permute-start | bytes 294920 | tf_op jit(solution)/shard_map/ppermute | solution.py:556
  25.0 5.7 %collective-permute-start.9 = (bf16[384,128]{1,0:T(8,128)(2,1)S(1)}, bf16[384,128]{1,0:T(8,128)(2,1)S(1)}, u32[]{:S(2)}, u32[]{:S(2)}) collective-permute-start(bf16[384,128]{1,0:T(8,128)(2,1)S(1)} %shard_map.133.refs_0_), channel_id=1, source_target_pairs={{0,1},{1,0},{2,3},{3,2},{4,5},{5,4},{6,7},{7,6},{8,9},{9,8},{10,11... | collective-permute-start | bytes 294920 | tf_op jit(solution)/shard_map/ppermute | solution.py:556
  26.4 6.5 %collective-permute-start.12 = (bf16[64,128]{1,0:T(8,128)(2,1)S(1)}, bf16[64,128]{1,0:T(8,128)(2,1)S(1)}, u32[]{:S(2)}, u32[]{:S(2)}) collective-permute-start(bf16[64,128]{1,0:T(8,128)(2,1)S(1)} %get-tuple-element.44.refs_4_), channel_id=1, source_target_pairs={{0,1},{1,0},{2,3},{3,2},{4,5},{5,4},{6,7},{7,6},{8,9},{9,8},{10,11... | collective-permute-start | bytes 49160 | tf_op jit(solution)/shard_map/ppermute | solution.py:556
  26.7 6.2 %collective-permute-start.13 = (bf16[64,128]{1,0:T(8,128)(2,1)S(1)}, bf16[64,128]{1,0:T(8,128)(2,1)S(1)}, u32[]{:S(2)}, u32[]{:S(2)}) collective-permute-start(bf16[64,128]{1,0:T(8,128)(2,1)S(1)} %get-tuple-element.44.refs_4_), channel_id=1, source_target_pairs={{0,2},{1,3},{2,0},{3,1},{4,6},{5,7},{6,4},{7,5},{8,10},{9,11},{10,... | collective-permute-start | bytes 49160 | tf_op jit(solution)/shard_map/ppermute | solution.py:556
  28.4 4.5 %collective-permute-start.14 = (bf16[64,128]{1,0:T(8,128)(2,1)S(1)}, bf16[64,128]{1,0:T(8,128)(2,1)S(1)}, u32[]{:S(2)}, u32[]{:S(2)}) collective-permute-start(bf16[64,128]{1,0:T(8,128)(2,1)S(1)} %get-tuple-element.44.refs_4_), channel_id=1, source_target_pairs={{0,3},{1,2},{2,1},{3,0},{4,7},{5,6},{6,5},{7,4},{8,11},{9,10},{10,... | collective-permute-start | bytes 49160 | tf_op jit(solution)/shard_map/ppermute | solution.py:556
  32.9 6.2 %copy-start.6 = (f32[2,64,128]{2,1,0:T(8,128)S(1)}, f32[2,64,128]{2,1,0:T(8,128)}, u32[]{:S(2)}) copy-start(f32[2,64,128]{2,1,0:T(8,128)} %currents.1) | copy-start | bytes 196612
  34.0 3.8 %collective-permute-start.15 = (bf16[192,128]{1,0:T(8,128)(2,1)S(1)}, bf16[192,128]{1,0:T(8,128)(2,1)S(1)}, u32[]{:S(2)}, u32[]{:S(2)}) collective-permute-start(bf16[192,128]{1,0:T(8,128)(2,1)S(1)} %get-tuple-element.48), channel_id=1, source_target_pairs={{0,3},{1,2},{2,1},{3,0},{4,7},{5,6},{6,5},{7,4},{8,11},{9,10},{10,... | collective-permute-start | bytes 147464 | tf_op jit(solution)/shard_map/ppermute | solution.py:562
  34.1 5.1 %collective-permute-start.16 = (bf16[192,128]{1,0:T(8,128)(2,1)S(1)}, bf16[192,128]{1,0:T(8,128)(2,1)S(1)}, u32[]{:S(2)}, u32[]{:S(2)}) collective-permute-start(bf16[192,128]{1,0:T(8,128)(2,1)S(1)} %get-tuple-element.49), channel_id=1, source_target_pairs={{0,2},{1,3},{2,0},{3,1},{4,6},{5,7},{6,4},{7,5},{8,10},{9,11},{10,... | collective-permute-start | bytes 147464 | tf_op jit(solution)/shard_map/ppermute | solution.py:562
  35.7 3.4 %collective-permute-start.17 = (bf16[192,128]{1,0:T(8,128)(2,1)S(1)}, bf16[192,128]{1,0:T(8,128)(2,1)S(1)}, u32[]{:S(2)}, u32[]{:S(2)}) collective-permute-start(bf16[192,128]{1,0:T(8,128)(2,1)S(1)} %get-tuple-element.50), channel_id=1, source_target_pairs={{0,1},{1,0},{2,3},{3,2},{4,5},{5,4},{6,7},{7,6},{8,9},{9,8},{10,11... | collective-permute-start | bytes 147464 | tf_op jit(solution)/shard_map/ppermute | solution.py:562

commit v8 on v7

--- a/solution.py
+++ b/solution.py
@@ -211,11 +211,9 @@
 
 
 def relay_kernel(tiles, *refs):
-    messages, pushes, out = refs[:tiles], refs[tiles : 2 * tiles], refs[2 * tiles]
+    messages, out = refs[:tiles][::-1], refs[tiles]
     for k in range(tiles):
-        at = k * BLOCK_ROWS
-        out[at : at + SIDE_ROWS] = messages[k][0:SIDE_ROWS]
-        out[at + SIDE_ROWS : at + BLOCK_ROWS] = pushes[k][...]
+        out[k * BLOCK_ROWS : (k + 1) * BLOCK_ROWS] = messages[k][0:BLOCK_ROWS]
 
 
 def nearby(me, members, distance, arrays):
@@ -246,7 +244,7 @@
     return total
 
 
-def forcing_kernel(group, side, levels, subs, place, mass, drag, wind, *refs):
+def forcing_kernel(group, side, levels, subs, place, mass, drag, wind, early, *refs):
     chunks = refs[:group][::-1]
     out, current_o, push_o, store = refs[group:]
     size = mass.shape[0]
@@ -272,19 +270,19 @@
     for l in range(levels):
         near = slice(2 * l, 2 * l + 1)
         store[CORNER_ROWS[l] : CORNER_ROWS[l] + 1] = jnp.where(line < side, left[near], right[near])
-    out[...] = store[...].astype(BF16)
+    out[0:PUSH_ROWS] = store[...].astype(BF16)
+    out[PUSH_ROWS:] = early[...]
 
 
 def ocean_kernel(counts, tile_place, member_place, water, mixing, *refs):
     tiles, subs, levs = counts
     members = subs * levs
-    messages, pushes = refs[:tiles], refs[tiles : 2 * tiles]
-    chunks, (warm_o, top_o) = refs[2 * tiles : -2], refs[-2:]
+    messages, chunks, (warm_o, top_o) = refs[:tiles], refs[tiles:-2], refs[-2:]
     levels, rows, width = water.shape
     my_tile, me = tile_place(), member_place()
     halo = {}
-    strips = [m[SIDE_ROWS : SIDE_ROWS + 4 * levels] for m in messages]
-    rims = [p[...] for p in pushes]
+    strips = [m[BLOCK_ROWS : BLOCK_ROWS + 4 * levels] for m in messages]
+    rims = [m[0:PUSH_ROWS] for m in messages]
     tails = [c[3 * rows + width :] for c in chunks]
     for dt in (-1, 1):
         beyond = nearby(my_tile, tiles, dt, strips)
@@ -365,14 +363,15 @@
     first, last = lane == 0, lane == size - 1
 
     def load(device, side, mask, with_push=True):
-        block = rims[device, side * 2 * high : (side + 1) * 2 * high].astype(F32)
+        start = PUSH_ROWS + side * 2 * high
+        block = rims[device, start : start + 2 * high].astype(F32)
         velocity, both = block[:high] * mask, block[high:]
         if not with_push:
             return velocity
         other = roll(both, half, 0)
         visc = jnp.where(sub < half, both, other)
         scale = jnp.where(sub < half, other, both) * mask
-        start = SIDE_ROWS + side // 2 * 2 * high
+        start = side // 2 * 2 * high
         pushed = rims[device, start : start + 2 * high].astype(F32)
         pushed = pushed[:high] if side % 2 == 0 else pushed[high:]
         return [velocity, visc, scale, pushed]
@@ -603,7 +602,7 @@
     )
     chunks = swap_each(sent)
 
-    message, viscous, gain, step_mass, drag, conduct, speed = call(
+    early, viscous, gain, step_mass, drag, conduct, speed = call(
         rims_kernel,
         [shape(SIDE_ROWS + 4 * levels, size, dtype=BF16)] + [plane] * 5 + [planes],
         (
@@ -614,21 +613,18 @@
         ),
         scratch=[pltpu.VMEM((SIDE_ROWS + 4 * levels, size), F32)],
     )
+    message, current_ice, push = call(
+        functools.partial(forcing_kernel, group, side, levels, sub_count, member_place),
+        [shape(BLOCK_ROWS + 4 * levels, size, dtype=BF16), planes, planes],
+        (step_mass, drag, wind, early, *chunks[::-1]),
+        scratch=[pltpu.VMEM((PUSH_ROWS, size), F32)],
+    )
     messages = swap(message, "tile", tile_count)
-
-    forcing_drag, _ = lax.optimization_barrier((drag, messages[2:]))
-    push_message, current_ice, push = call(
-        functools.partial(forcing_kernel, group, side, levels, sub_count, member_place),
-        [shape(PUSH_ROWS, size, dtype=BF16), planes, planes],
-        (step_mass, forcing_drag, wind, *chunks[::-1]),
-        scratch=[pltpu.VMEM((PUSH_ROWS, size), F32)],
-    )
-    push_messages = swap(push_message, "tile", tile_count)
 
     relay = call(
         functools.partial(relay_kernel, tile_count),
         shape(tile_count * BLOCK_ROWS, size, dtype=BF16),
-        (*messages, *push_messages),
+        messages[::-1],
     )
     relays = swap(relay, group_axes, group)
 
@@ -638,14 +634,14 @@
             ocean_kernel, (tile_count, sub_count, lev_count), tile_place, member_place
         ),
         [shape(levels, side, width), shape(side, width, dtype=BF16 if lev_count == 1 else F32)],
-        (water_heat_state, mixing, *messages, *push_messages, *chunks),
+        (water_heat_state, mixing, *messages, *chunks),
     )
     if lev_count > 1:
         top = lax.psum(top, "lev").astype(BF16)
     tops = swap(top, group_axes, group)
 
     names = jnp.stack(
-        [r.reshape(tile_count, BLOCK_ROWS, size)[:, SIDE_ROWS + NAMES_ROW, 0:8] for r in relays],
+        [r.reshape(tile_count, BLOCK_ROWS, size)[:, NAMES_ROW, 0:8] for r in relays],
         axis=1,
     )
     names = names.reshape(devices, 8).astype(jnp.int32)

time: 40.1 us -> 37.6 us (0.938)
  starting transfers between devices: 19.1 us -> 13.5 us
  waiting for transfers between devices: 11.2 us -> 14.3 us
    ppermute x12 -> x9, starting transfers between devices: 14.1 us -> 8.49 us  [swap(): got[k] = lax.ppermute(value, axes, [(i, i ^ k) for i in range(count)])]
    ppermute x6, waiting for transfers between devices: 3.24 us -> 7.6 us  [swap_each(): lax.ppermute(values[k], group_axes, [(i, i ^ k) for i in range(group)])]
    ppermute x12 -> x9, waiting for transfers between devices: 7.96 us -> 6.71 us  [swap(): got[k] = lax.ppermute(value, axes, [(i, i ^ k) for i in range(count)])]
  transfers between devices with their start and end apart: 18 -> 15, of which waited for: 8 -> 8; matrix products, arithmetic and copies ran while one was open for 0% -> 0% of each run, Pallas kernels for 10% -> 9%
where the time goes in v8:
time: 37.6 us; the launch traced here: 37.4 us
  waiting for transfers between devices  14.3 us (38%)
  starting transfers between devices  13.5 us (36%)
  Pallas kernels  8.66 us (23%)
  between operations  0.8 us (2%)
    pallas_call x8, Pallas kernels, call(): pl.pallas_call(kernel, out_shape=outs, in_specs=specs, out_specs=jax.tree...  8.66 us
    ppermute x9, starting transfers between devices, swap(): got[k] = lax.ppermute(value, axes, [(i, i ^ k) for i in range(count)])  8.49 us
    ppermute x6, waiting for transfers between devices, swap_each(): lax.ppermute(values[k], group_axes, [(i, i ^ k) for i in range(group)])  7.6 us
    ppermute x9, waiting for transfers between devices, swap(): got[k] = lax.ppermute(value, axes, [(i, i ^ k) for i in range(count)])  6.71 us
    ppermute x6, starting transfers between devices, swap_each(): lax.ppermute(values[k], group_axes, [(i, i ^ k) for i in range(group)])  4.99 us
  transfers between devices with their start and end apart: 15, of which 8 were waited for; matrix products, arithmetic and copies ran while one was open for 0% of the time, Pallas kernels for 9%

profile of v8, /device:TPU:0, one launch (start us, length us, event | category | flops | bytes accessed | tf_op | source)
XLA Modules:
  0.0 37.4 jit_solution(354876712610117683)
XLA Ops:
  0.6 0.0 copy-start.1
  0.6 0.0 copy-start.2
  0.7 0.0 copy-start.3
  0.7 0.0 copy-start.4
  0.7 2.7 %shard_map.131 = (bf16[336,128]{1,0:T(8,128)(2,1)}, bf16[336,128]{1,0:T(8,128)(2,1)}, bf16[336,128]{1,0:T(8,128)(2,1)}, bf16[336,128]{1,0:T(8,128)(2,1)}) custom-call(s32[1,1,4]{2,1,0:T(1,128)} %links_h.1, s32[1,4]{1,0:T(1,128)} %blocks_h.1, bf16[4,64,128]{2,1,0:T(8,128)(2,1)} %bitcast.38, bf16[4,128,128]{2,1,0:T(8,128)(2,1)} %bitcast.36, ...), custom_call_target="tpu_custom_call" | custom-call | flops 11500000256 | bytes 393248 | tf_op jit(solution)/shard_map/pallas_call | solution.py:42
  3.4 2.4 %collective-permute-start = (bf16[336,128]{1,0:T(8,128)(2,1)}, bf16[336,128]{1,0:T(8,128)(2,1)S(1)}, u32[]{:S(2)}, u32[]{:S(2)}) collective-permute-start(bf16[336,128]{1,0:T(8,128)(2,1)} %get-tuple-element.31), channel_id=1, source_target_pairs={{0,3},{1,2},{2,1},{3,0},{4,7},{5,6},{6,5},{7,4},{8,11},{9,10},{10,... | collective-permute-start | bytes 258056 | tf_op jit(solution)/shard_map/ppermute | solution.py:561
  5.8 0.6 %collective-permute-start.1 = (bf16[336,128]{1,0:T(8,128)(2,1)}, bf16[336,128]{1,0:T(8,128)(2,1)S(1)}, u32[]{:S(2)}, u32[]{:S(2)}) collective-permute-start(bf16[336,128]{1,0:T(8,128)(2,1)} %get-tuple-element.32), channel_id=1, source_target_pairs={{0,2},{1,3},{2,0},{3,1},{4,6},{5,7},{6,4},{7,5},{8,10},{9,11},{10,... | collective-permute-start | bytes 258056 | tf_op jit(solution)/shard_map/ppermute | solution.py:561
  6.5 0.0 collective-permute-start.2
  6.5 0.0 copy-done.1
  6.5 0.0 copy-done.2
  6.5 0.0 copy-done.3
  6.5 0.0 copy-done.4
  6.5 0.0 copy-start
  6.5 0.0 copy-start.5
  6.6 0.2 shard_map.130
  6.8 2.3 %collective-permute-done.refs_0_.refs_7_.refs_3_ = bf16[336,128]{1,0:T(8,128)(2,1)S(1)} collective-permute-done((bf16[336,128]{1,0:T(8,128)(2,1)}, bf16[336,128]{1,0:T(8,128)(2,1)S(1)}, u32[]{:S(2)}, u32[]{:S(2)}) %collective-permute-start) | collective-permute-done | bytes 86048 | tf_op jit(solution)/shard_map/ppermute | solution.py:561
  9.1 2.1 %collective-permute-done.1.refs_1_.refs_6_.refs_2_ = bf16[336,128]{1,0:T(8,128)(2,1)S(1)} collective-permute-done((bf16[336,128]{1,0:T(8,128)(2,1)}, bf16[336,128]{1,0:T(8,128)(2,1)S(1)}, u32[]{:S(2)}, u32[]{:S(2)}) %collective-permute-start.1) | collective-permute-done | bytes 86048 | tf_op jit(solution)/shard_map/ppermute | solution.py:561
  11.2 0.0 collective-permute-done.2.refs_2_.refs_5_.refs_1_
  11.2 0.0 copy-done
  11.2 0.0 copy-done.5
  11.2 0.6 %shard_map.132 = (bf16[112,128]{1,0:T(8,128)(2,1)S(1)}, f32[2,128,128]{2,1,0:T(8,128)S(1)}, f32[2,128,128]{2,1,0:T(8,128)S(1)}) custom-call(f32[128,128]{1,0:T(8,128)S(1)} %get-tuple-element.28.mass, f32[128,128]{1,0:T(8,128)S(1)} %get-tuple-element.29.drag, f32[256,128]{1,0:T(8,128)S(1)} %bitcast.31, bf16[80,128]{1,0:T(8,128)(2,1)S(1)} %get-tuple-element.30.early, ...), custom_call_target="tpu_custom_call" | custom-call | flops 11500000 | bytes 626688 | tf_op jit(solution)/shard_map/pallas_call | solution.py:42
  11.8 4.3 %collective-permute-start.3 = (bf16[112,128]{1,0:T(8,128)(2,1)S(1)}, bf16[112,128]{1,0:T(8,128)(2,1)S(1)}, u32[]{:S(2)}, u32[]{:S(2)}) collective-permute-start(bf16[112,128]{1,0:T(8,128)(2,1)S(1)} %get-tuple-element.35.refs_3_.refs_0_), channel_id=1, source_target_pairs={{0,12},{4,8},{8,4},{12,0},{1,13},{5,9},{9,5},{13,1},{2,14},{6,10},... | collective-permute-start | bytes 86024 | tf_op jit(solution)/shard_map/ppermute | solution.py:555
  16.0 0.0 collective-permute-start.4
  16.0 0.6 %collective-permute-start.5 = (bf16[112,128]{1,0:T(8,128)(2,1)S(1)}, bf16[112,128]{1,0:T(8,128)(2,1)S(1)}, u32[]{:S(2)}, u32[]{:S(2)}) collective-permute-start(bf16[112,128]{1,0:T(8,128)(2,1)S(1)} %get-tuple-element.35.refs_3_.refs_0_), channel_id=1, source_target_pairs={{0,4},{4,0},{8,12},{12,8},{1,5},{5,1},{9,13},{13,9},{2,6},{6,2},{1... | collective-permute-start | bytes 86024 | tf_op jit(solution)/shard_map/ppermute | solution.py:555
  16.7 1.2 %collective-permute-done.3.refs_0_.refs_3_ = bf16[112,128]{1,0:T(8,128)(2,1)S(1)} collective-permute-done((bf16[112,128]{1,0:T(8,128)(2,1)S(1)}, bf16[112,128]{1,0:T(8,128)(2,1)S(1)}, u32[]{:S(2)}, u32[]{:S(2)}) %collective-permute-start.3) | collective-permute-done | bytes 28704 | tf_op jit(solution)/shard_map/ppermute | solution.py:555
  17.9 2.9 %collective-permute-done.4.refs_1_.refs_2_ = bf16[112,128]{1,0:T(8,128)(2,1)S(1)} collective-permute-done((bf16[112,128]{1,0:T(8,128)(2,1)S(1)}, bf16[112,128]{1,0:T(8,128)(2,1)S(1)}, u32[]{:S(2)}, u32[]{:S(2)}) %collective-permute-start.4) | collective-permute-done | bytes 28704 | tf_op jit(solution)/shard_map/ppermute | solution.py:555
  20.8 0.0 collective-permute-done.5.refs_2_.refs_1_
  20.8 0.0 copy-start.7
  20.8 0.2 collective-permute-start.8
  21.0 1.5 %collective-permute-start.7 = (bf16[384,128]{1,0:T(8,128)(2,1)S(1)}, bf16[384,128]{1,0:T(8,128)(2,1)S(1)}, u32[]{:S(2)}, u32[]{:S(2)}) collective-permute-start(bf16[384,128]{1,0:T(8,128)(2,1)S(1)} %shard_map.133.refs_0_), channel_id=1, source_target_pairs={{0,2},{1,3},{2,0},{3,1},{4,6},{5,7},{6,4},{7,5},{8,10},{9,11},{10,... | collective-permute-start | bytes 294920 | tf_op jit(solution)/shard_map/ppermute | solution.py:555
  22.5 0.3 collective-permute-start.6
  22.8 0.0 copy-done.7
  22.8 1.1 %shard_map.134 = (f32[4,64,128]{2,1,0:T(8,128)S(1)}, bf16[64,128]{1,0:T(8,128)(2,1)S(1)}) custom-call(f32[4,64,128]{2,1,0:T(8,128)S(1)} %copy-done.1, f32[64,128]{1,0:T(8,128)S(1)} %copy-done.7, bf16[112,128]{1,0:T(8,128)(2,1)S(1)} %get-tuple-element.35.refs_3_.refs_0_, bf16[112,128]{1,0:T(8,128)(2,1)S(1)} %collective-permute-done.5.refs_2_.refs_1_, ...), custom_call_target="tpu_custom_call" | custom-call | flops 11500000 | bytes 622592 | tf_op jit(solution)/shard_map/pallas_call | solution.py:42
  23.9 0.3 collective-permute-start.9
  24.2 1.4 %collective-permute-start.10 = (bf16[64,128]{1,0:T(8,128)(2,1)S(1)}, bf16[64,128]{1,0:T(8,128)(2,1)S(1)}, u32[]{:S(2)}, u32[]{:S(2)}) collective-permute-start(bf16[64,128]{1,0:T(8,128)(2,1)S(1)} %get-tuple-element.42.refs_4_), channel_id=1, source_target_pairs={{0,2},{1,3},{2,0},{3,1},{4,6},{5,7},{6,4},{7,5},{8,10},{9,11},{10,... | collective-permute-start | bytes 49160 | tf_op jit(solution)/shard_map/ppermute | solution.py:555
  25.5 0.4 %collective-permute-done.8.refs_3_ = bf16[384,128]{1,0:T(8,128)(2,1)S(1)} collective-permute-done((bf16[384,128]{1,0:T(8,128)(2,1)S(1)}, bf16[384,128]{1,0:T(8,128)(2,1)S(1)}, u32[]{:S(2)}, u32[]{:S(2)}) %collective-permute-start.8) | collective-permute-done | bytes 98336 | tf_op jit(solution)/shard_map/ppermute | solution.py:555
  25.9 0.0 collective-permute-start.11
  25.9 2.2 %collective-permute-done.7.refs_2_ = bf16[384,128]{1,0:T(8,128)(2,1)S(1)} collective-permute-done((bf16[384,128]{1,0:T(8,128)(2,1)S(1)}, bf16[384,128]{1,0:T(8,128)(2,1)S(1)}, u32[]{:S(2)}, u32[]{:S(2)}) %collective-permute-start.7) | collective-permute-done | bytes 98336 | tf_op jit(solution)/shard_map/ppermute | solution.py:555
  28.1 0.0 collective-permute-done.6.refs_1_
  28.2 0.1 xor_select_fusion.table
  28.3 2.1 %shard_map.135.speed = f32[2,128,128]{2,1,0:T(8,128)S(1)} custom-call(s32[16,4]{1,0:T(8,128)S(1)} %xor_select_fusion.table, f32[128,128]{1,0:T(8,128)S(1)} %get-tuple-element.38.viscous, f32[128,128]{1,0:T(8,128)S(1)} %get-tuple-element.39.gain, f32[2,128,128]{2,1,0:T(8,128)S(1)} %get-tuple-element.40.speed, f32[2,128,128]{2,1,0:T(8,128)S(1)} %get-tuple-element.43.push, ...), custom_call_target="tpu_custom_call" | custom-call | flops 11500000 | bytes 786688 | tf_op jit(solution)/shard_map/pallas_call | solution.py:42
  30.4 0.0 collective-permute-done.9.refs_5_
  30.4 0.0 collective-permute-done.10.refs_6_
  30.4 0.0 collective-permute-done.11.refs_7_
  30.4 0.0 copy-start.6
  30.4 1.1 %shard_map.136 = (bf16[192,128]{1,0:T(8,128)(2,1)S(1)}, bf16[192,128]{1,0:T(8,128)(2,1)S(1)}, bf16[192,128]{1,0:T(8,128)(2,1)S(1)}, bf16[192,128]{1,0:T(8,128)(2,1)S(1)}) custom-call(f32[128,128]{1,0:T(8,128)S(1)} %get-tuple-element.29.drag, f32[128,128]{1,0:T(8,128)S(1)} %get-tuple-element.44.conduct, f32[2,128,128]{2,1,0:T(8,128)S(1)} %get-tuple-element.45.current, ...), custom_call_target="tpu_custom_call" | custom-call | flops 11500000 | bytes 802816 | tf_op jit(solution)/shard_map/pallas_call | solution.py:42
  31.6 0.1 collective-permute-start.12
  31.6 1.6 %collective-permute-start.13 = (bf16[192,128]{1,0:T(8,128)(2,1)S(1)}, bf16[192,128]{1,0:T(8,128)(2,1)S(1)}, u32[]{:S(2)}, u32[]{:S(2)}) collective-permute-start(bf16[192,128]{1,0:T(8,128)(2,1)S(1)} %get-tuple-element.47), channel_id=1, source_target_pairs={{0,2},{1,3},{2,0},{3,1},{4,6},{5,7},{6,4},{7,5},{8,10},{9,11},{10,... | collective-permute-start | bytes 147464 | tf_op jit(solution)/shard_map/ppermute | solution.py:561
  33.2 0.2 collective-permute-start.14
  33.4 2.0 %collective-permute-done.12.refs_0_ = bf16[192,128]{1,0:T(8,128)(2,1)S(1)} collective-permute-done((bf16[192,128]{1,0:T(8,128)(2,1)S(1)}, bf16[192,128]{1,0:T(8,128)(2,1)S(1)}, u32[]{:S(2)}, u32[]{:S(2)}) %collective-permute-start.12) | collective-permute-done | bytes 49184 | tf_op jit(solution)/shard_map/ppermute | solution.py:561
  35.4 1.3 %collective-permute-done.13.refs_1_ = bf16[192,128]{1,0:T(8,128)(2,1)S(1)} collective-permute-done((bf16[192,128]{1,0:T(8,128)(2,1)S(1)}, bf16[192,128]{1,0:T(8,128)(2,1)S(1)}, u32[]{:S(2)}, u32[]{:S(2)}) %collective-permute-start.13) | collective-permute-done | bytes 49184 | tf_op jit(solution)/shard_map/ppermute | solution.py:561
  36.7 0.0 collective-permute-done.14.refs_2_
  36.7 0.0 copy-done.6
  36.7 0.8 %shard_map.137 = (f32[256,128]{1,0:T(8,128)}, f32[4,64,128]{2,1,0:T(8,128)}, f32[2,64,128]{2,1,0:T(8,128)}) custom-call(f32[4,64,128]{2,1,0:T(8,128)S(1)} %get-tuple-element.37.warm, f32[2,64,128]{2,1,0:T(8,128)S(1)} %copy-done.6, f32[2,128,128]{2,1,0:T(8,128)S(1)} %shard_map.135.speed, bf16[192,128]{1,0:T(8,128)(2,1)S(1)} %collective-permute-done.12.refs_0_, ...), custom_call_target="tpu_custom_call" | custom-call | flops 11500000 | bytes 524288 | tf_op jit(solution)/shard_map/pallas_call | solution.py:42
  (7 shorter events, 0.1 us)
Async XLA Ops:
  0.6 5.9 %copy-start.1 = (f32[4,64,128]{2,1,0:T(8,128)S(1)}, f32[4,64,128]{2,1,0:T(8,128)}, u32[]{:S(2)}) copy-start(f32[4,64,128]{2,1,0:T(8,128)} %water.3) | copy-start | bytes 393220
  0.6 5.9 %copy-start.2 = (f32[1,1,5,16384]{3,1,2,0:T(1,128)S(1)}, f32[1,1,5,16384]{3,1,2,0:T(1,128)}, u32[]{:S(2)}) copy-start(f32[1,1,5,16384]{3,1,2,0:T(1,128)} %param.18) | copy-start | bytes 983044
  0.7 5.9 %copy-start.3 = (f32[1,1,5,16384]{3,1,2,0:T(1,128)S(1)}, f32[1,1,5,16384]{3,1,2,0:T(1,128)}, u32[]{:S(2)}) copy-start(f32[1,1,5,16384]{3,1,2,0:T(1,128)} %param.19) | copy-start | bytes 983044
  0.7 5.9 %copy-start.4 = (f32[1,1,2,16384]{3,2,1,0:T(2,128)S(1)}, f32[1,1,2,16384]{3,2,1,0:T(2,128)}, u32[]{:S(2)}) copy-start(f32[1,1,2,16384]{3,2,1,0:T(2,128)} %param.20) | copy-start | bytes 393220
  3.4 5.7 %collective-permute-start = (bf16[336,128]{1,0:T(8,128)(2,1)}, bf16[336,128]{1,0:T(8,128)(2,1)S(1)}, u32[]{:S(2)}, u32[]{:S(2)}) collective-permute-start(bf16[336,128]{1,0:T(8,128)(2,1)} %get-tuple-element.31), channel_id=1, source_target_pairs={{0,3},{1,2},{2,1},{3,0},{4,7},{5,6},{6,5},{7,4},{8,11},{9,10},{10,... | collective-permute-start | bytes 258056 | tf_op jit(solution)/shard_map/ppermute | solution.py:561
  5.8 5.3 %collective-permute-start.1 = (bf16[336,128]{1,0:T(8,128)(2,1)}, bf16[336,128]{1,0:T(8,128)(2,1)S(1)}, u32[]{:S(2)}, u32[]{:S(2)}) collective-permute-start(bf16[336,128]{1,0:T(8,128)(2,1)} %get-tuple-element.32), channel_id=1, source_target_pairs={{0,2},{1,3},{2,0},{3,1},{4,6},{5,7},{6,4},{7,5},{8,10},{9,11},{10,... | collective-permute-start | bytes 258056 | tf_op jit(solution)/shard_map/ppermute | solution.py:561
  6.5 4.7 %collective-permute-start.2 = (bf16[336,128]{1,0:T(8,128)(2,1)}, bf16[336,128]{1,0:T(8,128)(2,1)S(1)}, u32[]{:S(2)}, u32[]{:S(2)}) collective-permute-start(bf16[336,128]{1,0:T(8,128)(2,1)} %get-tuple-element.33), channel_id=1, source_target_pairs={{0,1},{1,0},{2,3},{3,2},{4,5},{5,4},{6,7},{7,6},{8,9},{9,8},{10,11... | collective-permute-start | bytes 258056 | tf_op jit(solution)/shard_map/ppermute | solution.py:561
  6.5 4.6 %copy-start = (bf16[336,128]{1,0:T(8,128)(2,1)S(1)}, bf16[336,128]{1,0:T(8,128)(2,1)}, u32[]{:S(2)}) copy-start(bf16[336,128]{1,0:T(8,128)(2,1)} %get-tuple-element.34.refs_3_.refs_4_.refs_0_) | copy-start | bytes 258052
  6.5 4.6 %copy-start.5 = (f32[1,1,2,16384]{3,2,1,0:T(2,128)S(1)}, f32[1,1,2,16384]{3,2,1,0:T(2,128)}, u32[]{:S(2)}) copy-start(f32[1,1,2,16384]{3,2,1,0:T(2,128)} %param.21) | copy-start | bytes 393220
  11.8 6.1 %collective-permute-start.3 = (bf16[112,128]{1,0:T(8,128)(2,1)S(1)}, bf16[112,128]{1,0:T(8,128)(2,1)S(1)}, u32[]{:S(2)}, u32[]{:S(2)}) collective-permute-start(bf16[112,128]{1,0:T(8,128)(2,1)S(1)} %get-tuple-element.35.refs_3_.refs_0_), channel_id=1, source_target_pairs={{0,12},{4,8},{8,4},{12,0},{1,13},{5,9},{9,5},{13,1},{2,14},{6,10},... | collective-permute-start | bytes 86024 | tf_op jit(solution)/shard_map/ppermute | solution.py:555
  16.0 4.8 %collective-permute-start.4 = (bf16[112,128]{1,0:T(8,128)(2,1)S(1)}, bf16[112,128]{1,0:T(8,128)(2,1)S(1)}, u32[]{:S(2)}, u32[]{:S(2)}) collective-permute-start(bf16[112,128]{1,0:T(8,128)(2,1)S(1)} %get-tuple-element.35.refs_3_.refs_0_), channel_id=1, source_target_pairs={{0,8},{4,12},{8,0},{12,4},{1,9},{5,13},{9,1},{13,5},{2,10},{6,14},... | collective-permute-start | bytes 86024 | tf_op jit(solution)/shard_map/ppermute | solution.py:555
  16.0 4.8 %collective-permute-start.5 = (bf16[112,128]{1,0:T(8,128)(2,1)S(1)}, bf16[112,128]{1,0:T(8,128)(2,1)S(1)}, u32[]{:S(2)}, u32[]{:S(2)}) collective-permute-start(bf16[112,128]{1,0:T(8,128)(2,1)S(1)} %get-tuple-element.35.refs_3_.refs_0_), channel_id=1, source_target_pairs={{0,4},{4,0},{8,12},{12,8},{1,5},{5,1},{9,13},{13,9},{2,6},{6,2},{1... | collective-permute-start | bytes 86024 | tf_op jit(solution)/shard_map/ppermute | solution.py:555
  20.8 1.9 %copy-start.7 = (f32[64,128]{1,0:T(8,128)S(1)}, f32[64,128]{1,0:T(8,128)}, u32[]{:S(2)}) copy-start(f32[64,128]{1,0:T(8,128)} %mixing) | copy-start | bytes 98308
  20.8 5.1 %collective-permute-start.8 = (bf16[384,128]{1,0:T(8,128)(2,1)S(1)}, bf16[384,128]{1,0:T(8,128)(2,1)S(1)}, u32[]{:S(2)}, u32[]{:S(2)}) collective-permute-start(bf16[384,128]{1,0:T(8,128)(2,1)S(1)} %shard_map.133.refs_0_), channel_id=1, source_target_pairs={{0,3},{1,2},{2,1},{3,0},{4,7},{5,6},{6,5},{7,4},{8,11},{9,10},{10,... | collective-permute-start | bytes 294920 | tf_op jit(solution)/shard_map/ppermute | solution.py:555
  21.0 7.2 %collective-permute-start.7 = (bf16[384,128]{1,0:T(8,128)(2,1)S(1)}, bf16[384,128]{1,0:T(8,128)(2,1)S(1)}, u32[]{:S(2)}, u32[]{:S(2)}) collective-permute-start(bf16[384,128]{1,0:T(8,128)(2,1)S(1)} %shard_map.133.refs_0_), channel_id=1, source_target_pairs={{0,2},{1,3},{2,0},{3,1},{4,6},{5,7},{6,4},{7,5},{8,10},{9,11},{10,... | collective-permute-start | bytes 294920 | tf_op jit(solution)/shard_map/ppermute | solution.py:555
  22.5 5.7 %collective-permute-start.6 = (bf16[384,128]{1,0:T(8,128)(2,1)S(1)}, bf16[384,128]{1,0:T(8,128)(2,1)S(1)}, u32[]{:S(2)}, u32[]{:S(2)}) collective-permute-start(bf16[384,128]{1,0:T(8,128)(2,1)S(1)} %shard_map.133.refs_0_), channel_id=1, source_target_pairs={{0,1},{1,0},{2,3},{3,2},{4,5},{5,4},{6,7},{7,6},{8,9},{9,8},{10,11... | collective-permute-start | bytes 294920 | tf_op jit(solution)/shard_map/ppermute | solution.py:555
  23.9 6.5 %collective-permute-start.9 = (bf16[64,128]{1,0:T(8,128)(2,1)S(1)}, bf16[64,128]{1,0:T(8,128)(2,1)S(1)}, u32[]{:S(2)}, u32[]{:S(2)}) collective-permute-start(bf16[64,128]{1,0:T(8,128)(2,1)S(1)} %get-tuple-element.42.refs_4_), channel_id=1, source_target_pairs={{0,1},{1,0},{2,3},{3,2},{4,5},{5,4},{6,7},{7,6},{8,9},{9,8},{10,11... | collective-permute-start | bytes 49160 | tf_op jit(solution)/shard_map/ppermute | solution.py:555
  24.2 6.2 %collective-permute-start.10 = (bf16[64,128]{1,0:T(8,128)(2,1)S(1)}, bf16[64,128]{1,0:T(8,128)(2,1)S(1)}, u32[]{:S(2)}, u32[]{:S(2)}) collective-permute-start(bf16[64,128]{1,0:T(8,128)(2,1)S(1)} %get-tuple-element.42.refs_4_), channel_id=1, source_target_pairs={{0,2},{1,3},{2,0},{3,1},{4,6},{5,7},{6,4},{7,5},{8,10},{9,11},{10,... | collective-permute-start | bytes 49160 | tf_op jit(solution)/shard_map/ppermute | solution.py:555
  25.9 4.5 %collective-permute-start.11 = (bf16[64,128]{1,0:T(8,128)(2,1)S(1)}, bf16[64,128]{1,0:T(8,128)(2,1)S(1)}, u32[]{:S(2)}, u32[]{:S(2)}) collective-permute-start(bf16[64,128]{1,0:T(8,128)(2,1)S(1)} %get-tuple-element.42.refs_4_), channel_id=1, source_target_pairs={{0,3},{1,2},{2,1},{3,0},{4,7},{5,6},{6,5},{7,4},{8,11},{9,10},{10,... | collective-permute-start | bytes 49160 | tf_op jit(solution)/shard_map/ppermute | solution.py:555
  30.4 6.2 %copy-start.6 = (f32[2,64,128]{2,1,0:T(8,128)S(1)}, f32[2,64,128]{2,1,0:T(8,128)}, u32[]{:S(2)}) copy-start(f32[2,64,128]{2,1,0:T(8,128)} %currents.1) | copy-start | bytes 196612
  31.6 3.8 %collective-permute-start.12 = (bf16[192,128]{1,0:T(8,128)(2,1)S(1)}, bf16[192,128]{1,0:T(8,128)(2,1)S(1)}, u32[]{:S(2)}, u32[]{:S(2)}) collective-permute-start(bf16[192,128]{1,0:T(8,128)(2,1)S(1)} %get-tuple-element.46), channel_id=1, source_target_pairs={{0,3},{1,2},{2,1},{3,0},{4,7},{5,6},{6,5},{7,4},{8,11},{9,10},{10,... | collective-permute-start | bytes 147464 | tf_op jit(solution)/shard_map/ppermute | solution.py:561
  31.6 5.0 %collective-permute-start.13 = (bf16[192,128]{1,0:T(8,128)(2,1)S(1)}, bf16[192,128]{1,0:T(8,128)(2,1)S(1)}, u32[]{:S(2)}, u32[]{:S(2)}) collective-permute-start(bf16[192,128]{1,0:T(8,128)(2,1)S(1)} %get-tuple-element.47), channel_id=1, source_target_pairs={{0,2},{1,3},{2,0},{3,1},{4,6},{5,7},{6,4},{7,5},{8,10},{9,11},{10,... | collective-permute-start | bytes 147464 | tf_op jit(solution)/shard_map/ppermute | solution.py:561
  33.2 3.4 %collective-permute-start.14 = (bf16[192,128]{1,0:T(8,128)(2,1)S(1)}, bf16[192,128]{1,0:T(8,128)(2,1)S(1)}, u32[]{:S(2)}, u32[]{:S(2)}) collective-permute-start(bf16[192,128]{1,0:T(8,128)(2,1)S(1)} %get-tuple-element.48), channel_id=1, source_target_pairs={{0,1},{1,0},{2,3},{3,2},{4,5},{5,4},{6,7},{7,6},{8,9},{9,8},{10,11... | collective-permute-start | bytes 147464 | tf_op jit(solution)/shard_map/ppermute | solution.py:561

commit v9 on v8

--- a/solution.py
+++ b/solution.py
@@ -102,10 +102,32 @@
     ]
     for load in loads:
         load.start()
-    for load in loads:
-        load.wait()
+    for i in (1, 3, 4):
+        loads[i].wait()
     me = place()
+    side, depth, pairs = rows.shape[1], cols.shape[1], rows.shape[0]
     owners = [lax.rem(lax.rem(blocks[0, m], devices), members) for m in range(pairs)]
+    copies, keeps = [], []
+    for k, out in enumerate(outs):
+        partner = me ^ k
+        pair, found = jnp.int32(0), jnp.int32(0)
+        for m in range(pairs):
+            pair = jnp.where(owners[m] == partner, m, pair)
+            found = jnp.where(owners[m] == partner, 1, found)
+        keeps.append(flag(found > 0))
+        at = 0
+        for i, source in enumerate((rows, cols)):
+            target = out.at[pl.ds(at, source.shape[1])]
+            copies.append(pltpu.make_async_copy(source.at[pair], target, left.at[4 * k + i]))
+            copies[-1].start()
+            at += source.shape[1]
+    for i in (0, 2, 5):
+        loads[i].wait()
+    plain = pairs == members
+    for k in range(1 if plain else members):
+        for c in range(2):
+            field = currents[c] if plain else currents[c] * keeps[k]
+            fields[k, c * side : (c + 1) * side] = field.astype(BF16)
     lane = iota((1, width), 1)
     numbers = jnp.zeros((1, width), F32)
     for q in range(4):
@@ -114,42 +136,13 @@
     ends = ocean_columns(water) + [numbers]
     blank = jnp.zeros((tail.shape[0] - len(ends), width), F32)
     tail[...] = jnp.concatenate(ends + [blank], axis=0).astype(BF16)
-    copies = []
     for k, out in enumerate(outs):
-        partner = me ^ k
-        pair, found = jnp.int32(0), jnp.int32(0)
-        for m in range(pairs):
-            pair = jnp.where(owners[m] == partner, m, pair)
-            found = jnp.where(owners[m] == partner, 1, found)
-        copies.append(
-            pltpu.make_async_copy(rows.at[pair], out.at[pl.ds(0, side)], left.at[3 * k])
-        )
-        copies.append(
-            pltpu.make_async_copy(cols.at[pair], out.at[pl.ds(side, depth)], left.at[3 * k + 1])
-        )
-        if pairs < members:
-            keep = jnp.where(found > 0, 1.0, 0.0).astype(F32)
-        else:
-            keep = None
-        copies.append(
-            pltpu.make_async_copy(
-                tail, out.at[pl.ds(3 * side + depth, tail.shape[0])], left.at[3 * members + k]
-            )
-        )
-        for copy in copies[-3:]:
-            copy.start()
-        if k == 0 or keep is not None:
-            for c in range(2):
-                field = currents[c] if keep is None else currents[c] * keep
-                fields[0 if keep is None else k, c * side : (c + 1) * side] = field.astype(BF16)
-        copies.append(
-            pltpu.make_async_copy(
-                fields.at[0 if keep is None else k],
-                out.at[pl.ds(side + depth, 2 * side)],
-                left.at[3 * k + 2],
-            )
-        )
-        copies[-1].start()
+        at = side + depth
+        for i, source in enumerate((fields.at[0 if plain else k], tail)):
+            target = out.at[pl.ds(at, source.shape[0])]
+            copies.append(pltpu.make_async_copy(source, target, left.at[4 * k + 2 + i]))
+            copies[-1].start()
+            at += source.shape[0]
     for copy in copies:
         copy.wait()
 
@@ -349,7 +342,9 @@
 
 
 def subcycles_kernel(tiles, members, table, viscous, gain, speed, push, *refs):
-    relays, (out, rims) = refs[:members], refs[members:]
+    relays, (out, rims, names, named) = refs[:members], refs[members:]
+    load_names = pltpu.make_async_copy(table, names, named)
+    load_names.start()
     size = viscous.shape[0]
     for k in range(tiles):
         for m in range(members):
@@ -377,7 +372,7 @@
         return [velocity, visc, scale, pushed]
 
     def follow(device, side):
-        name = table[device, side]
+        name = names[device, side]
         return jnp.where(name >= 0, name, 0), name >= 0
 
     def step(state, left, right, inner, outer):
@@ -385,6 +380,35 @@
         spread = left + right + inner + outer - 4.0 * c
         return scale * (c + visc * spread + pushed + turn * roll(c, half, 0))
 
+    row = iota((size, size), 0)
+    col = iota((size, size), 1)
+    vx, vy = speed[0], speed[1]
+    visc, scale, push_x, push_y = viscous[...], gain[...], push[0], push[1]
+
+    def interior(v):
+        up = jnp.where(row == size - 1, 0.0, roll(v, -1, 0))
+        down = jnp.where(row == 0, 0.0, roll(v, 1, 0))
+        right = jnp.where(col == size - 1, 0.0, roll(v, -1, 1))
+        left = jnp.where(col == 0, 0.0, roll(v, 1, 1))
+        return up + down + right + left - 4.0 * v
+
+    def rim_of(north, south, east, west):
+        up = jnp.where(row == size - 1, north, jnp.where(row == 0, south, 0.0))
+        return up + jnp.where(col == size - 1, east, jnp.where(col == 0, west, 0.0))
+
+    def own_edges(vx, vy):
+        mixed = jnp.where(col < half, roll(vx, 1, 1), roll(vy, 1 + half, 1))
+        across = mixed.T[0:high]
+        return [
+            jnp.where(sub < half, vx[size - 1 :], vy[size - 1 :]),
+            jnp.where(sub < half, vx[0:1], vy[0:1]),
+            across,
+            roll(across, -1, 0),
+        ]
+
+    own = own_edges(vx, vy)
+    inner_x, inner_y = interior(vx), interior(vy)
+    load_names.wait()
     strips = []
     for q in range(4):
         x, has_x = follow(0, q)
@@ -403,29 +427,11 @@
             )
         strips.append((strip, sides))
 
-    row = iota((size, size), 0)
-    col = iota((size, size), 1)
-    vx, vy = speed[0], speed[1]
-    visc, scale, push_x, push_y = viscous[...], gain[...], push[0], push[1]
-
-    def spread_of(v, north, south, east, west):
-        up = jnp.where(row == size - 1, north, roll(v, -1, 0))
-        down = jnp.where(row == 0, south, roll(v, 1, 0))
-        right = jnp.where(col == size - 1, east, roll(v, -1, 1))
-        left = jnp.where(col == 0, west, roll(v, 1, 1))
-        return up + down + right + left - 4.0 * v
-
     for t in range(SUBCYCLES):
         cells = [strip[0] for strip, _ in strips]
         if t < SUBCYCLES - 1:
-            mixed = jnp.where(col < half, roll(vx, 1, 1), roll(vy, 1 + half, 1))
-            across = mixed.T[0:high]
-            own = [
-                jnp.where(sub < half, vx[size - 1 :], vy[size - 1 :]),
-                jnp.where(sub < half, vx[0:1], vy[0:1]),
-                across,
-                roll(across, -1, 0),
-            ]
+            if t > 0:
+                own = own_edges(vx, vy)
             for q in range(4):
                 strip, (beyond, before) = strips[q]
                 c, y_hi, y_lo = strip[0], beyond[0][0], before[0][0]
@@ -456,9 +462,11 @@
         sides = jnp.where(edge, cells[2], roll(cells[3], 1, 0)).T
         east_x, west_x = sides[:, 0:1], sides[:, 1:2]
         east_y, west_y = sides[:, half : half + 1], sides[:, half + 1 : half + 2]
-        spread_x = spread_of(vx, north[0:1], south[0:1], east_x, west_x)
-        spread_y = spread_of(
-            vy, north[half : half + 1], south[half : half + 1], east_y, west_y
+        if t > 0:
+            inner_x, inner_y = interior(vx), interior(vy)
+        spread_x = inner_x + rim_of(north[0:1], south[0:1], east_x, west_x)
+        spread_y = inner_y + rim_of(
+            north[half : half + 1], south[half : half + 1], east_y, west_y
         )
         new_x = scale * (vx + visc * spread_x + push_x + CORIOLIS_TURN * vy)
         new_y = scale * (vy + visc * spread_y + push_y - CORIOLIS_TURN * vx)
@@ -554,6 +562,17 @@
         for k in far_first(count):
             got[k] = lax.ppermute(value, axes, [(i, i ^ k) for i in range(count)])
         return [got[k] for k in range(count)]
+
+    def swap_chips(value):
+        return {0: value} | {
+            k: lax.ppermute(value, group_axes, [(i, i ^ k) for i in range(group)])
+            for k in range(2, group, 2)
+        }
+
+    def swap_cores(got):
+        beside = [(i, i ^ 1) for i in range(group)]
+        got = got | {k + 1: lax.ppermute(got[k], group_axes, beside) for k in got}
+        return [got[k] for k in range(group)]
 
     def swap_each(values):
         got = {0: values[0]}
@@ -626,7 +645,7 @@
         shape(tile_count * BLOCK_ROWS, size, dtype=BF16),
         messages[::-1],
     )
-    relays = swap(relay, group_axes, group)
+    relays = swap_chips(relay)
 
     mixing, _ = lax.optimization_barrier((diffusion_coefficient, relay))
     warm, top = call(
@@ -639,6 +658,10 @@
     if lev_count > 1:
         top = lax.psum(top, "lev").astype(BF16)
     tops = swap(top, group_axes, group)
+
+    far = sorted(k for k in relays if k)
+    relayed, _ = lax.optimization_barrier(([relays[k] for k in far], tops[1]))
+    relays = swap_cores({0: relay} | dict(zip(far, relayed)))
 
     names = jnp.stack(
         [r.reshape(tile_count, BLOCK_ROWS, size)[:, NAMES_ROW, 0:8] for r in relays],
@@ -652,8 +675,12 @@
         functools.partial(subcycles_kernel, tile_count, group),
         planes,
         (table, viscous, gain, speed, push, *relays),
-        scratch=[pltpu.VMEM((devices, BLOCK_ROWS, size), BF16)],
-        smem=(0,),
+        scratch=[
+            pltpu.VMEM((devices, BLOCK_ROWS, size), BF16),
+            pltpu.SMEM((devices, 4), jnp.int32),
+            pltpu.SemaphoreType.DMA,
+        ],
+        hbm=(0,),
     )
 
     replies = call(

time: 37.6 us -> 37.2 us (0.989)
  waiting for transfers between devices: 14.3 us -> 13.7 us
  starting transfers between devices: 13.5 us -> 13.9 us
    ppermute x0 -> x3, starting transfers between devices: none -> 2.06 us  [the longest x1 1.56 us: swap_chips(): lax.ppermute(value, group_axes, [(i, i ^ k) for i in range(group)])]
    ppermute x9 -> x6, starting transfers between devices: 8.49 us -> 6.87 us  [swap(): got[k] = lax.ppermute(value, axes, [(i, i ^ k) for i in range(count)])]
    ppermute x9 -> x6, waiting for transfers between devices: 6.71 us -> 5.34 us  [swap(): got[k] = lax.ppermute(value, axes, [(i, i ^ k) for i in range(count)])]
    ppermute x0 -> x3, waiting for transfers between devices: none -> 0.73 us  [the longest x1 0.72 us: swap_chips(): lax.ppermute(value, group_axes, [(i, i ^ k) for i in range(group)])]
  transfers between devices with their start and end apart: 15 -> 15, of which waited for: 8 -> 9; matrix products, arithmetic and copies ran while one was open for 0% -> 0% of each run, Pallas kernels for 9% -> 9%
where the time goes in v9:
time: 37.2 us; the launch traced here: 37.1 us
  starting transfers between devices  13.9 us (37%)
  waiting for transfers between devices  13.7 us (37%)
  Pallas kernels  8.51 us (23%)
  between operations  0.81 us (2%)
    pallas_call x8, Pallas kernels, call(): pl.pallas_call(kernel, out_shape=outs, in_specs=specs, out_specs=jax.tree...  8.51 us
    ppermute x6, waiting for transfers between devices, swap_each(): lax.ppermute(values[k], group_axes, [(i, i ^ k) for i in range(group)])  7.6 us
    ppermute x6, starting transfers between devices, swap(): got[k] = lax.ppermute(value, axes, [(i, i ^ k) for i in range(count)])  6.87 us
    ppermute x6, waiting for transfers between devices, swap(): got[k] = lax.ppermute(value, axes, [(i, i ^ k) for i in range(count)])  5.34 us
    ppermute x6, starting transfers between devices, swap_each(): lax.ppermute(values[k], group_axes, [(i, i ^ k) for i in range(group)])  4.99 us
    ppermute x1, starting transfers between devices, swap_chips(): lax.ppermute(value, group_axes, [(i, i ^ k) for i in range(group)])  1.56 us
  transfers between devices with their start and end apart: 15, of which 9 were waited for; matrix products, arithmetic and copies ran while one was open for 0% of the time, Pallas kernels for 9%

profile of v9, /device:TPU:0, one launch (start us, length us, event | category | flops | bytes accessed | tf_op | source)
XLA Modules:
  0.0 37.1 jit_solution(14829054436393310666)
XLA Ops:
  0.6 0.0 copy-start.1
  0.6 0.0 copy-start.2
  0.7 0.0 copy-start.3
  0.7 0.0 copy-start.4
  0.7 2.6 %shard_map.131 = (bf16[336,128]{1,0:T(8,128)(2,1)}, bf16[336,128]{1,0:T(8,128)(2,1)}, bf16[336,128]{1,0:T(8,128)(2,1)}, bf16[336,128]{1,0:T(8,128)(2,1)}) custom-call(s32[1,1,4]{2,1,0:T(1,128)} %links_h.1, s32[1,4]{1,0:T(1,128)} %blocks_h.1, bf16[4,64,128]{2,1,0:T(8,128)(2,1)} %bitcast.38, bf16[4,128,128]{2,1,0:T(8,128)(2,1)} %bitcast.36, ...), custom_call_target="tpu_custom_call" | custom-call | flops 11500000256 | bytes 393248 | tf_op jit(solution)/shard_map/pallas_call | solution.py:42
  3.3 2.4 %collective-permute-start = (bf16[336,128]{1,0:T(8,128)(2,1)}, bf16[336,128]{1,0:T(8,128)(2,1)S(1)}, u32[]{:S(2)}, u32[]{:S(2)}) collective-permute-start(bf16[336,128]{1,0:T(8,128)(2,1)} %get-tuple-element.32), channel_id=1, source_target_pairs={{0,3},{1,2},{2,1},{3,0},{4,7},{5,6},{6,5},{7,4},{8,11},{9,10},{10,... | collective-permute-start | bytes 258056 | tf_op jit(solution)/shard_map/ppermute | solution.py:580
  5.7 0.6 %collective-permute-start.1 = (bf16[336,128]{1,0:T(8,128)(2,1)}, bf16[336,128]{1,0:T(8,128)(2,1)S(1)}, u32[]{:S(2)}, u32[]{:S(2)}) collective-permute-start(bf16[336,128]{1,0:T(8,128)(2,1)} %get-tuple-element.33), channel_id=1, source_target_pairs={{0,2},{1,3},{2,0},{3,1},{4,6},{5,7},{6,4},{7,5},{8,10},{9,11},{10,... | collective-permute-start | bytes 258056 | tf_op jit(solution)/shard_map/ppermute | solution.py:580
  6.4 0.0 collective-permute-start.2
  6.4 0.0 copy-done.1
  6.4 0.0 copy-done.2
  6.4 0.0 copy-done.3
  6.4 0.0 copy-done.4
  6.4 0.0 copy-start
  6.5 0.0 copy-start.5
  6.5 0.2 shard_map.130
  6.7 2.3 %collective-permute-done.refs_0_.refs_7_.refs_3_ = bf16[336,128]{1,0:T(8,128)(2,1)S(1)} collective-permute-done((bf16[336,128]{1,0:T(8,128)(2,1)}, bf16[336,128]{1,0:T(8,128)(2,1)S(1)}, u32[]{:S(2)}, u32[]{:S(2)}) %collective-permute-start) | collective-permute-done | bytes 86048 | tf_op jit(solution)/shard_map/ppermute | solution.py:580
  9.0 2.1 %collective-permute-done.1.refs_1_.refs_6_.refs_2_ = bf16[336,128]{1,0:T(8,128)(2,1)S(1)} collective-permute-done((bf16[336,128]{1,0:T(8,128)(2,1)}, bf16[336,128]{1,0:T(8,128)(2,1)S(1)}, u32[]{:S(2)}, u32[]{:S(2)}) %collective-permute-start.1) | collective-permute-done | bytes 86048 | tf_op jit(solution)/shard_map/ppermute | solution.py:580
  11.1 0.0 collective-permute-done.2.refs_2_.refs_5_.refs_1_
  11.1 0.0 copy-done
  11.1 0.0 copy-done.5
  11.1 0.6 %shard_map.132 = (bf16[112,128]{1,0:T(8,128)(2,1)S(1)}, f32[2,128,128]{2,1,0:T(8,128)S(1)}, f32[2,128,128]{2,1,0:T(8,128)S(1)}) custom-call(f32[128,128]{1,0:T(8,128)S(1)} %get-tuple-element.29.mass, f32[128,128]{1,0:T(8,128)S(1)} %get-tuple-element.30.drag, f32[256,128]{1,0:T(8,128)S(1)} %bitcast.31, bf16[80,128]{1,0:T(8,128)(2,1)S(1)} %get-tuple-element.31.early, ...), custom_call_target="tpu_custom_call" | custom-call | flops 11500000 | bytes 626688 | tf_op jit(solution)/shard_map/pallas_call | solution.py:42
  11.7 0.0 copy-start.7
  11.7 4.3 %collective-permute-start.3 = (bf16[112,128]{1,0:T(8,128)(2,1)S(1)}, bf16[112,128]{1,0:T(8,128)(2,1)S(1)}, u32[]{:S(2)}, u32[]{:S(2)}) collective-permute-start(bf16[112,128]{1,0:T(8,128)(2,1)S(1)} %get-tuple-element.36.refs_3_.refs_0_), channel_id=1, source_target_pairs={{0,12},{4,8},{8,4},{12,0},{1,13},{5,9},{9,5},{13,1},{2,14},{6,10},... | collective-permute-start | bytes 86024 | tf_op jit(solution)/shard_map/ppermute | solution.py:563
  16.0 0.0 collective-permute-start.4
  16.0 0.6 %collective-permute-start.5 = (bf16[112,128]{1,0:T(8,128)(2,1)S(1)}, bf16[112,128]{1,0:T(8,128)(2,1)S(1)}, u32[]{:S(2)}, u32[]{:S(2)}) collective-permute-start(bf16[112,128]{1,0:T(8,128)(2,1)S(1)} %get-tuple-element.36.refs_3_.refs_0_), channel_id=1, source_target_pairs={{0,4},{4,0},{8,12},{12,8},{1,5},{5,1},{9,13},{13,9},{2,6},{6,2},{1... | collective-permute-start | bytes 86024 | tf_op jit(solution)/shard_map/ppermute | solution.py:563
  16.6 1.2 %collective-permute-done.3.refs_0_.refs_3_ = bf16[112,128]{1,0:T(8,128)(2,1)S(1)} collective-permute-done((bf16[112,128]{1,0:T(8,128)(2,1)S(1)}, bf16[112,128]{1,0:T(8,128)(2,1)S(1)}, u32[]{:S(2)}, u32[]{:S(2)}) %collective-permute-start.3) | collective-permute-done | bytes 28704 | tf_op jit(solution)/shard_map/ppermute | solution.py:563
  17.8 2.9 %collective-permute-done.4.refs_1_.refs_2_ = bf16[112,128]{1,0:T(8,128)(2,1)S(1)} collective-permute-done((bf16[112,128]{1,0:T(8,128)(2,1)S(1)}, bf16[112,128]{1,0:T(8,128)(2,1)S(1)}, u32[]{:S(2)}, u32[]{:S(2)}) %collective-permute-start.4) | collective-permute-done | bytes 28704 | tf_op jit(solution)/shard_map/ppermute | solution.py:563
  20.7 0.0 collective-permute-done.5.refs_2_.refs_1_
  20.8 1.6 %collective-permute-start.7 = (bf16[384,128]{1,0:T(8,128)(2,1)S(1)}, bf16[384,128]{1,0:T(8,128)(2,1)S(1)}, u32[]{:S(2)}, u32[]{:S(2)}) collective-permute-start(bf16[384,128]{1,0:T(8,128)(2,1)S(1)} %shard_map.133.refs_0_), channel_id=1, source_target_pairs={{0,2},{1,3},{2,0},{3,1},{4,6},{5,7},{6,4},{7,5},{8,10},{9,11},{10,... | collective-permute-start | bytes 294920 | tf_op jit(solution)/shard_map/ppermute | solution.py:568
  22.3 0.0 copy-done.7
  22.3 1.1 %shard_map.134 = (f32[4,64,128]{2,1,0:T(8,128)S(1)}, bf16[64,128]{1,0:T(8,128)(2,1)S(1)}) custom-call(f32[4,64,128]{2,1,0:T(8,128)S(1)} %copy-done.1, f32[64,128]{1,0:T(8,128)S(1)} %copy-done.7, bf16[112,128]{1,0:T(8,128)(2,1)S(1)} %get-tuple-element.36.refs_3_.refs_0_, bf16[112,128]{1,0:T(8,128)(2,1)S(1)} %collective-permute-done.5.refs_2_.refs_1_, ...), custom_call_target="tpu_custom_call" | custom-call | flops 11500000 | bytes 622592 | tf_op jit(solution)/shard_map/pallas_call | solution.py:42
  23.5 0.1 collective-permute-start.8
  23.5 0.5 %collective-permute-start.6 = (bf16[384,128]{1,0:T(8,128)(2,1)S(1)}, bf16[384,128]{1,0:T(8,128)(2,1)S(1)}, u32[]{:S(2)}, u32[]{:S(2)}) collective-permute-start(bf16[384,128]{1,0:T(8,128)(2,1)S(1)} %shard_map.133.refs_0_), channel_id=1, source_target_pairs={{0,1},{1,0},{2,3},{3,2},{4,5},{5,4},{6,7},{7,6},{8,9},{9,8},{10,11... | collective-permute-start | bytes 294920 | tf_op jit(solution)/shard_map/ppermute | solution.py:574
  24.0 0.7 %collective-permute-done.8.refs_5_ = bf16[64,128]{1,0:T(8,128)(2,1)S(1)} collective-permute-done((bf16[64,128]{1,0:T(8,128)(2,1)S(1)}, bf16[64,128]{1,0:T(8,128)(2,1)S(1)}, u32[]{:S(2)}, u32[]{:S(2)}) %collective-permute-start.8) | collective-permute-done | bytes 16416 | tf_op jit(solution)/shard_map/ppermute | solution.py:563
  24.7 0.7 %collective-permute-done.7.refs_2_ = bf16[384,128]{1,0:T(8,128)(2,1)S(1)} collective-permute-done((bf16[384,128]{1,0:T(8,128)(2,1)S(1)}, bf16[384,128]{1,0:T(8,128)(2,1)S(1)}, u32[]{:S(2)}, u32[]{:S(2)}) %collective-permute-start.7) | collective-permute-done | bytes 98336 | tf_op jit(solution)/shard_map/ppermute | solution.py:568
  25.4 0.0 collective-permute-start.9
  25.4 1.5 %collective-permute-start.10 = (bf16[64,128]{1,0:T(8,128)(2,1)S(1)}, bf16[64,128]{1,0:T(8,128)(2,1)S(1)}, u32[]{:S(2)}, u32[]{:S(2)}) collective-permute-start(bf16[64,128]{1,0:T(8,128)(2,1)S(1)} %get-tuple-element.39.refs_4_), channel_id=1, source_target_pairs={{0,2},{1,3},{2,0},{3,1},{4,6},{5,7},{6,4},{7,5},{8,10},{9,11},{10,... | collective-permute-start | bytes 49160 | tf_op jit(solution)/shard_map/ppermute | solution.py:563
  26.9 0.4 collective-permute-start.11
  27.3 0.0 collective-permute-done.6.refs_1_
  27.3 0.0 collective-permute-done.9.refs_3_
  27.4 0.1 xor_select_fusion.table
  27.5 2.1 %shard_map.135.speed = f32[2,128,128]{2,1,0:T(8,128)S(1)} custom-call(s32[16,4]{1,0:T(8,128)S(1)} %xor_select_fusion.table, f32[128,128]{1,0:T(8,128)S(1)} %get-tuple-element.41.viscous, f32[128,128]{1,0:T(8,128)S(1)} %get-tuple-element.42.gain, f32[2,128,128]{2,1,0:T(8,128)S(1)} %get-tuple-element.43.speed, f32[2,128,128]{2,1,0:T(8,128)S(1)} %get-tuple-element.45.push, ...), custom_call_target="tpu_custom_call" | custom-call | flops 11500000 | bytes 786688 | tf_op jit(solution)/shard_map/pallas_call | solution.py:42
  29.6 0.0 collective-permute-done.10.refs_6_
  29.6 0.5 %collective-permute-done.11.refs_7_ = bf16[64,128]{1,0:T(8,128)(2,1)S(1)} collective-permute-done((bf16[64,128]{1,0:T(8,128)(2,1)S(1)}, bf16[64,128]{1,0:T(8,128)(2,1)S(1)}, u32[]{:S(2)}, u32[]{:S(2)}) %collective-permute-start.11) | collective-permute-done | bytes 16416 | tf_op jit(solution)/shard_map/ppermute | solution.py:563
  30.1 0.0 copy-start.6
  30.1 1.1 %shard_map.136 = (bf16[192,128]{1,0:T(8,128)(2,1)S(1)}, bf16[192,128]{1,0:T(8,128)(2,1)S(1)}, bf16[192,128]{1,0:T(8,128)(2,1)S(1)}, bf16[192,128]{1,0:T(8,128)(2,1)S(1)}) custom-call(f32[128,128]{1,0:T(8,128)S(1)} %get-tuple-element.30.drag, f32[128,128]{1,0:T(8,128)S(1)} %get-tuple-element.46.conduct, f32[2,128,128]{2,1,0:T(8,128)S(1)} %get-tuple-element.47.current, ...), custom_call_target="tpu_custom_call" | custom-call | flops 11500000 | bytes 802816 | tf_op jit(solution)/shard_map/pallas_call | solution.py:42
  31.2 0.9 %collective-permute-start.12 = (bf16[192,128]{1,0:T(8,128)(2,1)S(1)}, bf16[192,128]{1,0:T(8,128)(2,1)S(1)}, u32[]{:S(2)}, u32[]{:S(2)}) collective-permute-start(bf16[192,128]{1,0:T(8,128)(2,1)S(1)} %get-tuple-element.48), channel_id=1, source_target_pairs={{0,3},{1,2},{2,1},{3,0},{4,7},{5,6},{6,5},{7,4},{8,11},{9,10},{10,... | collective-permute-start | bytes 147464 | tf_op jit(solution)/shard_map/ppermute | solution.py:580
  32.1 1.0 %collective-permute-start.13 = (bf16[192,128]{1,0:T(8,128)(2,1)S(1)}, bf16[192,128]{1,0:T(8,128)(2,1)S(1)}, u32[]{:S(2)}, u32[]{:S(2)}) collective-permute-start(bf16[192,128]{1,0:T(8,128)(2,1)S(1)} %get-tuple-element.49), channel_id=1, source_target_pairs={{0,2},{1,3},{2,0},{3,1},{4,6},{5,7},{6,4},{7,5},{8,10},{9,11},{10,... | collective-permute-start | bytes 147464 | tf_op jit(solution)/shard_map/ppermute | solution.py:580
  33.1 0.0 collective-permute-start.14
  33.1 1.9 %collective-permute-done.12.refs_0_ = bf16[192,128]{1,0:T(8,128)(2,1)S(1)} collective-permute-done((bf16[192,128]{1,0:T(8,128)(2,1)S(1)}, bf16[192,128]{1,0:T(8,128)(2,1)S(1)}, u32[]{:S(2)}, u32[]{:S(2)}) %collective-permute-start.12) | collective-permute-done | bytes 49184 | tf_op jit(solution)/shard_map/ppermute | solution.py:580
  34.9 1.4 %collective-permute-done.13.refs_1_ = bf16[192,128]{1,0:T(8,128)(2,1)S(1)} collective-permute-done((bf16[192,128]{1,0:T(8,128)(2,1)S(1)}, bf16[192,128]{1,0:T(8,128)(2,1)S(1)}, u32[]{:S(2)}, u32[]{:S(2)}) %collective-permute-start.13) | collective-permute-done | bytes 49184 | tf_op jit(solution)/shard_map/ppermute | solution.py:580
  36.3 0.0 collective-permute-done.14.refs_2_
  36.3 0.0 copy-done.6
  36.3 0.8 %shard_map.137 = (f32[256,128]{1,0:T(8,128)}, f32[4,64,128]{2,1,0:T(8,128)}, f32[2,64,128]{2,1,0:T(8,128)}) custom-call(f32[4,64,128]{2,1,0:T(8,128)S(1)} %get-tuple-element.38.warm, f32[2,64,128]{2,1,0:T(8,128)S(1)} %copy-done.6, f32[2,128,128]{2,1,0:T(8,128)S(1)} %shard_map.135.speed, bf16[192,128]{1,0:T(8,128)(2,1)S(1)} %collective-permute-done.12.refs_0_, ...), custom_call_target="tpu_custom_call" | custom-call | flops 11500000 | bytes 524288 | tf_op jit(solution)/shard_map/pallas_call | solution.py:42
  (7 shorter events, 0.1 us)
Async XLA Ops:
  0.6 5.8 %copy-start.1 = (f32[4,64,128]{2,1,0:T(8,128)S(1)}, f32[4,64,128]{2,1,0:T(8,128)}, u32[]{:S(2)}) copy-start(f32[4,64,128]{2,1,0:T(8,128)} %water.3) | copy-start | bytes 393220
  0.6 5.8 %copy-start.2 = (f32[1,1,5,16384]{3,1,2,0:T(1,128)S(1)}, f32[1,1,5,16384]{3,1,2,0:T(1,128)}, u32[]{:S(2)}) copy-start(f32[1,1,5,16384]{3,1,2,0:T(1,128)} %param.18) | copy-start | bytes 983044
  0.7 5.8 %copy-start.3 = (f32[1,1,5,16384]{3,1,2,0:T(1,128)S(1)}, f32[1,1,5,16384]{3,1,2,0:T(1,128)}, u32[]{:S(2)}) copy-start(f32[1,1,5,16384]{3,1,2,0:T(1,128)} %param.19) | copy-start | bytes 983044
  0.7 5.8 %copy-start.4 = (f32[1,1,2,16384]{3,2,1,0:T(2,128)S(1)}, f32[1,1,2,16384]{3,2,1,0:T(2,128)}, u32[]{:S(2)}) copy-start(f32[1,1,2,16384]{3,2,1,0:T(2,128)} %param.20) | copy-start | bytes 393220
  3.3 5.7 %collective-permute-start = (bf16[336,128]{1,0:T(8,128)(2,1)}, bf16[336,128]{1,0:T(8,128)(2,1)S(1)}, u32[]{:S(2)}, u32[]{:S(2)}) collective-permute-start(bf16[336,128]{1,0:T(8,128)(2,1)} %get-tuple-element.32), channel_id=1, source_target_pairs={{0,3},{1,2},{2,1},{3,0},{4,7},{5,6},{6,5},{7,4},{8,11},{9,10},{10,... | collective-permute-start | bytes 258056 | tf_op jit(solution)/shard_map/ppermute | solution.py:580
  5.7 5.3 %collective-permute-start.1 = (bf16[336,128]{1,0:T(8,128)(2,1)}, bf16[336,128]{1,0:T(8,128)(2,1)S(1)}, u32[]{:S(2)}, u32[]{:S(2)}) collective-permute-start(bf16[336,128]{1,0:T(8,128)(2,1)} %get-tuple-element.33), channel_id=1, source_target_pairs={{0,2},{1,3},{2,0},{3,1},{4,6},{5,7},{6,4},{7,5},{8,10},{9,11},{10,... | collective-permute-start | bytes 258056 | tf_op jit(solution)/shard_map/ppermute | solution.py:580
  6.4 4.7 %collective-permute-start.2 = (bf16[336,128]{1,0:T(8,128)(2,1)}, bf16[336,128]{1,0:T(8,128)(2,1)S(1)}, u32[]{:S(2)}, u32[]{:S(2)}) collective-permute-start(bf16[336,128]{1,0:T(8,128)(2,1)} %get-tuple-element.34), channel_id=1, source_target_pairs={{0,1},{1,0},{2,3},{3,2},{4,5},{5,4},{6,7},{7,6},{8,9},{9,8},{10,11... | collective-permute-start | bytes 258056 | tf_op jit(solution)/shard_map/ppermute | solution.py:580
  6.4 4.6 %copy-start = (bf16[336,128]{1,0:T(8,128)(2,1)S(1)}, bf16[336,128]{1,0:T(8,128)(2,1)}, u32[]{:S(2)}) copy-start(bf16[336,128]{1,0:T(8,128)(2,1)} %get-tuple-element.35.refs_3_.refs_4_.refs_0_) | copy-start | bytes 258052
  6.5 4.6 %copy-start.5 = (f32[1,1,2,16384]{3,2,1,0:T(2,128)S(1)}, f32[1,1,2,16384]{3,2,1,0:T(2,128)}, u32[]{:S(2)}) copy-start(f32[1,1,2,16384]{3,2,1,0:T(2,128)} %param.21) | copy-start | bytes 393220
  11.7 10.7 %copy-start.7 = (f32[64,128]{1,0:T(8,128)S(1)}, f32[64,128]{1,0:T(8,128)}, u32[]{:S(2)}) copy-start(f32[64,128]{1,0:T(8,128)} %mixing) | copy-start | bytes 98308
  11.7 6.1 %collective-permute-start.3 = (bf16[112,128]{1,0:T(8,128)(2,1)S(1)}, bf16[112,128]{1,0:T(8,128)(2,1)S(1)}, u32[]{:S(2)}, u32[]{:S(2)}) collective-permute-start(bf16[112,128]{1,0:T(8,128)(2,1)S(1)} %get-tuple-element.36.refs_3_.refs_0_), channel_id=1, source_target_pairs={{0,12},{4,8},{8,4},{12,0},{1,13},{5,9},{9,5},{13,1},{2,14},{6,10},... | collective-permute-start | bytes 86024 | tf_op jit(solution)/shard_map/ppermute | solution.py:563
  16.0 4.8 %collective-permute-start.4 = (bf16[112,128]{1,0:T(8,128)(2,1)S(1)}, bf16[112,128]{1,0:T(8,128)(2,1)S(1)}, u32[]{:S(2)}, u32[]{:S(2)}) collective-permute-start(bf16[112,128]{1,0:T(8,128)(2,1)S(1)} %get-tuple-element.36.refs_3_.refs_0_), channel_id=1, source_target_pairs={{0,8},{4,12},{8,0},{12,4},{1,9},{5,13},{9,1},{13,5},{2,10},{6,14},... | collective-permute-start | bytes 86024 | tf_op jit(solution)/shard_map/ppermute | solution.py:563
  16.0 4.8 %collective-permute-start.5 = (bf16[112,128]{1,0:T(8,128)(2,1)S(1)}, bf16[112,128]{1,0:T(8,128)(2,1)S(1)}, u32[]{:S(2)}, u32[]{:S(2)}) collective-permute-start(bf16[112,128]{1,0:T(8,128)(2,1)S(1)} %get-tuple-element.36.refs_3_.refs_0_), channel_id=1, source_target_pairs={{0,4},{4,0},{8,12},{12,8},{1,5},{5,1},{9,13},{13,9},{2,6},{6,2},{1... | collective-permute-start | bytes 86024 | tf_op jit(solution)/shard_map/ppermute | solution.py:563
  20.8 4.7 %collective-permute-start.7 = (bf16[384,128]{1,0:T(8,128)(2,1)S(1)}, bf16[384,128]{1,0:T(8,128)(2,1)S(1)}, u32[]{:S(2)}, u32[]{:S(2)}) collective-permute-start(bf16[384,128]{1,0:T(8,128)(2,1)S(1)} %shard_map.133.refs_0_), channel_id=1, source_target_pairs={{0,2},{1,3},{2,0},{3,1},{4,6},{5,7},{6,4},{7,5},{8,10},{9,11},{10,... | collective-permute-start | bytes 294920 | tf_op jit(solution)/shard_map/ppermute | solution.py:568
  23.5 1.2 %collective-permute-start.8 = (bf16[64,128]{1,0:T(8,128)(2,1)S(1)}, bf16[64,128]{1,0:T(8,128)(2,1)S(1)}, u32[]{:S(2)}, u32[]{:S(2)}) collective-permute-start(bf16[64,128]{1,0:T(8,128)(2,1)S(1)} %get-tuple-element.39.refs_4_), channel_id=1, source_target_pairs={{0,1},{1,0},{2,3},{3,2},{4,5},{5,4},{6,7},{7,6},{8,9},{9,8},{10,11... | collective-permute-start | bytes 49160 | tf_op jit(solution)/shard_map/ppermute | solution.py:563
  23.5 3.8 %collective-permute-start.6 = (bf16[384,128]{1,0:T(8,128)(2,1)S(1)}, bf16[384,128]{1,0:T(8,128)(2,1)S(1)}, u32[]{:S(2)}, u32[]{:S(2)}) collective-permute-start(bf16[384,128]{1,0:T(8,128)(2,1)S(1)} %shard_map.133.refs_0_), channel_id=1, source_target_pairs={{0,1},{1,0},{2,3},{3,2},{4,5},{5,4},{6,7},{7,6},{8,9},{9,8},{10,11... | collective-permute-start | bytes 294920 | tf_op jit(solution)/shard_map/ppermute | solution.py:574
  25.4 1.9 %collective-permute-start.9 = (bf16[384,128]{1,0:T(8,128)(2,1)S(1)}, bf16[384,128]{1,0:T(8,128)(2,1)S(1)}, u32[]{:S(2)}, u32[]{:S(2)}) collective-permute-start(bf16[384,128]{1,0:T(8,128)(2,1)S(1)} %collective-permute-done.7.refs_2_), channel_id=1, source_target_pairs={{0,1},{1,0},{2,3},{3,2},{4,5},{5,4},{6,7},{7,6},{8,9},{9,8},{10,11... | collective-permute-start | bytes 294920 | tf_op jit(solution)/shard_map/ppermute | solution.py:574
  25.4 4.1 %collective-permute-start.10 = (bf16[64,128]{1,0:T(8,128)(2,1)S(1)}, bf16[64,128]{1,0:T(8,128)(2,1)S(1)}, u32[]{:S(2)}, u32[]{:S(2)}) collective-permute-start(bf16[64,128]{1,0:T(8,128)(2,1)S(1)} %get-tuple-element.39.refs_4_), channel_id=1, source_target_pairs={{0,2},{1,3},{2,0},{3,1},{4,6},{5,7},{6,4},{7,5},{8,10},{9,11},{10,... | collective-permute-start | bytes 49160 | tf_op jit(solution)/shard_map/ppermute | solution.py:563
  26.9 3.2 %collective-permute-start.11 = (bf16[64,128]{1,0:T(8,128)(2,1)S(1)}, bf16[64,128]{1,0:T(8,128)(2,1)S(1)}, u32[]{:S(2)}, u32[]{:S(2)}) collective-permute-start(bf16[64,128]{1,0:T(8,128)(2,1)S(1)} %get-tuple-element.39.refs_4_), channel_id=1, source_target_pairs={{0,3},{1,2},{2,1},{3,0},{4,7},{5,6},{6,5},{7,4},{8,11},{9,10},{10,... | collective-permute-start | bytes 49160 | tf_op jit(solution)/shard_map/ppermute | solution.py:563
  30.1 6.2 %copy-start.6 = (f32[2,64,128]{2,1,0:T(8,128)S(1)}, f32[2,64,128]{2,1,0:T(8,128)}, u32[]{:S(2)}) copy-start(f32[2,64,128]{2,1,0:T(8,128)} %currents.1) | copy-start | bytes 196612
  31.2 3.7 %collective-permute-start.12 = (bf16[192,128]{1,0:T(8,128)(2,1)S(1)}, bf16[192,128]{1,0:T(8,128)(2,1)S(1)}, u32[]{:S(2)}, u32[]{:S(2)}) collective-permute-start(bf16[192,128]{1,0:T(8,128)(2,1)S(1)} %get-tuple-element.48), channel_id=1, source_target_pairs={{0,3},{1,2},{2,1},{3,0},{4,7},{5,6},{6,5},{7,4},{8,11},{9,10},{10,... | collective-permute-start | bytes 147464 | tf_op jit(solution)/shard_map/ppermute | solution.py:580
  32.1 4.2 %collective-permute-start.13 = (bf16[192,128]{1,0:T(8,128)(2,1)S(1)}, bf16[192,128]{1,0:T(8,128)(2,1)S(1)}, u32[]{:S(2)}, u32[]{:S(2)}) collective-permute-start(bf16[192,128]{1,0:T(8,128)(2,1)S(1)} %get-tuple-element.49), channel_id=1, source_target_pairs={{0,2},{1,3},{2,0},{3,1},{4,6},{5,7},{6,4},{7,5},{8,10},{9,11},{10,... | collective-permute-start | bytes 147464 | tf_op jit(solution)/shard_map/ppermute | solution.py:580
  33.1 3.2 %collective-permute-start.14 = (bf16[192,128]{1,0:T(8,128)(2,1)S(1)}, bf16[192,128]{1,0:T(8,128)(2,1)S(1)}, u32[]{:S(2)}, u32[]{:S(2)}) collective-permute-start(bf16[192,128]{1,0:T(8,128)(2,1)S(1)} %get-tuple-element.50), channel_id=1, source_target_pairs={{0,1},{1,0},{2,3},{3,2},{4,5},{5,4},{6,7},{7,6},{8,9},{9,8},{10,11... | collective-permute-start | bytes 147464 | tf_op jit(solution)/shard_map/ppermute | solution.py:580

commit v10 on v9

--- a/solution.py
+++ b/solution.py
@@ -84,7 +84,7 @@
 def forward_kernel(group, links_h, blocks_h, rows_h, cols_h, currents_h, water_h, *refs):
     devices, members, place = group
     outs, scratch = refs[:members], refs[members:]
-    links, blocks, currents, rows, cols, water, fields, tail, arrived, left = scratch
+    links, blocks, currents, rows, cols, water, fields, tail, kept, arrived, left = scratch
     pairs, side, width = rows_h.shape
     depth = cols_h.shape[1]
     loads = [
@@ -107,27 +107,29 @@
     me = place()
     side, depth, pairs = rows.shape[1], cols.shape[1], rows.shape[0]
     owners = [lax.rem(lax.rem(blocks[0, m], devices), members) for m in range(pairs)]
-    copies, keeps = [], []
+    copies = []
     for k, out in enumerate(outs):
         partner = me ^ k
-        pair, found = jnp.int32(0), jnp.int32(0)
+        pair = jnp.int32(0)
         for m in range(pairs):
             pair = jnp.where(owners[m] == partner, m, pair)
-            found = jnp.where(owners[m] == partner, 1, found)
-        keeps.append(flag(found > 0))
+        if pairs < members:
+            found = sum(flag(owners[m] == partner) for m in range(pairs))
+            kept[k] = (rows[pair].astype(F32) * found).astype(BF16)
         at = 0
         for i, source in enumerate((rows, cols)):
+            if i == 0 and pairs < members:
+                source, pair_at = kept, k
+            else:
+                pair_at = pair
             target = out.at[pl.ds(at, source.shape[1])]
-            copies.append(pltpu.make_async_copy(source.at[pair], target, left.at[4 * k + i]))
+            copies.append(pltpu.make_async_copy(source.at[pair_at], target, left.at[4 * k + i]))
             copies[-1].start()
             at += source.shape[1]
     for i in (0, 2, 5):
         loads[i].wait()
-    plain = pairs == members
-    for k in range(1 if plain else members):
-        for c in range(2):
-            field = currents[c] if plain else currents[c] * keeps[k]
-            fields[k, c * side : (c + 1) * side] = field.astype(BF16)
+    for c in range(2):
+        fields[0, c * side : (c + 1) * side] = currents[c].astype(BF16)
     lane = iota((1, width), 1)
     numbers = jnp.zeros((1, width), F32)
     for q in range(4):
@@ -138,7 +140,9 @@
     tail[...] = jnp.concatenate(ends + [blank], axis=0).astype(BF16)
     for k, out in enumerate(outs):
         at = side + depth
-        for i, source in enumerate((fields.at[0 if plain else k], tail)):
+        if out.shape[0] == at:
+            continue
+        for i, source in enumerate((fields.at[0], tail)):
             target = out.at[pl.ds(at, source.shape[0])]
             copies.append(pltpu.make_async_copy(source, target, left.at[4 * k + 2 + i]))
             copies[-1].start()
@@ -203,12 +207,6 @@
     out[...] = store[...].astype(BF16)
 
 
-def relay_kernel(tiles, *refs):
-    messages, out = refs[:tiles][::-1], refs[tiles]
-    for k in range(tiles):
-        out[k * BLOCK_ROWS : (k + 1) * BLOCK_ROWS] = messages[k][0:BLOCK_ROWS]
-
-
 def nearby(me, members, distance, arrays):
     at = me + distance
     inside = (at >= 0) & (at < members)
@@ -237,14 +235,18 @@
     return total
 
 
+def tails_of(chunks, hops):
+    at = min(c.shape[0] for c in chunks)
+    return [hops[k // 2 - 1][...] if k > 1 and k % 2 else c[at:] for k, c in enumerate(chunks)]
+
+
 def forcing_kernel(group, side, levels, subs, place, mass, drag, wind, early, *refs):
     chunks = refs[:group][::-1]
-    out, current_o, push_o, store = refs[group:]
+    hops, (out, current_o, push_o, store) = refs[group:-4], refs[-4:]
     size = mass.shape[0]
     depth = chunks[0].shape[1]
-    fields = [
-        [c[side + depth : 2 * side + depth], c[2 * side + depth : 3 * side + depth]] for c in chunks
-    ]
+    tails = tails_of(chunks, hops)
+    fields = [[t[0:side], t[side : 2 * side]] for t in tails]
     total = remap_forward(chunks, fields, side, depth)
     pushes = []
     for c in range(2):
@@ -255,7 +257,7 @@
         push_o[c] = push
         pushes.append(push)
     put_side_rims(store, pushes, lambda q: q * 2 * DEPTH)
-    tail = [c[3 * side + depth :] for c in chunks]
+    tail = [t[2 * side :] for t in tails]
     store[NAMES_ROW : NAMES_ROW + 1] = tail[0].astype(F32)[2 * levels : 2 * levels + 1]
     me, step = place(), group // subs
     left, right = (nearby(me, group, d * step, tail) for d in (-1, 1))
@@ -267,36 +269,33 @@
     out[PUSH_ROWS:] = early[...]
 
 
-def ocean_kernel(counts, tile_place, member_place, water, mixing, *refs):
+def ocean_halos(counts, tile_place, member_place, shape, messages, tails):
     tiles, subs, levs = counts
-    members = subs * levs
-    messages, chunks, (warm_o, top_o) = refs[:tiles], refs[tiles:-2], refs[-2:]
-    levels, rows, width = water.shape
+    levels, rows, width = shape
     my_tile, me = tile_place(), member_place()
     halo = {}
     strips = [m[BLOCK_ROWS : BLOCK_ROWS + 4 * levels] for m in messages]
     rims = [m[0:PUSH_ROWS] for m in messages]
-    tails = [c[3 * rows + width :] for c in chunks]
+    ends = [t[2 * rows :] for t in tails]
     for dt in (-1, 1):
         beyond = nearby(my_tile, tiles, dt, strips)
         halo[dt, 0] = beyond[: 2 * levels] if dt < 0 else beyond[2 * levels :]
         corners = nearby(my_tile, tiles, dt, rims)
+        corners = jnp.concatenate([corners[r : r + 1] for r in CORNER_ROWS[:levels]], axis=0)
         at = rows - 1 if dt < 0 else 0
         for ds in (-1, 1):
             lane_at = at if ds < 0 else rows + at
-            halo[dt, ds] = [
-                corners[CORNER_ROWS[l] : CORNER_ROWS[l] + 1, lane_at : lane_at + 1]
-                for l in range(levels)
-            ]
+            halo[dt, ds] = corners[:, lane_at : lane_at + 1]
     for ds in (-1, 1):
-        beside = nearby(me, members, ds * levs, tails)[: 2 * levels]
+        beside = nearby(me, subs * levs, ds * levs, ends)[: 2 * levels]
         halo[0, ds] = roll(beside, -rows, 1) if ds > 0 else beside
-    left_cols = halo[0, -1].T
-    right_cols = halo[0, 1].T
-    row = iota((rows, width), 0)
-    lane = iota((rows, width), 1)
+    return halo
+
+
+def biharmonic(x, top, bottom, left, right, corner):
+    rows, width = x.shape
+    row, lane = iota(x.shape, 0), iota(x.shape, 1)
     line = iota((1, width), 1)
-    total = None
 
     def laplacian(x, top, bottom, left, right):
         up = jnp.where(row == 0, top, roll(x, 1, 0))
@@ -305,40 +304,81 @@
         east = jnp.where(lane == width - 1, right, roll(x, -1, 1))
         return up + down + west + east - 4.0 * x
 
+    def ring_row(mid, out_row, in_row, dt):
+        west = jnp.where(line == 0, corner[dt, -1], roll(mid, 1, 1))
+        east = jnp.where(line == width - 1, corner[dt, 1], roll(mid, -1, 1))
+        return west + east + out_row + in_row - 4.0 * mid
+
+    def ring_col(mid, out_col, in_col, ds):
+        up = jnp.concatenate([corner[-1, ds], mid[:-1]], axis=0)
+        down = jnp.concatenate([mid[1:], corner[1, ds]], axis=0)
+        return up + down + out_col + in_col - 4.0 * mid
+
+    return laplacian(
+        laplacian(x, top[0], bottom[0], left[0], right[0]),
+        ring_row(*top, x[0:1], -1),
+        ring_row(*bottom, x[rows - 1 :], 1),
+        ring_col(*left, x[:, 0:1], -1),
+        ring_col(*right, x[:, width - 1 :], 1),
+    )
+
+
+def split_refs(tiles, members, refs, outs):
+    messages, chunks = refs[:tiles], refs[tiles : tiles + members]
+    return messages, tails_of(chunks, refs[tiles + members : -outs]), refs[-outs:]
+
+
+def relay_kernel(counts, tile_place, member_place, water, mixing, *refs):
+    tiles, subs, levs = counts
+    outs = 1 if levs == 1 else 2
+    messages, tails, outs = split_refs(tiles, subs * levs, refs, outs)
+    for k in range(tiles):
+        outs[0][k * BLOCK_ROWS : (k + 1) * BLOCK_ROWS] = messages[k][0:BLOCK_ROWS]
+    levels, rows, width = water.shape
+    halo = ocean_halos(counts, tile_place, member_place, water.shape, messages, tails)
+
+    def both(strip):
+        near = sum(strip[2 * l : 2 * l + 1] for l in range(levels))
+        far = sum(strip[2 * l + 1 : 2 * l + 2] for l in range(levels))
+        return near, far
+
+    def as_columns(strip):
+        near, far = both(strip)
+        across = jnp.concatenate([near, far] + [jnp.zeros_like(near)] * 6, axis=0).T
+        return across[0:rows, 0:1], across[0:rows, 1:2]
+
+    corner = {
+        (dt, ds): jnp.sum(halo[dt, ds], axis=0, keepdims=True) for dt in (-1, 1) for ds in (-1, 1)
+    }
+    x = sum(water[l] for l in range(levels))
+    twice = biharmonic(
+        x, both(halo[-1, 0]), both(halo[1, 0]), as_columns(halo[0, -1]), as_columns(halo[0, 1]), corner
+    )
+    top = (x - mixing[...] * twice) / (levels * levs)
+    if levs == 1:
+        outs[0][tiles * BLOCK_ROWS :] = top.astype(BF16)
+    else:
+        outs[1][...] = top
+
+
+def ocean_kernel(counts, tile_place, member_place, water, mixing, *refs):
+    tiles, subs, levs = counts
+    messages, tails, (warm_o,) = split_refs(tiles, subs * levs, refs, 1)
+    levels, rows, width = water.shape
+    halo = ocean_halos(counts, tile_place, member_place, water.shape, messages, tails)
+    left, right = halo[0, -1].T, halo[0, 1].T
     for l in range(levels):
         x = water[l]
-        near, far = 2 * l, 2 * l + 1
-        top, top_far = halo[-1, 0][near : near + 1], halo[-1, 0][far : far + 1]
-        bottom, bottom_far = halo[1, 0][near : near + 1], halo[1, 0][far : far + 1]
-        left, left_far = left_cols[0:rows, near : near + 1], left_cols[0:rows, far : far + 1]
-        right, right_far = right_cols[0:rows, near : near + 1], right_cols[0:rows, far : far + 1]
-        corner = {}
-        for dt in (-1, 1):
-            for ds in (-1, 1):
-                corner[dt, ds] = halo[dt, ds][l]
-
-        def ring_row(mid, out_row, in_row, dt):
-            west = jnp.where(line == 0, corner[dt, -1], roll(mid, 1, 1))
-            east = jnp.where(line == width - 1, corner[dt, 1], roll(mid, -1, 1))
-            return west + east + out_row + in_row - 4.0 * mid
-
-        def ring_col(mid, out_col, in_col, ds):
-            up = jnp.concatenate([corner[-1, ds], mid[:-1]], axis=0)
-            down = jnp.concatenate([mid[1:], corner[1, ds]], axis=0)
-            return up + down + out_col + in_col - 4.0 * mid
-
-        once = laplacian(x, top, bottom, left, right)
-        twice = laplacian(
-            once,
-            ring_row(top, top_far, x[0:1], -1),
-            ring_row(bottom, bottom_far, x[rows - 1 :], 1),
-            ring_col(left, left_far, x[:, 0:1], -1),
-            ring_col(right, right_far, x[:, width - 1 :], 1),
+        pair = (2 * l, 2 * l + 1)
+        twice = biharmonic(
+            x,
+            [halo[-1, 0][i : i + 1] for i in pair],
+            [halo[1, 0][i : i + 1] for i in pair],
+            [left[0:rows, i : i + 1] for i in pair],
+            [right[0:rows, i : i + 1] for i in pair],
+            {(dt, ds): halo[dt, ds][l : l + 1] for dt in (-1, 1) for ds in (-1, 1)},
         )
-        warm = x - mixing[...] * twice
-        warm_o[l] = warm
-        total = warm if total is None else total + warm
-    top_o[...] = (total / (levels * levs)).astype(top_o.dtype)
+        warm_o[l] = x - mixing[...] * twice
 
 
 def subcycles_kernel(tiles, members, table, viscous, gain, speed, push, *refs):
@@ -476,12 +516,10 @@
 
 
 def back_kernel(group, side, drag, conduct, current, speed, *refs):
-    chunks = refs[:group]
-    tops = refs[group : 2 * group]
-    outs = refs[2 * group :]
+    chunks, relays, outs = refs[:group], refs[group : 2 * group], refs[2 * group :]
     size = drag.shape[0]
     depth = chunks[0].shape[1]
-    warm = remap_forward(chunks, [[t[...]] for t in tops], side, depth)
+    warm = remap_forward(chunks, [[r[r.shape[0] - side :]] for r in relays], side, depth)
     heat = conduct[...] * warm
     fluxes = [heat.astype(BF16)]
     for c in range(2):
@@ -591,10 +629,14 @@
     wind = interleaved(wind_stress)
 
     tail_rows = -(-(2 * levels + 1) // TILE_ROWS) * TILE_ROWS
-    chunk_rows = 3 * side + width + tail_rows
+    pair_rows = side + width
+    chunk_rows = pair_rows + 2 * side + tail_rows
     sent = call(
         functools.partial(forward_kernel, (devices, group, member_place)),
-        [shape(chunk_rows, width, dtype=BF16)] * group,
+        [
+            shape(pair_rows if k > 1 and k % 2 else chunk_rows, width, dtype=BF16)
+            for k in range(group)
+        ],
         (
             neighbors,
             remap_blocks,
@@ -610,8 +652,9 @@
             pltpu.VMEM((pairs, side, size), BF16),
             pltpu.VMEM((pairs, size, width), BF16),
             pltpu.VMEM((levels, side, width), F32),
-            pltpu.VMEM((1 if pairs == group else group, 2 * side, width), BF16),
+            pltpu.VMEM((1, 2 * side, width), BF16),
             pltpu.VMEM((tail_rows, width), BF16),
+            pltpu.VMEM((1 if pairs == group else group, side, size), BF16),
             pltpu.SemaphoreType.DMA((6,)),
             pltpu.SemaphoreType.DMA((4 * group,)),
         ],
@@ -620,6 +663,10 @@
         micros=10,
     )
     chunks = swap_each(sent)
+    hops = [
+        lax.ppermute(chunks[k][pair_rows:], group_axes, [(i, i ^ 1) for i in range(group)])
+        for k in range(2, group, 2)
+    ]
 
     early, viscous, gain, step_mass, drag, conduct, speed = call(
         rims_kernel,
@@ -635,42 +682,46 @@
     message, current_ice, push = call(
         functools.partial(forcing_kernel, group, side, levels, sub_count, member_place),
         [shape(BLOCK_ROWS + 4 * levels, size, dtype=BF16), planes, planes],
-        (step_mass, drag, wind, early, *chunks[::-1]),
+        (step_mass, drag, wind, early, *chunks[::-1], *hops),
         scratch=[pltpu.VMEM((PUSH_ROWS, size), F32)],
     )
     messages = swap(message, "tile", tile_count)
 
-    relay = call(
-        functools.partial(relay_kernel, tile_count),
-        shape(tile_count * BLOCK_ROWS, size, dtype=BF16),
-        messages[::-1],
-    )
+    counts = (tile_count, sub_count, lev_count)
+    ocean = (*messages, *chunks, *hops)
+    relay_rows = tile_count * BLOCK_ROWS
+    relay_shapes = [shape(relay_rows + (side if lev_count == 1 else 0), size, dtype=BF16)]
+    if lev_count > 1:
+        relay_shapes.append(shape(side, width))
+    relay, *top = call(
+        functools.partial(relay_kernel, counts, tile_place, member_place),
+        relay_shapes,
+        (water_heat_state, diffusion_coefficient, *ocean),
+    )
+    if lev_count > 1:
+        relay = jnp.concatenate([relay, lax.psum(top[0], "lev").astype(BF16)], axis=0)
     relays = swap_chips(relay)
 
     mixing, _ = lax.optimization_barrier((diffusion_coefficient, relay))
-    warm, top = call(
-        functools.partial(
-            ocean_kernel, (tile_count, sub_count, lev_count), tile_place, member_place
-        ),
-        [shape(levels, side, width), shape(side, width, dtype=BF16 if lev_count == 1 else F32)],
-        (water_heat_state, mixing, *messages, *chunks),
-    )
-    if lev_count > 1:
-        top = lax.psum(top, "lev").astype(BF16)
-    tops = swap(top, group_axes, group)
-
+    (warm,) = call(
+        functools.partial(ocean_kernel, counts, tile_place, member_place),
+        [shape(levels, side, width)],
+        (water_heat_state, mixing, *ocean),
+    )
     far = sorted(k for k in relays if k)
-    relayed, _ = lax.optimization_barrier(([relays[k] for k in far], tops[1]))
+    relayed, _ = lax.optimization_barrier(([relays[k] for k in far], warm))
     relays = swap_cores({0: relay} | dict(zip(far, relayed)))
 
     names = jnp.stack(
-        [r.reshape(tile_count, BLOCK_ROWS, size)[:, NAMES_ROW, 0:8] for r in relays],
+        [
+            r[:relay_rows].reshape(tile_count, BLOCK_ROWS, size)[:, NAMES_ROW, 0:8]
+            for r in relays
+        ],
         axis=1,
     )
     names = names.reshape(devices, 8).astype(jnp.int32)
     table = names[:, 0:4] * 128 + names[:, 4:8]
     table = jnp.where(table < 0, -1, table ^ device_place())
-    push, _ = lax.optimization_barrier((push, top))
     speed = call(
         functools.partial(subcycles_kernel, tile_count, group),
         planes,
@@ -686,7 +737,7 @@
     replies = call(
         functools.partial(back_kernel, group, side),
         [shape(3 * side, width, dtype=BF16)] * group,
-        (drag, conduct, current_ice, speed, *chunks, *tops),
+        (drag, conduct, current_ice, speed, *chunks, *relays),
     )
     replies = swap_each(replies)
     if lev_count > 1:

time: 37.2 us -> 36.4 us (0.978)
  starting transfers between devices: 13.9 us -> 12.1 us
  waiting for transfers between devices: 13.7 us -> 14.2 us
    ppermute x6 -> x3, starting transfers between devices: 6.87 us -> 4.76 us  [swap(): got[k] = lax.ppermute(value, axes, [(i, i ^ k) for i in range(count)])]
    ppermute x2, waiting for transfers between devices: 0.01 us -> 1.23 us  [swap_cores(): got = got | {k + 1: lax.ppermute(got[k], group_axes, beside) for k in got}]
    ppermute x6 -> x3, waiting for transfers between devices: 5.34 us -> 4.13 us  [swap(): got[k] = lax.ppermute(value, axes, [(i, i ^ k) for i in range(count)])]
    ppermute x1, waiting for transfers between devices: 0.72 us -> 1.69 us  [swap_chips(): lax.ppermute(value, group_axes, [(i, i ^ k) for i in range(group)])]
    ppermute x6, waiting for transfers between devices: 7.6 us -> 6.95 us  [swap_each(): lax.ppermute(values[k], group_axes, [(i, i ^ k) for i in range(group)])]
    ppermute x2, starting transfers between devices: 0.5 us -> 0.01 us  [swap_cores(): got = got | {k + 1: lax.ppermute(got[k], group_axes, beside) for k in got}]
    ppermute x1, starting transfers between devices: 1.56 us -> 2.05 us  [swap_chips(): lax.ppermute(value, group_axes, [(i, i ^ k) for i in range(group)])]
  transfers between devices with their start and end apart: 15 -> 13, of which waited for: 9 -> 9; matrix products, arithmetic and copies ran while one was open for 0% -> 0% of each run, Pallas kernels for 9% -> 4%
where the time goes in v10:
time: 36.4 us; the launch traced here: 36.2 us
  waiting for transfers between devices  14.2 us (39%)
  starting transfers between devices  12.1 us (33%)
  Pallas kernels  8.85 us (24%)
  between operations  0.84 us (2%)
    pallas_call x8, Pallas kernels, call(): pl.pallas_call(kernel, out_shape=outs, in_specs=specs, out_specs=jax.tree...  8.85 us
    ppermute x6, waiting for transfers between devices, swap_each(): lax.ppermute(values[k], group_axes, [(i, i ^ k) for i in range(group)])  6.95 us
    ppermute x6, starting transfers between devices, swap_each(): lax.ppermute(values[k], group_axes, [(i, i ^ k) for i in range(group)])  5.31 us
    ppermute x3, starting transfers between devices, swap(): got[k] = lax.ppermute(value, axes, [(i, i ^ k) for i in range(count)])  4.76 us
    ppermute x3, waiting for transfers between devices, swap(): got[k] = lax.ppermute(value, axes, [(i, i ^ k) for i in range(count)])  4.13 us
    ppermute x1, starting transfers between devices, swap_chips(): lax.ppermute(value, group_axes, [(i, i ^ k) for i in range(group)])  2.05 us
    ppermute x1, waiting for transfers between devices, swap_chips(): lax.ppermute(value, group_axes, [(i, i ^ k) for i in range(group)])  1.69 us
    ppermute x2, waiting for transfers between devices, swap_cores(): got = got | {k + 1: lax.ppermute(got[k], group_axes, beside) for k in got}  1.23 us
  transfers between devices with their start and end apart: 13, of which 9 were waited for; matrix products, arithmetic and copies ran while one was open for 0% of the time, Pallas kernels for 4%

profile of v10, /device:TPU:0, one launch (start us, length us, event | category | flops | bytes accessed | tf_op | source)
XLA Modules:
  0.0 36.2 jit_solution(32617271644291331)
XLA Ops:
  0.6 0.0 copy-start.1
  0.6 0.0 copy-start.2
  0.7 0.0 copy-start.3
  0.7 0.0 copy-start.4
  0.7 2.6 %shard_map.131 = (bf16[336,128]{1,0:T(8,128)(2,1)}, bf16[336,128]{1,0:T(8,128)(2,1)}, bf16[336,128]{1,0:T(8,128)(2,1)}, bf16[192,128]{1,0:T(8,128)(2,1)}) custom-call(s32[1,1,4]{2,1,0:T(1,128)} %links_h.1, s32[1,4]{1,0:T(1,128)} %blocks_h.1, bf16[4,64,128]{2,1,0:T(8,128)(2,1)} %bitcast.38, bf16[4,128,128]{2,1,0:T(8,128)(2,1)} %bitcast.36, ...), custom_call_target="tpu_custom_call" | custom-call | flops 11500000256 | bytes 393248 | tf_op jit(solution)/shard_map/pallas_call | solution.py:42
  3.3 3.0 %collective-permute-start.1 = (bf16[336,128]{1,0:T(8,128)(2,1)}, bf16[336,128]{1,0:T(8,128)(2,1)S(1)}, u32[]{:S(2)}, u32[]{:S(2)}) collective-permute-start(bf16[336,128]{1,0:T(8,128)(2,1)} %get-tuple-element.30), channel_id=1, source_target_pairs={{0,2},{1,3},{2,0},{3,1},{4,6},{5,7},{6,4},{7,5},{8,10},{9,11},{10,... | collective-permute-start | bytes 258056 | tf_op jit(solution)/shard_map/ppermute | solution.py:618
  6.3 0.0 collective-permute-start.2
  6.3 0.2 collective-permute-start
  6.5 2.5 %collective-permute-done.1.refs_1_.refs_6_.refs_2_ = bf16[336,128]{1,0:T(8,128)(2,1)S(1)} collective-permute-done((bf16[336,128]{1,0:T(8,128)(2,1)}, bf16[336,128]{1,0:T(8,128)(2,1)S(1)}, u32[]{:S(2)}, u32[]{:S(2)}) %collective-permute-start.1) | collective-permute-done | bytes 86048 | tf_op jit(solution)/shard_map/ppermute | solution.py:618
  9.0 0.0 collective-permute-start.3
  9.0 0.0 copy-done.1
  9.0 0.0 copy-done.2
  9.0 0.0 copy-done.3
  9.0 0.0 copy-done.4
  9.0 0.0 copy-start
  9.1 0.0 copy-start.5
  9.1 0.2 shard_map.130
  9.3 0.7 %collective-permute-done.refs_0_.refs_7_.refs_3_ = bf16[192,128]{1,0:T(8,128)(2,1)S(1)} collective-permute-done((bf16[192,128]{1,0:T(8,128)(2,1)}, bf16[192,128]{1,0:T(8,128)(2,1)S(1)}, u32[]{:S(2)}, u32[]{:S(2)}) %collective-permute-start) | collective-permute-done | bytes 49184 | tf_op jit(solution)/shard_map/ppermute | solution.py:618
  10.0 0.0 collective-permute-done.2.refs_2_.refs_5_.refs_1_
  10.0 0.2 collective-permute-done.3.refs_4_.refs_8_
  10.2 0.0 copy-done
  10.2 0.0 copy-done.5
  10.2 0.0 copy-start.6
  10.2 0.6 %shard_map.132 = (bf16[112,128]{1,0:T(8,128)(2,1)S(1)}, f32[2,128,128]{2,1,0:T(8,128)S(1)}, f32[2,128,128]{2,1,0:T(8,128)S(1)}) custom-call(f32[128,128]{1,0:T(8,128)S(1)} %get-tuple-element.26.mass, f32[128,128]{1,0:T(8,128)S(1)} %get-tuple-element.27.drag, f32[256,128]{1,0:T(8,128)S(1)} %bitcast.30, bf16[80,128]{1,0:T(8,128)(2,1)S(1)} %get-tuple-element.28.early, ...), custom_call_target="tpu_custom_call" | custom-call | flops 11500000 | bytes 626688 | tf_op jit(solution)/shard_map/pallas_call | solution.py:42
  10.8 4.1 %collective-permute-start.6 = (bf16[112,128]{1,0:T(8,128)(2,1)S(1)}, bf16[112,128]{1,0:T(8,128)(2,1)S(1)}, u32[]{:S(2)}, u32[]{:S(2)}) collective-permute-start(bf16[112,128]{1,0:T(8,128)(2,1)S(1)} %get-tuple-element.33.refs_0_), channel_id=1, source_target_pairs={{0,12},{4,8},{8,4},{12,0},{1,13},{5,9},{9,5},{13,1},{2,14},{6,10},... | collective-permute-start | bytes 86024 | tf_op jit(solution)/shard_map/ppermute | solution.py:601
  14.9 0.0 collective-permute-start.5
  14.9 0.6 %collective-permute-start.4 = (bf16[112,128]{1,0:T(8,128)(2,1)S(1)}, bf16[112,128]{1,0:T(8,128)(2,1)S(1)}, u32[]{:S(2)}, u32[]{:S(2)}) collective-permute-start(bf16[112,128]{1,0:T(8,128)(2,1)S(1)} %get-tuple-element.33.refs_0_), channel_id=1, source_target_pairs={{0,4},{4,0},{8,12},{12,8},{1,5},{5,1},{9,13},{13,9},{2,6},{6,2},{1... | collective-permute-start | bytes 86024 | tf_op jit(solution)/shard_map/ppermute | solution.py:601
  15.6 1.2 %collective-permute-done.6.refs_3_ = bf16[112,128]{1,0:T(8,128)(2,1)S(1)} collective-permute-done((bf16[112,128]{1,0:T(8,128)(2,1)S(1)}, bf16[112,128]{1,0:T(8,128)(2,1)S(1)}, u32[]{:S(2)}, u32[]{:S(2)}) %collective-permute-start.6) | collective-permute-done | bytes 28704 | tf_op jit(solution)/shard_map/ppermute | solution.py:601
  16.8 2.9 %collective-permute-done.5.refs_2_ = bf16[112,128]{1,0:T(8,128)(2,1)S(1)} collective-permute-done((bf16[112,128]{1,0:T(8,128)(2,1)S(1)}, bf16[112,128]{1,0:T(8,128)(2,1)S(1)}, u32[]{:S(2)}, u32[]{:S(2)}) %collective-permute-start.5) | collective-permute-done | bytes 28704 | tf_op jit(solution)/shard_map/ppermute | solution.py:601
  19.7 0.0 collective-permute-done.4.refs_1_
  19.7 0.0 copy-done.6
  19.7 0.4 %shard_map.133.refs_0_.refs_4_ = bf16[448,128]{1,0:T(8,128)(2,1)S(1)} custom-call(f32[4,64,128]{2,1,0:T(8,128)S(1)} %copy-done.1, f32[64,128]{1,0:T(8,128)S(1)} %copy-done.6, bf16[112,128]{1,0:T(8,128)(2,1)S(1)} %get-tuple-element.33.refs_0_, bf16[112,128]{1,0:T(8,128)(2,1)S(1)} %collective-permute-done.4.refs_1_, ...), custom_call_target="tpu_custom_call" | custom-call | flops 11500000 | bytes 622592 | tf_op jit(solution)/shard_map/pallas_call | solution.py:42
  20.1 2.0 %collective-permute-start.8 = (bf16[448,128]{1,0:T(8,128)(2,1)S(1)}, bf16[448,128]{1,0:T(8,128)(2,1)S(1)}, u32[]{:S(2)}, u32[]{:S(2)}) collective-permute-start(bf16[448,128]{1,0:T(8,128)(2,1)S(1)} %shard_map.133.refs_0_.refs_4_), channel_id=1, source_target_pairs={{0,2},{1,3},{2,0},{3,1},{4,6},{5,7},{6,4},{7,5},{8,10},{9,11},{10,... | collective-permute-start | bytes 344072 | tf_op jit(solution)/shard_map/ppermute | solution.py:606
  22.2 0.0 collective-permute-start.7
  22.2 1.1 %shard_map.134.warm = f32[4,64,128]{2,1,0:T(8,128)S(1)} custom-call(f32[4,64,128]{2,1,0:T(8,128)S(1)} %copy-done.1, f32[64,128]{1,0:T(8,128)S(1)} %copy-done.6, bf16[112,128]{1,0:T(8,128)(2,1)S(1)} %get-tuple-element.33.refs_0_, bf16[112,128]{1,0:T(8,128)(2,1)S(1)} %collective-permute-done.4.refs_1_, bf16[112,128]{1,0:T(8,128)(2,1)S(1)} %collective-permute-done.5.refs_2_, ...), custom_call_target="tpu_custom_call" | custom-call | flops 11500000 | bytes 622592 | tf_op jit(solution)/shard_map/pallas_call | solution.py:42
  23.3 1.7 %collective-permute-done.8.refs_2_.refs_6_ = bf16[448,128]{1,0:T(8,128)(2,1)S(1)} collective-permute-done((bf16[448,128]{1,0:T(8,128)(2,1)S(1)}, bf16[448,128]{1,0:T(8,128)(2,1)S(1)}, u32[]{:S(2)}, u32[]{:S(2)}) %collective-permute-start.8) | collective-permute-done | bytes 114720 | tf_op jit(solution)/shard_map/ppermute | solution.py:606
  25.0 0.0 collective-permute-start.9
  25.0 0.0 collective-permute-done.7.refs_1_.refs_5_
  25.1 1.2 %collective-permute-done.9.refs_3_.refs_7_ = bf16[448,128]{1,0:T(8,128)(2,1)S(1)} collective-permute-done((bf16[448,128]{1,0:T(8,128)(2,1)S(1)}, bf16[448,128]{1,0:T(8,128)(2,1)S(1)}, u32[]{:S(2)}, u32[]{:S(2)}) %collective-permute-start.9) | collective-permute-done | bytes 114720 | tf_op jit(solution)/shard_map/ppermute | solution.py:612
  26.4 0.1 xor_select_fusion.table
  26.5 2.1 %shard_map.135.speed = f32[2,128,128]{2,1,0:T(8,128)S(1)} custom-call(s32[16,4]{1,0:T(8,128)S(1)} %xor_select_fusion.table, f32[128,128]{1,0:T(8,128)S(1)} %get-tuple-element.36.viscous, f32[128,128]{1,0:T(8,128)S(1)} %get-tuple-element.37.gain, f32[2,128,128]{2,1,0:T(8,128)S(1)} %get-tuple-element.38.speed, f32[2,128,128]{2,1,0:T(8,128)S(1)} %get-tuple-element.39.push, ...), custom_call_target="tpu_custom_call" | custom-call | flops 11500000 | bytes 852224 | tf_op jit(solution)/shard_map/pallas_call | solution.py:42
  28.5 0.0 copy-start.7
  28.5 1.1 %shard_map.136 = (bf16[192,128]{1,0:T(8,128)(2,1)S(1)}, bf16[192,128]{1,0:T(8,128)(2,1)S(1)}, bf16[192,128]{1,0:T(8,128)(2,1)S(1)}, bf16[192,128]{1,0:T(8,128)(2,1)S(1)}) custom-call(f32[128,128]{1,0:T(8,128)S(1)} %get-tuple-element.27.drag, f32[128,128]{1,0:T(8,128)S(1)} %get-tuple-element.40.conduct, f32[2,128,128]{2,1,0:T(8,128)S(1)} %get-tuple-element.41.current, ...), custom_call_target="tpu_custom_call" | custom-call | flops 11500000 | bytes 1159168 | tf_op jit(solution)/shard_map/pallas_call | solution.py:42
  29.6 1.7 %collective-permute-start.10 = (bf16[192,128]{1,0:T(8,128)(2,1)S(1)}, bf16[192,128]{1,0:T(8,128)(2,1)S(1)}, u32[]{:S(2)}, u32[]{:S(2)}) collective-permute-start(bf16[192,128]{1,0:T(8,128)(2,1)S(1)} %get-tuple-element.42), channel_id=1, source_target_pairs={{0,3},{1,2},{2,1},{3,0},{4,7},{5,6},{6,5},{7,4},{8,11},{9,10},{10,... | collective-permute-start | bytes 147464 | tf_op jit(solution)/shard_map/ppermute | solution.py:618
  31.4 0.3 collective-permute-start.11
  31.7 0.0 collective-permute-start.12
  31.7 1.8 %collective-permute-done.10.refs_0_ = bf16[192,128]{1,0:T(8,128)(2,1)S(1)} collective-permute-done((bf16[192,128]{1,0:T(8,128)(2,1)S(1)}, bf16[192,128]{1,0:T(8,128)(2,1)S(1)}, u32[]{:S(2)}, u32[]{:S(2)}) %collective-permute-start.10) | collective-permute-done | bytes 49184 | tf_op jit(solution)/shard_map/ppermute | solution.py:618
  33.5 2.0 %collective-permute-done.11.refs_1_ = bf16[192,128]{1,0:T(8,128)(2,1)S(1)} collective-permute-done((bf16[192,128]{1,0:T(8,128)(2,1)S(1)}, bf16[192,128]{1,0:T(8,128)(2,1)S(1)}, u32[]{:S(2)}, u32[]{:S(2)}) %collective-permute-start.11) | collective-permute-done | bytes 49184 | tf_op jit(solution)/shard_map/ppermute | solution.py:618
  35.5 0.0 collective-permute-done.12.refs_2_
  35.5 0.0 copy-done.7
  35.5 0.8 %shard_map.137 = (f32[256,128]{1,0:T(8,128)}, f32[4,64,128]{2,1,0:T(8,128)}, f32[2,64,128]{2,1,0:T(8,128)}) custom-call(f32[4,64,128]{2,1,0:T(8,128)S(1)} %shard_map.134.warm, f32[2,64,128]{2,1,0:T(8,128)S(1)} %copy-done.7, f32[2,128,128]{2,1,0:T(8,128)S(1)} %shard_map.135.speed, bf16[192,128]{1,0:T(8,128)(2,1)S(1)} %collective-permute-done.10.refs_0_, ...), custom_call_target="tpu_custom_call" | custom-call | flops 11500000 | bytes 524288 | tf_op jit(solution)/shard_map/pallas_call | solution.py:42
  (11 shorter events, 0.1 us)
Async XLA Ops:
  0.6 8.4 %copy-start.1 = (f32[4,64,128]{2,1,0:T(8,128)S(1)}, f32[4,64,128]{2,1,0:T(8,128)}, u32[]{:S(2)}) copy-start(f32[4,64,128]{2,1,0:T(8,128)} %water.5) | copy-start | bytes 393220
  0.6 8.4 %copy-start.2 = (f32[1,1,5,16384]{3,1,2,0:T(1,128)S(1)}, f32[1,1,5,16384]{3,1,2,0:T(1,128)}, u32[]{:S(2)}) copy-start(f32[1,1,5,16384]{3,1,2,0:T(1,128)} %param.18) | copy-start | bytes 983044
  0.7 8.4 %copy-start.3 = (f32[1,1,5,16384]{3,1,2,0:T(1,128)S(1)}, f32[1,1,5,16384]{3,1,2,0:T(1,128)}, u32[]{:S(2)}) copy-start(f32[1,1,5,16384]{3,1,2,0:T(1,128)} %param.19) | copy-start | bytes 983044
  0.7 8.4 %copy-start.4 = (f32[1,1,2,16384]{3,2,1,0:T(2,128)S(1)}, f32[1,1,2,16384]{3,2,1,0:T(2,128)}, u32[]{:S(2)}) copy-start(f32[1,1,2,16384]{3,2,1,0:T(2,128)} %param.20) | copy-start | bytes 393220
  3.3 5.7 %collective-permute-start.1 = (bf16[336,128]{1,0:T(8,128)(2,1)}, bf16[336,128]{1,0:T(8,128)(2,1)S(1)}, u32[]{:S(2)}, u32[]{:S(2)}) collective-permute-start(bf16[336,128]{1,0:T(8,128)(2,1)} %get-tuple-element.30), channel_id=1, source_target_pairs={{0,2},{1,3},{2,0},{3,1},{4,6},{5,7},{6,4},{7,5},{8,10},{9,11},{10,... | collective-permute-start | bytes 258056 | tf_op jit(solution)/shard_map/ppermute | solution.py:618
  6.3 3.7 %collective-permute-start.2 = (bf16[336,128]{1,0:T(8,128)(2,1)}, bf16[336,128]{1,0:T(8,128)(2,1)S(1)}, u32[]{:S(2)}, u32[]{:S(2)}) collective-permute-start(bf16[336,128]{1,0:T(8,128)(2,1)} %get-tuple-element.31), channel_id=1, source_target_pairs={{0,1},{1,0},{2,3},{3,2},{4,5},{5,4},{6,7},{7,6},{8,9},{9,8},{10,11... | collective-permute-start | bytes 258056 | tf_op jit(solution)/shard_map/ppermute | solution.py:618
  6.3 3.7 %collective-permute-start = (bf16[192,128]{1,0:T(8,128)(2,1)}, bf16[192,128]{1,0:T(8,128)(2,1)S(1)}, u32[]{:S(2)}, u32[]{:S(2)}) collective-permute-start(bf16[192,128]{1,0:T(8,128)(2,1)} %get-tuple-element.29), channel_id=1, source_target_pairs={{0,3},{1,2},{2,1},{3,0},{4,7},{5,6},{6,5},{7,4},{8,11},{9,10},{10,... | collective-permute-start | bytes 147464 | tf_op jit(solution)/shard_map/ppermute | solution.py:618
  9.0 1.2 %collective-permute-start.3 = (bf16[144,128]{1,0:T(8,128)(2,1)S(1)}, bf16[144,128]{1,0:T(8,128)(2,1)S(1)}, u32[]{:S(2)}, u32[]{:S(2)}) collective-permute-start(bf16[144,128]{1,0:T(8,128)(2,1)S(1)} %slice.44), channel_id=1, source_target_pairs={{0,1},{1,0},{2,3},{3,2},{4,5},{5,4},{6,7},{7,6},{8,9},{9,8},{10,11... | collective-permute-start | bytes 110600 | tf_op jit(solution)/shard_map/ppermute | solution.py:667
  9.0 1.2 %copy-start = (bf16[336,128]{1,0:T(8,128)(2,1)S(1)}, bf16[336,128]{1,0:T(8,128)(2,1)}, u32[]{:S(2)}) copy-start(bf16[336,128]{1,0:T(8,128)(2,1)} %get-tuple-element.32.refs_3_.refs_4_.refs_0_) | copy-start | bytes 258052
  9.1 1.2 %copy-start.5 = (f32[1,1,2,16384]{3,2,1,0:T(2,128)S(1)}, f32[1,1,2,16384]{3,2,1,0:T(2,128)}, u32[]{:S(2)}) copy-start(f32[1,1,2,16384]{3,2,1,0:T(2,128)} %param.21) | copy-start | bytes 393220
  10.2 9.5 %copy-start.6 = (f32[64,128]{1,0:T(8,128)S(1)}, f32[64,128]{1,0:T(8,128)}, u32[]{:S(2)}) copy-start(f32[64,128]{1,0:T(8,128)} %mixing.2) | copy-start | bytes 98308
  10.8 6.0 %collective-permute-start.6 = (bf16[112,128]{1,0:T(8,128)(2,1)S(1)}, bf16[112,128]{1,0:T(8,128)(2,1)S(1)}, u32[]{:S(2)}, u32[]{:S(2)}) collective-permute-start(bf16[112,128]{1,0:T(8,128)(2,1)S(1)} %get-tuple-element.33.refs_0_), channel_id=1, source_target_pairs={{0,12},{4,8},{8,4},{12,0},{1,13},{5,9},{9,5},{13,1},{2,14},{6,10},... | collective-permute-start | bytes 86024 | tf_op jit(solution)/shard_map/ppermute | solution.py:601
  14.9 4.8 %collective-permute-start.5 = (bf16[112,128]{1,0:T(8,128)(2,1)S(1)}, bf16[112,128]{1,0:T(8,128)(2,1)S(1)}, u32[]{:S(2)}, u32[]{:S(2)}) collective-permute-start(bf16[112,128]{1,0:T(8,128)(2,1)S(1)} %get-tuple-element.33.refs_0_), channel_id=1, source_target_pairs={{0,8},{4,12},{8,0},{12,4},{1,9},{5,13},{9,1},{13,5},{2,10},{6,14},... | collective-permute-start | bytes 86024 | tf_op jit(solution)/shard_map/ppermute | solution.py:601
  14.9 4.8 %collective-permute-start.4 = (bf16[112,128]{1,0:T(8,128)(2,1)S(1)}, bf16[112,128]{1,0:T(8,128)(2,1)S(1)}, u32[]{:S(2)}, u32[]{:S(2)}) collective-permute-start(bf16[112,128]{1,0:T(8,128)(2,1)S(1)} %get-tuple-element.33.refs_0_), channel_id=1, source_target_pairs={{0,4},{4,0},{8,12},{12,8},{1,5},{5,1},{9,13},{13,9},{2,6},{6,2},{1... | collective-permute-start | bytes 86024 | tf_op jit(solution)/shard_map/ppermute | solution.py:601
  20.1 4.9 %collective-permute-start.8 = (bf16[448,128]{1,0:T(8,128)(2,1)S(1)}, bf16[448,128]{1,0:T(8,128)(2,1)S(1)}, u32[]{:S(2)}, u32[]{:S(2)}) collective-permute-start(bf16[448,128]{1,0:T(8,128)(2,1)S(1)} %shard_map.133.refs_0_.refs_4_), channel_id=1, source_target_pairs={{0,2},{1,3},{2,0},{3,1},{4,6},{5,7},{6,4},{7,5},{8,10},{9,11},{10,... | collective-permute-start | bytes 344072 | tf_op jit(solution)/shard_map/ppermute | solution.py:606
  22.2 2.9 %collective-permute-start.7 = (bf16[448,128]{1,0:T(8,128)(2,1)S(1)}, bf16[448,128]{1,0:T(8,128)(2,1)S(1)}, u32[]{:S(2)}, u32[]{:S(2)}) collective-permute-start(bf16[448,128]{1,0:T(8,128)(2,1)S(1)} %shard_map.133.refs_0_.refs_4_), channel_id=1, source_target_pairs={{0,1},{1,0},{2,3},{3,2},{4,5},{5,4},{6,7},{7,6},{8,9},{9,8},{10,11... | collective-permute-start | bytes 344072 | tf_op jit(solution)/shard_map/ppermute | solution.py:612
  25.0 1.3 %collective-permute-start.9 = (bf16[448,128]{1,0:T(8,128)(2,1)S(1)}, bf16[448,128]{1,0:T(8,128)(2,1)S(1)}, u32[]{:S(2)}, u32[]{:S(2)}) collective-permute-start(bf16[448,128]{1,0:T(8,128)(2,1)S(1)} %collective-permute-done.8.refs_2_.refs_6_), channel_id=1, source_target_pairs={{0,1},{1,0},{2,3},{3,2},{4,5},{5,4},{6,7},{7,6},{8,9},{9,8},{10,11... | collective-permute-start | bytes 344072 | tf_op jit(solution)/shard_map/ppermute | solution.py:612
  28.5 7.0 %copy-start.7 = (f32[2,64,128]{2,1,0:T(8,128)S(1)}, f32[2,64,128]{2,1,0:T(8,128)}, u32[]{:S(2)}) copy-start(f32[2,64,128]{2,1,0:T(8,128)} %currents.1) | copy-start | bytes 196612
  29.6 3.9 %collective-permute-start.10 = (bf16[192,128]{1,0:T(8,128)(2,1)S(1)}, bf16[192,128]{1,0:T(8,128)(2,1)S(1)}, u32[]{:S(2)}, u32[]{:S(2)}) collective-permute-start(bf16[192,128]{1,0:T(8,128)(2,1)S(1)} %get-tuple-element.42), channel_id=1, source_target_pairs={{0,3},{1,2},{2,1},{3,0},{4,7},{5,6},{6,5},{7,4},{8,11},{9,10},{10,... | collective-permute-start | bytes 147464 | tf_op jit(solution)/shard_map/ppermute | solution.py:618
  31.4 4.1 %collective-permute-start.11 = (bf16[192,128]{1,0:T(8,128)(2,1)S(1)}, bf16[192,128]{1,0:T(8,128)(2,1)S(1)}, u32[]{:S(2)}, u32[]{:S(2)}) collective-permute-start(bf16[192,128]{1,0:T(8,128)(2,1)S(1)} %get-tuple-element.43), channel_id=1, source_target_pairs={{0,2},{1,3},{2,0},{3,1},{4,6},{5,7},{6,4},{7,5},{8,10},{9,11},{10,... | collective-permute-start | bytes 147464 | tf_op jit(solution)/shard_map/ppermute | solution.py:618
  31.7 3.8 %collective-permute-start.12 = (bf16[192,128]{1,0:T(8,128)(2,1)S(1)}, bf16[192,128]{1,0:T(8,128)(2,1)S(1)}, u32[]{:S(2)}, u32[]{:S(2)}) collective-permute-start(bf16[192,128]{1,0:T(8,128)(2,1)S(1)} %get-tuple-element.44), channel_id=1, source_target_pairs={{0,1},{1,0},{2,3},{3,2},{4,5},{5,4},{6,7},{7,6},{8,9},{9,8},{10,11... | collective-permute-start | bytes 147464 | tf_op jit(solution)/shard_map/ppermute | solution.py:618

commit v11 on v10

--- a/solution.py
+++ b/solution.py
@@ -525,14 +525,27 @@
     for c in range(2):
         fluxes.append((drag[...] * (speed[c] - current[c])).astype(BF16))
     wide = jnp.concatenate(fluxes, axis=1)
-    for chunk, out in zip(chunks, outs):
+    own, beside = outs
+    step = 3 * side
+    for k, chunk in enumerate(chunks):
         part = jnp.dot(chunk[0:side], wide, preferred_element_type=F32).astype(BF16)
         part = jnp.concatenate([part[:, c * size : (c + 1) * size] for c in range(3)], axis=0)
         reply = jnp.dot(part, chunk[side : side + depth], preferred_element_type=F32)
-        out[...] = reply.astype(BF16)
-
-
-def finish_kernel(warm, currents, speed, *refs):
+        at = k // 2 * step
+        if k % 2:
+            beside[at : at + step] = reply.astype(BF16)
+        else:
+            own[at : at + step] = reply
+
+
+def pair_kernel(own, beside, *outs):
+    step = outs[0].shape[0]
+    for k, out in enumerate(outs):
+        at = (k + 1) * step
+        out[...] = (own[at : at + step] + beside[at : at + step].astype(F32)).astype(BF16)
+
+
+def finish_kernel(warm, currents, speed, own, beside, *refs):
     outs, (flat, heat_v, current_v, left) = refs[-7:-4], refs[-4:]
     replies = refs[:-7]
     flat_o, heat_o, current_o = outs
@@ -546,10 +559,10 @@
     for c in range(2):
         flat[pl.ds(c, size, stride=2), :] = speed[c]
     copies[0].start()
-    total = replies[0][...].astype(F32)
-    for reply in replies[1:]:
+    side = currents.shape[1]
+    total = own[0 : 3 * side] + beside[0 : 3 * side].astype(F32)
+    for reply in replies:
         total = total + reply[...].astype(F32)
-    side = currents.shape[1]
     heat = THERMAL_DIFFUSE * total[0:side]
     for l in range(warm.shape[0]):
         heat_v[l] = warm[l] + heat
@@ -592,12 +605,9 @@
     def device_place():
         return lax.axis_index("tile") * group + member_place()
 
-    def far_first(count):
-        return [*range(2, count), 1]
-
     def swap(value, axes, count):
         got = {0: value}
-        for k in far_first(count):
+        for k in range(1, count):
             got[k] = lax.ppermute(value, axes, [(i, i ^ k) for i in range(count)])
         return [got[k] for k in range(count)]
 
@@ -614,7 +624,7 @@
 
     def swap_each(values):
         got = {0: values[0]}
-        for k in far_first(group):
+        for k in range(1, group):
             got[k] = lax.ppermute(values[k], group_axes, [(i, i ^ k) for i in range(group)])
         return [got[k] for k in range(group)]
 
@@ -734,18 +744,27 @@
         hbm=(0,),
     )
 
-    replies = call(
+    step = 3 * side
+    own, beside = call(
         functools.partial(back_kernel, group, side),
-        [shape(3 * side, width, dtype=BF16)] * group,
+        [shape(group // 2 * step, width), shape(group // 2 * step, width, dtype=BF16)],
         (drag, conduct, current_ice, speed, *chunks, *relays),
     )
-    replies = swap_each(replies)
+    beside = lax.ppermute(beside, group_axes, [(i, i ^ 1) for i in range(group)])
+    paired = call(
+        pair_kernel, [shape(step, width, dtype=BF16)] * (group // 2 - 1), (own, beside)
+    )
+    replies = [
+        lax.ppermute(value, group_axes, [(i, i ^ (2 * k + 2)) for i in range(group)])
+        for k, value in enumerate(paired)
+    ]
     if lev_count > 1:
-        replies = [lax.psum(sum(r.astype(F32) for r in replies), "lev")]
+        parts = [r.astype(F32) for r in (own[:step], beside[:step], *replies)]
+        own, beside, replies = lax.psum(sum(parts), "lev"), jnp.zeros_like(beside[:step]), []
     flat, heat, current = call(
         finish_kernel,
         [shape(2 * size, size), shape(levels, side, width), shape(2, side, width)],
-        (warm, upper_current_vector, speed, *replies[::-1]),
+        (warm, upper_current_vector, speed, own, beside, *replies),
         scratch=[
             pltpu.VMEM((2 * size, size), F32),
             pltpu.VMEM((levels, side, width), F32),

time: 36.4 us -> 36 us (0.989)
  waiting for transfers between devices: 14.2 us -> 13.7 us
    ppermute x6 -> x3, waiting for transfers between devices: 6.95 us -> 3.21 us  [swap_each(): lax.ppermute(values[k], group_axes, [(i, i ^ k) for i in range(group)])]
    ppermute x0 -> x2, waiting for transfers between devices: none -> 3.27 us  [the longest x1 2.11 us: shards(): lax.ppermute(value, group_axes, [(i, i ^ 2 * k + 2) for i in range(group)])]
    ppermute x0 -> x2, starting transfers between devices: none -> 2.2 us  [the longest x1 2.05 us: shards(): lax.ppermute(value, group_axes, [(i, i ^ 2 * k + 2) for i in range(group)])]
    ppermute x6 -> x3, starting transfers between devices: 5.31 us -> 3.21 us  [swap_each(): lax.ppermute(values[k], group_axes, [(i, i ^ k) for i in range(group)])]
    pallas_call x8 -> x9, Pallas kernels: 8.85 us -> 8.86 us  [call(): pl.pallas_call(kernel, out_shape=outs, in_specs=specs, out_specs=jax.tree...]
  transfers between devices with their start and end apart: 13 -> 12, of which waited for: 9 -> 9; matrix products, arithmetic and copies ran while one was open for 0% -> 0% of each run, Pallas kernels for 4% -> 4%
where the time goes in v11:
time: 36 us; the launch traced here: 35.9 us
  waiting for transfers between devices  13.7 us (38%)
  starting transfers between devices  12.2 us (34%)
  Pallas kernels  8.86 us (25%)
  between operations  0.83 us (2%)
    pallas_call x9, Pallas kernels, call(): pl.pallas_call(kernel, out_shape=outs, in_specs=specs, out_specs=jax.tree...  8.86 us
    ppermute x3, starting transfers between devices, swap(): got[k] = lax.ppermute(value, axes, [(i, i ^ k) for i in range(count)])  4.76 us
    ppermute x3, waiting for transfers between devices, swap(): got[k] = lax.ppermute(value, axes, [(i, i ^ k) for i in range(count)])  4.13 us
    ppermute x3, waiting for transfers between devices, swap_each(): lax.ppermute(values[k], group_axes, [(i, i ^ k) for i in range(group)])  3.21 us
    ppermute x3, starting transfers between devices, swap_each(): lax.ppermute(values[k], group_axes, [(i, i ^ k) for i in range(group)])  3.21 us
    ppermute x1, waiting for transfers between devices, shards(): lax.ppermute(value, group_axes, [(i, i ^ 2 * k + 2) for i in range(group)])  2.11 us
    ppermute x1, starting transfers between devices, swap_chips(): lax.ppermute(value, group_axes, [(i, i ^ k) for i in range(group)])  2.05 us
    ppermute x1, starting transfers between devices, shards(): lax.ppermute(value, group_axes, [(i, i ^ 2 * k + 2) for i in range(group)])  2.05 us
  transfers between devices with their start and end apart: 12, of which 9 were waited for; matrix products, arithmetic and copies ran while one was open for 0% of the time, Pallas kernels for 4%

profile of v11, /device:TPU:0, one launch (start us, length us, event | category | flops | bytes accessed | tf_op | source)
XLA Modules:
  0.0 35.9 jit_solution(10491614827036769455)
XLA Ops:
  0.6 0.0 copy-start.1
  0.6 0.0 copy-start.2
  0.7 0.0 copy-start.3
  0.7 0.0 copy-start.4
  0.7 2.6 %shard_map.131 = (bf16[336,128]{1,0:T(8,128)(2,1)}, bf16[336,128]{1,0:T(8,128)(2,1)}, bf16[336,128]{1,0:T(8,128)(2,1)}, bf16[192,128]{1,0:T(8,128)(2,1)}) custom-call(s32[1,1,4]{2,1,0:T(1,128)} %links_h.1, s32[1,4]{1,0:T(1,128)} %blocks_h.1, bf16[4,64,128]{2,1,0:T(8,128)(2,1)} %bitcast.38, bf16[4,128,128]{2,1,0:T(8,128)(2,1)} %bitcast.36, ...), custom_call_target="tpu_custom_call" | custom-call | flops 11500000256 | bytes 393248 | tf_op jit(solution)/shard_map/pallas_call | solution.py:42
  3.3 3.0 %collective-permute-start.1 = (bf16[336,128]{1,0:T(8,128)(2,1)}, bf16[336,128]{1,0:T(8,128)(2,1)S(1)}, u32[]{:S(2)}, u32[]{:S(2)}) collective-permute-start(bf16[336,128]{1,0:T(8,128)(2,1)} %get-tuple-element.28), channel_id=1, source_target_pairs={{0,2},{1,3},{2,0},{3,1},{4,6},{5,7},{6,4},{7,5},{8,10},{9,11},{10,... | collective-permute-start | bytes 258056 | tf_op jit(solution)/shard_map/ppermute | solution.py:628
  6.3 0.0 collective-permute-start.2
  6.3 0.2 collective-permute-start
  6.5 2.5 %collective-permute-done.1.refs_1_.refs_6_.refs_2_ = bf16[336,128]{1,0:T(8,128)(2,1)S(1)} collective-permute-done((bf16[336,128]{1,0:T(8,128)(2,1)}, bf16[336,128]{1,0:T(8,128)(2,1)S(1)}, u32[]{:S(2)}, u32[]{:S(2)}) %collective-permute-start.1) | collective-permute-done | bytes 86048 | tf_op jit(solution)/shard_map/ppermute | solution.py:628
  9.0 0.0 collective-permute-start.3
  9.0 0.0 copy-done.1
  9.0 0.0 copy-done.2
  9.0 0.0 copy-done.3
  9.0 0.0 copy-done.4
  9.0 0.0 copy-start
  9.1 0.0 copy-start.5
  9.1 0.2 shard_map.130
  9.3 0.7 %collective-permute-done.refs_0_.refs_7_.refs_3_ = bf16[192,128]{1,0:T(8,128)(2,1)S(1)} collective-permute-done((bf16[192,128]{1,0:T(8,128)(2,1)}, bf16[192,128]{1,0:T(8,128)(2,1)S(1)}, u32[]{:S(2)}, u32[]{:S(2)}) %collective-permute-start) | collective-permute-done | bytes 49184 | tf_op jit(solution)/shard_map/ppermute | solution.py:628
  10.0 0.0 collective-permute-done.2.refs_2_.refs_5_.refs_1_
  10.0 0.2 collective-permute-done.3.refs_4_.refs_8_
  10.2 0.0 copy-done
  10.2 0.0 copy-done.5
  10.2 0.0 copy-start.6
  10.2 0.6 %shard_map.132 = (bf16[112,128]{1,0:T(8,128)(2,1)S(1)}, f32[2,128,128]{2,1,0:T(8,128)S(1)}, f32[2,128,128]{2,1,0:T(8,128)S(1)}) custom-call(f32[128,128]{1,0:T(8,128)S(1)} %get-tuple-element.24.mass, f32[128,128]{1,0:T(8,128)S(1)} %get-tuple-element.25.drag, f32[256,128]{1,0:T(8,128)S(1)} %bitcast.30, bf16[80,128]{1,0:T(8,128)(2,1)S(1)} %get-tuple-element.26.early, ...), custom_call_target="tpu_custom_call" | custom-call | flops 11500000 | bytes 626688 | tf_op jit(solution)/shard_map/pallas_call | solution.py:42
  10.8 4.1 %collective-permute-start.6 = (bf16[112,128]{1,0:T(8,128)(2,1)S(1)}, bf16[112,128]{1,0:T(8,128)(2,1)S(1)}, u32[]{:S(2)}, u32[]{:S(2)}) collective-permute-start(bf16[112,128]{1,0:T(8,128)(2,1)S(1)} %get-tuple-element.31.refs_0_), channel_id=1, source_target_pairs={{0,12},{4,8},{8,4},{12,0},{1,13},{5,9},{9,5},{13,1},{2,14},{6,10},... | collective-permute-start | bytes 86024 | tf_op jit(solution)/shard_map/ppermute | solution.py:611
  14.9 0.0 collective-permute-start.5
  14.9 0.6 %collective-permute-start.4 = (bf16[112,128]{1,0:T(8,128)(2,1)S(1)}, bf16[112,128]{1,0:T(8,128)(2,1)S(1)}, u32[]{:S(2)}, u32[]{:S(2)}) collective-permute-start(bf16[112,128]{1,0:T(8,128)(2,1)S(1)} %get-tuple-element.31.refs_0_), channel_id=1, source_target_pairs={{0,4},{4,0},{8,12},{12,8},{1,5},{5,1},{9,13},{13,9},{2,6},{6,2},{1... | collective-permute-start | bytes 86024 | tf_op jit(solution)/shard_map/ppermute | solution.py:611
  15.6 1.2 %collective-permute-done.6.refs_3_ = bf16[112,128]{1,0:T(8,128)(2,1)S(1)} collective-permute-done((bf16[112,128]{1,0:T(8,128)(2,1)S(1)}, bf16[112,128]{1,0:T(8,128)(2,1)S(1)}, u32[]{:S(2)}, u32[]{:S(2)}) %collective-permute-start.6) | collective-permute-done | bytes 28704 | tf_op jit(solution)/shard_map/ppermute | solution.py:611
  16.8 2.9 %collective-permute-done.5.refs_2_ = bf16[112,128]{1,0:T(8,128)(2,1)S(1)} collective-permute-done((bf16[112,128]{1,0:T(8,128)(2,1)S(1)}, bf16[112,128]{1,0:T(8,128)(2,1)S(1)}, u32[]{:S(2)}, u32[]{:S(2)}) %collective-permute-start.5) | collective-permute-done | bytes 28704 | tf_op jit(solution)/shard_map/ppermute | solution.py:611
  19.7 0.0 collective-permute-done.4.refs_1_
  19.7 0.0 copy-done.6
  19.7 0.4 %shard_map.133.refs_0_.refs_4_ = bf16[448,128]{1,0:T(8,128)(2,1)S(1)} custom-call(f32[4,64,128]{2,1,0:T(8,128)S(1)} %copy-done.1, f32[64,128]{1,0:T(8,128)S(1)} %copy-done.6, bf16[112,128]{1,0:T(8,128)(2,1)S(1)} %get-tuple-element.31.refs_0_, bf16[112,128]{1,0:T(8,128)(2,1)S(1)} %collective-permute-done.4.refs_1_, ...), custom_call_target="tpu_custom_call" | custom-call | flops 11500000 | bytes 622592 | tf_op jit(solution)/shard_map/pallas_call | solution.py:42
  20.1 2.0 %collective-permute-start.8 = (bf16[448,128]{1,0:T(8,128)(2,1)S(1)}, bf16[448,128]{1,0:T(8,128)(2,1)S(1)}, u32[]{:S(2)}, u32[]{:S(2)}) collective-permute-start(bf16[448,128]{1,0:T(8,128)(2,1)S(1)} %shard_map.133.refs_0_.refs_4_), channel_id=1, source_target_pairs={{0,2},{1,3},{2,0},{3,1},{4,6},{5,7},{6,4},{7,5},{8,10},{9,11},{10,... | collective-permute-start | bytes 344072 | tf_op jit(solution)/shard_map/ppermute | solution.py:616
  22.2 0.0 collective-permute-start.7
  22.2 1.1 %shard_map.134.warm = f32[4,64,128]{2,1,0:T(8,128)S(1)} custom-call(f32[4,64,128]{2,1,0:T(8,128)S(1)} %copy-done.1, f32[64,128]{1,0:T(8,128)S(1)} %copy-done.6, bf16[112,128]{1,0:T(8,128)(2,1)S(1)} %get-tuple-element.31.refs_0_, bf16[112,128]{1,0:T(8,128)(2,1)S(1)} %collective-permute-done.4.refs_1_, bf16[112,128]{1,0:T(8,128)(2,1)S(1)} %collective-permute-done.5.refs_2_, ...), custom_call_target="tpu_custom_call" | custom-call | flops 11500000 | bytes 622592 | tf_op jit(solution)/shard_map/pallas_call | solution.py:42
  23.3 1.7 %collective-permute-done.8.refs_2_.refs_6_ = bf16[448,128]{1,0:T(8,128)(2,1)S(1)} collective-permute-done((bf16[448,128]{1,0:T(8,128)(2,1)S(1)}, bf16[448,128]{1,0:T(8,128)(2,1)S(1)}, u32[]{:S(2)}, u32[]{:S(2)}) %collective-permute-start.8) | collective-permute-done | bytes 114720 | tf_op jit(solution)/shard_map/ppermute | solution.py:616
  25.0 0.0 collective-permute-start.9
  25.0 0.0 collective-permute-done.7.refs_1_.refs_5_
  25.1 1.2 %collective-permute-done.9.refs_3_.refs_7_ = bf16[448,128]{1,0:T(8,128)(2,1)S(1)} collective-permute-done((bf16[448,128]{1,0:T(8,128)(2,1)S(1)}, bf16[448,128]{1,0:T(8,128)(2,1)S(1)}, u32[]{:S(2)}, u32[]{:S(2)}) %collective-permute-start.9) | collective-permute-done | bytes 114720 | tf_op jit(solution)/shard_map/ppermute | solution.py:622
  26.4 0.1 xor_select_fusion.table
  26.5 2.1 %shard_map.135.speed = f32[2,128,128]{2,1,0:T(8,128)S(1)} custom-call(s32[16,4]{1,0:T(8,128)S(1)} %xor_select_fusion.table, f32[128,128]{1,0:T(8,128)S(1)} %get-tuple-element.34.viscous, f32[128,128]{1,0:T(8,128)S(1)} %get-tuple-element.35.gain, f32[2,128,128]{2,1,0:T(8,128)S(1)} %get-tuple-element.36.speed, f32[2,128,128]{2,1,0:T(8,128)S(1)} %get-tuple-element.37.push, ...), custom_call_target="tpu_custom_call" | custom-call | flops 11500000 | bytes 852224 | tf_op jit(solution)/shard_map/pallas_call | solution.py:42
  28.5 1.1 %shard_map.136 = (f32[384,128]{1,0:T(8,128)S(1)}, bf16[384,128]{1,0:T(8,128)(2,1)S(1)}) custom-call(f32[128,128]{1,0:T(8,128)S(1)} %get-tuple-element.25.drag, f32[128,128]{1,0:T(8,128)S(1)} %get-tuple-element.38.conduct, f32[2,128,128]{2,1,0:T(8,128)S(1)} %get-tuple-element.39.current, f32[2,128,128]{2,1,0:T(8,128)S(1)} %shard_map.135.speed, ...), custom_call_target="tpu_custom_call" | custom-call | flops 11500000 | bytes 1159168 | tf_op jit(solution)/shard_map/pallas_call | solution.py:42
  29.6 0.2 collective-permute-start.10
  29.8 1.2 %collective-permute-done.10.beside = bf16[384,128]{1,0:T(8,128)(2,1)S(1)} collective-permute-done((bf16[384,128]{1,0:T(8,128)(2,1)S(1)}, bf16[384,128]{1,0:T(8,128)(2,1)S(1)}, u32[]{:S(2)}, u32[]{:S(2)}) %collective-permute-start.10) | collective-permute-done | bytes 98336 | tf_op jit(solution)/shard_map/ppermute | solution.py:753
  30.9 0.0 copy-start.7
  31.0 2.0 %collective-permute-start.11 = (bf16[192,128]{1,0:T(8,128)(2,1)S(1)}, bf16[192,128]{1,0:T(8,128)(2,1)S(1)}, u32[]{:S(2)}, u32[]{:S(2)}) collective-permute-start(bf16[192,128]{1,0:T(8,128)(2,1)S(1)} %shard_map.137), channel_id=1, source_target_pairs={{0,2},{1,3},{2,0},{3,1},{4,6},{5,7},{6,4},{7,5},{8,10},{9,11},{10,... | collective-permute-start | bytes 147464 | tf_op jit(solution)/shard_map/ppermute | solution.py:758
  33.0 2.1 %collective-permute-done.11.refs_0_ = bf16[192,128]{1,0:T(8,128)(2,1)S(1)} collective-permute-done((bf16[192,128]{1,0:T(8,128)(2,1)S(1)}, bf16[192,128]{1,0:T(8,128)(2,1)S(1)}, u32[]{:S(2)}, u32[]{:S(2)}) %collective-permute-start.11) | collective-permute-done | bytes 49184 | tf_op jit(solution)/shard_map/ppermute | solution.py:758
  35.1 0.0 copy-done.7
  35.1 0.8 %shard_map.138 = (f32[256,128]{1,0:T(8,128)}, f32[4,64,128]{2,1,0:T(8,128)}, f32[2,64,128]{2,1,0:T(8,128)}) custom-call(f32[4,64,128]{2,1,0:T(8,128)S(1)} %shard_map.134.warm, f32[2,64,128]{2,1,0:T(8,128)S(1)} %copy-done.7, f32[2,128,128]{2,1,0:T(8,128)S(1)} %shard_map.135.speed, f32[384,128]{1,0:T(8,128)S(1)} %get-tuple-element.40.own, ...), custom_call_target="tpu_custom_call" | custom-call | flops 11500000 | bytes 671744 | tf_op jit(solution)/shard_map/pallas_call | solution.py:42
  (12 shorter events, 0.1 us)
Async XLA Ops:
  0.6 8.4 %copy-start.1 = (f32[4,64,128]{2,1,0:T(8,128)S(1)}, f32[4,64,128]{2,1,0:T(8,128)}, u32[]{:S(2)}) copy-start(f32[4,64,128]{2,1,0:T(8,128)} %water.5) | copy-start | bytes 393220
  0.6 8.4 %copy-start.2 = (f32[1,1,5,16384]{3,1,2,0:T(1,128)S(1)}, f32[1,1,5,16384]{3,1,2,0:T(1,128)}, u32[]{:S(2)}) copy-start(f32[1,1,5,16384]{3,1,2,0:T(1,128)} %param.18) | copy-start | bytes 983044
  0.7 8.4 %copy-start.3 = (f32[1,1,5,16384]{3,1,2,0:T(1,128)S(1)}, f32[1,1,5,16384]{3,1,2,0:T(1,128)}, u32[]{:S(2)}) copy-start(f32[1,1,5,16384]{3,1,2,0:T(1,128)} %param.19) | copy-start | bytes 983044
  0.7 8.4 %copy-start.4 = (f32[1,1,2,16384]{3,2,1,0:T(2,128)S(1)}, f32[1,1,2,16384]{3,2,1,0:T(2,128)}, u32[]{:S(2)}) copy-start(f32[1,1,2,16384]{3,2,1,0:T(2,128)} %param.20) | copy-start | bytes 393220
  3.3 5.7 %collective-permute-start.1 = (bf16[336,128]{1,0:T(8,128)(2,1)}, bf16[336,128]{1,0:T(8,128)(2,1)S(1)}, u32[]{:S(2)}, u32[]{:S(2)}) collective-permute-start(bf16[336,128]{1,0:T(8,128)(2,1)} %get-tuple-element.28), channel_id=1, source_target_pairs={{0,2},{1,3},{2,0},{3,1},{4,6},{5,7},{6,4},{7,5},{8,10},{9,11},{10,... | collective-permute-start | bytes 258056 | tf_op jit(solution)/shard_map/ppermute | solution.py:628
  6.3 3.7 %collective-permute-start.2 = (bf16[336,128]{1,0:T(8,128)(2,1)}, bf16[336,128]{1,0:T(8,128)(2,1)S(1)}, u32[]{:S(2)}, u32[]{:S(2)}) collective-permute-start(bf16[336,128]{1,0:T(8,128)(2,1)} %get-tuple-element.29), channel_id=1, source_target_pairs={{0,1},{1,0},{2,3},{3,2},{4,5},{5,4},{6,7},{7,6},{8,9},{9,8},{10,11... | collective-permute-start | bytes 258056 | tf_op jit(solution)/shard_map/ppermute | solution.py:628
  6.3 3.7 %collective-permute-start = (bf16[192,128]{1,0:T(8,128)(2,1)}, bf16[192,128]{1,0:T(8,128)(2,1)S(1)}, u32[]{:S(2)}, u32[]{:S(2)}) collective-permute-start(bf16[192,128]{1,0:T(8,128)(2,1)} %get-tuple-element.27), channel_id=1, source_target_pairs={{0,3},{1,2},{2,1},{3,0},{4,7},{5,6},{6,5},{7,4},{8,11},{9,10},{10,... | collective-permute-start | bytes 147464 | tf_op jit(solution)/shard_map/ppermute | solution.py:628
  9.0 1.2 %collective-permute-start.3 = (bf16[144,128]{1,0:T(8,128)(2,1)S(1)}, bf16[144,128]{1,0:T(8,128)(2,1)S(1)}, u32[]{:S(2)}, u32[]{:S(2)}) collective-permute-start(bf16[144,128]{1,0:T(8,128)(2,1)S(1)} %slice.44), channel_id=1, source_target_pairs={{0,1},{1,0},{2,3},{3,2},{4,5},{5,4},{6,7},{7,6},{8,9},{9,8},{10,11... | collective-permute-start | bytes 110600 | tf_op jit(solution)/shard_map/ppermute | solution.py:677
  9.0 1.2 %copy-start = (bf16[336,128]{1,0:T(8,128)(2,1)S(1)}, bf16[336,128]{1,0:T(8,128)(2,1)}, u32[]{:S(2)}) copy-start(bf16[336,128]{1,0:T(8,128)(2,1)} %get-tuple-element.30.refs_3_.refs_4_.refs_0_) | copy-start | bytes 258052
  9.1 1.2 %copy-start.5 = (f32[1,1,2,16384]{3,2,1,0:T(2,128)S(1)}, f32[1,1,2,16384]{3,2,1,0:T(2,128)}, u32[]{:S(2)}) copy-start(f32[1,1,2,16384]{3,2,1,0:T(2,128)} %param.21) | copy-start | bytes 393220
  10.2 9.5 %copy-start.6 = (f32[64,128]{1,0:T(8,128)S(1)}, f32[64,128]{1,0:T(8,128)}, u32[]{:S(2)}) copy-start(f32[64,128]{1,0:T(8,128)} %mixing.2) | copy-start | bytes 98308
  10.8 6.0 %collective-permute-start.6 = (bf16[112,128]{1,0:T(8,128)(2,1)S(1)}, bf16[112,128]{1,0:T(8,128)(2,1)S(1)}, u32[]{:S(2)}, u32[]{:S(2)}) collective-permute-start(bf16[112,128]{1,0:T(8,128)(2,1)S(1)} %get-tuple-element.31.refs_0_), channel_id=1, source_target_pairs={{0,12},{4,8},{8,4},{12,0},{1,13},{5,9},{9,5},{13,1},{2,14},{6,10},... | collective-permute-start | bytes 86024 | tf_op jit(solution)/shard_map/ppermute | solution.py:611
  14.9 4.8 %collective-permute-start.5 = (bf16[112,128]{1,0:T(8,128)(2,1)S(1)}, bf16[112,128]{1,0:T(8,128)(2,1)S(1)}, u32[]{:S(2)}, u32[]{:S(2)}) collective-permute-start(bf16[112,128]{1,0:T(8,128)(2,1)S(1)} %get-tuple-element.31.refs_0_), channel_id=1, source_target_pairs={{0,8},{4,12},{8,0},{12,4},{1,9},{5,13},{9,1},{13,5},{2,10},{6,14},... | collective-permute-start | bytes 86024 | tf_op jit(solution)/shard_map/ppermute | solution.py:611
  14.9 4.8 %collective-permute-start.4 = (bf16[112,128]{1,0:T(8,128)(2,1)S(1)}, bf16[112,128]{1,0:T(8,128)(2,1)S(1)}, u32[]{:S(2)}, u32[]{:S(2)}) collective-permute-start(bf16[112,128]{1,0:T(8,128)(2,1)S(1)} %get-tuple-element.31.refs_0_), channel_id=1, source_target_pairs={{0,4},{4,0},{8,12},{12,8},{1,5},{5,1},{9,13},{13,9},{2,6},{6,2},{1... | collective-permute-start | bytes 86024 | tf_op jit(solution)/shard_map/ppermute | solution.py:611
  20.1 4.9 %collective-permute-start.8 = (bf16[448,128]{1,0:T(8,128)(2,1)S(1)}, bf16[448,128]{1,0:T(8,128)(2,1)S(1)}, u32[]{:S(2)}, u32[]{:S(2)}) collective-permute-start(bf16[448,128]{1,0:T(8,128)(2,1)S(1)} %shard_map.133.refs_0_.refs_4_), channel_id=1, source_target_pairs={{0,2},{1,3},{2,0},{3,1},{4,6},{5,7},{6,4},{7,5},{8,10},{9,11},{10,... | collective-permute-start | bytes 344072 | tf_op jit(solution)/shard_map/ppermute | solution.py:616
  22.2 2.9 %collective-permute-start.7 = (bf16[448,128]{1,0:T(8,128)(2,1)S(1)}, bf16[448,128]{1,0:T(8,128)(2,1)S(1)}, u32[]{:S(2)}, u32[]{:S(2)}) collective-permute-start(bf16[448,128]{1,0:T(8,128)(2,1)S(1)} %shard_map.133.refs_0_.refs_4_), channel_id=1, source_target_pairs={{0,1},{1,0},{2,3},{3,2},{4,5},{5,4},{6,7},{7,6},{8,9},{9,8},{10,11... | collective-permute-start | bytes 344072 | tf_op jit(solution)/shard_map/ppermute | solution.py:622
  25.0 1.3 %collective-permute-start.9 = (bf16[448,128]{1,0:T(8,128)(2,1)S(1)}, bf16[448,128]{1,0:T(8,128)(2,1)S(1)}, u32[]{:S(2)}, u32[]{:S(2)}) collective-permute-start(bf16[448,128]{1,0:T(8,128)(2,1)S(1)} %collective-permute-done.8.refs_2_.refs_6_), channel_id=1, source_target_pairs={{0,1},{1,0},{2,3},{3,2},{4,5},{5,4},{6,7},{7,6},{8,9},{9,8},{10,11... | collective-permute-start | bytes 344072 | tf_op jit(solution)/shard_map/ppermute | solution.py:622
  29.6 1.3 %collective-permute-start.10 = (bf16[384,128]{1,0:T(8,128)(2,1)S(1)}, bf16[384,128]{1,0:T(8,128)(2,1)S(1)}, u32[]{:S(2)}, u32[]{:S(2)}) collective-permute-start(bf16[384,128]{1,0:T(8,128)(2,1)S(1)} %get-tuple-element.41), channel_id=1, source_target_pairs={{0,1},{1,0},{2,3},{3,2},{4,5},{5,4},{6,7},{7,6},{8,9},{9,8},{10,11... | collective-permute-start | bytes 294920 | tf_op jit(solution)/shard_map/ppermute | solution.py:753
  30.9 4.2 %copy-start.7 = (f32[2,64,128]{2,1,0:T(8,128)S(1)}, f32[2,64,128]{2,1,0:T(8,128)}, u32[]{:S(2)}) copy-start(f32[2,64,128]{2,1,0:T(8,128)} %currents.1) | copy-start | bytes 196612
  31.0 4.2 %collective-permute-start.11 = (bf16[192,128]{1,0:T(8,128)(2,1)S(1)}, bf16[192,128]{1,0:T(8,128)(2,1)S(1)}, u32[]{:S(2)}, u32[]{:S(2)}) collective-permute-start(bf16[192,128]{1,0:T(8,128)(2,1)S(1)} %shard_map.137), channel_id=1, source_target_pairs={{0,2},{1,3},{2,0},{3,1},{4,6},{5,7},{6,4},{7,5},{8,10},{9,11},{10,... | collective-permute-start | bytes 147464 | tf_op jit(solution)/shard_map/ppermute | solution.py:758

commit v12 on v11

--- a/solution.py
+++ b/solution.py
@@ -84,9 +84,9 @@
 def forward_kernel(group, links_h, blocks_h, rows_h, cols_h, currents_h, water_h, *refs):
     devices, members, place = group
     outs, scratch = refs[:members], refs[members:]
-    links, blocks, currents, rows, cols, water, fields, tail, kept, arrived, left = scratch
+    links, blocks, currents, weights, water, fields, kept, arrived, left = scratch
     pairs, side, width = rows_h.shape
-    depth = cols_h.shape[1]
+    both = weights.shape[1]
     loads = [
         pltpu.make_async_copy(source, target, arrived.at[i])
         for i, (source, target) in enumerate(
@@ -94,8 +94,8 @@
                 (links_h, links),
                 (blocks_h, blocks),
                 (currents_h, currents),
-                (rows_h, rows),
-                (cols_h, cols),
+                (rows_h, weights.at[:, pl.ds(0, side)]),
+                (cols_h, weights.at[:, pl.ds(side, both - side)]),
                 (water_h, water),
             )
         )
@@ -105,7 +105,6 @@
     for i in (1, 3, 4):
         loads[i].wait()
     me = place()
-    side, depth, pairs = rows.shape[1], cols.shape[1], rows.shape[0]
     owners = [lax.rem(lax.rem(blocks[0, m], devices), members) for m in range(pairs)]
     copies = []
     for k, out in enumerate(outs):
@@ -113,40 +112,30 @@
         pair = jnp.int32(0)
         for m in range(pairs):
             pair = jnp.where(owners[m] == partner, m, pair)
+        source = weights.at[pair]
         if pairs < members:
             found = sum(flag(owners[m] == partner) for m in range(pairs))
-            kept[k] = (rows[pair].astype(F32) * found).astype(BF16)
-        at = 0
-        for i, source in enumerate((rows, cols)):
-            if i == 0 and pairs < members:
-                source, pair_at = kept, k
-            else:
-                pair_at = pair
-            target = out.at[pl.ds(at, source.shape[1])]
-            copies.append(pltpu.make_async_copy(source.at[pair_at], target, left.at[4 * k + i]))
-            copies[-1].start()
-            at += source.shape[1]
+            kept[k] = (weights[pair].astype(F32) * found).astype(BF16)
+            source = kept.at[k]
+        copies.append(pltpu.make_async_copy(source, out.at[pl.ds(0, both)], left.at[2 * k]))
+        copies[-1].start()
     for i in (0, 2, 5):
         loads[i].wait()
     for c in range(2):
-        fields[0, c * side : (c + 1) * side] = currents[c].astype(BF16)
+        fields[c * side : (c + 1) * side] = currents[c].astype(BF16)
     lane = iota((1, width), 1)
     numbers = jnp.zeros((1, width), F32)
     for q in range(4):
         numbers = jnp.where(lane == q, (links[0, 0, q] >> 7).astype(F32), numbers)
         numbers = jnp.where(lane == 4 + q, (links[0, 0, q] & 127).astype(F32), numbers)
     ends = ocean_columns(water) + [numbers]
-    blank = jnp.zeros((tail.shape[0] - len(ends), width), F32)
-    tail[...] = jnp.concatenate(ends + [blank], axis=0).astype(BF16)
+    blank = jnp.zeros((fields.shape[0] - 2 * side - len(ends), width), F32)
+    fields[2 * side :] = jnp.concatenate(ends + [blank], axis=0).astype(BF16)
     for k, out in enumerate(outs):
-        at = side + depth
-        if out.shape[0] == at:
-            continue
-        for i, source in enumerate((fields.at[0], tail)):
-            target = out.at[pl.ds(at, source.shape[0])]
-            copies.append(pltpu.make_async_copy(source, target, left.at[4 * k + 2 + i]))
+        if out.shape[0] > both:
+            target = out.at[pl.ds(both, fields.shape[0])]
+            copies.append(pltpu.make_async_copy(fields, target, left.at[2 * k + 1]))
             copies[-1].start()
-            at += source.shape[0]
     for copy in copies:
         copy.wait()
 
@@ -381,11 +370,17 @@
         warm_o[l] = x - mixing[...] * twice
 
 
-def subcycles_kernel(tiles, members, table, viscous, gain, speed, push, *refs):
-    relays, (out, rims, names, named) = refs[:members], refs[members:]
+def ice_kernel(
+    tiles, members, side, table, viscous, gain, drag, conduct, current, speed, push, *refs
+):
+    chunks, relays = refs[:members], refs[members : 2 * members]
+    out, own_o, beside_o, rims, names, named = refs[2 * members :]
     load_names = pltpu.make_async_copy(table, names, named)
     load_names.start()
     size = viscous.shape[0]
+    depth = chunks[0].shape[1]
+    warm = remap_forward(chunks, [[r[r.shape[0] - side :]] for r in relays], side, depth)
+    heat = (conduct[...] * warm).astype(BF16)
     for k in range(tiles):
         for m in range(members):
             rims[k * members + m] = relays[m][k * BLOCK_ROWS : (k + 1) * BLOCK_ROWS]
@@ -513,19 +508,13 @@
         vx, vy = new_x, new_y
     out[0] = vx
     out[1] = vy
-
-
-def back_kernel(group, side, drag, conduct, current, speed, *refs):
-    chunks, relays, outs = refs[:group], refs[group : 2 * group], refs[2 * group :]
-    size = drag.shape[0]
-    depth = chunks[0].shape[1]
-    warm = remap_forward(chunks, [[r[r.shape[0] - side :]] for r in relays], side, depth)
-    heat = conduct[...] * warm
-    fluxes = [heat.astype(BF16)]
-    for c in range(2):
-        fluxes.append((drag[...] * (speed[c] - current[c])).astype(BF16))
+    stress = [(drag[...] * (v - current[c])).astype(BF16) for c, v in enumerate((vx, vy))]
+    return_fluxes([heat, *stress], chunks, side, depth, own_o, beside_o)
+
+
+def return_fluxes(fluxes, chunks, side, depth, own, beside):
+    size = fluxes[0].shape[0]
     wide = jnp.concatenate(fluxes, axis=1)
-    own, beside = outs
     step = 3 * side
     for k, chunk in enumerate(chunks):
         part = jnp.dot(chunk[0:side], wide, preferred_element_type=F32).astype(BF16)
@@ -659,14 +648,12 @@
             pltpu.SMEM(neighbors.shape, jnp.int32),
             pltpu.SMEM((1, pairs), jnp.int32),
             pltpu.VMEM((2, side, width), F32),
-            pltpu.VMEM((pairs, side, size), BF16),
-            pltpu.VMEM((pairs, size, width), BF16),
+            pltpu.VMEM((pairs, pair_rows, width), BF16),
             pltpu.VMEM((levels, side, width), F32),
-            pltpu.VMEM((1, 2 * side, width), BF16),
-            pltpu.VMEM((tail_rows, width), BF16),
-            pltpu.VMEM((1 if pairs == group else group, side, size), BF16),
+            pltpu.VMEM((chunk_rows - pair_rows, width), BF16),
+            pltpu.VMEM((1 if pairs == group else group, pair_rows, width), BF16),
             pltpu.SemaphoreType.DMA((6,)),
-            pltpu.SemaphoreType.DMA((4 * group,)),
+            pltpu.SemaphoreType.DMA((2 * group,)),
         ],
         hbm=(0, 1, 2, 3, 4, 5),
         grant=60 * 2**20,
@@ -732,23 +719,21 @@
     names = names.reshape(devices, 8).astype(jnp.int32)
     table = names[:, 0:4] * 128 + names[:, 4:8]
     table = jnp.where(table < 0, -1, table ^ device_place())
-    speed = call(
-        functools.partial(subcycles_kernel, tile_count, group),
-        planes,
-        (table, viscous, gain, speed, push, *relays),
+    step = 3 * side
+    speed, own, beside = call(
+        functools.partial(ice_kernel, tile_count, group, side),
+        [
+            planes,
+            shape(group // 2 * step, width),
+            shape(group // 2 * step, width, dtype=BF16),
+        ],
+        (table, viscous, gain, drag, conduct, current_ice, speed, push, *chunks, *relays),
         scratch=[
             pltpu.VMEM((devices, BLOCK_ROWS, size), BF16),
             pltpu.SMEM((devices, 4), jnp.int32),
             pltpu.SemaphoreType.DMA,
         ],
         hbm=(0,),
-    )
-
-    step = 3 * side
-    own, beside = call(
-        functools.partial(back_kernel, group, side),
-        [shape(group // 2 * step, width), shape(group // 2 * step, width, dtype=BF16)],
-        (drag, conduct, current_ice, speed, *chunks, *relays),
     )
     beside = lax.ppermute(beside, group_axes, [(i, i ^ 1) for i in range(group)])
     paired = call(

time: 36 us -> 35.8 us (level)
    pallas_call x9 -> x8, Pallas kernels: 8.86 us -> 8.59 us  [call(): pl.pallas_call(kernel, out_shape=outs, in_specs=specs, out_specs=jax.tree...]
where the time goes in v12:
time: 35.8 us; the launch traced here: 35.7 us
  waiting for transfers between devices  13.7 us (38%)
  starting transfers between devices  12.3 us (34%)
  Pallas kernels  8.59 us (24%)
  between operations  0.83 us (2%)
    pallas_call x8, Pallas kernels, call(): pl.pallas_call(kernel, out_shape=outs, in_specs=specs, out_specs=jax.tree...  8.59 us
    ppermute x3, starting transfers between devices, swap(): got[k] = lax.ppermute(value, axes, [(i, i ^ k) for i in range(count)])  4.76 us
    ppermute x3, waiting for transfers between devices, swap(): got[k] = lax.ppermute(value, axes, [(i, i ^ k) for i in range(count)])  4.13 us
    ppermute x3, starting transfers between devices, swap_each(): lax.ppermute(values[k], group_axes, [(i, i ^ k) for i in range(group)])  3.21 us
    ppermute x3, waiting for transfers between devices, swap_each(): lax.ppermute(values[k], group_axes, [(i, i ^ k) for i in range(group)])  3.21 us
    ppermute x1, waiting for transfers between devices, shards(): lax.ppermute(value, group_axes, [(i, i ^ 2 * k + 2) for i in range(group)])  2.11 us
    ppermute x1, starting transfers between devices, swap_chips(): lax.ppermute(value, group_axes, [(i, i ^ k) for i in range(group)])  2.05 us
    ppermute x1, starting transfers between devices, shards(): lax.ppermute(value, group_axes, [(i, i ^ 2 * k + 2) for i in range(group)])  2.05 us
  transfers between devices with their start and end apart: 12, of which 9 were waited for; matrix products, arithmetic and copies ran while one was open for 0% of the time, Pallas kernels for 4%

profile of v12, /device:TPU:0, one launch (start us, length us, event | category | flops | bytes accessed | tf_op | source)
XLA Modules:
  0.0 35.7 jit_solution(17237106659129453439)
XLA Ops:
  0.6 0.0 copy-start.1
  0.6 0.0 copy-start.2
  0.7 0.0 copy-start.3
  0.7 0.0 copy-start.4
  0.7 2.5 %shard_map.131 = (bf16[336,128]{1,0:T(8,128)(2,1)}, bf16[336,128]{1,0:T(8,128)(2,1)}, bf16[336,128]{1,0:T(8,128)(2,1)}, bf16[192,128]{1,0:T(8,128)(2,1)}) custom-call(s32[1,1,4]{2,1,0:T(1,128)} %links_h.1, s32[1,4]{1,0:T(1,128)} %blocks_h.1, bf16[4,64,128]{2,1,0:T(8,128)(2,1)} %bitcast.38, bf16[4,128,128]{2,1,0:T(8,128)(2,1)} %bitcast.36, ...), custom_call_target="tpu_custom_call" | custom-call | flops 11500000256 | bytes 393248 | tf_op jit(solution)/shard_map/pallas_call | solution.py:42
  3.2 3.0 %collective-permute-start.1 = (bf16[336,128]{1,0:T(8,128)(2,1)}, bf16[336,128]{1,0:T(8,128)(2,1)S(1)}, u32[]{:S(2)}, u32[]{:S(2)}) collective-permute-start(bf16[336,128]{1,0:T(8,128)(2,1)} %get-tuple-element.29), channel_id=1, source_target_pairs={{0,2},{1,3},{2,0},{3,1},{4,6},{5,7},{6,4},{7,5},{8,10},{9,11},{10,... | collective-permute-start | bytes 258056 | tf_op jit(solution)/shard_map/ppermute | solution.py:617
  6.2 0.0 collective-permute-start.2
  6.2 0.2 collective-permute-start
  6.4 2.5 %collective-permute-done.1.refs_1_.refs_6_.refs_2_ = bf16[336,128]{1,0:T(8,128)(2,1)S(1)} collective-permute-done((bf16[336,128]{1,0:T(8,128)(2,1)}, bf16[336,128]{1,0:T(8,128)(2,1)S(1)}, u32[]{:S(2)}, u32[]{:S(2)}) %collective-permute-start.1) | collective-permute-done | bytes 86048 | tf_op jit(solution)/shard_map/ppermute | solution.py:617
  8.9 0.0 collective-permute-start.3
  8.9 0.0 copy-done.1
  8.9 0.0 copy-done.2
  8.9 0.0 copy-done.3
  8.9 0.0 copy-done.4
  9.0 0.0 copy-start
  9.0 0.0 copy-start.5
  9.0 0.2 shard_map.130
  9.2 0.7 %collective-permute-done.refs_0_.refs_7_.refs_3_ = bf16[192,128]{1,0:T(8,128)(2,1)S(1)} collective-permute-done((bf16[192,128]{1,0:T(8,128)(2,1)}, bf16[192,128]{1,0:T(8,128)(2,1)S(1)}, u32[]{:S(2)}, u32[]{:S(2)}) %collective-permute-start) | collective-permute-done | bytes 49184 | tf_op jit(solution)/shard_map/ppermute | solution.py:617
  9.9 0.0 collective-permute-done.2.refs_2_.refs_5_.refs_1_
  9.9 0.2 collective-permute-done.3.refs_4_.refs_8_
  10.1 0.0 copy-done
  10.1 0.0 copy-done.5
  10.1 0.0 copy-start.6
  10.1 0.6 %shard_map.132 = (bf16[112,128]{1,0:T(8,128)(2,1)S(1)}, f32[2,128,128]{2,1,0:T(8,128)S(1)}, f32[2,128,128]{2,1,0:T(8,128)S(1)}) custom-call(f32[128,128]{1,0:T(8,128)S(1)} %get-tuple-element.25.mass, f32[128,128]{1,0:T(8,128)S(1)} %get-tuple-element.26.drag, f32[256,128]{1,0:T(8,128)S(1)} %bitcast.30, bf16[80,128]{1,0:T(8,128)(2,1)S(1)} %get-tuple-element.27.early, ...), custom_call_target="tpu_custom_call" | custom-call | flops 11500000 | bytes 626688 | tf_op jit(solution)/shard_map/pallas_call | solution.py:42
  10.7 4.1 %collective-permute-start.6 = (bf16[112,128]{1,0:T(8,128)(2,1)S(1)}, bf16[112,128]{1,0:T(8,128)(2,1)S(1)}, u32[]{:S(2)}, u32[]{:S(2)}) collective-permute-start(bf16[112,128]{1,0:T(8,128)(2,1)S(1)} %get-tuple-element.32.refs_0_), channel_id=1, source_target_pairs={{0,12},{4,8},{8,4},{12,0},{1,13},{5,9},{9,5},{13,1},{2,14},{6,10},... | collective-permute-start | bytes 86024 | tf_op jit(solution)/shard_map/ppermute | solution.py:600
  14.8 0.0 collective-permute-start.5
  14.8 0.6 %collective-permute-start.4 = (bf16[112,128]{1,0:T(8,128)(2,1)S(1)}, bf16[112,128]{1,0:T(8,128)(2,1)S(1)}, u32[]{:S(2)}, u32[]{:S(2)}) collective-permute-start(bf16[112,128]{1,0:T(8,128)(2,1)S(1)} %get-tuple-element.32.refs_0_), channel_id=1, source_target_pairs={{0,4},{4,0},{8,12},{12,8},{1,5},{5,1},{9,13},{13,9},{2,6},{6,2},{1... | collective-permute-start | bytes 86024 | tf_op jit(solution)/shard_map/ppermute | solution.py:600
  15.5 1.2 %collective-permute-done.6.refs_3_ = bf16[112,128]{1,0:T(8,128)(2,1)S(1)} collective-permute-done((bf16[112,128]{1,0:T(8,128)(2,1)S(1)}, bf16[112,128]{1,0:T(8,128)(2,1)S(1)}, u32[]{:S(2)}, u32[]{:S(2)}) %collective-permute-start.6) | collective-permute-done | bytes 28704 | tf_op jit(solution)/shard_map/ppermute | solution.py:600
  16.7 2.9 %collective-permute-done.5.refs_2_ = bf16[112,128]{1,0:T(8,128)(2,1)S(1)} collective-permute-done((bf16[112,128]{1,0:T(8,128)(2,1)S(1)}, bf16[112,128]{1,0:T(8,128)(2,1)S(1)}, u32[]{:S(2)}, u32[]{:S(2)}) %collective-permute-start.5) | collective-permute-done | bytes 28704 | tf_op jit(solution)/shard_map/ppermute | solution.py:600
  19.6 0.0 collective-permute-done.4.refs_1_
  19.6 0.0 copy-done.6
  19.6 0.4 %shard_map.133.refs_4_ = bf16[448,128]{1,0:T(8,128)(2,1)S(1)} custom-call(f32[4,64,128]{2,1,0:T(8,128)S(1)} %copy-done.1, f32[64,128]{1,0:T(8,128)S(1)} %copy-done.6, bf16[112,128]{1,0:T(8,128)(2,1)S(1)} %get-tuple-element.32.refs_0_, bf16[112,128]{1,0:T(8,128)(2,1)S(1)} %collective-permute-done.4.refs_1_, ...), custom_call_target="tpu_custom_call" | custom-call | flops 11500000 | bytes 622592 | tf_op jit(solution)/shard_map/pallas_call | solution.py:42
  20.0 2.0 %collective-permute-start.8 = (bf16[448,128]{1,0:T(8,128)(2,1)S(1)}, bf16[448,128]{1,0:T(8,128)(2,1)S(1)}, u32[]{:S(2)}, u32[]{:S(2)}) collective-permute-start(bf16[448,128]{1,0:T(8,128)(2,1)S(1)} %shard_map.133.refs_4_), channel_id=1, source_target_pairs={{0,2},{1,3},{2,0},{3,1},{4,6},{5,7},{6,4},{7,5},{8,10},{9,11},{10,... | collective-permute-start | bytes 344072 | tf_op jit(solution)/shard_map/ppermute | solution.py:605
  22.1 0.0 collective-permute-start.7
  22.1 1.1 %shard_map.134.warm = f32[4,64,128]{2,1,0:T(8,128)S(1)} custom-call(f32[4,64,128]{2,1,0:T(8,128)S(1)} %copy-done.1, f32[64,128]{1,0:T(8,128)S(1)} %copy-done.6, bf16[112,128]{1,0:T(8,128)(2,1)S(1)} %get-tuple-element.32.refs_0_, bf16[112,128]{1,0:T(8,128)(2,1)S(1)} %collective-permute-done.4.refs_1_, bf16[112,128]{1,0:T(8,128)(2,1)S(1)} %collective-permute-done.5.refs_2_, ...), custom_call_target="tpu_custom_call" | custom-call | flops 11500000 | bytes 622592 | tf_op jit(solution)/shard_map/pallas_call | solution.py:42
  23.2 1.7 %collective-permute-done.8.refs_6_ = bf16[448,128]{1,0:T(8,128)(2,1)S(1)} collective-permute-done((bf16[448,128]{1,0:T(8,128)(2,1)S(1)}, bf16[448,128]{1,0:T(8,128)(2,1)S(1)}, u32[]{:S(2)}, u32[]{:S(2)}) %collective-permute-start.8) | collective-permute-done | bytes 114720 | tf_op jit(solution)/shard_map/ppermute | solution.py:605
  24.9 0.0 collective-permute-start.9
  25.0 0.0 collective-permute-done.7.refs_5_
  25.0 1.2 %collective-permute-done.9.refs_7_ = bf16[448,128]{1,0:T(8,128)(2,1)S(1)} collective-permute-done((bf16[448,128]{1,0:T(8,128)(2,1)S(1)}, bf16[448,128]{1,0:T(8,128)(2,1)S(1)}, u32[]{:S(2)}, u32[]{:S(2)}) %collective-permute-start.9) | collective-permute-done | bytes 114720 | tf_op jit(solution)/shard_map/ppermute | solution.py:611
  26.3 0.1 xor_select_fusion.table
  26.4 3.0 %shard_map.135 = (f32[2,128,128]{2,1,0:T(8,128)S(1)}, f32[384,128]{1,0:T(8,128)S(1)}, bf16[384,128]{1,0:T(8,128)(2,1)S(1)}) custom-call(s32[16,4]{1,0:T(8,128)S(1)} %xor_select_fusion.table, f32[128,128]{1,0:T(8,128)S(1)} %get-tuple-element.35.viscous, f32[128,128]{1,0:T(8,128)S(1)} %get-tuple-element.36.gain, f32[128,128]{1,0:T(8,128)S(1)} %get-tuple-element.26.drag, ...), custom_call_target="tpu_custom_call" | custom-call | flops 11500000 | bytes 1421568 | tf_op jit(solution)/shard_map/pallas_call | solution.py:42
  29.4 0.2 collective-permute-start.10
  29.6 1.2 %collective-permute-done.10.beside = bf16[384,128]{1,0:T(8,128)(2,1)S(1)} collective-permute-done((bf16[384,128]{1,0:T(8,128)(2,1)S(1)}, bf16[384,128]{1,0:T(8,128)(2,1)S(1)}, u32[]{:S(2)}, u32[]{:S(2)}) %collective-permute-start.10) | collective-permute-done | bytes 98336 | tf_op jit(solution)/shard_map/ppermute | solution.py:738
  30.7 0.0 copy-start.7
  30.7 2.0 %collective-permute-start.11 = (bf16[192,128]{1,0:T(8,128)(2,1)S(1)}, bf16[192,128]{1,0:T(8,128)(2,1)S(1)}, u32[]{:S(2)}, u32[]{:S(2)}) collective-permute-start(bf16[192,128]{1,0:T(8,128)(2,1)S(1)} %shard_map.136), channel_id=1, source_target_pairs={{0,2},{1,3},{2,0},{3,1},{4,6},{5,7},{6,4},{7,5},{8,10},{9,11},{10,... | collective-permute-start | bytes 147464 | tf_op jit(solution)/shard_map/ppermute | solution.py:743
  32.8 2.1 %collective-permute-done.11.refs_0_ = bf16[192,128]{1,0:T(8,128)(2,1)S(1)} collective-permute-done((bf16[192,128]{1,0:T(8,128)(2,1)S(1)}, bf16[192,128]{1,0:T(8,128)(2,1)S(1)}, u32[]{:S(2)}, u32[]{:S(2)}) %collective-permute-start.11) | collective-permute-done | bytes 49184 | tf_op jit(solution)/shard_map/ppermute | solution.py:743
  34.9 0.0 copy-done.7
  34.9 0.7 %shard_map.137 = (f32[256,128]{1,0:T(8,128)}, f32[4,64,128]{2,1,0:T(8,128)}, f32[2,64,128]{2,1,0:T(8,128)}) custom-call(f32[4,64,128]{2,1,0:T(8,128)S(1)} %shard_map.134.warm, f32[2,64,128]{2,1,0:T(8,128)S(1)} %copy-done.7, f32[2,128,128]{2,1,0:T(8,128)S(1)} %get-tuple-element.41.speed, f32[384,128]{1,0:T(8,128)S(1)} %get-tuple-element.42.own, ...), custom_call_target="tpu_custom_call" | custom-call | flops 11500000 | bytes 671744 | tf_op jit(solution)/shard_map/pallas_call | solution.py:42
  (12 shorter events, 0.1 us)
Async XLA Ops:
  0.6 8.3 %copy-start.1 = (f32[4,64,128]{2,1,0:T(8,128)S(1)}, f32[4,64,128]{2,1,0:T(8,128)}, u32[]{:S(2)}) copy-start(f32[4,64,128]{2,1,0:T(8,128)} %water.5) | copy-start | bytes 393220
  0.6 8.3 %copy-start.2 = (f32[1,1,5,16384]{3,1,2,0:T(1,128)S(1)}, f32[1,1,5,16384]{3,1,2,0:T(1,128)}, u32[]{:S(2)}) copy-start(f32[1,1,5,16384]{3,1,2,0:T(1,128)} %param.18) | copy-start | bytes 983044
  0.7 8.3 %copy-start.3 = (f32[1,1,5,16384]{3,1,2,0:T(1,128)S(1)}, f32[1,1,5,16384]{3,1,2,0:T(1,128)}, u32[]{:S(2)}) copy-start(f32[1,1,5,16384]{3,1,2,0:T(1,128)} %param.19) | copy-start | bytes 983044
  0.7 8.3 %copy-start.4 = (f32[1,1,2,16384]{3,2,1,0:T(2,128)S(1)}, f32[1,1,2,16384]{3,2,1,0:T(2,128)}, u32[]{:S(2)}) copy-start(f32[1,1,2,16384]{3,2,1,0:T(2,128)} %param.20) | copy-start | bytes 393220
  3.2 5.7 %collective-permute-start.1 = (bf16[336,128]{1,0:T(8,128)(2,1)}, bf16[336,128]{1,0:T(8,128)(2,1)S(1)}, u32[]{:S(2)}, u32[]{:S(2)}) collective-permute-start(bf16[336,128]{1,0:T(8,128)(2,1)} %get-tuple-element.29), channel_id=1, source_target_pairs={{0,2},{1,3},{2,0},{3,1},{4,6},{5,7},{6,4},{7,5},{8,10},{9,11},{10,... | collective-permute-start | bytes 258056 | tf_op jit(solution)/shard_map/ppermute | solution.py:617
  6.2 3.7 %collective-permute-start.2 = (bf16[336,128]{1,0:T(8,128)(2,1)}, bf16[336,128]{1,0:T(8,128)(2,1)S(1)}, u32[]{:S(2)}, u32[]{:S(2)}) collective-permute-start(bf16[336,128]{1,0:T(8,128)(2,1)} %get-tuple-element.30), channel_id=1, source_target_pairs={{0,1},{1,0},{2,3},{3,2},{4,5},{5,4},{6,7},{7,6},{8,9},{9,8},{10,11... | collective-permute-start | bytes 258056 | tf_op jit(solution)/shard_map/ppermute | solution.py:617
  6.2 3.7 %collective-permute-start = (bf16[192,128]{1,0:T(8,128)(2,1)}, bf16[192,128]{1,0:T(8,128)(2,1)S(1)}, u32[]{:S(2)}, u32[]{:S(2)}) collective-permute-start(bf16[192,128]{1,0:T(8,128)(2,1)} %get-tuple-element.28), channel_id=1, source_target_pairs={{0,3},{1,2},{2,1},{3,0},{4,7},{5,6},{6,5},{7,4},{8,11},{9,10},{10,... | collective-permute-start | bytes 147464 | tf_op jit(solution)/shard_map/ppermute | solution.py:617
  8.9 1.2 %collective-permute-start.3 = (bf16[144,128]{1,0:T(8,128)(2,1)S(1)}, bf16[144,128]{1,0:T(8,128)(2,1)S(1)}, u32[]{:S(2)}, u32[]{:S(2)}) collective-permute-start(bf16[144,128]{1,0:T(8,128)(2,1)S(1)} %slice.44), channel_id=1, source_target_pairs={{0,1},{1,0},{2,3},{3,2},{4,5},{5,4},{6,7},{7,6},{8,9},{9,8},{10,11... | collective-permute-start | bytes 110600 | tf_op jit(solution)/shard_map/ppermute | solution.py:664
  9.0 1.2 %copy-start = (bf16[336,128]{1,0:T(8,128)(2,1)S(1)}, bf16[336,128]{1,0:T(8,128)(2,1)}, u32[]{:S(2)}) copy-start(bf16[336,128]{1,0:T(8,128)(2,1)} %get-tuple-element.31.refs_3_.refs_4_.refs_0_) | copy-start | bytes 258052
  9.0 1.2 %copy-start.5 = (f32[1,1,2,16384]{3,2,1,0:T(2,128)S(1)}, f32[1,1,2,16384]{3,2,1,0:T(2,128)}, u32[]{:S(2)}) copy-start(f32[1,1,2,16384]{3,2,1,0:T(2,128)} %param.21) | copy-start | bytes 393220
  10.1 9.5 %copy-start.6 = (f32[64,128]{1,0:T(8,128)S(1)}, f32[64,128]{1,0:T(8,128)}, u32[]{:S(2)}) copy-start(f32[64,128]{1,0:T(8,128)} %mixing.2) | copy-start | bytes 98308
  10.7 6.0 %collective-permute-start.6 = (bf16[112,128]{1,0:T(8,128)(2,1)S(1)}, bf16[112,128]{1,0:T(8,128)(2,1)S(1)}, u32[]{:S(2)}, u32[]{:S(2)}) collective-permute-start(bf16[112,128]{1,0:T(8,128)(2,1)S(1)} %get-tuple-element.32.refs_0_), channel_id=1, source_target_pairs={{0,12},{4,8},{8,4},{12,0},{1,13},{5,9},{9,5},{13,1},{2,14},{6,10},... | collective-permute-start | bytes 86024 | tf_op jit(solution)/shard_map/ppermute | solution.py:600
  14.8 4.8 %collective-permute-start.5 = (bf16[112,128]{1,0:T(8,128)(2,1)S(1)}, bf16[112,128]{1,0:T(8,128)(2,1)S(1)}, u32[]{:S(2)}, u32[]{:S(2)}) collective-permute-start(bf16[112,128]{1,0:T(8,128)(2,1)S(1)} %get-tuple-element.32.refs_0_), channel_id=1, source_target_pairs={{0,8},{4,12},{8,0},{12,4},{1,9},{5,13},{9,1},{13,5},{2,10},{6,14},... | collective-permute-start | bytes 86024 | tf_op jit(solution)/shard_map/ppermute | solution.py:600
  14.8 4.8 %collective-permute-start.4 = (bf16[112,128]{1,0:T(8,128)(2,1)S(1)}, bf16[112,128]{1,0:T(8,128)(2,1)S(1)}, u32[]{:S(2)}, u32[]{:S(2)}) collective-permute-start(bf16[112,128]{1,0:T(8,128)(2,1)S(1)} %get-tuple-element.32.refs_0_), channel_id=1, source_target_pairs={{0,4},{4,0},{8,12},{12,8},{1,5},{5,1},{9,13},{13,9},{2,6},{6,2},{1... | collective-permute-start | bytes 86024 | tf_op jit(solution)/shard_map/ppermute | solution.py:600
  20.0 4.9 %collective-permute-start.8 = (bf16[448,128]{1,0:T(8,128)(2,1)S(1)}, bf16[448,128]{1,0:T(8,128)(2,1)S(1)}, u32[]{:S(2)}, u32[]{:S(2)}) collective-permute-start(bf16[448,128]{1,0:T(8,128)(2,1)S(1)} %shard_map.133.refs_4_), channel_id=1, source_target_pairs={{0,2},{1,3},{2,0},{3,1},{4,6},{5,7},{6,4},{7,5},{8,10},{9,11},{10,... | collective-permute-start | bytes 344072 | tf_op jit(solution)/shard_map/ppermute | solution.py:605
  22.1 2.9 %collective-permute-start.7 = (bf16[448,128]{1,0:T(8,128)(2,1)S(1)}, bf16[448,128]{1,0:T(8,128)(2,1)S(1)}, u32[]{:S(2)}, u32[]{:S(2)}) collective-permute-start(bf16[448,128]{1,0:T(8,128)(2,1)S(1)} %shard_map.133.refs_4_), channel_id=1, source_target_pairs={{0,1},{1,0},{2,3},{3,2},{4,5},{5,4},{6,7},{7,6},{8,9},{9,8},{10,11... | collective-permute-start | bytes 344072 | tf_op jit(solution)/shard_map/ppermute | solution.py:611
  24.9 1.3 %collective-permute-start.9 = (bf16[448,128]{1,0:T(8,128)(2,1)S(1)}, bf16[448,128]{1,0:T(8,128)(2,1)S(1)}, u32[]{:S(2)}, u32[]{:S(2)}) collective-permute-start(bf16[448,128]{1,0:T(8,128)(2,1)S(1)} %collective-permute-done.8.refs_6_), channel_id=1, source_target_pairs={{0,1},{1,0},{2,3},{3,2},{4,5},{5,4},{6,7},{7,6},{8,9},{9,8},{10,11... | collective-permute-start | bytes 344072 | tf_op jit(solution)/shard_map/ppermute | solution.py:611
  29.4 1.4 %collective-permute-start.10 = (bf16[384,128]{1,0:T(8,128)(2,1)S(1)}, bf16[384,128]{1,0:T(8,128)(2,1)S(1)}, u32[]{:S(2)}, u32[]{:S(2)}) collective-permute-start(bf16[384,128]{1,0:T(8,128)(2,1)S(1)} %get-tuple-element.43), channel_id=1, source_target_pairs={{0,1},{1,0},{2,3},{3,2},{4,5},{5,4},{6,7},{7,6},{8,9},{9,8},{10,11... | collective-permute-start | bytes 294920 | tf_op jit(solution)/shard_map/ppermute | solution.py:738
  30.7 4.2 %copy-start.7 = (f32[2,64,128]{2,1,0:T(8,128)S(1)}, f32[2,64,128]{2,1,0:T(8,128)}, u32[]{:S(2)}) copy-start(f32[2,64,128]{2,1,0:T(8,128)} %currents.1) | copy-start | bytes 196612
  30.7 4.2 %collective-permute-start.11 = (bf16[192,128]{1,0:T(8,128)(2,1)S(1)}, bf16[192,128]{1,0:T(8,128)(2,1)S(1)}, u32[]{:S(2)}, u32[]{:S(2)}) collective-permute-start(bf16[192,128]{1,0:T(8,128)(2,1)S(1)} %shard_map.136), channel_id=1, source_target_pairs={{0,2},{1,3},{2,0},{3,1},{4,6},{5,7},{6,4},{7,5},{8,10},{9,11},{10,... | collective-permute-start | bytes 147464 | tf_op jit(solution)/shard_map/ppermute | solution.py:743

commit v13 on v12

--- a/solution.py
+++ b/solution.py
@@ -374,7 +374,7 @@
     tiles, members, side, table, viscous, gain, drag, conduct, current, speed, push, *refs
 ):
     chunks, relays = refs[:members], refs[members : 2 * members]
-    out, own_o, beside_o, rims, names, named = refs[2 * members :]
+    out, own_o, beside_o, rims, names, named, field = refs[2 * members :]
     load_names = pltpu.make_async_copy(table, names, named)
     load_names.start()
     size = viscous.shape[0]
@@ -415,23 +415,13 @@
         spread = left + right + inner + outer - 4.0 * c
         return scale * (c + visc * spread + pushed + turn * roll(c, half, 0))
 
-    row = iota((size, size), 0)
     col = iota((size, size), 1)
-    vx, vy = speed[0], speed[1]
-    visc, scale, push_x, push_y = viscous[...], gain[...], push[0], push[1]
-
-    def interior(v):
-        up = jnp.where(row == size - 1, 0.0, roll(v, -1, 0))
-        down = jnp.where(row == 0, 0.0, roll(v, 1, 0))
-        right = jnp.where(col == size - 1, 0.0, roll(v, -1, 1))
-        left = jnp.where(col == 0, 0.0, roll(v, 1, 1))
-        return up + down + right + left - 4.0 * v
-
-    def rim_of(north, south, east, west):
-        up = jnp.where(row == size - 1, north, jnp.where(row == 0, south, 0.0))
-        return up + jnp.where(col == size - 1, east, jnp.where(col == 0, west, 0.0))
-
-    def own_edges(vx, vy):
+    base = high
+    for c in range(2):
+        field[0, c, base : base + size] = speed[c]
+
+    def own_edges(now):
+        vx, vy = (field[now, c, base : base + size] for c in range(2))
         mixed = jnp.where(col < half, roll(vx, 1, 1), roll(vy, 1 + half, 1))
         across = mixed.T[0:high]
         return [
@@ -441,8 +431,7 @@
             roll(across, -1, 0),
         ]
 
-    own = own_edges(vx, vy)
-    inner_x, inner_y = interior(vx), interior(vy)
+    own = own_edges(0)
     load_names.wait()
     strips = []
     for q in range(4):
@@ -466,7 +455,7 @@
         cells = [strip[0] for strip, _ in strips]
         if t < SUBCYCLES - 1:
             if t > 0:
-                own = own_edges(vx, vy)
+                own = own_edges(t % 2)
             for q in range(4):
                 strip, (beyond, before) = strips[q]
                 c, y_hi, y_lo = strip[0], beyond[0][0], before[0][0]
@@ -493,22 +482,29 @@
                         item[0][0] = new_y
                         item[1][0] = new_z
                 strip[0] = new_strip
-        north, south = cells[0], cells[1]
+        now, later = t % 2, (t + 1) % 2
         sides = jnp.where(edge, cells[2], roll(cells[3], 1, 0)).T
-        east_x, west_x = sides[:, 0:1], sides[:, 1:2]
-        east_y, west_y = sides[:, half : half + 1], sides[:, half + 1 : half + 2]
-        if t > 0:
-            inner_x, inner_y = interior(vx), interior(vy)
-        spread_x = inner_x + rim_of(north[0:1], south[0:1], east_x, west_x)
-        spread_y = inner_y + rim_of(
-            north[half : half + 1], south[half : half + 1], east_y, west_y
-        )
-        new_x = scale * (vx + visc * spread_x + push_x + CORIOLIS_TURN * vy)
-        new_y = scale * (vy + visc * spread_y + push_y - CORIOLIS_TURN * vx)
-        vx, vy = new_x, new_y
-    out[0] = vx
-    out[1] = vy
-    stress = [(drag[...] * (v - current[c])).astype(BF16) for c, v in enumerate((vx, vy))]
+        for c in range(2):
+            at = c * half
+            field[now, c, base + size : base + size + 1] = cells[0][at : at + 1]
+            field[now, c, base - 1 : base] = cells[1][at : at + 1]
+        for i in range(size // high):
+            rows = slice(i * high, (i + 1) * high)
+            held = [field[now, c, base + i * high : base + (i + 1) * high] for c in range(2)]
+            for c in range(2):
+                v, at = held[c], base + i * high
+                up = field[now, c, at + 1 : at + 1 + high]
+                down = field[now, c, at - 1 : at - 1 + high]
+                east = jnp.where(last, sides[rows, c * half : c * half + 1], roll(v, -1, 1))
+                west = jnp.where(first, sides[rows, c * half + 1 : c * half + 2], roll(v, 1, 1))
+                spread = up + down + east + west - 4.0 * v
+                turned = (CORIOLIS_TURN if c == 0 else -CORIOLIS_TURN) * held[1 - c]
+                new = gain[rows] * (v + viscous[rows] * spread + push[c, rows] + turned)
+                if t == SUBCYCLES - 1:
+                    out[c, rows] = new
+                else:
+                    field[later, c, at : at + high] = new
+    stress = [(drag[...] * (out[c] - current[c])).astype(BF16) for c in range(2)]
     return_fluxes([heat, *stress], chunks, side, depth, own_o, beside_o)
 
 
@@ -732,6 +728,7 @@
             pltpu.VMEM((devices, BLOCK_ROWS, size), BF16),
             pltpu.SMEM((devices, 4), jnp.int32),
             pltpu.SemaphoreType.DMA,
+            pltpu.VMEM((2, 2, size + 4 * DEPTH, size), F32),
         ],
         hbm=(0,),
     )

time: 35.8 us -> 35.9 us (level)
  no operation moved by 1% of the time
where the time goes in v13:
time: 35.9 us; the launch traced here: 35.7 us
  waiting for transfers between devices  13.7 us (38%)
  starting transfers between devices  12.3 us (34%)
  Pallas kernels  8.69 us (24%)
  between operations  0.83 us (2%)
    pallas_call x8, Pallas kernels, call(): pl.pallas_call(kernel, out_shape=outs, in_specs=specs, out_specs=jax.tree...  8.69 us
    ppermute x3, starting transfers between devices, swap(): got[k] = lax.ppermute(value, axes, [(i, i ^ k) for i in range(count)])  4.76 us
    ppermute x3, waiting for transfers between devices, swap(): got[k] = lax.ppermute(value, axes, [(i, i ^ k) for i in range(count)])  4.13 us
    ppermute x3, starting transfers between devices, swap_each(): lax.ppermute(values[k], group_axes, [(i, i ^ k) for i in range(group)])  3.21 us
    ppermute x3, waiting for transfers between devices, swap_each(): lax.ppermute(values[k], group_axes, [(i, i ^ k) for i in range(group)])  3.21 us
    ppermute x1, waiting for transfers between devices, shards(): lax.ppermute(value, group_axes, [(i, i ^ 2 * k + 2) for i in range(group)])  2.11 us
    ppermute x1, starting transfers between devices, shards(): lax.ppermute(value, group_axes, [(i, i ^ 2 * k + 2) for i in range(group)])  2.05 us
    ppermute x1, starting transfers between devices, swap_chips(): lax.ppermute(value, group_axes, [(i, i ^ k) for i in range(group)])  2.05 us
  transfers between devices with their start and end apart: 12, of which 9 were waited for; matrix products, arithmetic and copies ran while one was open for 0% of the time, Pallas kernels for 4%

profile of v13, /device:TPU:0, one launch (start us, length us, event | category | flops | bytes accessed | tf_op | source)
XLA Modules:
  0.0 35.7 jit_solution(13889990246734646239)
XLA Ops:
  0.6 0.0 copy-start.1
  0.6 0.0 copy-start.2
  0.7 0.0 copy-start.3
  0.7 0.0 copy-start.4
  0.7 2.5 %shard_map.131 = (bf16[336,128]{1,0:T(8,128)(2,1)}, bf16[336,128]{1,0:T(8,128)(2,1)}, bf16[336,128]{1,0:T(8,128)(2,1)}, bf16[192,128]{1,0:T(8,128)(2,1)}) custom-call(s32[1,1,4]{2,1,0:T(1,128)} %links_h.1, s32[1,4]{1,0:T(1,128)} %blocks_h.1, bf16[4,64,128]{2,1,0:T(8,128)(2,1)} %bitcast.38, bf16[4,128,128]{2,1,0:T(8,128)(2,1)} %bitcast.36, ...), custom_call_target="tpu_custom_call" | custom-call | flops 11500000256 | bytes 393248 | tf_op jit(solution)/shard_map/pallas_call | solution.py:42
  3.2 3.0 %collective-permute-start.1 = (bf16[336,128]{1,0:T(8,128)(2,1)}, bf16[336,128]{1,0:T(8,128)(2,1)S(1)}, u32[]{:S(2)}, u32[]{:S(2)}) collective-permute-start(bf16[336,128]{1,0:T(8,128)(2,1)} %get-tuple-element.29), channel_id=1, source_target_pairs={{0,2},{1,3},{2,0},{3,1},{4,6},{5,7},{6,4},{7,5},{8,10},{9,11},{10,... | collective-permute-start | bytes 258056 | tf_op jit(solution)/shard_map/ppermute | solution.py:613
  6.2 0.0 collective-permute-start.2
  6.2 0.2 collective-permute-start
  6.4 2.5 %collective-permute-done.1.refs_1_.refs_6_.refs_2_ = bf16[336,128]{1,0:T(8,128)(2,1)S(1)} collective-permute-done((bf16[336,128]{1,0:T(8,128)(2,1)}, bf16[336,128]{1,0:T(8,128)(2,1)S(1)}, u32[]{:S(2)}, u32[]{:S(2)}) %collective-permute-start.1) | collective-permute-done | bytes 86048 | tf_op jit(solution)/shard_map/ppermute | solution.py:613
  8.9 0.0 collective-permute-start.3
  8.9 0.0 copy-done.1
  8.9 0.0 copy-done.2
  8.9 0.0 copy-done.3
  8.9 0.0 copy-done.4
  9.0 0.0 copy-start
  9.0 0.0 copy-start.5
  9.0 0.2 shard_map.130
  9.2 0.7 %collective-permute-done.refs_0_.refs_7_.refs_3_ = bf16[192,128]{1,0:T(8,128)(2,1)S(1)} collective-permute-done((bf16[192,128]{1,0:T(8,128)(2,1)}, bf16[192,128]{1,0:T(8,128)(2,1)S(1)}, u32[]{:S(2)}, u32[]{:S(2)}) %collective-permute-start) | collective-permute-done | bytes 49184 | tf_op jit(solution)/shard_map/ppermute | solution.py:613
  9.9 0.0 collective-permute-done.2.refs_2_.refs_5_.refs_1_
  9.9 0.2 collective-permute-done.3.refs_4_.refs_8_
  10.1 0.0 copy-done
  10.1 0.0 copy-done.5
  10.1 0.0 copy-start.6
  10.1 0.6 %shard_map.132 = (bf16[112,128]{1,0:T(8,128)(2,1)S(1)}, f32[2,128,128]{2,1,0:T(8,128)S(1)}, f32[2,128,128]{2,1,0:T(8,128)S(1)}) custom-call(f32[128,128]{1,0:T(8,128)S(1)} %get-tuple-element.25.mass, f32[128,128]{1,0:T(8,128)S(1)} %get-tuple-element.26.drag, f32[256,128]{1,0:T(8,128)S(1)} %bitcast.30, bf16[80,128]{1,0:T(8,128)(2,1)S(1)} %get-tuple-element.27.early, ...), custom_call_target="tpu_custom_call" | custom-call | flops 11500000 | bytes 626688 | tf_op jit(solution)/shard_map/pallas_call | solution.py:42
  10.7 4.1 %collective-permute-start.6 = (bf16[112,128]{1,0:T(8,128)(2,1)S(1)}, bf16[112,128]{1,0:T(8,128)(2,1)S(1)}, u32[]{:S(2)}, u32[]{:S(2)}) collective-permute-start(bf16[112,128]{1,0:T(8,128)(2,1)S(1)} %get-tuple-element.32.refs_0_), channel_id=1, source_target_pairs={{0,12},{4,8},{8,4},{12,0},{1,13},{5,9},{9,5},{13,1},{2,14},{6,10},... | collective-permute-start | bytes 86024 | tf_op jit(solution)/shard_map/ppermute | solution.py:596
  14.8 0.0 collective-permute-start.5
  14.8 0.6 %collective-permute-start.4 = (bf16[112,128]{1,0:T(8,128)(2,1)S(1)}, bf16[112,128]{1,0:T(8,128)(2,1)S(1)}, u32[]{:S(2)}, u32[]{:S(2)}) collective-permute-start(bf16[112,128]{1,0:T(8,128)(2,1)S(1)} %get-tuple-element.32.refs_0_), channel_id=1, source_target_pairs={{0,4},{4,0},{8,12},{12,8},{1,5},{5,1},{9,13},{13,9},{2,6},{6,2},{1... | collective-permute-start | bytes 86024 | tf_op jit(solution)/shard_map/ppermute | solution.py:596
  15.5 1.2 %collective-permute-done.6.refs_3_ = bf16[112,128]{1,0:T(8,128)(2,1)S(1)} collective-permute-done((bf16[112,128]{1,0:T(8,128)(2,1)S(1)}, bf16[112,128]{1,0:T(8,128)(2,1)S(1)}, u32[]{:S(2)}, u32[]{:S(2)}) %collective-permute-start.6) | collective-permute-done | bytes 28704 | tf_op jit(solution)/shard_map/ppermute | solution.py:596
  16.7 2.9 %collective-permute-done.5.refs_2_ = bf16[112,128]{1,0:T(8,128)(2,1)S(1)} collective-permute-done((bf16[112,128]{1,0:T(8,128)(2,1)S(1)}, bf16[112,128]{1,0:T(8,128)(2,1)S(1)}, u32[]{:S(2)}, u32[]{:S(2)}) %collective-permute-start.5) | collective-permute-done | bytes 28704 | tf_op jit(solution)/shard_map/ppermute | solution.py:596
  19.6 0.0 collective-permute-done.4.refs_1_
  19.6 0.0 copy-done.6
  19.6 0.4 %shard_map.133.refs_4_ = bf16[448,128]{1,0:T(8,128)(2,1)S(1)} custom-call(f32[4,64,128]{2,1,0:T(8,128)S(1)} %copy-done.1, f32[64,128]{1,0:T(8,128)S(1)} %copy-done.6, bf16[112,128]{1,0:T(8,128)(2,1)S(1)} %get-tuple-element.32.refs_0_, bf16[112,128]{1,0:T(8,128)(2,1)S(1)} %collective-permute-done.4.refs_1_, ...), custom_call_target="tpu_custom_call" | custom-call | flops 11500000 | bytes 622592 | tf_op jit(solution)/shard_map/pallas_call | solution.py:42
  20.0 2.0 %collective-permute-start.8 = (bf16[448,128]{1,0:T(8,128)(2,1)S(1)}, bf16[448,128]{1,0:T(8,128)(2,1)S(1)}, u32[]{:S(2)}, u32[]{:S(2)}) collective-permute-start(bf16[448,128]{1,0:T(8,128)(2,1)S(1)} %shard_map.133.refs_4_), channel_id=1, source_target_pairs={{0,2},{1,3},{2,0},{3,1},{4,6},{5,7},{6,4},{7,5},{8,10},{9,11},{10,... | collective-permute-start | bytes 344072 | tf_op jit(solution)/shard_map/ppermute | solution.py:601
  22.1 0.0 collective-permute-start.7
  22.1 1.1 %shard_map.134.warm = f32[4,64,128]{2,1,0:T(8,128)S(1)} custom-call(f32[4,64,128]{2,1,0:T(8,128)S(1)} %copy-done.1, f32[64,128]{1,0:T(8,128)S(1)} %copy-done.6, bf16[112,128]{1,0:T(8,128)(2,1)S(1)} %get-tuple-element.32.refs_0_, bf16[112,128]{1,0:T(8,128)(2,1)S(1)} %collective-permute-done.4.refs_1_, bf16[112,128]{1,0:T(8,128)(2,1)S(1)} %collective-permute-done.5.refs_2_, ...), custom_call_target="tpu_custom_call" | custom-call | flops 11500000 | bytes 622592 | tf_op jit(solution)/shard_map/pallas_call | solution.py:42
  23.2 1.7 %collective-permute-done.8.refs_6_ = bf16[448,128]{1,0:T(8,128)(2,1)S(1)} collective-permute-done((bf16[448,128]{1,0:T(8,128)(2,1)S(1)}, bf16[448,128]{1,0:T(8,128)(2,1)S(1)}, u32[]{:S(2)}, u32[]{:S(2)}) %collective-permute-start.8) | collective-permute-done | bytes 114720 | tf_op jit(solution)/shard_map/ppermute | solution.py:601
  24.9 0.0 collective-permute-start.9
  25.0 0.0 collective-permute-done.7.refs_5_
  25.0 1.2 %collective-permute-done.9.refs_7_ = bf16[448,128]{1,0:T(8,128)(2,1)S(1)} collective-permute-done((bf16[448,128]{1,0:T(8,128)(2,1)S(1)}, bf16[448,128]{1,0:T(8,128)(2,1)S(1)}, u32[]{:S(2)}, u32[]{:S(2)}) %collective-permute-start.9) | collective-permute-done | bytes 114720 | tf_op jit(solution)/shard_map/ppermute | solution.py:607
  26.3 0.1 xor_select_fusion.table
  26.4 3.1 %shard_map.135 = (f32[2,128,128]{2,1,0:T(8,128)S(1)}, f32[384,128]{1,0:T(8,128)S(1)}, bf16[384,128]{1,0:T(8,128)(2,1)S(1)}) custom-call(s32[16,4]{1,0:T(8,128)S(1)} %xor_select_fusion.table, f32[128,128]{1,0:T(8,128)S(1)} %get-tuple-element.35.viscous, f32[128,128]{1,0:T(8,128)S(1)} %get-tuple-element.36.gain, f32[128,128]{1,0:T(8,128)S(1)} %get-tuple-element.26.drag, ...), custom_call_target="tpu_custom_call" | custom-call | flops 11500000 | bytes 1421568 | tf_op jit(solution)/shard_map/pallas_call | solution.py:42
  29.5 0.2 collective-permute-start.10
  29.7 1.2 %collective-permute-done.10.beside = bf16[384,128]{1,0:T(8,128)(2,1)S(1)} collective-permute-done((bf16[384,128]{1,0:T(8,128)(2,1)S(1)}, bf16[384,128]{1,0:T(8,128)(2,1)S(1)}, u32[]{:S(2)}, u32[]{:S(2)}) %collective-permute-start.10) | collective-permute-done | bytes 98336 | tf_op jit(solution)/shard_map/ppermute | solution.py:735
  30.8 0.0 copy-start.7
  30.8 2.0 %collective-permute-start.11 = (bf16[192,128]{1,0:T(8,128)(2,1)S(1)}, bf16[192,128]{1,0:T(8,128)(2,1)S(1)}, u32[]{:S(2)}, u32[]{:S(2)}) collective-permute-start(bf16[192,128]{1,0:T(8,128)(2,1)S(1)} %shard_map.136), channel_id=1, source_target_pairs={{0,2},{1,3},{2,0},{3,1},{4,6},{5,7},{6,4},{7,5},{8,10},{9,11},{10,... | collective-permute-start | bytes 147464 | tf_op jit(solution)/shard_map/ppermute | solution.py:740
  32.9 2.1 %collective-permute-done.11.refs_0_ = bf16[192,128]{1,0:T(8,128)(2,1)S(1)} collective-permute-done((bf16[192,128]{1,0:T(8,128)(2,1)S(1)}, bf16[192,128]{1,0:T(8,128)(2,1)S(1)}, u32[]{:S(2)}, u32[]{:S(2)}) %collective-permute-start.11) | collective-permute-done | bytes 49184 | tf_op jit(solution)/shard_map/ppermute | solution.py:740
  35.0 0.0 copy-done.7
  35.0 0.7 %shard_map.137 = (f32[256,128]{1,0:T(8,128)}, f32[4,64,128]{2,1,0:T(8,128)}, f32[2,64,128]{2,1,0:T(8,128)}) custom-call(f32[4,64,128]{2,1,0:T(8,128)S(1)} %shard_map.134.warm, f32[2,64,128]{2,1,0:T(8,128)S(1)} %copy-done.7, f32[2,128,128]{2,1,0:T(8,128)S(1)} %get-tuple-element.41.speed, f32[384,128]{1,0:T(8,128)S(1)} %get-tuple-element.42.own, ...), custom_call_target="tpu_custom_call" | custom-call | flops 11500000 | bytes 671744 | tf_op jit(solution)/shard_map/pallas_call | solution.py:42
  (12 shorter events, 0.1 us)
Async XLA Ops:
  0.6 8.3 %copy-start.1 = (f32[4,64,128]{2,1,0:T(8,128)S(1)}, f32[4,64,128]{2,1,0:T(8,128)}, u32[]{:S(2)}) copy-start(f32[4,64,128]{2,1,0:T(8,128)} %water.5) | copy-start | bytes 393220
  0.6 8.3 %copy-start.2 = (f32[1,1,5,16384]{3,1,2,0:T(1,128)S(1)}, f32[1,1,5,16384]{3,1,2,0:T(1,128)}, u32[]{:S(2)}) copy-start(f32[1,1,5,16384]{3,1,2,0:T(1,128)} %param.18) | copy-start | bytes 983044
  0.7 8.3 %copy-start.3 = (f32[1,1,5,16384]{3,1,2,0:T(1,128)S(1)}, f32[1,1,5,16384]{3,1,2,0:T(1,128)}, u32[]{:S(2)}) copy-start(f32[1,1,5,16384]{3,1,2,0:T(1,128)} %param.19) | copy-start | bytes 983044
  0.7 8.3 %copy-start.4 = (f32[1,1,2,16384]{3,2,1,0:T(2,128)S(1)}, f32[1,1,2,16384]{3,2,1,0:T(2,128)}, u32[]{:S(2)}) copy-start(f32[1,1,2,16384]{3,2,1,0:T(2,128)} %param.20) | copy-start | bytes 393220
  3.2 5.7 %collective-permute-start.1 = (bf16[336,128]{1,0:T(8,128)(2,1)}, bf16[336,128]{1,0:T(8,128)(2,1)S(1)}, u32[]{:S(2)}, u32[]{:S(2)}) collective-permute-start(bf16[336,128]{1,0:T(8,128)(2,1)} %get-tuple-element.29), channel_id=1, source_target_pairs={{0,2},{1,3},{2,0},{3,1},{4,6},{5,7},{6,4},{7,5},{8,10},{9,11},{10,... | collective-permute-start | bytes 258056 | tf_op jit(solution)/shard_map/ppermute | solution.py:613
  6.2 3.7 %collective-permute-start.2 = (bf16[336,128]{1,0:T(8,128)(2,1)}, bf16[336,128]{1,0:T(8,128)(2,1)S(1)}, u32[]{:S(2)}, u32[]{:S(2)}) collective-permute-start(bf16[336,128]{1,0:T(8,128)(2,1)} %get-tuple-element.30), channel_id=1, source_target_pairs={{0,1},{1,0},{2,3},{3,2},{4,5},{5,4},{6,7},{7,6},{8,9},{9,8},{10,11... | collective-permute-start | bytes 258056 | tf_op jit(solution)/shard_map/ppermute | solution.py:613
  6.2 3.7 %collective-permute-start = (bf16[192,128]{1,0:T(8,128)(2,1)}, bf16[192,128]{1,0:T(8,128)(2,1)S(1)}, u32[]{:S(2)}, u32[]{:S(2)}) collective-permute-start(bf16[192,128]{1,0:T(8,128)(2,1)} %get-tuple-element.28), channel_id=1, source_target_pairs={{0,3},{1,2},{2,1},{3,0},{4,7},{5,6},{6,5},{7,4},{8,11},{9,10},{10,... | collective-permute-start | bytes 147464 | tf_op jit(solution)/shard_map/ppermute | solution.py:613
  8.9 1.2 %collective-permute-start.3 = (bf16[144,128]{1,0:T(8,128)(2,1)S(1)}, bf16[144,128]{1,0:T(8,128)(2,1)S(1)}, u32[]{:S(2)}, u32[]{:S(2)}) collective-permute-start(bf16[144,128]{1,0:T(8,128)(2,1)S(1)} %slice.44), channel_id=1, source_target_pairs={{0,1},{1,0},{2,3},{3,2},{4,5},{5,4},{6,7},{7,6},{8,9},{9,8},{10,11... | collective-permute-start | bytes 110600 | tf_op jit(solution)/shard_map/ppermute | solution.py:660
  9.0 1.2 %copy-start = (bf16[336,128]{1,0:T(8,128)(2,1)S(1)}, bf16[336,128]{1,0:T(8,128)(2,1)}, u32[]{:S(2)}) copy-start(bf16[336,128]{1,0:T(8,128)(2,1)} %get-tuple-element.31.refs_3_.refs_4_.refs_0_) | copy-start | bytes 258052
  9.0 1.2 %copy-start.5 = (f32[1,1,2,16384]{3,2,1,0:T(2,128)S(1)}, f32[1,1,2,16384]{3,2,1,0:T(2,128)}, u32[]{:S(2)}) copy-start(f32[1,1,2,16384]{3,2,1,0:T(2,128)} %param.21) | copy-start | bytes 393220
  10.1 9.5 %copy-start.6 = (f32[64,128]{1,0:T(8,128)S(1)}, f32[64,128]{1,0:T(8,128)}, u32[]{:S(2)}) copy-start(f32[64,128]{1,0:T(8,128)} %mixing.2) | copy-start | bytes 98308
  10.7 6.0 %collective-permute-start.6 = (bf16[112,128]{1,0:T(8,128)(2,1)S(1)}, bf16[112,128]{1,0:T(8,128)(2,1)S(1)}, u32[]{:S(2)}, u32[]{:S(2)}) collective-permute-start(bf16[112,128]{1,0:T(8,128)(2,1)S(1)} %get-tuple-element.32.refs_0_), channel_id=1, source_target_pairs={{0,12},{4,8},{8,4},{12,0},{1,13},{5,9},{9,5},{13,1},{2,14},{6,10},... | collective-permute-start | bytes 86024 | tf_op jit(solution)/shard_map/ppermute | solution.py:596
  14.8 4.8 %collective-permute-start.5 = (bf16[112,128]{1,0:T(8,128)(2,1)S(1)}, bf16[112,128]{1,0:T(8,128)(2,1)S(1)}, u32[]{:S(2)}, u32[]{:S(2)}) collective-permute-start(bf16[112,128]{1,0:T(8,128)(2,1)S(1)} %get-tuple-element.32.refs_0_), channel_id=1, source_target_pairs={{0,8},{4,12},{8,0},{12,4},{1,9},{5,13},{9,1},{13,5},{2,10},{6,14},... | collective-permute-start | bytes 86024 | tf_op jit(solution)/shard_map/ppermute | solution.py:596
  14.8 4.8 %collective-permute-start.4 = (bf16[112,128]{1,0:T(8,128)(2,1)S(1)}, bf16[112,128]{1,0:T(8,128)(2,1)S(1)}, u32[]{:S(2)}, u32[]{:S(2)}) collective-permute-start(bf16[112,128]{1,0:T(8,128)(2,1)S(1)} %get-tuple-element.32.refs_0_), channel_id=1, source_target_pairs={{0,4},{4,0},{8,12},{12,8},{1,5},{5,1},{9,13},{13,9},{2,6},{6,2},{1... | collective-permute-start | bytes 86024 | tf_op jit(solution)/shard_map/ppermute | solution.py:596
  20.0 4.9 %collective-permute-start.8 = (bf16[448,128]{1,0:T(8,128)(2,1)S(1)}, bf16[448,128]{1,0:T(8,128)(2,1)S(1)}, u32[]{:S(2)}, u32[]{:S(2)}) collective-permute-start(bf16[448,128]{1,0:T(8,128)(2,1)S(1)} %shard_map.133.refs_4_), channel_id=1, source_target_pairs={{0,2},{1,3},{2,0},{3,1},{4,6},{5,7},{6,4},{7,5},{8,10},{9,11},{10,... | collective-permute-start | bytes 344072 | tf_op jit(solution)/shard_map/ppermute | solution.py:601
  22.1 2.9 %collective-permute-start.7 = (bf16[448,128]{1,0:T(8,128)(2,1)S(1)}, bf16[448,128]{1,0:T(8,128)(2,1)S(1)}, u32[]{:S(2)}, u32[]{:S(2)}) collective-permute-start(bf16[448,128]{1,0:T(8,128)(2,1)S(1)} %shard_map.133.refs_4_), channel_id=1, source_target_pairs={{0,1},{1,0},{2,3},{3,2},{4,5},{5,4},{6,7},{7,6},{8,9},{9,8},{10,11... | collective-permute-start | bytes 344072 | tf_op jit(solution)/shard_map/ppermute | solution.py:607
  24.9 1.3 %collective-permute-start.9 = (bf16[448,128]{1,0:T(8,128)(2,1)S(1)}, bf16[448,128]{1,0:T(8,128)(2,1)S(1)}, u32[]{:S(2)}, u32[]{:S(2)}) collective-permute-start(bf16[448,128]{1,0:T(8,128)(2,1)S(1)} %collective-permute-done.8.refs_6_), channel_id=1, source_target_pairs={{0,1},{1,0},{2,3},{3,2},{4,5},{5,4},{6,7},{7,6},{8,9},{9,8},{10,11... | collective-permute-start | bytes 344072 | tf_op jit(solution)/shard_map/ppermute | solution.py:607
  29.5 1.4 %collective-permute-start.10 = (bf16[384,128]{1,0:T(8,128)(2,1)S(1)}, bf16[384,128]{1,0:T(8,128)(2,1)S(1)}, u32[]{:S(2)}, u32[]{:S(2)}) collective-permute-start(bf16[384,128]{1,0:T(8,128)(2,1)S(1)} %get-tuple-element.43), channel_id=1, source_target_pairs={{0,1},{1,0},{2,3},{3,2},{4,5},{5,4},{6,7},{7,6},{8,9},{9,8},{10,11... | collective-permute-start | bytes 294920 | tf_op jit(solution)/shard_map/ppermute | solution.py:735
  30.8 4.2 %copy-start.7 = (f32[2,64,128]{2,1,0:T(8,128)S(1)}, f32[2,64,128]{2,1,0:T(8,128)}, u32[]{:S(2)}) copy-start(f32[2,64,128]{2,1,0:T(8,128)} %currents.1) | copy-start | bytes 196612
  30.8 4.2 %collective-permute-start.11 = (bf16[192,128]{1,0:T(8,128)(2,1)S(1)}, bf16[192,128]{1,0:T(8,128)(2,1)S(1)}, u32[]{:S(2)}, u32[]{:S(2)}) collective-permute-start(bf16[192,128]{1,0:T(8,128)(2,1)S(1)} %shard_map.136), channel_id=1, source_target_pairs={{0,2},{1,3},{2,0},{3,1},{4,6},{5,7},{6,4},{7,5},{8,10},{9,11},{10,... | collective-permute-start | bytes 147464 | tf_op jit(solution)/shard_map/ppermute | solution.py:740

commit v14 on v13

--- a/solution.py
+++ b/solution.py
@@ -21,11 +21,11 @@
 OPPOSITE = (1, 0, 3, 2)
 LATERAL = ((2, 3), (2, 3), (0, 1), (0, 1))
 DEPTH = SUBCYCLES
-SIDE_ROWS = 16 * DEPTH
-PUSH_ROWS = 8 * DEPTH
-BLOCK_ROWS = SIDE_ROWS + PUSH_ROWS
-NAMES_ROW = 2 * DEPTH - 1
-CORNER_ROWS = tuple(DEPTH * i - 1 for i in (1, 3, 4, 5, 6, 7, 8))
+EARLY_DEPTHS = (DEPTH, DEPTH, DEPTH - 1, DEPTH - 1)
+LATE_DEPTHS = (DEPTH - 1, DEPTH - 1)
+EARLY_SIDE, LATE_SIDE = sum(EARLY_DEPTHS), sum(LATE_DEPTHS)
+EARLY_ROWS = 4 * EARLY_SIDE
+BLOCK_ROWS = EARLY_ROWS + 4 * LATE_SIDE
 TILE_ROWS = 16
 F32 = jnp.float32
 BF16 = jnp.bfloat16
@@ -140,7 +140,7 @@
         copy.wait()
 
 
-def put_side_rims(store, planes, at):
+def put_side_rims(store, planes, depths, at):
     size = planes[0].shape[0]
     lane = iota((size, size), 1)
     mixed = jnp.zeros((size, size), F32)
@@ -148,20 +148,21 @@
         turned = roll(plane, DEPTH + 2 * DEPTH * i, 1)
         mixed = jnp.where(lane // (2 * DEPTH) == i, turned, mixed)
     across = mixed.T
+    base = 0
     for i, plane in enumerate(planes):
-        for k in range(DEPTH):
-            base = i * DEPTH + k
+        for k in range(depths[i]):
+            east = 2 * DEPTH * i + DEPTH - 1 - k
+            west = 2 * DEPTH * i + DEPTH + k
             store[at(0) + base : at(0) + base + 1] = plane[size - 1 - k : size - k]
             store[at(1) + base : at(1) + base + 1] = plane[k : k + 1]
-            east = 2 * DEPTH * i + DEPTH - 1 - k
-            west = 2 * DEPTH * i + DEPTH + k
             store[at(2) + base : at(2) + base + 1] = across[east : east + 1]
             store[at(3) + base : at(3) + base + 1] = across[west : west + 1]
+            base += 1
 
 
 def rims_kernel(
     thick, conc, ice, water, out, viscous_o, gain_o, mass_o, drag_o, conduct_o,
-    speed_o, store,
+    speed_o,
 ):
     size = thick.shape[1]
     cover = jnp.zeros((size, size), F32)
@@ -185,15 +186,15 @@
     conduct_o[...] = -HEAT_RATE * conduct
     speed_o[0] = speed_x
     speed_o[1] = speed_y
-    put_side_rims(store, [speed_x, speed_y, viscous, gain], lambda side: side * 4 * DEPTH)
+    put_side_rims(
+        out, [speed_x, speed_y, viscous, gain], EARLY_DEPTHS, lambda side: side * EARLY_SIDE
+    )
     levels, rows, width = water.shape
-    start = SIDE_ROWS
     for l in range(levels):
         for j in range(2):
-            at = start + 2 * l + j
-            store[at : at + 1] = water[l, rows - 1 - j : rows - j]
-            store[at + 2 * levels : at + 2 * levels + 1] = water[l, j : j + 1]
-    out[...] = store[...].astype(BF16)
+            at = EARLY_ROWS + 2 * l + j
+            out[at : at + 1] = water[l, rows - 1 - j : rows - j]
+            out[at + 2 * levels : at + 2 * levels + 1] = water[l, j : j + 1]
 
 
 def nearby(me, members, distance, arrays):
@@ -245,17 +246,25 @@
         push = mass[...] * (force + drag[...] * current)
         push_o[c] = push
         pushes.append(push)
-    put_side_rims(store, pushes, lambda q: q * 2 * DEPTH)
-    tail = [t[2 * side :] for t in tails]
-    store[NAMES_ROW : NAMES_ROW + 1] = tail[0].astype(F32)[2 * levels : 2 * levels + 1]
+    store[0:EARLY_ROWS] = early[0:EARLY_ROWS]
+    put_side_rims(store, pushes, LATE_DEPTHS, lambda side: EARLY_ROWS + side * LATE_SIDE)
+    tail = [t[2 * side :].astype(F32) for t in tails]
+    line = iota((1, size), 1)
+    names = jnp.zeros((1, size), F32)
+    for k in range(group):
+        names = jnp.where(line // 8 == k, roll(tail[k][2 * levels : 2 * levels + 1], 8 * k, 1), names)
     me, step = place(), group // subs
     left, right = (nearby(me, group, d * step, tail) for d in (-1, 1))
-    line = iota((1, size), 1)
+    extra = [names]
     for l in range(levels):
         near = slice(2 * l, 2 * l + 1)
-        store[CORNER_ROWS[l] : CORNER_ROWS[l] + 1] = jnp.where(line < side, left[near], right[near])
-    out[0:PUSH_ROWS] = store[...].astype(BF16)
-    out[PUSH_ROWS:] = early[...]
+        extra.append(jnp.where(line < side, left[near], right[near]))
+    extra.append(early[EARLY_ROWS:])
+    used = BLOCK_ROWS + 1 + 5 * levels
+    store[BLOCK_ROWS:] = jnp.concatenate(
+        extra + [jnp.zeros((store.shape[0] - used, size), F32)], axis=0
+    )
+    out[...] = store[...].astype(BF16)
 
 
 def ocean_halos(counts, tile_place, member_place, shape, messages, tails):
@@ -263,14 +272,12 @@
     levels, rows, width = shape
     my_tile, me = tile_place(), member_place()
     halo = {}
-    strips = [m[BLOCK_ROWS : BLOCK_ROWS + 4 * levels] for m in messages]
-    rims = [m[0:PUSH_ROWS] for m in messages]
+    extras = [m[BLOCK_ROWS:] for m in messages]
     ends = [t[2 * rows :] for t in tails]
     for dt in (-1, 1):
-        beyond = nearby(my_tile, tiles, dt, strips)
-        halo[dt, 0] = beyond[: 2 * levels] if dt < 0 else beyond[2 * levels :]
-        corners = nearby(my_tile, tiles, dt, rims)
-        corners = jnp.concatenate([corners[r : r + 1] for r in CORNER_ROWS[:levels]], axis=0)
+        extra = nearby(my_tile, tiles, dt, extras)
+        corners, strips = extra[1 : 1 + levels], extra[1 + levels : 1 + 5 * levels]
+        halo[dt, 0] = strips[: 2 * levels] if dt < 0 else strips[2 * levels :]
         at = rows - 1 if dt < 0 else 0
         for ds in (-1, 1):
             lane_at = at if ds < 0 else rows + at
@@ -383,7 +390,9 @@
     heat = (conduct[...] * warm).astype(BF16)
     for k in range(tiles):
         for m in range(members):
-            rims[k * members + m] = relays[m][k * BLOCK_ROWS : (k + 1) * BLOCK_ROWS]
+            block = relays[m][k * BLOCK_ROWS : (k + 1) * BLOCK_ROWS]
+            rims[k * members + m, 0:BLOCK_ROWS] = block.astype(F32)
+            rims[k * members + m, BLOCK_ROWS:] = jnp.zeros((2 * DEPTH, size), F32)
     half = DEPTH
     high = 2 * DEPTH
     sub = iota((high, size), 0)
@@ -393,17 +402,16 @@
     first, last = lane == 0, lane == size - 1
 
     def load(device, side, mask, with_push=True):
-        start = PUSH_ROWS + side * 2 * high
-        block = rims[device, start : start + 2 * high].astype(F32)
-        velocity, both = block[:high] * mask, block[high:]
+        start = side * EARLY_SIDE
+        velocity = rims[device, start : start + high] * mask
         if not with_push:
             return velocity
-        other = roll(both, half, 0)
-        visc = jnp.where(sub < half, both, other)
-        scale = jnp.where(sub < half, other, both) * mask
-        start = side // 2 * 2 * high
-        pushed = rims[device, start : start + 2 * high].astype(F32)
-        pushed = pushed[:high] if side % 2 == 0 else pushed[high:]
+        both = rims[device, start + high : start + 2 * high]
+        visc = jnp.where(sub < half, both, roll(both, half, 0))
+        scale = jnp.where(sub < half, roll(both, 1 - half, 0), roll(both, 1, 0)) * mask
+        start = EARLY_ROWS + side * LATE_SIDE
+        late = rims[device, start : start + high]
+        pushed = jnp.where(sub < half, late, roll(late, 1, 0))
         return [velocity, visc, scale, pushed]
 
     def follow(device, side):
@@ -663,20 +671,20 @@
 
     early, viscous, gain, step_mass, drag, conduct, speed = call(
         rims_kernel,
-        [shape(SIDE_ROWS + 4 * levels, size, dtype=BF16)] + [plane] * 5 + [planes],
+        [shape(EARLY_ROWS + 4 * levels, size)] + [plane] * 5 + [planes],
         (
             thickness.reshape(categories, size, size),
             concentration.reshape(categories, size, size),
             interleaved(ice_velocity),
             water_heat_state,
         ),
-        scratch=[pltpu.VMEM((SIDE_ROWS + 4 * levels, size), F32)],
-    )
+    )
+    extra_rows = -(-(1 + 5 * levels) // TILE_ROWS) * TILE_ROWS
     message, current_ice, push = call(
         functools.partial(forcing_kernel, group, side, levels, sub_count, member_place),
-        [shape(BLOCK_ROWS + 4 * levels, size, dtype=BF16), planes, planes],
+        [shape(BLOCK_ROWS + extra_rows, size, dtype=BF16), planes, planes],
         (step_mass, drag, wind, early, *chunks[::-1], *hops),
-        scratch=[pltpu.VMEM((PUSH_ROWS, size), F32)],
+        scratch=[pltpu.VMEM((BLOCK_ROWS + extra_rows, size), F32)],
     )
     messages = swap(message, "tile", tile_count)
 
@@ -705,13 +713,7 @@
     relayed, _ = lax.optimization_barrier(([relays[k] for k in far], warm))
     relays = swap_cores({0: relay} | dict(zip(far, relayed)))
 
-    names = jnp.stack(
-        [
-            r[:relay_rows].reshape(tile_count, BLOCK_ROWS, size)[:, NAMES_ROW, 0:8]
-            for r in relays
-        ],
-        axis=1,
-    )
+    names = jnp.stack([m[BLOCK_ROWS, : 8 * group] for m in messages])
     names = names.reshape(devices, 8).astype(jnp.int32)
     table = names[:, 0:4] * 128 + names[:, 4:8]
     table = jnp.where(table < 0, -1, table ^ device_place())
@@ -725,7 +727,7 @@
         ],
         (table, viscous, gain, drag, conduct, current_ice, speed, push, *chunks, *relays),
         scratch=[
-            pltpu.VMEM((devices, BLOCK_ROWS, size), BF16),
+            pltpu.VMEM((devices, BLOCK_ROWS + 2 * DEPTH, size), F32),
             pltpu.SMEM((devices, 4), jnp.int32),
             pltpu.SemaphoreType.DMA,
             pltpu.VMEM((2, 2, size + 4 * DEPTH, size), F32),

time: 35.9 us -> 35.5 us (0.989)
  no operation moved by 1% of the time
where the time goes in v14:
time: 35.5 us; the launch traced here: 35.4 us
  waiting for transfers between devices  13.5 us (38%)
  starting transfers between devices  12.3 us (35%)
  Pallas kernels  8.65 us (24%)
  between operations  0.77 us (2%)
    pallas_call x8, Pallas kernels, call(): pl.pallas_call(kernel, out_shape=outs, in_specs=specs, out_specs=jax.tree...  8.65 us
    ppermute x3, starting transfers between devices, swap(): got[k] = lax.ppermute(value, axes, [(i, i ^ k) for i in range(count)])  4.74 us
    ppermute x3, waiting for transfers between devices, swap(): got[k] = lax.ppermute(value, axes, [(i, i ^ k) for i in range(count)])  4.13 us
    ppermute x3, waiting for transfers between devices, swap_each(): lax.ppermute(values[k], group_axes, [(i, i ^ k) for i in range(group)])  3.23 us
    ppermute x3, starting transfers between devices, swap_each(): lax.ppermute(values[k], group_axes, [(i, i ^ k) for i in range(group)])  3.21 us
    ppermute x1, waiting for transfers between devices, shards(): lax.ppermute(value, group_axes, [(i, i ^ 2 * k + 2) for i in range(group)])  2.11 us
    ppermute x1, starting transfers between devices, swap_chips(): lax.ppermute(value, group_axes, [(i, i ^ k) for i in range(group)])  2.05 us
    ppermute x1, starting transfers between devices, shards(): lax.ppermute(value, group_axes, [(i, i ^ 2 * k + 2) for i in range(group)])  2.05 us
  transfers between devices with their start and end apart: 12, of which 9 were waited for; matrix products, arithmetic and copies ran while one was open for 0% of the time, Pallas kernels for 4%

profile of v14, /device:TPU:0, one launch (start us, length us, event | category | flops | bytes accessed | tf_op | source)
XLA Modules:
  0.0 35.4 jit_solution(15760440266562107694)
XLA Ops:
  0.6 0.0 copy-start.1
  0.6 0.0 copy-start.2
  0.7 0.0 copy-start.3
  0.7 0.0 copy-start.4
  0.7 2.5 %shard_map.131 = (bf16[336,128]{1,0:T(8,128)(2,1)}, bf16[336,128]{1,0:T(8,128)(2,1)}, bf16[336,128]{1,0:T(8,128)(2,1)}, bf16[192,128]{1,0:T(8,128)(2,1)}) custom-call(s32[1,1,4]{2,1,0:T(1,128)} %links_h.1, s32[1,4]{1,0:T(1,128)} %blocks_h.1, bf16[4,64,128]{2,1,0:T(8,128)(2,1)} %bitcast.27, bf16[4,128,128]{2,1,0:T(8,128)(2,1)} %bitcast.25, ...), custom_call_target="tpu_custom_call" | custom-call | flops 11500000256 | bytes 393248 | tf_op jit(solution)/shard_map/pallas_call | solution.py:42
  3.2 3.0 %collective-permute-start.1 = (bf16[336,128]{1,0:T(8,128)(2,1)}, bf16[336,128]{1,0:T(8,128)(2,1)S(1)}, u32[]{:S(2)}, u32[]{:S(2)}) collective-permute-start(bf16[336,128]{1,0:T(8,128)(2,1)} %get-tuple-element.29), channel_id=1, source_target_pairs={{0,2},{1,3},{2,0},{3,1},{4,6},{5,7},{6,4},{7,5},{8,10},{9,11},{10,... | collective-permute-start | bytes 258056 | tf_op jit(solution)/shard_map/ppermute | solution.py:621
  6.2 0.0 collective-permute-start.2
  6.2 0.2 collective-permute-start
  6.4 2.5 %collective-permute-done.1.refs_1_.refs_6_.refs_2_ = bf16[336,128]{1,0:T(8,128)(2,1)S(1)} collective-permute-done((bf16[336,128]{1,0:T(8,128)(2,1)}, bf16[336,128]{1,0:T(8,128)(2,1)S(1)}, u32[]{:S(2)}, u32[]{:S(2)}) %collective-permute-start.1) | collective-permute-done | bytes 86048 | tf_op jit(solution)/shard_map/ppermute | solution.py:621
  8.9 0.0 collective-permute-start.3
  8.9 0.0 copy-done.1
  8.9 0.0 copy-done.2
  8.9 0.0 copy-done.3
  8.9 0.0 copy-done.4
  9.0 0.0 copy-start
  9.0 0.0 copy-start.5
  9.0 0.2 shard_map.130
  9.2 0.7 %collective-permute-done.refs_0_.refs_7_.refs_3_ = bf16[192,128]{1,0:T(8,128)(2,1)S(1)} collective-permute-done((bf16[192,128]{1,0:T(8,128)(2,1)}, bf16[192,128]{1,0:T(8,128)(2,1)S(1)}, u32[]{:S(2)}, u32[]{:S(2)}) %collective-permute-start) | collective-permute-done | bytes 49184 | tf_op jit(solution)/shard_map/ppermute | solution.py:621
  9.9 0.0 collective-permute-done.2.refs_2_.refs_5_.refs_1_
  9.9 0.2 collective-permute-done.3.refs_4_.refs_8_
  10.1 0.0 copy-done
  10.1 0.0 copy-done.5
  10.1 0.0 copy-start.6
  10.1 0.6 %shard_map.132 = (bf16[112,128]{1,0:T(8,128)(2,1)S(1)}, f32[2,128,128]{2,1,0:T(8,128)S(1)}, f32[2,128,128]{2,1,0:T(8,128)S(1)}) custom-call(f32[128,128]{1,0:T(8,128)S(1)} %get-tuple-element.25.mass, f32[128,128]{1,0:T(8,128)S(1)} %get-tuple-element.26.drag, f32[256,128]{1,0:T(8,128)S(1)} %bitcast.24, f32[72,128]{1,0:T(8,128)S(1)} %get-tuple-element.27.early, ...), custom_call_target="tpu_custom_call" | custom-call | flops 11500000 | bytes 643072 | tf_op jit(solution)/shard_map/pallas_call | solution.py:42
  10.7 4.1 %collective-permute-start.6 = (bf16[112,128]{1,0:T(8,128)(2,1)S(1)}, bf16[112,128]{1,0:T(8,128)(2,1)S(1)}, u32[]{:S(2)}, u32[]{:S(2)}) collective-permute-start(bf16[112,128]{1,0:T(8,128)(2,1)S(1)} %get-tuple-element.32.refs_0_), channel_id=1, source_target_pairs={{0,12},{4,8},{8,4},{12,0},{1,13},{5,9},{9,5},{13,1},{2,14},{6,10},... | collective-permute-start | bytes 86024 | tf_op jit(solution)/shard_map/ppermute | solution.py:604
  14.8 0.0 collective-permute-start.5
  14.8 0.6 %collective-permute-start.4 = (bf16[112,128]{1,0:T(8,128)(2,1)S(1)}, bf16[112,128]{1,0:T(8,128)(2,1)S(1)}, u32[]{:S(2)}, u32[]{:S(2)}) collective-permute-start(bf16[112,128]{1,0:T(8,128)(2,1)S(1)} %get-tuple-element.32.refs_0_), channel_id=1, source_target_pairs={{0,4},{4,0},{8,12},{12,8},{1,5},{5,1},{9,13},{13,9},{2,6},{6,2},{1... | collective-permute-start | bytes 86024 | tf_op jit(solution)/shard_map/ppermute | solution.py:604
  15.5 1.2 %collective-permute-done.6.refs_3_ = bf16[112,128]{1,0:T(8,128)(2,1)S(1)} collective-permute-done((bf16[112,128]{1,0:T(8,128)(2,1)S(1)}, bf16[112,128]{1,0:T(8,128)(2,1)S(1)}, u32[]{:S(2)}, u32[]{:S(2)}) %collective-permute-start.6) | collective-permute-done | bytes 28704 | tf_op jit(solution)/shard_map/ppermute | solution.py:604
  16.7 2.9 %collective-permute-done.5.refs_2_ = bf16[112,128]{1,0:T(8,128)(2,1)S(1)} collective-permute-done((bf16[112,128]{1,0:T(8,128)(2,1)S(1)}, bf16[112,128]{1,0:T(8,128)(2,1)S(1)}, u32[]{:S(2)}, u32[]{:S(2)}) %collective-permute-start.5) | collective-permute-done | bytes 28704 | tf_op jit(solution)/shard_map/ppermute | solution.py:604
  19.6 0.0 collective-permute-done.4.refs_1_
  19.6 0.0 copy-done.6
  19.6 0.4 %shard_map.133.refs_4_ = bf16[384,128]{1,0:T(8,128)(2,1)S(1)} custom-call(f32[4,64,128]{2,1,0:T(8,128)S(1)} %copy-done.1, f32[64,128]{1,0:T(8,128)S(1)} %copy-done.6, bf16[112,128]{1,0:T(8,128)(2,1)S(1)} %get-tuple-element.32.refs_0_, bf16[112,128]{1,0:T(8,128)(2,1)S(1)} %collective-permute-done.4.refs_1_, ...), custom_call_target="tpu_custom_call" | custom-call | flops 11500000 | bytes 622592 | tf_op jit(solution)/shard_map/pallas_call | solution.py:42
  20.0 2.0 %collective-permute-start.8 = (bf16[384,128]{1,0:T(8,128)(2,1)S(1)}, bf16[384,128]{1,0:T(8,128)(2,1)S(1)}, u32[]{:S(2)}, u32[]{:S(2)}) collective-permute-start(bf16[384,128]{1,0:T(8,128)(2,1)S(1)} %shard_map.133.refs_4_), channel_id=1, source_target_pairs={{0,2},{1,3},{2,0},{3,1},{4,6},{5,7},{6,4},{7,5},{8,10},{9,11},{10,... | collective-permute-start | bytes 294920 | tf_op jit(solution)/shard_map/ppermute | solution.py:609
  22.1 0.0 collective-permute-start.7
  22.1 0.1 reshape.41
  22.2 1.1 %shard_map.134.warm = f32[4,64,128]{2,1,0:T(8,128)S(1)} custom-call(f32[4,64,128]{2,1,0:T(8,128)S(1)} %copy-done.1, f32[64,128]{1,0:T(8,128)S(1)} %copy-done.6, bf16[112,128]{1,0:T(8,128)(2,1)S(1)} %get-tuple-element.32.refs_0_, bf16[112,128]{1,0:T(8,128)(2,1)S(1)} %collective-permute-done.4.refs_1_, bf16[112,128]{1,0:T(8,128)(2,1)S(1)} %collective-permute-done.5.refs_2_, ...), custom_call_target="tpu_custom_call" | custom-call | flops 11500000 | bytes 622592 | tf_op jit(solution)/shard_map/pallas_call | solution.py:42
  23.3 1.4 %collective-permute-done.8.refs_6_ = bf16[384,128]{1,0:T(8,128)(2,1)S(1)} collective-permute-done((bf16[384,128]{1,0:T(8,128)(2,1)S(1)}, bf16[384,128]{1,0:T(8,128)(2,1)S(1)}, u32[]{:S(2)}, u32[]{:S(2)}) %collective-permute-start.8) | collective-permute-done | bytes 98336 | tf_op jit(solution)/shard_map/ppermute | solution.py:609
  24.7 0.0 collective-permute-start.9
  24.7 0.1 xor_select_fusion.table
  24.8 0.0 collective-permute-done.7.refs_5_
  24.8 1.2 %collective-permute-done.9.refs_7_ = bf16[384,128]{1,0:T(8,128)(2,1)S(1)} collective-permute-done((bf16[384,128]{1,0:T(8,128)(2,1)S(1)}, bf16[384,128]{1,0:T(8,128)(2,1)S(1)}, u32[]{:S(2)}, u32[]{:S(2)}) %collective-permute-start.9) | collective-permute-done | bytes 98336 | tf_op jit(solution)/shard_map/ppermute | solution.py:615
  26.0 3.1 %shard_map.135 = (f32[2,128,128]{2,1,0:T(8,128)S(1)}, f32[384,128]{1,0:T(8,128)S(1)}, bf16[384,128]{1,0:T(8,128)(2,1)S(1)}) custom-call(s32[16,4]{1,0:T(8,128)S(1)} %xor_select_fusion.table, f32[128,128]{1,0:T(8,128)S(1)} %get-tuple-element.34.viscous, f32[128,128]{1,0:T(8,128)S(1)} %get-tuple-element.35.gain, f32[128,128]{1,0:T(8,128)S(1)} %get-tuple-element.26.drag, ...), custom_call_target="tpu_custom_call" | custom-call | flops 11500000 | bytes 1356032 | tf_op jit(solution)/shard_map/pallas_call | solution.py:42
  29.1 0.2 collective-permute-start.10
  29.3 1.1 %collective-permute-done.10.beside = bf16[384,128]{1,0:T(8,128)(2,1)S(1)} collective-permute-done((bf16[384,128]{1,0:T(8,128)(2,1)S(1)}, bf16[384,128]{1,0:T(8,128)(2,1)S(1)}, u32[]{:S(2)}, u32[]{:S(2)}) %collective-permute-start.10) | collective-permute-done | bytes 98336 | tf_op jit(solution)/shard_map/ppermute | solution.py:737
  30.4 0.0 copy-start.7
  30.5 2.0 %collective-permute-start.11 = (bf16[192,128]{1,0:T(8,128)(2,1)S(1)}, bf16[192,128]{1,0:T(8,128)(2,1)S(1)}, u32[]{:S(2)}, u32[]{:S(2)}) collective-permute-start(bf16[192,128]{1,0:T(8,128)(2,1)S(1)} %shard_map.136), channel_id=1, source_target_pairs={{0,2},{1,3},{2,0},{3,1},{4,6},{5,7},{6,4},{7,5},{8,10},{9,11},{10,... | collective-permute-start | bytes 147464 | tf_op jit(solution)/shard_map/ppermute | solution.py:742
  32.5 2.1 %collective-permute-done.11.refs_0_ = bf16[192,128]{1,0:T(8,128)(2,1)S(1)} collective-permute-done((bf16[192,128]{1,0:T(8,128)(2,1)S(1)}, bf16[192,128]{1,0:T(8,128)(2,1)S(1)}, u32[]{:S(2)}, u32[]{:S(2)}) %collective-permute-start.11) | collective-permute-done | bytes 49184 | tf_op jit(solution)/shard_map/ppermute | solution.py:742
  34.6 0.0 copy-done.7
  34.6 0.7 %shard_map.137 = (f32[256,128]{1,0:T(8,128)}, f32[4,64,128]{2,1,0:T(8,128)}, f32[2,64,128]{2,1,0:T(8,128)}) custom-call(f32[4,64,128]{2,1,0:T(8,128)S(1)} %shard_map.134.warm, f32[2,64,128]{2,1,0:T(8,128)S(1)} %copy-done.7, f32[2,128,128]{2,1,0:T(8,128)S(1)} %get-tuple-element.41.speed, f32[384,128]{1,0:T(8,128)S(1)} %get-tuple-element.42.own, ...), custom_call_target="tpu_custom_call" | custom-call | flops 11500000 | bytes 671744 | tf_op jit(solution)/shard_map/pallas_call | solution.py:42
  (7 shorter events, 0.0 us)
Async XLA Ops:
  0.6 8.3 %copy-start.1 = (f32[4,64,128]{2,1,0:T(8,128)S(1)}, f32[4,64,128]{2,1,0:T(8,128)}, u32[]{:S(2)}) copy-start(f32[4,64,128]{2,1,0:T(8,128)} %water.5) | copy-start | bytes 393220
  0.6 8.3 %copy-start.2 = (f32[1,1,5,16384]{3,1,2,0:T(1,128)S(1)}, f32[1,1,5,16384]{3,1,2,0:T(1,128)}, u32[]{:S(2)}) copy-start(f32[1,1,5,16384]{3,1,2,0:T(1,128)} %param.18) | copy-start | bytes 983044
  0.7 8.3 %copy-start.3 = (f32[1,1,5,16384]{3,1,2,0:T(1,128)S(1)}, f32[1,1,5,16384]{3,1,2,0:T(1,128)}, u32[]{:S(2)}) copy-start(f32[1,1,5,16384]{3,1,2,0:T(1,128)} %param.19) | copy-start | bytes 983044
  0.7 8.3 %copy-start.4 = (f32[1,1,2,16384]{3,2,1,0:T(2,128)S(1)}, f32[1,1,2,16384]{3,2,1,0:T(2,128)}, u32[]{:S(2)}) copy-start(f32[1,1,2,16384]{3,2,1,0:T(2,128)} %param.20) | copy-start | bytes 393220
  3.2 5.7 %collective-permute-start.1 = (bf16[336,128]{1,0:T(8,128)(2,1)}, bf16[336,128]{1,0:T(8,128)(2,1)S(1)}, u32[]{:S(2)}, u32[]{:S(2)}) collective-permute-start(bf16[336,128]{1,0:T(8,128)(2,1)} %get-tuple-element.29), channel_id=1, source_target_pairs={{0,2},{1,3},{2,0},{3,1},{4,6},{5,7},{6,4},{7,5},{8,10},{9,11},{10,... | collective-permute-start | bytes 258056 | tf_op jit(solution)/shard_map/ppermute | solution.py:621
  6.2 3.7 %collective-permute-start.2 = (bf16[336,128]{1,0:T(8,128)(2,1)}, bf16[336,128]{1,0:T(8,128)(2,1)S(1)}, u32[]{:S(2)}, u32[]{:S(2)}) collective-permute-start(bf16[336,128]{1,0:T(8,128)(2,1)} %get-tuple-element.30), channel_id=1, source_target_pairs={{0,1},{1,0},{2,3},{3,2},{4,5},{5,4},{6,7},{7,6},{8,9},{9,8},{10,11... | collective-permute-start | bytes 258056 | tf_op jit(solution)/shard_map/ppermute | solution.py:621
  6.2 3.7 %collective-permute-start = (bf16[192,128]{1,0:T(8,128)(2,1)}, bf16[192,128]{1,0:T(8,128)(2,1)S(1)}, u32[]{:S(2)}, u32[]{:S(2)}) collective-permute-start(bf16[192,128]{1,0:T(8,128)(2,1)} %get-tuple-element.28), channel_id=1, source_target_pairs={{0,3},{1,2},{2,1},{3,0},{4,7},{5,6},{6,5},{7,4},{8,11},{9,10},{10,... | collective-permute-start | bytes 147464 | tf_op jit(solution)/shard_map/ppermute | solution.py:621
  8.9 1.2 %collective-permute-start.3 = (bf16[144,128]{1,0:T(8,128)(2,1)S(1)}, bf16[144,128]{1,0:T(8,128)(2,1)S(1)}, u32[]{:S(2)}, u32[]{:S(2)}) collective-permute-start(bf16[144,128]{1,0:T(8,128)(2,1)S(1)} %slice.28), channel_id=1, source_target_pairs={{0,1},{1,0},{2,3},{3,2},{4,5},{5,4},{6,7},{7,6},{8,9},{9,8},{10,11... | collective-permute-start | bytes 110600 | tf_op jit(solution)/shard_map/ppermute | solution.py:668
  9.0 1.2 %copy-start = (bf16[336,128]{1,0:T(8,128)(2,1)S(1)}, bf16[336,128]{1,0:T(8,128)(2,1)}, u32[]{:S(2)}) copy-start(bf16[336,128]{1,0:T(8,128)(2,1)} %get-tuple-element.31.refs_3_.refs_4_.refs_0_) | copy-start | bytes 258052
  9.0 1.2 %copy-start.5 = (f32[1,1,2,16384]{3,2,1,0:T(2,128)S(1)}, f32[1,1,2,16384]{3,2,1,0:T(2,128)}, u32[]{:S(2)}) copy-start(f32[1,1,2,16384]{3,2,1,0:T(2,128)} %param.21) | copy-start | bytes 393220
  10.1 9.5 %copy-start.6 = (f32[64,128]{1,0:T(8,128)S(1)}, f32[64,128]{1,0:T(8,128)}, u32[]{:S(2)}) copy-start(f32[64,128]{1,0:T(8,128)} %mixing.2) | copy-start | bytes 98308
  10.7 6.0 %collective-permute-start.6 = (bf16[112,128]{1,0:T(8,128)(2,1)S(1)}, bf16[112,128]{1,0:T(8,128)(2,1)S(1)}, u32[]{:S(2)}, u32[]{:S(2)}) collective-permute-start(bf16[112,128]{1,0:T(8,128)(2,1)S(1)} %get-tuple-element.32.refs_0_), channel_id=1, source_target_pairs={{0,12},{4,8},{8,4},{12,0},{1,13},{5,9},{9,5},{13,1},{2,14},{6,10},... | collective-permute-start | bytes 86024 | tf_op jit(solution)/shard_map/ppermute | solution.py:604
  14.8 4.8 %collective-permute-start.5 = (bf16[112,128]{1,0:T(8,128)(2,1)S(1)}, bf16[112,128]{1,0:T(8,128)(2,1)S(1)}, u32[]{:S(2)}, u32[]{:S(2)}) collective-permute-start(bf16[112,128]{1,0:T(8,128)(2,1)S(1)} %get-tuple-element.32.refs_0_), channel_id=1, source_target_pairs={{0,8},{4,12},{8,0},{12,4},{1,9},{5,13},{9,1},{13,5},{2,10},{6,14},... | collective-permute-start | bytes 86024 | tf_op jit(solution)/shard_map/ppermute | solution.py:604
  14.8 4.8 %collective-permute-start.4 = (bf16[112,128]{1,0:T(8,128)(2,1)S(1)}, bf16[112,128]{1,0:T(8,128)(2,1)S(1)}, u32[]{:S(2)}, u32[]{:S(2)}) collective-permute-start(bf16[112,128]{1,0:T(8,128)(2,1)S(1)} %get-tuple-element.32.refs_0_), channel_id=1, source_target_pairs={{0,4},{4,0},{8,12},{12,8},{1,5},{5,1},{9,13},{13,9},{2,6},{6,2},{1... | collective-permute-start | bytes 86024 | tf_op jit(solution)/shard_map/ppermute | solution.py:604
  20.0 4.7 %collective-permute-start.8 = (bf16[384,128]{1,0:T(8,128)(2,1)S(1)}, bf16[384,128]{1,0:T(8,128)(2,1)S(1)}, u32[]{:S(2)}, u32[]{:S(2)}) collective-permute-start(bf16[384,128]{1,0:T(8,128)(2,1)S(1)} %shard_map.133.refs_4_), channel_id=1, source_target_pairs={{0,2},{1,3},{2,0},{3,1},{4,6},{5,7},{6,4},{7,5},{8,10},{9,11},{10,... | collective-permute-start | bytes 294920 | tf_op jit(solution)/shard_map/ppermute | solution.py:609
  22.1 2.7 %collective-permute-start.7 = (bf16[384,128]{1,0:T(8,128)(2,1)S(1)}, bf16[384,128]{1,0:T(8,128)(2,1)S(1)}, u32[]{:S(2)}, u32[]{:S(2)}) collective-permute-start(bf16[384,128]{1,0:T(8,128)(2,1)S(1)} %shard_map.133.refs_4_), channel_id=1, source_target_pairs={{0,1},{1,0},{2,3},{3,2},{4,5},{5,4},{6,7},{7,6},{8,9},{9,8},{10,11... | collective-permute-start | bytes 294920 | tf_op jit(solution)/shard_map/ppermute | solution.py:615
  24.7 1.3 %collective-permute-start.9 = (bf16[384,128]{1,0:T(8,128)(2,1)S(1)}, bf16[384,128]{1,0:T(8,128)(2,1)S(1)}, u32[]{:S(2)}, u32[]{:S(2)}) collective-permute-start(bf16[384,128]{1,0:T(8,128)(2,1)S(1)} %collective-permute-done.8.refs_6_), channel_id=1, source_target_pairs={{0,1},{1,0},{2,3},{3,2},{4,5},{5,4},{6,7},{7,6},{8,9},{9,8},{10,11... | collective-permute-start | bytes 294920 | tf_op jit(solution)/shard_map/ppermute | solution.py:615
  29.1 1.4 %collective-permute-start.10 = (bf16[384,128]{1,0:T(8,128)(2,1)S(1)}, bf16[384,128]{1,0:T(8,128)(2,1)S(1)}, u32[]{:S(2)}, u32[]{:S(2)}) collective-permute-start(bf16[384,128]{1,0:T(8,128)(2,1)S(1)} %get-tuple-element.43), channel_id=1, source_target_pairs={{0,1},{1,0},{2,3},{3,2},{4,5},{5,4},{6,7},{7,6},{8,9},{9,8},{10,11... | collective-permute-start | bytes 294920 | tf_op jit(solution)/shard_map/ppermute | solution.py:737
  30.4 4.2 %copy-start.7 = (f32[2,64,128]{2,1,0:T(8,128)S(1)}, f32[2,64,128]{2,1,0:T(8,128)}, u32[]{:S(2)}) copy-start(f32[2,64,128]{2,1,0:T(8,128)} %currents.1) | copy-start | bytes 196612
  30.5 4.2 %collective-permute-start.11 = (bf16[192,128]{1,0:T(8,128)(2,1)S(1)}, bf16[192,128]{1,0:T(8,128)(2,1)S(1)}, u32[]{:S(2)}, u32[]{:S(2)}) collective-permute-start(bf16[192,128]{1,0:T(8,128)(2,1)S(1)} %shard_map.136), channel_id=1, source_target_pairs={{0,2},{1,3},{2,0},{3,1},{4,6},{5,7},{6,4},{7,5},{8,10},{9,11},{10,... | collective-permute-start | bytes 147464 | tf_op jit(solution)/shard_map/ppermute | solution.py:742

commit v15 on v14

--- a/solution.py
+++ b/solution.py
@@ -319,8 +319,13 @@
     )
 
 
+def spread_out(count):
+    return sorted(range(count), key=lambda k: (k == count // 2, k))
+
+
 def split_refs(tiles, members, refs, outs):
-    messages, chunks = refs[:tiles], refs[tiles : tiles + members]
+    messages = [refs[spread_out(tiles).index(k)] for k in range(tiles)]
+    chunks = refs[tiles : tiles + members]
     return messages, tails_of(chunks, refs[tiles + members : -outs]), refs[-outs:]
 
 
@@ -386,8 +391,6 @@
     load_names.start()
     size = viscous.shape[0]
     depth = chunks[0].shape[1]
-    warm = remap_forward(chunks, [[r[r.shape[0] - side :]] for r in relays], side, depth)
-    heat = (conduct[...] * warm).astype(BF16)
     for k in range(tiles):
         for m in range(members):
             block = relays[m][k * BLOCK_ROWS : (k + 1) * BLOCK_ROWS]
@@ -458,6 +461,9 @@
                 ]
             )
         strips.append((strip, sides))
+
+    warm = remap_forward(chunks, [[r[r.shape[0] - side :]] for r in relays], side, depth)
+    heat = (conduct[...] * warm).astype(BF16)
 
     for t in range(SUBCYCLES):
         cells = [strip[0] for strip, _ in strips]
@@ -689,7 +695,7 @@
     messages = swap(message, "tile", tile_count)
 
     counts = (tile_count, sub_count, lev_count)
-    ocean = (*messages, *chunks, *hops)
+    ocean = (*(messages[k] for k in spread_out(tile_count)), *chunks, *hops)
     relay_rows = tile_count * BLOCK_ROWS
     relay_shapes = [shape(relay_rows + (side if lev_count == 1 else 0), size, dtype=BF16)]
     if lev_count > 1:

time: 35.5 us -> 35.2 us (level)
  no operation moved by 1% of the time
where the time goes in v15:
time: 35.2 us; the launch traced here: 35.1 us
  waiting for transfers between devices  13.4 us (38%)
  starting transfers between devices  12.2 us (35%)
  Pallas kernels  8.46 us (24%)
  between operations  0.77 us (2%)
    pallas_call x8, Pallas kernels, call(): pl.pallas_call(kernel, out_shape=outs, in_specs=specs, out_specs=jax.tree...  8.46 us
    ppermute x3, starting transfers between devices, swap(): got[k] = lax.ppermute(value, axes, [(i, i ^ k) for i in range(count)])  4.67 us
    ppermute x3, waiting for transfers between devices, swap(): got[k] = lax.ppermute(value, axes, [(i, i ^ k) for i in range(count)])  4.09 us
    ppermute x3, waiting for transfers between devices, swap_each(): lax.ppermute(values[k], group_axes, [(i, i ^ k) for i in range(group)])  3.23 us
    ppermute x3, starting transfers between devices, swap_each(): lax.ppermute(values[k], group_axes, [(i, i ^ k) for i in range(group)])  3.21 us
    ppermute x1, waiting for transfers between devices, shards(): lax.ppermute(value, group_axes, [(i, i ^ 2 * k + 2) for i in range(group)])  2.11 us
    ppermute x1, starting transfers between devices, swap_chips(): lax.ppermute(value, group_axes, [(i, i ^ k) for i in range(group)])  2.05 us
    ppermute x1, starting transfers between devices, shards(): lax.ppermute(value, group_axes, [(i, i ^ 2 * k + 2) for i in range(group)])  2.05 us
  transfers between devices with their start and end apart: 12, of which 9 were waited for; matrix products, arithmetic and copies ran while one was open for 0% of the time, Pallas kernels for 4%

profile of v15, /device:TPU:0, one launch (start us, length us, event | category | flops | bytes accessed | tf_op | source)
XLA Modules:
  0.0 35.1 jit_solution(15996054425414841550)
XLA Ops:
  0.6 0.0 copy-start.1
  0.6 0.0 copy-start.2
  0.7 0.0 copy-start.3
  0.7 0.0 copy-start.4
  0.7 2.5 %shard_map.131 = (bf16[336,128]{1,0:T(8,128)(2,1)}, bf16[336,128]{1,0:T(8,128)(2,1)}, bf16[336,128]{1,0:T(8,128)(2,1)}, bf16[192,128]{1,0:T(8,128)(2,1)}) custom-call(s32[1,1,4]{2,1,0:T(1,128)} %links_h.1, s32[1,4]{1,0:T(1,128)} %blocks_h.1, bf16[4,64,128]{2,1,0:T(8,128)(2,1)} %bitcast.27, bf16[4,128,128]{2,1,0:T(8,128)(2,1)} %bitcast.25, ...), custom_call_target="tpu_custom_call" | custom-call | flops 11500000256 | bytes 393248 | tf_op jit(solution)/shard_map/pallas_call | solution.py:42
  3.2 3.0 %collective-permute-start.1 = (bf16[336,128]{1,0:T(8,128)(2,1)}, bf16[336,128]{1,0:T(8,128)(2,1)S(1)}, u32[]{:S(2)}, u32[]{:S(2)}) collective-permute-start(bf16[336,128]{1,0:T(8,128)(2,1)} %get-tuple-element.29), channel_id=1, source_target_pairs={{0,2},{1,3},{2,0},{3,1},{4,6},{5,7},{6,4},{7,5},{8,10},{9,11},{10,... | collective-permute-start | bytes 258056 | tf_op jit(solution)/shard_map/ppermute | solution.py:627
  6.2 0.0 collective-permute-start.2
  6.2 0.2 collective-permute-start
  6.4 2.5 %collective-permute-done.1.refs_1_.refs_6_.refs_2_ = bf16[336,128]{1,0:T(8,128)(2,1)S(1)} collective-permute-done((bf16[336,128]{1,0:T(8,128)(2,1)}, bf16[336,128]{1,0:T(8,128)(2,1)S(1)}, u32[]{:S(2)}, u32[]{:S(2)}) %collective-permute-start.1) | collective-permute-done | bytes 86048 | tf_op jit(solution)/shard_map/ppermute | solution.py:627
  8.9 0.0 collective-permute-start.3
  8.9 0.0 copy-done.1
  8.9 0.0 copy-done.2
  8.9 0.0 copy-done.3
  8.9 0.0 copy-done.4
  9.0 0.0 copy-start
  9.0 0.0 copy-start.5
  9.0 0.2 shard_map.130
  9.2 0.7 %collective-permute-done.refs_0_.refs_7_.refs_3_ = bf16[192,128]{1,0:T(8,128)(2,1)S(1)} collective-permute-done((bf16[192,128]{1,0:T(8,128)(2,1)}, bf16[192,128]{1,0:T(8,128)(2,1)S(1)}, u32[]{:S(2)}, u32[]{:S(2)}) %collective-permute-start) | collective-permute-done | bytes 49184 | tf_op jit(solution)/shard_map/ppermute | solution.py:627
  9.9 0.0 collective-permute-done.2.refs_2_.refs_5_.refs_1_
  9.9 0.2 collective-permute-done.3.refs_4_.refs_8_
  10.1 0.0 copy-done
  10.1 0.0 copy-done.5
  10.1 0.0 copy-start.6
  10.1 0.6 %shard_map.132 = (bf16[112,128]{1,0:T(8,128)(2,1)S(1)}, f32[2,128,128]{2,1,0:T(8,128)S(1)}, f32[2,128,128]{2,1,0:T(8,128)S(1)}) custom-call(f32[128,128]{1,0:T(8,128)S(1)} %get-tuple-element.25.mass, f32[128,128]{1,0:T(8,128)S(1)} %get-tuple-element.26.drag, f32[256,128]{1,0:T(8,128)S(1)} %bitcast.24, f32[72,128]{1,0:T(8,128)S(1)} %get-tuple-element.27.early, ...), custom_call_target="tpu_custom_call" | custom-call | flops 11500000 | bytes 643072 | tf_op jit(solution)/shard_map/pallas_call | solution.py:42
  10.7 3.1 %collective-permute-start.6 = (bf16[112,128]{1,0:T(8,128)(2,1)S(1)}, bf16[112,128]{1,0:T(8,128)(2,1)S(1)}, u32[]{:S(2)}, u32[]{:S(2)}) collective-permute-start(bf16[112,128]{1,0:T(8,128)(2,1)S(1)} %get-tuple-element.32.refs_0_), channel_id=1, source_target_pairs={{0,8},{4,12},{8,0},{12,4},{1,9},{5,13},{9,1},{13,5},{2,10},{6,14},... | collective-permute-start | bytes 86024 | tf_op jit(solution)/shard_map/ppermute | solution.py:610
  13.8 1.3 %collective-permute-start.5 = (bf16[112,128]{1,0:T(8,128)(2,1)S(1)}, bf16[112,128]{1,0:T(8,128)(2,1)S(1)}, u32[]{:S(2)}, u32[]{:S(2)}) collective-permute-start(bf16[112,128]{1,0:T(8,128)(2,1)S(1)} %get-tuple-element.32.refs_0_), channel_id=1, source_target_pairs={{0,12},{4,8},{8,4},{12,0},{1,13},{5,9},{9,5},{13,1},{2,14},{6,10},... | collective-permute-start | bytes 86024 | tf_op jit(solution)/shard_map/ppermute | solution.py:610
  15.2 0.2 collective-permute-start.4
  15.4 0.3 collective-permute-done.6.refs_3_
  15.7 3.8 %collective-permute-done.5.refs_2_ = bf16[112,128]{1,0:T(8,128)(2,1)S(1)} collective-permute-done((bf16[112,128]{1,0:T(8,128)(2,1)S(1)}, bf16[112,128]{1,0:T(8,128)(2,1)S(1)}, u32[]{:S(2)}, u32[]{:S(2)}) %collective-permute-start.5) | collective-permute-done | bytes 28704 | tf_op jit(solution)/shard_map/ppermute | solution.py:610
  19.5 0.0 collective-permute-done.4.refs_1_
  19.5 0.0 copy-done.6
  19.5 0.4 %shard_map.133.refs_4_ = bf16[384,128]{1,0:T(8,128)(2,1)S(1)} custom-call(f32[4,64,128]{2,1,0:T(8,128)S(1)} %copy-done.1, f32[64,128]{1,0:T(8,128)S(1)} %copy-done.6, bf16[112,128]{1,0:T(8,128)(2,1)S(1)} %get-tuple-element.32.refs_0_, bf16[112,128]{1,0:T(8,128)(2,1)S(1)} %collective-permute-done.4.refs_1_, ...), custom_call_target="tpu_custom_call" | custom-call | flops 11500000 | bytes 622592 | tf_op jit(solution)/shard_map/pallas_call | solution.py:42
  19.9 2.0 %collective-permute-start.8 = (bf16[384,128]{1,0:T(8,128)(2,1)S(1)}, bf16[384,128]{1,0:T(8,128)(2,1)S(1)}, u32[]{:S(2)}, u32[]{:S(2)}) collective-permute-start(bf16[384,128]{1,0:T(8,128)(2,1)S(1)} %shard_map.133.refs_4_), channel_id=1, source_target_pairs={{0,2},{1,3},{2,0},{3,1},{4,6},{5,7},{6,4},{7,5},{8,10},{9,11},{10,... | collective-permute-start | bytes 294920 | tf_op jit(solution)/shard_map/ppermute | solution.py:615
  22.0 0.0 collective-permute-start.7
  22.0 0.1 reshape.41
  22.1 1.1 %shard_map.134.warm = f32[4,64,128]{2,1,0:T(8,128)S(1)} custom-call(f32[4,64,128]{2,1,0:T(8,128)S(1)} %copy-done.1, f32[64,128]{1,0:T(8,128)S(1)} %copy-done.6, bf16[112,128]{1,0:T(8,128)(2,1)S(1)} %get-tuple-element.32.refs_0_, bf16[112,128]{1,0:T(8,128)(2,1)S(1)} %collective-permute-done.4.refs_1_, bf16[112,128]{1,0:T(8,128)(2,1)S(1)} %collective-permute-done.5.refs_2_, ...), custom_call_target="tpu_custom_call" | custom-call | flops 11500000 | bytes 622592 | tf_op jit(solution)/shard_map/pallas_call | solution.py:42
  23.2 1.4 %collective-permute-done.8.refs_6_ = bf16[384,128]{1,0:T(8,128)(2,1)S(1)} collective-permute-done((bf16[384,128]{1,0:T(8,128)(2,1)S(1)}, bf16[384,128]{1,0:T(8,128)(2,1)S(1)}, u32[]{:S(2)}, u32[]{:S(2)}) %collective-permute-start.8) | collective-permute-done | bytes 98336 | tf_op jit(solution)/shard_map/ppermute | solution.py:615
  24.6 0.0 collective-permute-start.9
  24.6 0.1 xor_select_fusion.table
  24.7 0.0 collective-permute-done.7.refs_5_
  24.7 1.2 %collective-permute-done.9.refs_7_ = bf16[384,128]{1,0:T(8,128)(2,1)S(1)} collective-permute-done((bf16[384,128]{1,0:T(8,128)(2,1)S(1)}, bf16[384,128]{1,0:T(8,128)(2,1)S(1)}, u32[]{:S(2)}, u32[]{:S(2)}) %collective-permute-start.9) | collective-permute-done | bytes 98336 | tf_op jit(solution)/shard_map/ppermute | solution.py:621
  25.9 2.9 %shard_map.135 = (f32[2,128,128]{2,1,0:T(8,128)S(1)}, f32[384,128]{1,0:T(8,128)S(1)}, bf16[384,128]{1,0:T(8,128)(2,1)S(1)}) custom-call(s32[16,4]{1,0:T(8,128)S(1)} %xor_select_fusion.table, f32[128,128]{1,0:T(8,128)S(1)} %get-tuple-element.34.viscous, f32[128,128]{1,0:T(8,128)S(1)} %get-tuple-element.35.gain, f32[128,128]{1,0:T(8,128)S(1)} %get-tuple-element.26.drag, ...), custom_call_target="tpu_custom_call" | custom-call | flops 11500000 | bytes 1356032 | tf_op jit(solution)/shard_map/pallas_call | solution.py:42
  28.8 0.2 collective-permute-start.10
  29.0 1.1 %collective-permute-done.10.beside = bf16[384,128]{1,0:T(8,128)(2,1)S(1)} collective-permute-done((bf16[384,128]{1,0:T(8,128)(2,1)S(1)}, bf16[384,128]{1,0:T(8,128)(2,1)S(1)}, u32[]{:S(2)}, u32[]{:S(2)}) %collective-permute-start.10) | collective-permute-done | bytes 98336 | tf_op jit(solution)/shard_map/ppermute | solution.py:743
  30.1 0.0 copy-start.7
  30.2 2.0 %collective-permute-start.11 = (bf16[192,128]{1,0:T(8,128)(2,1)S(1)}, bf16[192,128]{1,0:T(8,128)(2,1)S(1)}, u32[]{:S(2)}, u32[]{:S(2)}) collective-permute-start(bf16[192,128]{1,0:T(8,128)(2,1)S(1)} %shard_map.136), channel_id=1, source_target_pairs={{0,2},{1,3},{2,0},{3,1},{4,6},{5,7},{6,4},{7,5},{8,10},{9,11},{10,... | collective-permute-start | bytes 147464 | tf_op jit(solution)/shard_map/ppermute | solution.py:748
  32.2 2.1 %collective-permute-done.11.refs_0_ = bf16[192,128]{1,0:T(8,128)(2,1)S(1)} collective-permute-done((bf16[192,128]{1,0:T(8,128)(2,1)S(1)}, bf16[192,128]{1,0:T(8,128)(2,1)S(1)}, u32[]{:S(2)}, u32[]{:S(2)}) %collective-permute-start.11) | collective-permute-done | bytes 49184 | tf_op jit(solution)/shard_map/ppermute | solution.py:748
  34.3 0.0 copy-done.7
  34.3 0.7 %shard_map.137 = (f32[256,128]{1,0:T(8,128)}, f32[4,64,128]{2,1,0:T(8,128)}, f32[2,64,128]{2,1,0:T(8,128)}) custom-call(f32[4,64,128]{2,1,0:T(8,128)S(1)} %shard_map.134.warm, f32[2,64,128]{2,1,0:T(8,128)S(1)} %copy-done.7, f32[2,128,128]{2,1,0:T(8,128)S(1)} %get-tuple-element.41.speed, f32[384,128]{1,0:T(8,128)S(1)} %get-tuple-element.42.own, ...), custom_call_target="tpu_custom_call" | custom-call | flops 11500000 | bytes 671744 | tf_op jit(solution)/shard_map/pallas_call | solution.py:42
  (7 shorter events, 0.0 us)
Async XLA Ops:
  0.6 8.3 %copy-start.1 = (f32[4,64,128]{2,1,0:T(8,128)S(1)}, f32[4,64,128]{2,1,0:T(8,128)}, u32[]{:S(2)}) copy-start(f32[4,64,128]{2,1,0:T(8,128)} %water.5) | copy-start | bytes 393220
  0.6 8.3 %copy-start.2 = (f32[1,1,5,16384]{3,1,2,0:T(1,128)S(1)}, f32[1,1,5,16384]{3,1,2,0:T(1,128)}, u32[]{:S(2)}) copy-start(f32[1,1,5,16384]{3,1,2,0:T(1,128)} %param.18) | copy-start | bytes 983044
  0.7 8.3 %copy-start.3 = (f32[1,1,5,16384]{3,1,2,0:T(1,128)S(1)}, f32[1,1,5,16384]{3,1,2,0:T(1,128)}, u32[]{:S(2)}) copy-start(f32[1,1,5,16384]{3,1,2,0:T(1,128)} %param.19) | copy-start | bytes 983044
  0.7 8.3 %copy-start.4 = (f32[1,1,2,16384]{3,2,1,0:T(2,128)S(1)}, f32[1,1,2,16384]{3,2,1,0:T(2,128)}, u32[]{:S(2)}) copy-start(f32[1,1,2,16384]{3,2,1,0:T(2,128)} %param.20) | copy-start | bytes 393220
  3.2 5.7 %collective-permute-start.1 = (bf16[336,128]{1,0:T(8,128)(2,1)}, bf16[336,128]{1,0:T(8,128)(2,1)S(1)}, u32[]{:S(2)}, u32[]{:S(2)}) collective-permute-start(bf16[336,128]{1,0:T(8,128)(2,1)} %get-tuple-element.29), channel_id=1, source_target_pairs={{0,2},{1,3},{2,0},{3,1},{4,6},{5,7},{6,4},{7,5},{8,10},{9,11},{10,... | collective-permute-start | bytes 258056 | tf_op jit(solution)/shard_map/ppermute | solution.py:627
  6.2 3.7 %collective-permute-start.2 = (bf16[336,128]{1,0:T(8,128)(2,1)}, bf16[336,128]{1,0:T(8,128)(2,1)S(1)}, u32[]{:S(2)}, u32[]{:S(2)}) collective-permute-start(bf16[336,128]{1,0:T(8,128)(2,1)} %get-tuple-element.30), channel_id=1, source_target_pairs={{0,1},{1,0},{2,3},{3,2},{4,5},{5,4},{6,7},{7,6},{8,9},{9,8},{10,11... | collective-permute-start | bytes 258056 | tf_op jit(solution)/shard_map/ppermute | solution.py:627
  6.2 3.7 %collective-permute-start = (bf16[192,128]{1,0:T(8,128)(2,1)}, bf16[192,128]{1,0:T(8,128)(2,1)S(1)}, u32[]{:S(2)}, u32[]{:S(2)}) collective-permute-start(bf16[192,128]{1,0:T(8,128)(2,1)} %get-tuple-element.28), channel_id=1, source_target_pairs={{0,3},{1,2},{2,1},{3,0},{4,7},{5,6},{6,5},{7,4},{8,11},{9,10},{10,... | collective-permute-start | bytes 147464 | tf_op jit(solution)/shard_map/ppermute | solution.py:627
  8.9 1.2 %collective-permute-start.3 = (bf16[144,128]{1,0:T(8,128)(2,1)S(1)}, bf16[144,128]{1,0:T(8,128)(2,1)S(1)}, u32[]{:S(2)}, u32[]{:S(2)}) collective-permute-start(bf16[144,128]{1,0:T(8,128)(2,1)S(1)} %slice.28), channel_id=1, source_target_pairs={{0,1},{1,0},{2,3},{3,2},{4,5},{5,4},{6,7},{7,6},{8,9},{9,8},{10,11... | collective-permute-start | bytes 110600 | tf_op jit(solution)/shard_map/ppermute | solution.py:674
  9.0 1.2 %copy-start = (bf16[336,128]{1,0:T(8,128)(2,1)S(1)}, bf16[336,128]{1,0:T(8,128)(2,1)}, u32[]{:S(2)}) copy-start(bf16[336,128]{1,0:T(8,128)(2,1)} %get-tuple-element.31.refs_3_.refs_4_.refs_0_) | copy-start | bytes 258052
  9.0 1.2 %copy-start.5 = (f32[1,1,2,16384]{3,2,1,0:T(2,128)S(1)}, f32[1,1,2,16384]{3,2,1,0:T(2,128)}, u32[]{:S(2)}) copy-start(f32[1,1,2,16384]{3,2,1,0:T(2,128)} %param.21) | copy-start | bytes 393220
  10.1 9.3 %copy-start.6 = (f32[64,128]{1,0:T(8,128)S(1)}, f32[64,128]{1,0:T(8,128)}, u32[]{:S(2)}) copy-start(f32[64,128]{1,0:T(8,128)} %mixing.2) | copy-start | bytes 98308
  10.7 4.9 %collective-permute-start.6 = (bf16[112,128]{1,0:T(8,128)(2,1)S(1)}, bf16[112,128]{1,0:T(8,128)(2,1)S(1)}, u32[]{:S(2)}, u32[]{:S(2)}) collective-permute-start(bf16[112,128]{1,0:T(8,128)(2,1)S(1)} %get-tuple-element.32.refs_0_), channel_id=1, source_target_pairs={{0,8},{4,12},{8,0},{12,4},{1,9},{5,13},{9,1},{13,5},{2,10},{6,14},... | collective-permute-start | bytes 86024 | tf_op jit(solution)/shard_map/ppermute | solution.py:610
  13.8 5.7 %collective-permute-start.5 = (bf16[112,128]{1,0:T(8,128)(2,1)S(1)}, bf16[112,128]{1,0:T(8,128)(2,1)S(1)}, u32[]{:S(2)}, u32[]{:S(2)}) collective-permute-start(bf16[112,128]{1,0:T(8,128)(2,1)S(1)} %get-tuple-element.32.refs_0_), channel_id=1, source_target_pairs={{0,12},{4,8},{8,4},{12,0},{1,13},{5,9},{9,5},{13,1},{2,14},{6,10},... | collective-permute-start | bytes 86024 | tf_op jit(solution)/shard_map/ppermute | solution.py:610
  15.2 4.3 %collective-permute-start.4 = (bf16[112,128]{1,0:T(8,128)(2,1)S(1)}, bf16[112,128]{1,0:T(8,128)(2,1)S(1)}, u32[]{:S(2)}, u32[]{:S(2)}) collective-permute-start(bf16[112,128]{1,0:T(8,128)(2,1)S(1)} %get-tuple-element.32.refs_0_), channel_id=1, source_target_pairs={{0,4},{4,0},{8,12},{12,8},{1,5},{5,1},{9,13},{13,9},{2,6},{6,2},{1... | collective-permute-start | bytes 86024 | tf_op jit(solution)/shard_map/ppermute | solution.py:610
  19.9 4.7 %collective-permute-start.8 = (bf16[384,128]{1,0:T(8,128)(2,1)S(1)}, bf16[384,128]{1,0:T(8,128)(2,1)S(1)}, u32[]{:S(2)}, u32[]{:S(2)}) collective-permute-start(bf16[384,128]{1,0:T(8,128)(2,1)S(1)} %shard_map.133.refs_4_), channel_id=1, source_target_pairs={{0,2},{1,3},{2,0},{3,1},{4,6},{5,7},{6,4},{7,5},{8,10},{9,11},{10,... | collective-permute-start | bytes 294920 | tf_op jit(solution)/shard_map/ppermute | solution.py:615
  22.0 2.7 %collective-permute-start.7 = (bf16[384,128]{1,0:T(8,128)(2,1)S(1)}, bf16[384,128]{1,0:T(8,128)(2,1)S(1)}, u32[]{:S(2)}, u32[]{:S(2)}) collective-permute-start(bf16[384,128]{1,0:T(8,128)(2,1)S(1)} %shard_map.133.refs_4_), channel_id=1, source_target_pairs={{0,1},{1,0},{2,3},{3,2},{4,5},{5,4},{6,7},{7,6},{8,9},{9,8},{10,11... | collective-permute-start | bytes 294920 | tf_op jit(solution)/shard_map/ppermute | solution.py:621
  24.6 1.3 %collective-permute-start.9 = (bf16[384,128]{1,0:T(8,128)(2,1)S(1)}, bf16[384,128]{1,0:T(8,128)(2,1)S(1)}, u32[]{:S(2)}, u32[]{:S(2)}) collective-permute-start(bf16[384,128]{1,0:T(8,128)(2,1)S(1)} %collective-permute-done.8.refs_6_), channel_id=1, source_target_pairs={{0,1},{1,0},{2,3},{3,2},{4,5},{5,4},{6,7},{7,6},{8,9},{9,8},{10,11... | collective-permute-start | bytes 294920 | tf_op jit(solution)/shard_map/ppermute | solution.py:621
  28.8 1.4 %collective-permute-start.10 = (bf16[384,128]{1,0:T(8,128)(2,1)S(1)}, bf16[384,128]{1,0:T(8,128)(2,1)S(1)}, u32[]{:S(2)}, u32[]{:S(2)}) collective-permute-start(bf16[384,128]{1,0:T(8,128)(2,1)S(1)} %get-tuple-element.43), channel_id=1, source_target_pairs={{0,1},{1,0},{2,3},{3,2},{4,5},{5,4},{6,7},{7,6},{8,9},{9,8},{10,11... | collective-permute-start | bytes 294920 | tf_op jit(solution)/shard_map/ppermute | solution.py:743
  30.1 4.2 %copy-start.7 = (f32[2,64,128]{2,1,0:T(8,128)S(1)}, f32[2,64,128]{2,1,0:T(8,128)}, u32[]{:S(2)}) copy-start(f32[2,64,128]{2,1,0:T(8,128)} %currents.1) | copy-start | bytes 196612
  30.2 4.2 %collective-permute-start.11 = (bf16[192,128]{1,0:T(8,128)(2,1)S(1)}, bf16[192,128]{1,0:T(8,128)(2,1)S(1)}, u32[]{:S(2)}, u32[]{:S(2)}) collective-permute-start(bf16[192,128]{1,0:T(8,128)(2,1)S(1)} %shard_map.136), channel_id=1, source_target_pairs={{0,2},{1,3},{2,0},{3,1},{4,6},{5,7},{6,4},{7,5},{8,10},{9,11},{10,... | collective-permute-start | bytes 147464 | tf_op jit(solution)/shard_map/ppermute | solution.py:748

commit v16 on v15

--- a/solution.py
+++ b/solution.py
@@ -426,78 +426,73 @@
         spread = left + right + inner + outer - 4.0 * c
         return scale * (c + visc * spread + pushed + turn * roll(c, half, 0))
 
-    col = iota((size, size), 1)
     base = high
     for c in range(2):
         field[0, c, base : base + size] = speed[c]
-
-    def own_edges(now):
-        vx, vy = (field[now, c, base : base + size] for c in range(2))
-        mixed = jnp.where(col < half, roll(vx, 1, 1), roll(vy, 1 + half, 1))
-        across = mixed.T[0:high]
-        return [
-            jnp.where(sub < half, vx[size - 1 :], vy[size - 1 :]),
-            jnp.where(sub < half, vx[0:1], vy[0:1]),
-            across,
-            roll(across, -1, 0),
-        ]
-
-    own = own_edges(0)
     load_names.wait()
-    strips = []
+    def along(cells, before, beyond):
+        left = jnp.where(first, roll(before, 1, 1), roll(cells, 1, 1))
+        return left, jnp.where(last, roll(beyond, -1, 1), roll(cells, -1, 1))
+
+    def step_end(state, inside, across, away):
+        cells = state[0]
+        toward = jnp.where(first if away > 0 else last, roll(inside, away, 1), roll(cells, away, 1))
+        inner = jnp.where(edge, across, roll(cells, 1, 0))
+        return step(state, toward, roll(cells, -away, 1), inner, roll(cells, -1, 0))
+
+    halos = [[] for _ in range(SUBCYCLES)]
     for q in range(4):
         x, has_x = follow(0, q)
-        strip = load(x, OPPOSITE[q], flag(has_x))
-        sides = []
+        halo = load(x, OPPOSITE[q], flag(has_x))
+        own = load(0, q, 1.0)
+        ends = []
         for s in LATERAL[q]:
             y, has_y = follow(x, s)
             z, has_z = follow(y, OPPOSITE[q])
             w, has_w = follow(z, OPPOSITE[s])
-            sides.append(
+            u, has_u = follow(0, s)
+            v, has_v = follow(u, q)
+            ends.append(
                 [
                     load(y, OPPOSITE[q], flag(has_y)),
                     load(z, q, flag(has_z)),
                     load(w, q, flag(has_w), with_push=False),
+                    load(u, q, flag(has_u)),
+                    load(v, OPPOSITE[q], flag(has_v), with_push=False),
                 ]
             )
-        strips.append((strip, sides))
+        (y_hi, z_hi, w_hi, u_hi, v_hi), (y_lo, z_lo, w_lo, u_lo, v_lo) = ends
+        for t in range(SUBCYCLES):
+            halos[t].append(halo[0])
+            if t == SUBCYCLES - 1:
+                break
+            c, o = halo[0], own[0]
+            left, right = along(c, y_lo[0], y_hi[0])
+            inner = jnp.where(edge, o, roll(c, 1, 0))
+            new_halo = step(halo, left, right, inner, roll(c, -1, 0))
+            if t < SUBCYCLES - 2:
+                left, right = along(o, u_lo[0], u_hi[0])
+                inner = jnp.where(edge, c, roll(o, 1, 0))
+                new_own = step(own, left, right, inner, roll(o, -1, 0))
+                new_y = step_end(y_hi, c, z_hi[0], 1), step_end(y_lo, c, z_lo[0], -1)
+            if t < SUBCYCLES - 3:
+                z_hi[0], z_lo[0] = (
+                    step_end(z_hi, w_hi, y_hi[0], 1),
+                    step_end(z_lo, w_lo, y_lo[0], -1),
+                )
+                u_hi[0], u_lo[0] = step_end(u_hi, o, v_hi, 1), step_end(u_lo, o, v_lo, -1)
+            halo[0] = new_halo
+            if t < SUBCYCLES - 2:
+                own[0] = new_own
+                y_hi[0], y_lo[0] = new_y
+    columns = [jnp.where(edge, cells[2], roll(cells[3], 1, 0)).T for cells in halos]
 
     warm = remap_forward(chunks, [[r[r.shape[0] - side :]] for r in relays], side, depth)
     heat = (conduct[...] * warm).astype(BF16)
 
     for t in range(SUBCYCLES):
-        cells = [strip[0] for strip, _ in strips]
-        if t < SUBCYCLES - 1:
-            if t > 0:
-                own = own_edges(t % 2)
-            for q in range(4):
-                strip, (beyond, before) = strips[q]
-                c, y_hi, y_lo = strip[0], beyond[0][0], before[0][0]
-                left = jnp.where(first, roll(y_lo, 1, 1), roll(c, 1, 1))
-                right = jnp.where(last, roll(y_hi, -1, 1), roll(c, -1, 1))
-                inner = jnp.where(edge, own[q], roll(c, 1, 0))
-                new_strip = step(strip, left, right, inner, roll(c, -1, 0))
-                if t < SUBCYCLES - 2:
-                    new_sides = []
-                    for i, (y, z, w) in enumerate((beyond, before)):
-                        away = 1 if i == 0 else -1
-                        boundary = first if i == 0 else last
-                        yc, zc = y[0], z[0]
-                        toward = jnp.where(boundary, roll(c, away, 1), roll(yc, away, 1))
-                        inner = jnp.where(edge, zc, roll(yc, 1, 0))
-                        new_y = step(y, toward, roll(yc, -away, 1), inner, roll(yc, -1, 0))
-                        new_z = zc
-                        if t < SUBCYCLES - 3:
-                            toward = jnp.where(boundary, roll(w, away, 1), roll(zc, away, 1))
-                            inner = jnp.where(edge, yc, roll(zc, 1, 0))
-                            new_z = step(z, toward, roll(zc, -away, 1), inner, roll(zc, -1, 0))
-                        new_sides.append((new_y, new_z))
-                    for item, (new_y, new_z) in zip((beyond, before), new_sides):
-                        item[0][0] = new_y
-                        item[1][0] = new_z
-                strip[0] = new_strip
+        cells, sides = halos[t], columns[t]
         now, later = t % 2, (t + 1) % 2
-        sides = jnp.where(edge, cells[2], roll(cells[3], 1, 0)).T
         for c in range(2):
             at = c * half
             field[now, c, base + size : base + size + 1] = cells[0][at : at + 1]

time: 35.2 us -> 35 us (level)
  transfers between devices with their start and end apart: 12 -> 12, of which waited for: 9 -> 9; matrix products, arithmetic and copies ran while one was open for 0% -> 1% of each run, Pallas kernels for 4% -> 4%
where the time goes in v16:
time: 35 us; the launch traced here: 34.9 us
  waiting for transfers between devices  13.4 us (38%)
  starting transfers between devices  12.2 us (35%)
  Pallas kernels  8.28 us (24%)
  between operations  0.77 us (2%)
    pallas_call x8, Pallas kernels, call(): pl.pallas_call(kernel, out_shape=outs, in_specs=specs, out_specs=jax.tree...  8.28 us
    ppermute x3, starting transfers between devices, swap(): got[k] = lax.ppermute(value, axes, [(i, i ^ k) for i in range(count)])  4.67 us
    ppermute x3, waiting for transfers between devices, swap(): got[k] = lax.ppermute(value, axes, [(i, i ^ k) for i in range(count)])  4.09 us
    ppermute x3, waiting for transfers between devices, swap_each(): lax.ppermute(values[k], group_axes, [(i, i ^ k) for i in range(group)])  3.23 us
    ppermute x3, starting transfers between devices, swap_each(): lax.ppermute(values[k], group_axes, [(i, i ^ k) for i in range(group)])  3.21 us
    ppermute x1, waiting for transfers between devices, shards(): lax.ppermute(value, group_axes, [(i, i ^ 2 * k + 2) for i in range(group)])  2.11 us
    ppermute x1, starting transfers between devices, swap_chips(): lax.ppermute(value, group_axes, [(i, i ^ k) for i in range(group)])  2.05 us
    ppermute x1, starting transfers between devices, shards(): lax.ppermute(value, group_axes, [(i, i ^ 2 * k + 2) for i in range(group)])  2.05 us
  transfers between devices with their start and end apart: 12, of which 9 were waited for; matrix products, arithmetic and copies ran while one was open for 1% of the time, Pallas kernels for 4%

profile of v16, /device:TPU:0, one launch (start us, length us, event | category | flops | bytes accessed | tf_op | source)
XLA Modules:
  0.0 34.9 jit_solution(3291655227833442986)
XLA Ops:
  0.6 0.0 copy-start.1
  0.6 0.0 copy-start.2
  0.7 0.0 copy-start.3
  0.7 0.0 copy-start.4
  0.7 2.5 %shard_map.131 = (bf16[336,128]{1,0:T(8,128)(2,1)}, bf16[336,128]{1,0:T(8,128)(2,1)}, bf16[336,128]{1,0:T(8,128)(2,1)}, bf16[192,128]{1,0:T(8,128)(2,1)}) custom-call(s32[1,1,4]{2,1,0:T(1,128)} %links_h.1, s32[1,4]{1,0:T(1,128)} %blocks_h.1, bf16[4,64,128]{2,1,0:T(8,128)(2,1)} %bitcast.27, bf16[4,128,128]{2,1,0:T(8,128)(2,1)} %bitcast.25, ...), custom_call_target="tpu_custom_call" | custom-call | flops 11500000256 | bytes 393248 | tf_op jit(solution)/shard_map/pallas_call | solution.py:42
  3.2 3.0 %collective-permute-start.1 = (bf16[336,128]{1,0:T(8,128)(2,1)}, bf16[336,128]{1,0:T(8,128)(2,1)S(1)}, u32[]{:S(2)}, u32[]{:S(2)}) collective-permute-start(bf16[336,128]{1,0:T(8,128)(2,1)} %get-tuple-element.29), channel_id=1, source_target_pairs={{0,2},{1,3},{2,0},{3,1},{4,6},{5,7},{6,4},{7,5},{8,10},{9,11},{10,... | collective-permute-start | bytes 258056 | tf_op jit(solution)/shard_map/ppermute | solution.py:622
  6.2 0.0 collective-permute-start.2
  6.2 0.2 collective-permute-start
  6.4 2.5 %collective-permute-done.1.refs_1_.refs_6_.refs_2_ = bf16[336,128]{1,0:T(8,128)(2,1)S(1)} collective-permute-done((bf16[336,128]{1,0:T(8,128)(2,1)}, bf16[336,128]{1,0:T(8,128)(2,1)S(1)}, u32[]{:S(2)}, u32[]{:S(2)}) %collective-permute-start.1) | collective-permute-done | bytes 86048 | tf_op jit(solution)/shard_map/ppermute | solution.py:622
  8.9 0.0 collective-permute-start.3
  8.9 0.0 copy-done.1
  8.9 0.0 copy-done.2
  8.9 0.0 copy-done.3
  8.9 0.0 copy-done.4
  9.0 0.0 copy-start
  9.0 0.0 copy-start.5
  9.0 0.2 shard_map.130
  9.2 0.7 %collective-permute-done.refs_0_.refs_7_.refs_3_ = bf16[192,128]{1,0:T(8,128)(2,1)S(1)} collective-permute-done((bf16[192,128]{1,0:T(8,128)(2,1)}, bf16[192,128]{1,0:T(8,128)(2,1)S(1)}, u32[]{:S(2)}, u32[]{:S(2)}) %collective-permute-start) | collective-permute-done | bytes 49184 | tf_op jit(solution)/shard_map/ppermute | solution.py:622
  9.9 0.0 collective-permute-done.2.refs_2_.refs_5_.refs_1_
  9.9 0.2 collective-permute-done.3.refs_4_.refs_8_
  10.1 0.0 copy-done
  10.1 0.0 copy-done.5
  10.1 0.0 copy-start.6
  10.1 0.6 %shard_map.132 = (bf16[112,128]{1,0:T(8,128)(2,1)S(1)}, f32[2,128,128]{2,1,0:T(8,128)S(1)}, f32[2,128,128]{2,1,0:T(8,128)S(1)}) custom-call(f32[128,128]{1,0:T(8,128)S(1)} %get-tuple-element.25.mass, f32[128,128]{1,0:T(8,128)S(1)} %get-tuple-element.26.drag, f32[256,128]{1,0:T(8,128)S(1)} %bitcast.24, f32[72,128]{1,0:T(8,128)S(1)} %get-tuple-element.27.early, ...), custom_call_target="tpu_custom_call" | custom-call | flops 11500000 | bytes 643072 | tf_op jit(solution)/shard_map/pallas_call | solution.py:42
  10.7 3.1 %collective-permute-start.6 = (bf16[112,128]{1,0:T(8,128)(2,1)S(1)}, bf16[112,128]{1,0:T(8,128)(2,1)S(1)}, u32[]{:S(2)}, u32[]{:S(2)}) collective-permute-start(bf16[112,128]{1,0:T(8,128)(2,1)S(1)} %get-tuple-element.32.refs_0_), channel_id=1, source_target_pairs={{0,8},{4,12},{8,0},{12,4},{1,9},{5,13},{9,1},{13,5},{2,10},{6,14},... | collective-permute-start | bytes 86024 | tf_op jit(solution)/shard_map/ppermute | solution.py:605
  13.8 1.3 %collective-permute-start.5 = (bf16[112,128]{1,0:T(8,128)(2,1)S(1)}, bf16[112,128]{1,0:T(8,128)(2,1)S(1)}, u32[]{:S(2)}, u32[]{:S(2)}) collective-permute-start(bf16[112,128]{1,0:T(8,128)(2,1)S(1)} %get-tuple-element.32.refs_0_), channel_id=1, source_target_pairs={{0,12},{4,8},{8,4},{12,0},{1,13},{5,9},{9,5},{13,1},{2,14},{6,10},... | collective-permute-start | bytes 86024 | tf_op jit(solution)/shard_map/ppermute | solution.py:605
  15.2 0.2 collective-permute-start.4
  15.4 0.3 collective-permute-done.6.refs_3_
  15.7 3.8 %collective-permute-done.5.refs_2_ = bf16[112,128]{1,0:T(8,128)(2,1)S(1)} collective-permute-done((bf16[112,128]{1,0:T(8,128)(2,1)S(1)}, bf16[112,128]{1,0:T(8,128)(2,1)S(1)}, u32[]{:S(2)}, u32[]{:S(2)}) %collective-permute-start.5) | collective-permute-done | bytes 28704 | tf_op jit(solution)/shard_map/ppermute | solution.py:605
  19.5 0.0 collective-permute-done.4.refs_1_
  19.5 0.0 copy-done.6
  19.5 0.4 %shard_map.133.refs_4_ = bf16[384,128]{1,0:T(8,128)(2,1)S(1)} custom-call(f32[4,64,128]{2,1,0:T(8,128)S(1)} %copy-done.1, f32[64,128]{1,0:T(8,128)S(1)} %copy-done.6, bf16[112,128]{1,0:T(8,128)(2,1)S(1)} %get-tuple-element.32.refs_0_, bf16[112,128]{1,0:T(8,128)(2,1)S(1)} %collective-permute-done.4.refs_1_, ...), custom_call_target="tpu_custom_call" | custom-call | flops 11500000 | bytes 622592 | tf_op jit(solution)/shard_map/pallas_call | solution.py:42
  19.9 2.0 %collective-permute-start.8 = (bf16[384,128]{1,0:T(8,128)(2,1)S(1)}, bf16[384,128]{1,0:T(8,128)(2,1)S(1)}, u32[]{:S(2)}, u32[]{:S(2)}) collective-permute-start(bf16[384,128]{1,0:T(8,128)(2,1)S(1)} %shard_map.133.refs_4_), channel_id=1, source_target_pairs={{0,2},{1,3},{2,0},{3,1},{4,6},{5,7},{6,4},{7,5},{8,10},{9,11},{10,... | collective-permute-start | bytes 294920 | tf_op jit(solution)/shard_map/ppermute | solution.py:610
  22.0 0.0 collective-permute-start.7
  22.0 0.1 reshape.41
  22.1 1.1 %shard_map.134.warm = f32[4,64,128]{2,1,0:T(8,128)S(1)} custom-call(f32[4,64,128]{2,1,0:T(8,128)S(1)} %copy-done.1, f32[64,128]{1,0:T(8,128)S(1)} %copy-done.6, bf16[112,128]{1,0:T(8,128)(2,1)S(1)} %get-tuple-element.32.refs_0_, bf16[112,128]{1,0:T(8,128)(2,1)S(1)} %collective-permute-done.4.refs_1_, bf16[112,128]{1,0:T(8,128)(2,1)S(1)} %collective-permute-done.5.refs_2_, ...), custom_call_target="tpu_custom_call" | custom-call | flops 11500000 | bytes 622592 | tf_op jit(solution)/shard_map/pallas_call | solution.py:42
  23.2 1.4 %collective-permute-done.8.refs_6_ = bf16[384,128]{1,0:T(8,128)(2,1)S(1)} collective-permute-done((bf16[384,128]{1,0:T(8,128)(2,1)S(1)}, bf16[384,128]{1,0:T(8,128)(2,1)S(1)}, u32[]{:S(2)}, u32[]{:S(2)}) %collective-permute-start.8) | collective-permute-done | bytes 98336 | tf_op jit(solution)/shard_map/ppermute | solution.py:610
  24.6 0.0 collective-permute-start.9
  24.6 0.1 xor_select_fusion.table
  24.7 0.0 collective-permute-done.7.refs_5_
  24.7 1.2 %collective-permute-done.9.refs_7_ = bf16[384,128]{1,0:T(8,128)(2,1)S(1)} collective-permute-done((bf16[384,128]{1,0:T(8,128)(2,1)S(1)}, bf16[384,128]{1,0:T(8,128)(2,1)S(1)}, u32[]{:S(2)}, u32[]{:S(2)}) %collective-permute-start.9) | collective-permute-done | bytes 98336 | tf_op jit(solution)/shard_map/ppermute | solution.py:616
  25.9 2.7 %shard_map.135 = (f32[2,128,128]{2,1,0:T(8,128)S(1)}, f32[384,128]{1,0:T(8,128)S(1)}, bf16[384,128]{1,0:T(8,128)(2,1)S(1)}) custom-call(s32[16,4]{1,0:T(8,128)S(1)} %xor_select_fusion.table, f32[128,128]{1,0:T(8,128)S(1)} %get-tuple-element.34.viscous, f32[128,128]{1,0:T(8,128)S(1)} %get-tuple-element.35.gain, f32[128,128]{1,0:T(8,128)S(1)} %get-tuple-element.26.drag, ...), custom_call_target="tpu_custom_call" | custom-call | flops 11500000 | bytes 1356032 | tf_op jit(solution)/shard_map/pallas_call | solution.py:42
  28.6 0.2 collective-permute-start.10
  28.8 1.2 %collective-permute-done.10.beside = bf16[384,128]{1,0:T(8,128)(2,1)S(1)} collective-permute-done((bf16[384,128]{1,0:T(8,128)(2,1)S(1)}, bf16[384,128]{1,0:T(8,128)(2,1)S(1)}, u32[]{:S(2)}, u32[]{:S(2)}) %collective-permute-start.10) | collective-permute-done | bytes 98336 | tf_op jit(solution)/shard_map/ppermute | solution.py:738
  30.0 0.0 copy-start.7
  30.0 2.0 %collective-permute-start.11 = (bf16[192,128]{1,0:T(8,128)(2,1)S(1)}, bf16[192,128]{1,0:T(8,128)(2,1)S(1)}, u32[]{:S(2)}, u32[]{:S(2)}) collective-permute-start(bf16[192,128]{1,0:T(8,128)(2,1)S(1)} %shard_map.136), channel_id=1, source_target_pairs={{0,2},{1,3},{2,0},{3,1},{4,6},{5,7},{6,4},{7,5},{8,10},{9,11},{10,... | collective-permute-start | bytes 147464 | tf_op jit(solution)/shard_map/ppermute | solution.py:743
  32.0 2.1 %collective-permute-done.11.refs_0_ = bf16[192,128]{1,0:T(8,128)(2,1)S(1)} collective-permute-done((bf16[192,128]{1,0:T(8,128)(2,1)S(1)}, bf16[192,128]{1,0:T(8,128)(2,1)S(1)}, u32[]{:S(2)}, u32[]{:S(2)}) %collective-permute-start.11) | collective-permute-done | bytes 49184 | tf_op jit(solution)/shard_map/ppermute | solution.py:743
  34.1 0.0 copy-done.7
  34.1 0.7 %shard_map.137 = (f32[256,128]{1,0:T(8,128)}, f32[4,64,128]{2,1,0:T(8,128)}, f32[2,64,128]{2,1,0:T(8,128)}) custom-call(f32[4,64,128]{2,1,0:T(8,128)S(1)} %shard_map.134.warm, f32[2,64,128]{2,1,0:T(8,128)S(1)} %copy-done.7, f32[2,128,128]{2,1,0:T(8,128)S(1)} %get-tuple-element.41.speed, f32[384,128]{1,0:T(8,128)S(1)} %get-tuple-element.42.own, ...), custom_call_target="tpu_custom_call" | custom-call | flops 11500000 | bytes 671744 | tf_op jit(solution)/shard_map/pallas_call | solution.py:42
  (7 shorter events, 0.0 us)
Async XLA Ops:
  0.6 8.3 %copy-start.1 = (f32[4,64,128]{2,1,0:T(8,128)S(1)}, f32[4,64,128]{2,1,0:T(8,128)}, u32[]{:S(2)}) copy-start(f32[4,64,128]{2,1,0:T(8,128)} %water.5) | copy-start | bytes 393220
  0.6 8.3 %copy-start.2 = (f32[1,1,5,16384]{3,1,2,0:T(1,128)S(1)}, f32[1,1,5,16384]{3,1,2,0:T(1,128)}, u32[]{:S(2)}) copy-start(f32[1,1,5,16384]{3,1,2,0:T(1,128)} %param.18) | copy-start | bytes 983044
  0.7 8.3 %copy-start.3 = (f32[1,1,5,16384]{3,1,2,0:T(1,128)S(1)}, f32[1,1,5,16384]{3,1,2,0:T(1,128)}, u32[]{:S(2)}) copy-start(f32[1,1,5,16384]{3,1,2,0:T(1,128)} %param.19) | copy-start | bytes 983044
  0.7 8.3 %copy-start.4 = (f32[1,1,2,16384]{3,2,1,0:T(2,128)S(1)}, f32[1,1,2,16384]{3,2,1,0:T(2,128)}, u32[]{:S(2)}) copy-start(f32[1,1,2,16384]{3,2,1,0:T(2,128)} %param.20) | copy-start | bytes 393220
  3.2 5.7 %collective-permute-start.1 = (bf16[336,128]{1,0:T(8,128)(2,1)}, bf16[336,128]{1,0:T(8,128)(2,1)S(1)}, u32[]{:S(2)}, u32[]{:S(2)}) collective-permute-start(bf16[336,128]{1,0:T(8,128)(2,1)} %get-tuple-element.29), channel_id=1, source_target_pairs={{0,2},{1,3},{2,0},{3,1},{4,6},{5,7},{6,4},{7,5},{8,10},{9,11},{10,... | collective-permute-start | bytes 258056 | tf_op jit(solution)/shard_map/ppermute | solution.py:622
  6.2 3.7 %collective-permute-start.2 = (bf16[336,128]{1,0:T(8,128)(2,1)}, bf16[336,128]{1,0:T(8,128)(2,1)S(1)}, u32[]{:S(2)}, u32[]{:S(2)}) collective-permute-start(bf16[336,128]{1,0:T(8,128)(2,1)} %get-tuple-element.30), channel_id=1, source_target_pairs={{0,1},{1,0},{2,3},{3,2},{4,5},{5,4},{6,7},{7,6},{8,9},{9,8},{10,11... | collective-permute-start | bytes 258056 | tf_op jit(solution)/shard_map/ppermute | solution.py:622
  6.2 3.7 %collective-permute-start = (bf16[192,128]{1,0:T(8,128)(2,1)}, bf16[192,128]{1,0:T(8,128)(2,1)S(1)}, u32[]{:S(2)}, u32[]{:S(2)}) collective-permute-start(bf16[192,128]{1,0:T(8,128)(2,1)} %get-tuple-element.28), channel_id=1, source_target_pairs={{0,3},{1,2},{2,1},{3,0},{4,7},{5,6},{6,5},{7,4},{8,11},{9,10},{10,... | collective-permute-start | bytes 147464 | tf_op jit(solution)/shard_map/ppermute | solution.py:622
  8.9 1.2 %collective-permute-start.3 = (bf16[144,128]{1,0:T(8,128)(2,1)S(1)}, bf16[144,128]{1,0:T(8,128)(2,1)S(1)}, u32[]{:S(2)}, u32[]{:S(2)}) collective-permute-start(bf16[144,128]{1,0:T(8,128)(2,1)S(1)} %slice.28), channel_id=1, source_target_pairs={{0,1},{1,0},{2,3},{3,2},{4,5},{5,4},{6,7},{7,6},{8,9},{9,8},{10,11... | collective-permute-start | bytes 110600 | tf_op jit(solution)/shard_map/ppermute | solution.py:669
  9.0 1.2 %copy-start = (bf16[336,128]{1,0:T(8,128)(2,1)S(1)}, bf16[336,128]{1,0:T(8,128)(2,1)}, u32[]{:S(2)}) copy-start(bf16[336,128]{1,0:T(8,128)(2,1)} %get-tuple-element.31.refs_3_.refs_4_.refs_0_) | copy-start | bytes 258052
  9.0 1.2 %copy-start.5 = (f32[1,1,2,16384]{3,2,1,0:T(2,128)S(1)}, f32[1,1,2,16384]{3,2,1,0:T(2,128)}, u32[]{:S(2)}) copy-start(f32[1,1,2,16384]{3,2,1,0:T(2,128)} %param.21) | copy-start | bytes 393220
  10.1 9.3 %copy-start.6 = (f32[64,128]{1,0:T(8,128)S(1)}, f32[64,128]{1,0:T(8,128)}, u32[]{:S(2)}) copy-start(f32[64,128]{1,0:T(8,128)} %mixing.2) | copy-start | bytes 98308
  10.7 4.9 %collective-permute-start.6 = (bf16[112,128]{1,0:T(8,128)(2,1)S(1)}, bf16[112,128]{1,0:T(8,128)(2,1)S(1)}, u32[]{:S(2)}, u32[]{:S(2)}) collective-permute-start(bf16[112,128]{1,0:T(8,128)(2,1)S(1)} %get-tuple-element.32.refs_0_), channel_id=1, source_target_pairs={{0,8},{4,12},{8,0},{12,4},{1,9},{5,13},{9,1},{13,5},{2,10},{6,14},... | collective-permute-start | bytes 86024 | tf_op jit(solution)/shard_map/ppermute | solution.py:605
  13.8 5.7 %collective-permute-start.5 = (bf16[112,128]{1,0:T(8,128)(2,1)S(1)}, bf16[112,128]{1,0:T(8,128)(2,1)S(1)}, u32[]{:S(2)}, u32[]{:S(2)}) collective-permute-start(bf16[112,128]{1,0:T(8,128)(2,1)S(1)} %get-tuple-element.32.refs_0_), channel_id=1, source_target_pairs={{0,12},{4,8},{8,4},{12,0},{1,13},{5,9},{9,5},{13,1},{2,14},{6,10},... | collective-permute-start | bytes 86024 | tf_op jit(solution)/shard_map/ppermute | solution.py:605
  15.2 4.3 %collective-permute-start.4 = (bf16[112,128]{1,0:T(8,128)(2,1)S(1)}, bf16[112,128]{1,0:T(8,128)(2,1)S(1)}, u32[]{:S(2)}, u32[]{:S(2)}) collective-permute-start(bf16[112,128]{1,0:T(8,128)(2,1)S(1)} %get-tuple-element.32.refs_0_), channel_id=1, source_target_pairs={{0,4},{4,0},{8,12},{12,8},{1,5},{5,1},{9,13},{13,9},{2,6},{6,2},{1... | collective-permute-start | bytes 86024 | tf_op jit(solution)/shard_map/ppermute | solution.py:605
  19.9 4.7 %collective-permute-start.8 = (bf16[384,128]{1,0:T(8,128)(2,1)S(1)}, bf16[384,128]{1,0:T(8,128)(2,1)S(1)}, u32[]{:S(2)}, u32[]{:S(2)}) collective-permute-start(bf16[384,128]{1,0:T(8,128)(2,1)S(1)} %shard_map.133.refs_4_), channel_id=1, source_target_pairs={{0,2},{1,3},{2,0},{3,1},{4,6},{5,7},{6,4},{7,5},{8,10},{9,11},{10,... | collective-permute-start | bytes 294920 | tf_op jit(solution)/shard_map/ppermute | solution.py:610
  22.0 2.7 %collective-permute-start.7 = (bf16[384,128]{1,0:T(8,128)(2,1)S(1)}, bf16[384,128]{1,0:T(8,128)(2,1)S(1)}, u32[]{:S(2)}, u32[]{:S(2)}) collective-permute-start(bf16[384,128]{1,0:T(8,128)(2,1)S(1)} %shard_map.133.refs_4_), channel_id=1, source_target_pairs={{0,1},{1,0},{2,3},{3,2},{4,5},{5,4},{6,7},{7,6},{8,9},{9,8},{10,11... | collective-permute-start | bytes 294920 | tf_op jit(solution)/shard_map/ppermute | solution.py:616
  24.6 1.3 %collective-permute-start.9 = (bf16[384,128]{1,0:T(8,128)(2,1)S(1)}, bf16[384,128]{1,0:T(8,128)(2,1)S(1)}, u32[]{:S(2)}, u32[]{:S(2)}) collective-permute-start(bf16[384,128]{1,0:T(8,128)(2,1)S(1)} %collective-permute-done.8.refs_6_), channel_id=1, source_target_pairs={{0,1},{1,0},{2,3},{3,2},{4,5},{5,4},{6,7},{7,6},{8,9},{9,8},{10,11... | collective-permute-start | bytes 294920 | tf_op jit(solution)/shard_map/ppermute | solution.py:616
  28.6 1.4 %collective-permute-start.10 = (bf16[384,128]{1,0:T(8,128)(2,1)S(1)}, bf16[384,128]{1,0:T(8,128)(2,1)S(1)}, u32[]{:S(2)}, u32[]{:S(2)}) collective-permute-start(bf16[384,128]{1,0:T(8,128)(2,1)S(1)} %get-tuple-element.43), channel_id=1, source_target_pairs={{0,1},{1,0},{2,3},{3,2},{4,5},{5,4},{6,7},{7,6},{8,9},{9,8},{10,11... | collective-permute-start | bytes 294920 | tf_op jit(solution)/shard_map/ppermute | solution.py:738
  30.0 4.2 %copy-start.7 = (f32[2,64,128]{2,1,0:T(8,128)S(1)}, f32[2,64,128]{2,1,0:T(8,128)}, u32[]{:S(2)}) copy-start(f32[2,64,128]{2,1,0:T(8,128)} %currents.1) | copy-start | bytes 196612
  30.0 4.2 %collective-permute-start.11 = (bf16[192,128]{1,0:T(8,128)(2,1)S(1)}, bf16[192,128]{1,0:T(8,128)(2,1)S(1)}, u32[]{:S(2)}, u32[]{:S(2)}) collective-permute-start(bf16[192,128]{1,0:T(8,128)(2,1)S(1)} %shard_map.136), channel_id=1, source_target_pairs={{0,2},{1,3},{2,0},{3,1},{4,6},{5,7},{6,4},{7,5},{8,10},{9,11},{10,... | collective-permute-start | bytes 147464 | tf_op jit(solution)/shard_map/ppermute | solution.py:743

commit v17 on v16

--- a/solution.py
+++ b/solution.py
@@ -33,7 +33,10 @@
 FLOPS_PER_MICRO = 1.15e9
 
 
-def call(kernel, outs, args, scratch=(), smem=(), hbm=(), out_space=pltpu.VMEM, grant=VMEM_LIMIT, micros=0.01):
+def call(
+    kernel, outs, args, scratch=(), smem=(), hbm=(), out_space=pltpu.VMEM, out_spaces=None,
+    grant=VMEM_LIMIT, micros=0.01,
+):
     def space(i):
         return pltpu.SMEM if i in smem else pltpu.HBM if i in hbm else pltpu.VMEM
 
@@ -43,7 +46,11 @@
         kernel,
         out_shape=outs,
         in_specs=specs,
-        out_specs=jax.tree.map(lambda _: pl.BlockSpec(memory_space=out_space), outs),
+        out_specs=(
+            jax.tree.map(lambda _: pl.BlockSpec(memory_space=out_space), outs)
+            if out_spaces is None
+            else [pl.BlockSpec(memory_space=space) for space in out_spaces]
+        ),
         scratch_shapes=list(scratch),
         compiler_params=pltpu.CompilerParams(vmem_limit_bytes=grant),
         cost_estimate=pl.CostEstimate(
@@ -521,8 +528,10 @@
     size = fluxes[0].shape[0]
     wide = jnp.concatenate(fluxes, axis=1)
     step = 3 * side
+    down = jnp.concatenate([chunk[0:side] for chunk in chunks], axis=0)
+    parts = jnp.dot(down, wide, preferred_element_type=F32).astype(BF16)
     for k, chunk in enumerate(chunks):
-        part = jnp.dot(chunk[0:side], wide, preferred_element_type=F32).astype(BF16)
+        part = parts[k * side : (k + 1) * side]
         part = jnp.concatenate([part[:, c * size : (c + 1) * size] for c in range(3)], axis=0)
         reply = jnp.dot(part, chunk[side : side + depth], preferred_element_type=F32)
         at = k // 2 * step
@@ -539,31 +548,34 @@
         out[...] = (own[at : at + step] + beside[at : at + step].astype(F32)).astype(BF16)
 
 
-def finish_kernel(warm, currents, speed, own, beside, *refs):
-    outs, (flat, heat_v, current_v, left) = refs[-7:-4], refs[-4:]
-    replies = refs[:-7]
-    flat_o, heat_o, current_o = outs
+def settle_kernel(speed, own, beside, flat_o, total_o, flat, left):
     size = speed.shape[1]
-    copies = [
-        pltpu.make_async_copy(source, target, left.at[i])
-        for i, (source, target) in enumerate(
-            ((flat, flat_o), (heat_v, heat_o), (current_v, current_o))
-        )
-    ]
     for c in range(2):
         flat[pl.ds(c, size, stride=2), :] = speed[c]
-    copies[0].start()
+    copy = pltpu.make_async_copy(flat, flat_o, left)
+    copy.start()
+    rows = total_o.shape[0]
+    total_o[...] = own[0:rows] + beside[0:rows].astype(F32)
+    copy.wait()
+
+
+def finish_kernel(warm, currents, total, *refs):
+    replies, (heat_o, current_o, heat_v, current_v, left) = refs[:-5], refs[-5:]
+    copies = [
+        pltpu.make_async_copy(heat_v, heat_o, left.at[0]),
+        pltpu.make_async_copy(current_v, current_o, left.at[1]),
+    ]
     side = currents.shape[1]
-    total = own[0 : 3 * side] + beside[0 : 3 * side].astype(F32)
+    total = total[...]
     for reply in replies:
         total = total + reply[...].astype(F32)
     heat = THERMAL_DIFFUSE * total[0:side]
     for l in range(warm.shape[0]):
         heat_v[l] = warm[l] + heat
-    copies[1].start()
+    copies[0].start()
     for c in range(2):
         current_v[c] = currents[c] + STRESS_MIXING * total[(c + 1) * side : (c + 2) * side]
-    copies[2].start()
+    copies[1].start()
     for copy in copies:
         copy.wait()
 
@@ -743,18 +755,24 @@
         lax.ppermute(value, group_axes, [(i, i ^ (2 * k + 2)) for i in range(group)])
         for k, value in enumerate(paired)
     ]
+    flat, total = call(
+        settle_kernel,
+        [shape(2 * size, size), shape(step, width)],
+        (speed, own, beside),
+        scratch=[pltpu.VMEM((2 * size, size), F32), pltpu.SemaphoreType.DMA],
+        out_spaces=(pltpu.HBM, pltpu.VMEM),
+    )
     if lev_count > 1:
-        parts = [r.astype(F32) for r in (own[:step], beside[:step], *replies)]
-        own, beside, replies = lax.psum(sum(parts), "lev"), jnp.zeros_like(beside[:step]), []
-    flat, heat, current = call(
+        total = lax.psum(total + sum(r.astype(F32) for r in replies), "lev")
+        replies = []
+    heat, current = call(
         finish_kernel,
-        [shape(2 * size, size), shape(levels, side, width), shape(2, side, width)],
-        (warm, upper_current_vector, speed, own, beside, *replies),
+        [shape(levels, side, width), shape(2, side, width)],
+        (warm, upper_current_vector, total, *replies),
         scratch=[
-            pltpu.VMEM((2 * size, size), F32),
             pltpu.VMEM((levels, side, width), F32),
             pltpu.VMEM((2, side, width), F32),
-            pltpu.SemaphoreType.DMA((3,)),
+            pltpu.SemaphoreType.DMA((2,)),
         ],
         out_space=pltpu.HBM,
     )

time: 35 us -> 34.9 us (level)
  waiting for transfers between devices: 13.4 us -> 12.7 us
  Pallas kernels: 8.28 us -> 8.8 us
    ppermute x1, waiting for transfers between devices: 2.11 us -> 1.42 us  [shards(): lax.ppermute(value, group_axes, [(i, i ^ 2 * k + 2) for i in range(group)])]
    pallas_call x8 -> x9, Pallas kernels: 8.28 us -> 8.8 us  [call(): pl.pallas_call(kernel, out_shape=outs, in_specs=specs, out_specs=jax.tree...]
  transfers between devices with their start and end apart: 12 -> 12, of which waited for: 9 -> 9; matrix products, arithmetic and copies ran while one was open for 1% -> 1% of each run, Pallas kernels for 4% -> 6%
where the time goes in v17:
time: 34.9 us; the launch traced here: 34.7 us
  waiting for transfers between devices  12.7 us (36%)
  starting transfers between devices  12.2 us (35%)
  Pallas kernels  8.8 us (25%)
  between operations  0.78 us (2%)
    pallas_call x9, Pallas kernels, call(): pl.pallas_call(kernel, out_shape=outs, in_specs=specs, out_specs=jax.tree...  8.8 us
    ppermute x3, starting transfers between devices, swap(): got[k] = lax.ppermute(value, axes, [(i, i ^ k) for i in range(count)])  4.67 us
    ppermute x3, waiting for transfers between devices, swap(): got[k] = lax.ppermute(value, axes, [(i, i ^ k) for i in range(count)])  4.09 us
    ppermute x3, waiting for transfers between devices, swap_each(): lax.ppermute(values[k], group_axes, [(i, i ^ k) for i in range(group)])  3.23 us
    ppermute x3, starting transfers between devices, swap_each(): lax.ppermute(values[k], group_axes, [(i, i ^ k) for i in range(group)])  3.21 us
    ppermute x1, starting transfers between devices, shards(): lax.ppermute(value, group_axes, [(i, i ^ 2 * k + 2) for i in range(group)])  2.05 us
    ppermute x1, starting transfers between devices, swap_chips(): lax.ppermute(value, group_axes, [(i, i ^ k) for i in range(group)])  2.05 us
    ppermute x1, waiting for transfers between devices, shards(): lax.ppermute(value, group_axes, [(i, i ^ 2 * k + 2) for i in range(group)])  1.42 us
  transfers between devices with their start and end apart: 12, of which 9 were waited for; matrix products, arithmetic and copies ran while one was open for 1% of the time, Pallas kernels for 6%

profile of v17, /device:TPU:0, one launch (start us, length us, event | category | flops | bytes accessed | tf_op | source)
XLA Modules:
  0.0 34.7 jit_solution(14169665492358458148)
XLA Ops:
  0.6 0.0 copy-start.1
  0.6 0.0 copy-start.2
  0.7 0.0 copy-start.3
  0.7 0.0 copy-start.4
  0.7 2.5 %shard_map.131 = (bf16[336,128]{1,0:T(8,128)(2,1)}, bf16[336,128]{1,0:T(8,128)(2,1)}, bf16[336,128]{1,0:T(8,128)(2,1)}, bf16[192,128]{1,0:T(8,128)(2,1)}) custom-call(s32[1,1,4]{2,1,0:T(1,128)} %links_h.1, s32[1,4]{1,0:T(1,128)} %blocks_h.1, bf16[4,64,128]{2,1,0:T(8,128)(2,1)} %bitcast.27, bf16[4,128,128]{2,1,0:T(8,128)(2,1)} %bitcast.25, ...), custom_call_target="tpu_custom_call" | custom-call | flops 11500000256 | bytes 393248 | tf_op jit(solution)/shard_map/pallas_call | solution.py:45
  3.2 3.0 %collective-permute-start.1 = (bf16[336,128]{1,0:T(8,128)(2,1)}, bf16[336,128]{1,0:T(8,128)(2,1)S(1)}, u32[]{:S(2)}, u32[]{:S(2)}) collective-permute-start(bf16[336,128]{1,0:T(8,128)(2,1)} %get-tuple-element.30), channel_id=1, source_target_pairs={{0,2},{1,3},{2,0},{3,1},{4,6},{5,7},{6,4},{7,5},{8,10},{9,11},{10,... | collective-permute-start | bytes 258056 | tf_op jit(solution)/shard_map/ppermute | solution.py:634
  6.2 0.0 collective-permute-start.2
  6.2 0.2 collective-permute-start
  6.4 2.5 %collective-permute-done.1.refs_1_.refs_6_.refs_2_ = bf16[336,128]{1,0:T(8,128)(2,1)S(1)} collective-permute-done((bf16[336,128]{1,0:T(8,128)(2,1)}, bf16[336,128]{1,0:T(8,128)(2,1)S(1)}, u32[]{:S(2)}, u32[]{:S(2)}) %collective-permute-start.1) | collective-permute-done | bytes 86048 | tf_op jit(solution)/shard_map/ppermute | solution.py:634
  8.9 0.0 collective-permute-start.3
  8.9 0.0 copy-done.1
  8.9 0.0 copy-done.2
  8.9 0.0 copy-done.3
  8.9 0.0 copy-done.4
  9.0 0.0 copy-start
  9.0 0.0 copy-start.5
  9.0 0.2 shard_map.130
  9.2 0.7 %collective-permute-done.refs_0_.refs_7_.refs_3_ = bf16[192,128]{1,0:T(8,128)(2,1)S(1)} collective-permute-done((bf16[192,128]{1,0:T(8,128)(2,1)}, bf16[192,128]{1,0:T(8,128)(2,1)S(1)}, u32[]{:S(2)}, u32[]{:S(2)}) %collective-permute-start) | collective-permute-done | bytes 49184 | tf_op jit(solution)/shard_map/ppermute | solution.py:634
  9.9 0.0 collective-permute-done.2.refs_2_.refs_5_.refs_1_
  9.9 0.2 collective-permute-done.3.refs_4_.refs_8_
  10.1 0.0 copy-done
  10.1 0.0 copy-done.5
  10.1 0.0 copy-start.6
  10.1 0.6 %shard_map.132 = (bf16[112,128]{1,0:T(8,128)(2,1)S(1)}, f32[2,128,128]{2,1,0:T(8,128)S(1)}, f32[2,128,128]{2,1,0:T(8,128)S(1)}) custom-call(f32[128,128]{1,0:T(8,128)S(1)} %get-tuple-element.26.mass, f32[128,128]{1,0:T(8,128)S(1)} %get-tuple-element.27.drag, f32[256,128]{1,0:T(8,128)S(1)} %bitcast.24, f32[72,128]{1,0:T(8,128)S(1)} %get-tuple-element.28.early, ...), custom_call_target="tpu_custom_call" | custom-call | flops 11500000 | bytes 643072 | tf_op jit(solution)/shard_map/pallas_call | solution.py:45
  10.7 3.1 %collective-permute-start.6 = (bf16[112,128]{1,0:T(8,128)(2,1)S(1)}, bf16[112,128]{1,0:T(8,128)(2,1)S(1)}, u32[]{:S(2)}, u32[]{:S(2)}) collective-permute-start(bf16[112,128]{1,0:T(8,128)(2,1)S(1)} %get-tuple-element.33.refs_0_), channel_id=1, source_target_pairs={{0,8},{4,12},{8,0},{12,4},{1,9},{5,13},{9,1},{13,5},{2,10},{6,14},... | collective-permute-start | bytes 86024 | tf_op jit(solution)/shard_map/ppermute | solution.py:617
  13.8 1.3 %collective-permute-start.5 = (bf16[112,128]{1,0:T(8,128)(2,1)S(1)}, bf16[112,128]{1,0:T(8,128)(2,1)S(1)}, u32[]{:S(2)}, u32[]{:S(2)}) collective-permute-start(bf16[112,128]{1,0:T(8,128)(2,1)S(1)} %get-tuple-element.33.refs_0_), channel_id=1, source_target_pairs={{0,12},{4,8},{8,4},{12,0},{1,13},{5,9},{9,5},{13,1},{2,14},{6,10},... | collective-permute-start | bytes 86024 | tf_op jit(solution)/shard_map/ppermute | solution.py:617
  15.2 0.2 collective-permute-start.4
  15.4 0.3 collective-permute-done.6.refs_3_
  15.7 3.8 %collective-permute-done.5.refs_2_ = bf16[112,128]{1,0:T(8,128)(2,1)S(1)} collective-permute-done((bf16[112,128]{1,0:T(8,128)(2,1)S(1)}, bf16[112,128]{1,0:T(8,128)(2,1)S(1)}, u32[]{:S(2)}, u32[]{:S(2)}) %collective-permute-start.5) | collective-permute-done | bytes 28704 | tf_op jit(solution)/shard_map/ppermute | solution.py:617
  19.5 0.0 collective-permute-done.4.refs_1_
  19.5 0.0 copy-done.6
  19.5 0.4 %shard_map.133.refs_4_ = bf16[384,128]{1,0:T(8,128)(2,1)S(1)} custom-call(f32[4,64,128]{2,1,0:T(8,128)S(1)} %copy-done.1, f32[64,128]{1,0:T(8,128)S(1)} %copy-done.6, bf16[112,128]{1,0:T(8,128)(2,1)S(1)} %get-tuple-element.33.refs_0_, bf16[112,128]{1,0:T(8,128)(2,1)S(1)} %collective-permute-done.4.refs_1_, ...), custom_call_target="tpu_custom_call" | custom-call | flops 11500000 | bytes 622592 | tf_op jit(solution)/shard_map/pallas_call | solution.py:45
  19.9 2.0 %collective-permute-start.8 = (bf16[384,128]{1,0:T(8,128)(2,1)S(1)}, bf16[384,128]{1,0:T(8,128)(2,1)S(1)}, u32[]{:S(2)}, u32[]{:S(2)}) collective-permute-start(bf16[384,128]{1,0:T(8,128)(2,1)S(1)} %shard_map.133.refs_4_), channel_id=1, source_target_pairs={{0,2},{1,3},{2,0},{3,1},{4,6},{5,7},{6,4},{7,5},{8,10},{9,11},{10,... | collective-permute-start | bytes 294920 | tf_op jit(solution)/shard_map/ppermute | solution.py:622
  22.0 0.0 collective-permute-start.7
  22.0 0.1 reshape.41
  22.1 1.1 %shard_map.134.warm = f32[4,64,128]{2,1,0:T(8,128)S(1)} custom-call(f32[4,64,128]{2,1,0:T(8,128)S(1)} %copy-done.1, f32[64,128]{1,0:T(8,128)S(1)} %copy-done.6, bf16[112,128]{1,0:T(8,128)(2,1)S(1)} %get-tuple-element.33.refs_0_, bf16[112,128]{1,0:T(8,128)(2,1)S(1)} %collective-permute-done.4.refs_1_, bf16[112,128]{1,0:T(8,128)(2,1)S(1)} %collective-permute-done.5.refs_2_, ...), custom_call_target="tpu_custom_call" | custom-call | flops 11500000 | bytes 622592 | tf_op jit(solution)/shard_map/pallas_call | solution.py:45
  23.2 1.4 %collective-permute-done.8.refs_6_ = bf16[384,128]{1,0:T(8,128)(2,1)S(1)} collective-permute-done((bf16[384,128]{1,0:T(8,128)(2,1)S(1)}, bf16[384,128]{1,0:T(8,128)(2,1)S(1)}, u32[]{:S(2)}, u32[]{:S(2)}) %collective-permute-start.8) | collective-permute-done | bytes 98336 | tf_op jit(solution)/shard_map/ppermute | solution.py:622
  24.6 0.0 collective-permute-start.9
  24.6 0.1 xor_select_fusion.table
  24.7 0.0 collective-permute-done.7.refs_5_
  24.7 1.2 %collective-permute-done.9.refs_7_ = bf16[384,128]{1,0:T(8,128)(2,1)S(1)} collective-permute-done((bf16[384,128]{1,0:T(8,128)(2,1)S(1)}, bf16[384,128]{1,0:T(8,128)(2,1)S(1)}, u32[]{:S(2)}, u32[]{:S(2)}) %collective-permute-start.9) | collective-permute-done | bytes 98336 | tf_op jit(solution)/shard_map/ppermute | solution.py:628
  25.9 2.6 %shard_map.135 = (f32[2,128,128]{2,1,0:T(8,128)S(1)}, f32[384,128]{1,0:T(8,128)S(1)}, bf16[384,128]{1,0:T(8,128)(2,1)S(1)}) custom-call(s32[16,4]{1,0:T(8,128)S(1)} %xor_select_fusion.table, f32[128,128]{1,0:T(8,128)S(1)} %get-tuple-element.35.viscous, f32[128,128]{1,0:T(8,128)S(1)} %get-tuple-element.36.gain, f32[128,128]{1,0:T(8,128)S(1)} %get-tuple-element.27.drag, ...), custom_call_target="tpu_custom_call" | custom-call | flops 11500000 | bytes 1356032 | tf_op jit(solution)/shard_map/pallas_call | solution.py:45
  28.5 0.2 collective-permute-start.10
  28.7 1.1 %collective-permute-done.10.beside = bf16[384,128]{1,0:T(8,128)(2,1)S(1)} collective-permute-done((bf16[384,128]{1,0:T(8,128)(2,1)S(1)}, bf16[384,128]{1,0:T(8,128)(2,1)S(1)}, u32[]{:S(2)}, u32[]{:S(2)}) %collective-permute-start.10) | collective-permute-done | bytes 98336 | tf_op jit(solution)/shard_map/ppermute | solution.py:750
  29.9 2.0 %collective-permute-start.11 = (bf16[192,128]{1,0:T(8,128)(2,1)S(1)}, bf16[192,128]{1,0:T(8,128)(2,1)S(1)}, u32[]{:S(2)}, u32[]{:S(2)}) collective-permute-start(bf16[192,128]{1,0:T(8,128)(2,1)S(1)} %shard_map.137), channel_id=1, source_target_pairs={{0,2},{1,3},{2,0},{3,1},{4,6},{5,7},{6,4},{7,5},{8,10},{9,11},{10,... | collective-permute-start | bytes 147464 | tf_op jit(solution)/shard_map/ppermute | solution.py:755
  31.9 0.0 copy-start.7
  31.9 0.7 %shard_map.136 = (f32[256,128]{1,0:T(8,128)}, f32[192,128]{1,0:T(8,128)S(1)}) custom-call(f32[2,128,128]{2,1,0:T(8,128)S(1)} %get-tuple-element.42.speed, f32[384,128]{1,0:T(8,128)S(1)} %get-tuple-element.43.own, bf16[384,128]{1,0:T(8,128)(2,1)S(1)} %collective-permute-done.10.beside), custom_call_target="tpu_custom_call" | custom-call | flops 11500000 | bytes 425984 | tf_op jit(solution)/shard_map/pallas_call | solution.py:45
  32.6 1.4 %collective-permute-done.11.refs_0_ = bf16[192,128]{1,0:T(8,128)(2,1)S(1)} collective-permute-done((bf16[192,128]{1,0:T(8,128)(2,1)S(1)}, bf16[192,128]{1,0:T(8,128)(2,1)S(1)}, u32[]{:S(2)}, u32[]{:S(2)}) %collective-permute-start.11) | collective-permute-done | bytes 49184 | tf_op jit(solution)/shard_map/ppermute | solution.py:755
  34.0 0.0 copy-done.7
  34.0 0.7 %shard_map.138 = (f32[4,64,128]{2,1,0:T(8,128)}, f32[2,64,128]{2,1,0:T(8,128)}) custom-call(f32[4,64,128]{2,1,0:T(8,128)S(1)} %shard_map.134.warm, f32[2,64,128]{2,1,0:T(8,128)S(1)} %copy-done.7, f32[192,128]{1,0:T(8,128)S(1)} %get-tuple-element.45.total, bf16[192,128]{1,0:T(8,128)(2,1)S(1)} %collective-permute-done.11.refs_0_), custom_call_target="tpu_custom_call" | custom-call | flops 11500000 | bytes 344064 | tf_op jit(solution)/shard_map/pallas_call | solution.py:45
  (7 shorter events, 0.0 us)
Async XLA Ops:
  0.6 8.3 %copy-start.1 = (f32[4,64,128]{2,1,0:T(8,128)S(1)}, f32[4,64,128]{2,1,0:T(8,128)}, u32[]{:S(2)}) copy-start(f32[4,64,128]{2,1,0:T(8,128)} %water.5) | copy-start | bytes 393220
  0.6 8.3 %copy-start.2 = (f32[1,1,5,16384]{3,1,2,0:T(1,128)S(1)}, f32[1,1,5,16384]{3,1,2,0:T(1,128)}, u32[]{:S(2)}) copy-start(f32[1,1,5,16384]{3,1,2,0:T(1,128)} %param.18) | copy-start | bytes 983044
  0.7 8.3 %copy-start.3 = (f32[1,1,5,16384]{3,1,2,0:T(1,128)S(1)}, f32[1,1,5,16384]{3,1,2,0:T(1,128)}, u32[]{:S(2)}) copy-start(f32[1,1,5,16384]{3,1,2,0:T(1,128)} %param.19) | copy-start | bytes 983044
  0.7 8.3 %copy-start.4 = (f32[1,1,2,16384]{3,2,1,0:T(2,128)S(1)}, f32[1,1,2,16384]{3,2,1,0:T(2,128)}, u32[]{:S(2)}) copy-start(f32[1,1,2,16384]{3,2,1,0:T(2,128)} %param.20) | copy-start | bytes 393220
  3.2 5.7 %collective-permute-start.1 = (bf16[336,128]{1,0:T(8,128)(2,1)}, bf16[336,128]{1,0:T(8,128)(2,1)S(1)}, u32[]{:S(2)}, u32[]{:S(2)}) collective-permute-start(bf16[336,128]{1,0:T(8,128)(2,1)} %get-tuple-element.30), channel_id=1, source_target_pairs={{0,2},{1,3},{2,0},{3,1},{4,6},{5,7},{6,4},{7,5},{8,10},{9,11},{10,... | collective-permute-start | bytes 258056 | tf_op jit(solution)/shard_map/ppermute | solution.py:634
  6.2 3.7 %collective-permute-start.2 = (bf16[336,128]{1,0:T(8,128)(2,1)}, bf16[336,128]{1,0:T(8,128)(2,1)S(1)}, u32[]{:S(2)}, u32[]{:S(2)}) collective-permute-start(bf16[336,128]{1,0:T(8,128)(2,1)} %get-tuple-element.31), channel_id=1, source_target_pairs={{0,1},{1,0},{2,3},{3,2},{4,5},{5,4},{6,7},{7,6},{8,9},{9,8},{10,11... | collective-permute-start | bytes 258056 | tf_op jit(solution)/shard_map/ppermute | solution.py:634
  6.2 3.7 %collective-permute-start = (bf16[192,128]{1,0:T(8,128)(2,1)}, bf16[192,128]{1,0:T(8,128)(2,1)S(1)}, u32[]{:S(2)}, u32[]{:S(2)}) collective-permute-start(bf16[192,128]{1,0:T(8,128)(2,1)} %get-tuple-element.29), channel_id=1, source_target_pairs={{0,3},{1,2},{2,1},{3,0},{4,7},{5,6},{6,5},{7,4},{8,11},{9,10},{10,... | collective-permute-start | bytes 147464 | tf_op jit(solution)/shard_map/ppermute | solution.py:634
  8.9 1.2 %collective-permute-start.3 = (bf16[144,128]{1,0:T(8,128)(2,1)S(1)}, bf16[144,128]{1,0:T(8,128)(2,1)S(1)}, u32[]{:S(2)}, u32[]{:S(2)}) collective-permute-start(bf16[144,128]{1,0:T(8,128)(2,1)S(1)} %slice.28), channel_id=1, source_target_pairs={{0,1},{1,0},{2,3},{3,2},{4,5},{5,4},{6,7},{7,6},{8,9},{9,8},{10,11... | collective-permute-start | bytes 110600 | tf_op jit(solution)/shard_map/ppermute | solution.py:681
  9.0 1.2 %copy-start = (bf16[336,128]{1,0:T(8,128)(2,1)S(1)}, bf16[336,128]{1,0:T(8,128)(2,1)}, u32[]{:S(2)}) copy-start(bf16[336,128]{1,0:T(8,128)(2,1)} %get-tuple-element.32.refs_3_.refs_4_.refs_0_) | copy-start | bytes 258052
  9.0 1.2 %copy-start.5 = (f32[1,1,2,16384]{3,2,1,0:T(2,128)S(1)}, f32[1,1,2,16384]{3,2,1,0:T(2,128)}, u32[]{:S(2)}) copy-start(f32[1,1,2,16384]{3,2,1,0:T(2,128)} %param.21) | copy-start | bytes 393220
  10.1 9.3 %copy-start.6 = (f32[64,128]{1,0:T(8,128)S(1)}, f32[64,128]{1,0:T(8,128)}, u32[]{:S(2)}) copy-start(f32[64,128]{1,0:T(8,128)} %mixing.2) | copy-start | bytes 98308
  10.7 4.9 %collective-permute-start.6 = (bf16[112,128]{1,0:T(8,128)(2,1)S(1)}, bf16[112,128]{1,0:T(8,128)(2,1)S(1)}, u32[]{:S(2)}, u32[]{:S(2)}) collective-permute-start(bf16[112,128]{1,0:T(8,128)(2,1)S(1)} %get-tuple-element.33.refs_0_), channel_id=1, source_target_pairs={{0,8},{4,12},{8,0},{12,4},{1,9},{5,13},{9,1},{13,5},{2,10},{6,14},... | collective-permute-start | bytes 86024 | tf_op jit(solution)/shard_map/ppermute | solution.py:617
  13.8 5.7 %collective-permute-start.5 = (bf16[112,128]{1,0:T(8,128)(2,1)S(1)}, bf16[112,128]{1,0:T(8,128)(2,1)S(1)}, u32[]{:S(2)}, u32[]{:S(2)}) collective-permute-start(bf16[112,128]{1,0:T(8,128)(2,1)S(1)} %get-tuple-element.33.refs_0_), channel_id=1, source_target_pairs={{0,12},{4,8},{8,4},{12,0},{1,13},{5,9},{9,5},{13,1},{2,14},{6,10},... | collective-permute-start | bytes 86024 | tf_op jit(solution)/shard_map/ppermute | solution.py:617
  15.2 4.3 %collective-permute-start.4 = (bf16[112,128]{1,0:T(8,128)(2,1)S(1)}, bf16[112,128]{1,0:T(8,128)(2,1)S(1)}, u32[]{:S(2)}, u32[]{:S(2)}) collective-permute-start(bf16[112,128]{1,0:T(8,128)(2,1)S(1)} %get-tuple-element.33.refs_0_), channel_id=1, source_target_pairs={{0,4},{4,0},{8,12},{12,8},{1,5},{5,1},{9,13},{13,9},{2,6},{6,2},{1... | collective-permute-start | bytes 86024 | tf_op jit(solution)/shard_map/ppermute | solution.py:617
  19.9 4.7 %collective-permute-start.8 = (bf16[384,128]{1,0:T(8,128)(2,1)S(1)}, bf16[384,128]{1,0:T(8,128)(2,1)S(1)}, u32[]{:S(2)}, u32[]{:S(2)}) collective-permute-start(bf16[384,128]{1,0:T(8,128)(2,1)S(1)} %shard_map.133.refs_4_), channel_id=1, source_target_pairs={{0,2},{1,3},{2,0},{3,1},{4,6},{5,7},{6,4},{7,5},{8,10},{9,11},{10,... | collective-permute-start | bytes 294920 | tf_op jit(solution)/shard_map/ppermute | solution.py:622
  22.0 2.7 %collective-permute-start.7 = (bf16[384,128]{1,0:T(8,128)(2,1)S(1)}, bf16[384,128]{1,0:T(8,128)(2,1)S(1)}, u32[]{:S(2)}, u32[]{:S(2)}) collective-permute-start(bf16[384,128]{1,0:T(8,128)(2,1)S(1)} %shard_map.133.refs_4_), channel_id=1, source_target_pairs={{0,1},{1,0},{2,3},{3,2},{4,5},{5,4},{6,7},{7,6},{8,9},{9,8},{10,11... | collective-permute-start | bytes 294920 | tf_op jit(solution)/shard_map/ppermute | solution.py:628
  24.6 1.3 %collective-permute-start.9 = (bf16[384,128]{1,0:T(8,128)(2,1)S(1)}, bf16[384,128]{1,0:T(8,128)(2,1)S(1)}, u32[]{:S(2)}, u32[]{:S(2)}) collective-permute-start(bf16[384,128]{1,0:T(8,128)(2,1)S(1)} %collective-permute-done.8.refs_6_), channel_id=1, source_target_pairs={{0,1},{1,0},{2,3},{3,2},{4,5},{5,4},{6,7},{7,6},{8,9},{9,8},{10,11... | collective-permute-start | bytes 294920 | tf_op jit(solution)/shard_map/ppermute | solution.py:628
  28.5 1.4 %collective-permute-start.10 = (bf16[384,128]{1,0:T(8,128)(2,1)S(1)}, bf16[384,128]{1,0:T(8,128)(2,1)S(1)}, u32[]{:S(2)}, u32[]{:S(2)}) collective-permute-start(bf16[384,128]{1,0:T(8,128)(2,1)S(1)} %get-tuple-element.44), channel_id=1, source_target_pairs={{0,1},{1,0},{2,3},{3,2},{4,5},{5,4},{6,7},{7,6},{8,9},{9,8},{10,11... | collective-permute-start | bytes 294920 | tf_op jit(solution)/shard_map/ppermute | solution.py:750
  29.9 4.2 %collective-permute-start.11 = (bf16[192,128]{1,0:T(8,128)(2,1)S(1)}, bf16[192,128]{1,0:T(8,128)(2,1)S(1)}, u32[]{:S(2)}, u32[]{:S(2)}) collective-permute-start(bf16[192,128]{1,0:T(8,128)(2,1)S(1)} %shard_map.137), channel_id=1, source_target_pairs={{0,2},{1,3},{2,0},{3,1},{4,6},{5,7},{6,4},{7,5},{8,10},{9,11},{10,... | collective-permute-start | bytes 147464 | tf_op jit(solution)/shard_map/ppermute | solution.py:755
  31.9 2.1 %copy-start.7 = (f32[2,64,128]{2,1,0:T(8,128)S(1)}, f32[2,64,128]{2,1,0:T(8,128)}, u32[]{:S(2)}) copy-start(f32[2,64,128]{2,1,0:T(8,128)} %currents.1) | copy-start | bytes 196612

commit v18 on v17

--- a/solution.py
+++ b/solution.py
@@ -90,7 +90,7 @@
 
 def forward_kernel(group, links_h, blocks_h, rows_h, cols_h, currents_h, water_h, *refs):
     devices, members, place = group
-    outs, scratch = refs[:members], refs[members:]
+    outs, fields_o, scratch = refs[:members], refs[members], refs[members + 1 :]
     links, blocks, currents, weights, water, fields, kept, arrived, left = scratch
     pairs, side, width = rows_h.shape
     both = weights.shape[1]
@@ -143,6 +143,8 @@
             target = out.at[pl.ds(both, fields.shape[0])]
             copies.append(pltpu.make_async_copy(fields, target, left.at[2 * k + 1]))
             copies[-1].start()
+    copies.append(pltpu.make_async_copy(fields, fields_o, left.at[2 * members]))
+    copies[-1].start()
     for copy in copies:
         copy.wait()
 
@@ -232,14 +234,14 @@
     return total
 
 
-def tails_of(chunks, hops):
+def tails_of(chunks, others):
     at = min(c.shape[0] for c in chunks)
-    return [hops[k // 2 - 1][...] if k > 1 and k % 2 else c[at:] for k, c in enumerate(chunks)]
+    return [c[at:] for c in chunks[:2]] + [other[...] for other in others]
 
 
 def forcing_kernel(group, side, levels, subs, place, mass, drag, wind, early, *refs):
-    chunks = refs[:group][::-1]
-    hops, (out, current_o, push_o, store) = refs[group:-4], refs[-4:]
+    hops, chunks = refs[: group - 2], refs[group - 2 : 2 * group - 2]
+    out, current_o, push_o, store = refs[2 * group - 2 :]
     size = mass.shape[0]
     depth = chunks[0].shape[1]
     tails = tails_of(chunks, hops)
@@ -647,12 +649,10 @@
     tail_rows = -(-(2 * levels + 1) // TILE_ROWS) * TILE_ROWS
     pair_rows = side + width
     chunk_rows = pair_rows + 2 * side + tail_rows
-    sent = call(
+    *sent, fields = call(
         functools.partial(forward_kernel, (devices, group, member_place)),
-        [
-            shape(pair_rows if k > 1 and k % 2 else chunk_rows, width, dtype=BF16)
-            for k in range(group)
-        ],
+        [shape(chunk_rows if k < 2 else pair_rows, width, dtype=BF16) for k in range(group)]
+        + [shape(chunk_rows - pair_rows, width, dtype=BF16)],
         (
             neighbors,
             remap_blocks,
@@ -670,17 +670,17 @@
             pltpu.VMEM((chunk_rows - pair_rows, width), BF16),
             pltpu.VMEM((1 if pairs == group else group, pair_rows, width), BF16),
             pltpu.SemaphoreType.DMA((6,)),
-            pltpu.SemaphoreType.DMA((2 * group,)),
+            pltpu.SemaphoreType.DMA((2 * group + 1,)),
         ],
         hbm=(0, 1, 2, 3, 4, 5),
         grant=60 * 2**20,
         micros=10,
     )
     chunks = swap_each(sent)
-    hops = [
-        lax.ppermute(chunks[k][pair_rows:], group_axes, [(i, i ^ 1) for i in range(group)])
-        for k in range(2, group, 2)
-    ]
+    hops = []
+    for k in range(2, group, 2):
+        far = lax.ppermute(fields, group_axes, [(i, i ^ k) for i in range(group)])
+        hops += [far, lax.ppermute(far, group_axes, [(i, i ^ 1) for i in range(group)])]
 
     early, viscous, gain, step_mass, drag, conduct, speed = call(
         rims_kernel,
@@ -696,7 +696,7 @@
     message, current_ice, push = call(
         functools.partial(forcing_kernel, group, side, levels, sub_count, member_place),
         [shape(BLOCK_ROWS + extra_rows, size, dtype=BF16), planes, planes],
-        (step_mass, drag, wind, early, *chunks[::-1], *hops),
+        (step_mass, drag, wind, early, *hops, *chunks),
         scratch=[pltpu.VMEM((BLOCK_ROWS + extra_rows, size), F32)],
     )
     messages = swap(message, "tile", tile_count)

time: 34.9 us -> 35.4 us (1.014)
  waiting for transfers between devices: 12.7 us -> 13.2 us
    ppermute x1 -> x2, starting transfers between devices: 0.01 us -> 2.57 us  [the longest x1 2.56 us: shards(): far = lax.ppermute(fields, group_axes, [(i, i ^ k) for i in range(group)])]
    ppermute x3, waiting for transfers between devices: 3.23 us -> 1.99 us  [swap_each(): lax.ppermute(values[k], group_axes, [(i, i ^ k) for i in range(group)])]
    ppermute x3, starting transfers between devices: 3.21 us -> 2.03 us  [swap_each(): lax.ppermute(values[k], group_axes, [(i, i ^ k) for i in range(group)])]
    ppermute x1, starting transfers between devices: 2.05 us -> 1.48 us  [swap_chips(): lax.ppermute(value, group_axes, [(i, i ^ k) for i in range(group)])]
    ppermute x1, waiting for transfers between devices: 1.42 us -> 1.99 us  [shards(): lax.ppermute(value, group_axes, [(i, i ^ 2 * k + 2) for i in range(group)])]
    ppermute x1, starting transfers between devices: 2.05 us -> 1.48 us  [shards(): lax.ppermute(value, group_axes, [(i, i ^ 2 * k + 2) for i in range(group)])]
    ppermute x1, waiting for transfers between devices: 1.4 us -> 1.97 us  [swap_chips(): lax.ppermute(value, group_axes, [(i, i ^ k) for i in range(group)])]
    ppermute x1 -> x2, waiting for transfers between devices: 0.23 us -> 0.77 us  [the longest x1 0.76 us: shards(): far = lax.ppermute(fields, group_axes, [(i, i ^ k) for i in range(group)])]
  transfers between devices with their start and end apart: 12 -> 13, of which waited for: 9 -> 8; matrix products, arithmetic and copies ran while one was open for 1% -> 0% of each run, Pallas kernels for 6% -> 6%
where the time goes in v18:
time: 35.4 us; the launch traced here: 35.2 us
  waiting for transfers between devices  13.2 us (37%)
  starting transfers between devices  12.2 us (34%)
  Pallas kernels  8.8 us (25%)
  between operations  0.79 us (2%)
    pallas_call x9, Pallas kernels, call(): pl.pallas_call(kernel, out_shape=outs, in_specs=specs, out_specs=jax.tree...  8.8 us
    ppermute x3, starting transfers between devices, swap(): got[k] = lax.ppermute(value, axes, [(i, i ^ k) for i in range(count)])  4.44 us
    ppermute x3, waiting for transfers between devices, swap(): got[k] = lax.ppermute(value, axes, [(i, i ^ k) for i in range(count)])  4.09 us
    ppermute x1, starting transfers between devices, shards(): far = lax.ppermute(fields, group_axes, [(i, i ^ k) for i in range(group)])  2.56 us
    ppermute x3, starting transfers between devices, swap_each(): lax.ppermute(values[k], group_axes, [(i, i ^ k) for i in range(group)])  2.03 us
    ppermute x1, waiting for transfers between devices, shards(): lax.ppermute(value, group_axes, [(i, i ^ 2 * k + 2) for i in range(group)])  1.99 us
    ppermute x3, waiting for transfers between devices, swap_each(): lax.ppermute(values[k], group_axes, [(i, i ^ k) for i in range(group)])  1.99 us
    ppermute x1, waiting for transfers between devices, swap_chips(): lax.ppermute(value, group_axes, [(i, i ^ k) for i in range(group)])  1.97 us
  transfers between devices with their start and end apart: 13, of which 8 were waited for; matrix products, arithmetic and copies ran while one was open for 0% of the time, Pallas kernels for 6%

profile of v18, /device:TPU:0, one launch (start us, length us, event | category | flops | bytes accessed | tf_op | source)
XLA Modules:
  0.0 35.2 jit_solution(10574276337436998654)
XLA Ops:
  0.6 0.0 copy-start.1
  0.6 0.0 copy-start.2
  0.7 0.0 copy-start.3
  0.7 0.0 copy-start.4
  0.7 2.5 %shard_map.131 = (bf16[336,128]{1,0:T(8,128)(2,1)}, bf16[336,128]{1,0:T(8,128)(2,1)}, bf16[192,128]{1,0:T(8,128)(2,1)}, bf16[192,128]{1,0:T(8,128)(2,1)}, bf16[144,128]{1,0:T(8,128)(2,1)}) custom-call(s32[1,1,4]{2,1,0:T(1,128)} %links_h.1, s32[1,4]{1,0:T(1,128)} %blocks_h.1, bf16[4,64,128]{2,1,0:T(8,128)(2,1)} %bitcast.27, bf16[4,128,128]{2,1,0:T(8,128)(2,1)} %bitcast.25, ...), custom_call_target="tpu_custom_call" | custom-call | flops 11500000256 | bytes 393248 | tf_op jit(solution)/shard_map/pallas_call | solution.py:45
  3.2 0.5 %collective-permute-start.2 = (bf16[336,128]{1,0:T(8,128)(2,1)}, bf16[336,128]{1,0:T(8,128)(2,1)S(1)}, u32[]{:S(2)}, u32[]{:S(2)}) collective-permute-start(bf16[336,128]{1,0:T(8,128)(2,1)} %get-tuple-element.32), channel_id=1, source_target_pairs={{0,1},{1,0},{2,3},{3,2},{4,5},{5,4},{6,7},{7,6},{8,9},{9,8},{10,11... | collective-permute-start | bytes 258056 | tf_op jit(solution)/shard_map/ppermute | solution.py:636
  3.7 2.6 %collective-permute-start = (bf16[144,128]{1,0:T(8,128)(2,1)}, bf16[144,128]{1,0:T(8,128)(2,1)S(1)}, u32[]{:S(2)}, u32[]{:S(2)}) collective-permute-start(bf16[144,128]{1,0:T(8,128)(2,1)} %get-tuple-element.30), channel_id=1, source_target_pairs={{0,2},{1,3},{2,0},{3,1},{4,6},{5,7},{6,4},{7,5},{8,10},{9,11},{10,... | collective-permute-start | bytes 110600 | tf_op jit(solution)/shard_map/ppermute | solution.py:682
  6.3 0.1 collective-permute-start.3
  6.3 1.4 %collective-permute-start.4 = (bf16[192,128]{1,0:T(8,128)(2,1)}, bf16[192,128]{1,0:T(8,128)(2,1)S(1)}, u32[]{:S(2)}, u32[]{:S(2)}) collective-permute-start(bf16[192,128]{1,0:T(8,128)(2,1)} %get-tuple-element.34), channel_id=1, source_target_pairs={{0,3},{1,2},{2,1},{3,0},{4,7},{5,6},{6,5},{7,4},{8,11},{9,10},{10,... | collective-permute-start | bytes 147464 | tf_op jit(solution)/shard_map/ppermute | solution.py:636
  7.8 0.8 %collective-permute-done.refs_0_.refs_8_ = bf16[144,128]{1,0:T(8,128)(2,1)S(1)} collective-permute-done((bf16[144,128]{1,0:T(8,128)(2,1)}, bf16[144,128]{1,0:T(8,128)(2,1)S(1)}, u32[]{:S(2)}, u32[]{:S(2)}) %collective-permute-start) | collective-permute-done | bytes 36896 | tf_op jit(solution)/shard_map/ppermute | solution.py:682
  8.5 0.0 collective-permute-start.1
  8.5 0.0 copy-done.1
  8.5 0.0 copy-done.2
  8.5 0.0 copy-done.3
  8.6 0.0 copy-done.4
  8.6 0.0 copy-start
  8.6 0.0 copy-start.5
  8.6 0.2 shard_map.130
  8.8 2.0 %collective-permute-done.3.refs_4_.refs_6_.refs_2_ = bf16[192,128]{1,0:T(8,128)(2,1)S(1)} collective-permute-done((bf16[192,128]{1,0:T(8,128)(2,1)}, bf16[192,128]{1,0:T(8,128)(2,1)S(1)}, u32[]{:S(2)}, u32[]{:S(2)}) %collective-permute-start.3) | collective-permute-done | bytes 49184 | tf_op jit(solution)/shard_map/ppermute | solution.py:636
  10.8 0.0 collective-permute-done.4.refs_5_.refs_7_.refs_3_
  10.8 0.0 collective-permute-done.1.refs_1_.refs_9_
  10.8 0.0 collective-permute-done.2.refs_3_.refs_5_.refs_1_
  10.8 0.0 copy-done
  10.8 0.0 copy-done.5
  10.8 0.0 copy-start.6
  10.8 0.6 %shard_map.132 = (bf16[112,128]{1,0:T(8,128)(2,1)S(1)}, f32[2,128,128]{2,1,0:T(8,128)S(1)}, f32[2,128,128]{2,1,0:T(8,128)S(1)}) custom-call(f32[128,128]{1,0:T(8,128)S(1)} %get-tuple-element.27.mass, f32[128,128]{1,0:T(8,128)S(1)} %get-tuple-element.28.drag, f32[256,128]{1,0:T(8,128)S(1)} %bitcast.24, f32[72,128]{1,0:T(8,128)S(1)} %get-tuple-element.29.early, ...), custom_call_target="tpu_custom_call" | custom-call | flops 11500000 | bytes 643072 | tf_op jit(solution)/shard_map/pallas_call | solution.py:45
  11.4 2.9 %collective-permute-start.7 = (bf16[112,128]{1,0:T(8,128)(2,1)S(1)}, bf16[112,128]{1,0:T(8,128)(2,1)S(1)}, u32[]{:S(2)}, u32[]{:S(2)}) collective-permute-start(bf16[112,128]{1,0:T(8,128)(2,1)S(1)} %get-tuple-element.35.refs_0_), channel_id=1, source_target_pairs={{0,8},{4,12},{8,0},{12,4},{1,9},{5,13},{9,1},{13,5},{2,10},{6,14},... | collective-permute-start | bytes 86024 | tf_op jit(solution)/shard_map/ppermute | solution.py:619
  14.3 1.3 %collective-permute-start.6 = (bf16[112,128]{1,0:T(8,128)(2,1)S(1)}, bf16[112,128]{1,0:T(8,128)(2,1)S(1)}, u32[]{:S(2)}, u32[]{:S(2)}) collective-permute-start(bf16[112,128]{1,0:T(8,128)(2,1)S(1)} %get-tuple-element.35.refs_0_), channel_id=1, source_target_pairs={{0,12},{4,8},{8,4},{12,0},{1,13},{5,9},{9,5},{13,1},{2,14},{6,10},... | collective-permute-start | bytes 86024 | tf_op jit(solution)/shard_map/ppermute | solution.py:619
  15.6 0.2 collective-permute-start.5
  15.9 0.4 %collective-permute-done.7.refs_3_ = bf16[112,128]{1,0:T(8,128)(2,1)S(1)} collective-permute-done((bf16[112,128]{1,0:T(8,128)(2,1)S(1)}, bf16[112,128]{1,0:T(8,128)(2,1)S(1)}, u32[]{:S(2)}, u32[]{:S(2)}) %collective-permute-start.7) | collective-permute-done | bytes 28704 | tf_op jit(solution)/shard_map/ppermute | solution.py:619
  16.2 3.7 %collective-permute-done.6.refs_2_ = bf16[112,128]{1,0:T(8,128)(2,1)S(1)} collective-permute-done((bf16[112,128]{1,0:T(8,128)(2,1)S(1)}, bf16[112,128]{1,0:T(8,128)(2,1)S(1)}, u32[]{:S(2)}, u32[]{:S(2)}) %collective-permute-start.6) | collective-permute-done | bytes 28704 | tf_op jit(solution)/shard_map/ppermute | solution.py:619
  20.0 0.0 collective-permute-done.5.refs_1_
  20.0 0.0 copy-done.6
  20.0 0.4 %shard_map.133.refs_4_ = bf16[384,128]{1,0:T(8,128)(2,1)S(1)} custom-call(f32[4,64,128]{2,1,0:T(8,128)S(1)} %copy-done.1, f32[64,128]{1,0:T(8,128)S(1)} %copy-done.6, bf16[112,128]{1,0:T(8,128)(2,1)S(1)} %get-tuple-element.35.refs_0_, bf16[112,128]{1,0:T(8,128)(2,1)S(1)} %collective-permute-done.5.refs_1_, ...), custom_call_target="tpu_custom_call" | custom-call | flops 11500000 | bytes 622592 | tf_op jit(solution)/shard_map/pallas_call | solution.py:45
  20.4 1.5 %collective-permute-start.9 = (bf16[384,128]{1,0:T(8,128)(2,1)S(1)}, bf16[384,128]{1,0:T(8,128)(2,1)S(1)}, u32[]{:S(2)}, u32[]{:S(2)}) collective-permute-start(bf16[384,128]{1,0:T(8,128)(2,1)S(1)} %shard_map.133.refs_4_), channel_id=1, source_target_pairs={{0,2},{1,3},{2,0},{3,1},{4,6},{5,7},{6,4},{7,5},{8,10},{9,11},{10,... | collective-permute-start | bytes 294920 | tf_op jit(solution)/shard_map/ppermute | solution.py:624
  21.9 0.0 collective-permute-start.8
  21.9 0.1 reshape.41
  22.0 1.1 %shard_map.134.warm = f32[4,64,128]{2,1,0:T(8,128)S(1)} custom-call(f32[4,64,128]{2,1,0:T(8,128)S(1)} %copy-done.1, f32[64,128]{1,0:T(8,128)S(1)} %copy-done.6, bf16[112,128]{1,0:T(8,128)(2,1)S(1)} %get-tuple-element.35.refs_0_, bf16[112,128]{1,0:T(8,128)(2,1)S(1)} %collective-permute-done.5.refs_1_, bf16[112,128]{1,0:T(8,128)(2,1)S(1)} %collective-permute-done.6.refs_2_, ...), custom_call_target="tpu_custom_call" | custom-call | flops 11500000 | bytes 622592 | tf_op jit(solution)/shard_map/pallas_call | solution.py:45
  23.1 2.0 %collective-permute-done.9.refs_6_ = bf16[384,128]{1,0:T(8,128)(2,1)S(1)} collective-permute-done((bf16[384,128]{1,0:T(8,128)(2,1)S(1)}, bf16[384,128]{1,0:T(8,128)(2,1)S(1)}, u32[]{:S(2)}, u32[]{:S(2)}) %collective-permute-start.9) | collective-permute-done | bytes 98336 | tf_op jit(solution)/shard_map/ppermute | solution.py:624
  25.1 0.0 collective-permute-start.10
  25.1 0.1 xor_select_fusion.table
  25.2 0.0 collective-permute-done.8.refs_5_
  25.2 1.2 %collective-permute-done.10.refs_7_ = bf16[384,128]{1,0:T(8,128)(2,1)S(1)} collective-permute-done((bf16[384,128]{1,0:T(8,128)(2,1)S(1)}, bf16[384,128]{1,0:T(8,128)(2,1)S(1)}, u32[]{:S(2)}, u32[]{:S(2)}) %collective-permute-start.10) | collective-permute-done | bytes 98336 | tf_op jit(solution)/shard_map/ppermute | solution.py:630
  26.4 2.6 %shard_map.135 = (f32[2,128,128]{2,1,0:T(8,128)S(1)}, f32[384,128]{1,0:T(8,128)S(1)}, bf16[384,128]{1,0:T(8,128)(2,1)S(1)}) custom-call(s32[16,4]{1,0:T(8,128)S(1)} %xor_select_fusion.table, f32[128,128]{1,0:T(8,128)S(1)} %get-tuple-element.37.viscous, f32[128,128]{1,0:T(8,128)S(1)} %get-tuple-element.38.gain, f32[128,128]{1,0:T(8,128)S(1)} %get-tuple-element.28.drag, ...), custom_call_target="tpu_custom_call" | custom-call | flops 11500000 | bytes 1319168 | tf_op jit(solution)/shard_map/pallas_call | solution.py:45
  29.0 0.2 collective-permute-start.11
  29.2 1.1 %collective-permute-done.11.beside = bf16[384,128]{1,0:T(8,128)(2,1)S(1)} collective-permute-done((bf16[384,128]{1,0:T(8,128)(2,1)S(1)}, bf16[384,128]{1,0:T(8,128)(2,1)S(1)}, u32[]{:S(2)}, u32[]{:S(2)}) %collective-permute-start.11) | collective-permute-done | bytes 98336 | tf_op jit(solution)/shard_map/ppermute | solution.py:750
  30.3 1.5 %collective-permute-start.12 = (bf16[192,128]{1,0:T(8,128)(2,1)S(1)}, bf16[192,128]{1,0:T(8,128)(2,1)S(1)}, u32[]{:S(2)}, u32[]{:S(2)}) collective-permute-start(bf16[192,128]{1,0:T(8,128)(2,1)S(1)} %shard_map.137), channel_id=1, source_target_pairs={{0,2},{1,3},{2,0},{3,1},{4,6},{5,7},{6,4},{7,5},{8,10},{9,11},{10,... | collective-permute-start | bytes 147464 | tf_op jit(solution)/shard_map/ppermute | solution.py:755
  31.8 0.0 copy-start.7
  31.8 0.7 %shard_map.136 = (f32[256,128]{1,0:T(8,128)}, f32[192,128]{1,0:T(8,128)S(1)}) custom-call(f32[2,128,128]{2,1,0:T(8,128)S(1)} %get-tuple-element.44.speed, f32[384,128]{1,0:T(8,128)S(1)} %get-tuple-element.45.own, bf16[384,128]{1,0:T(8,128)(2,1)S(1)} %collective-permute-done.11.beside), custom_call_target="tpu_custom_call" | custom-call | flops 11500000 | bytes 425984 | tf_op jit(solution)/shard_map/pallas_call | solution.py:45
  32.5 2.0 %collective-permute-done.12.refs_0_ = bf16[192,128]{1,0:T(8,128)(2,1)S(1)} collective-permute-done((bf16[192,128]{1,0:T(8,128)(2,1)S(1)}, bf16[192,128]{1,0:T(8,128)(2,1)S(1)}, u32[]{:S(2)}, u32[]{:S(2)}) %collective-permute-start.12) | collective-permute-done | bytes 49184 | tf_op jit(solution)/shard_map/ppermute | solution.py:755
  34.5 0.0 copy-done.7
  34.5 0.7 %shard_map.138 = (f32[4,64,128]{2,1,0:T(8,128)}, f32[2,64,128]{2,1,0:T(8,128)}) custom-call(f32[4,64,128]{2,1,0:T(8,128)S(1)} %shard_map.134.warm, f32[2,64,128]{2,1,0:T(8,128)S(1)} %copy-done.7, f32[192,128]{1,0:T(8,128)S(1)} %get-tuple-element.47.total, bf16[192,128]{1,0:T(8,128)(2,1)S(1)} %collective-permute-done.12.refs_0_), custom_call_target="tpu_custom_call" | custom-call | flops 11500000 | bytes 344064 | tf_op jit(solution)/shard_map/pallas_call | solution.py:45
  (6 shorter events, 0.0 us)
Async XLA Ops:
  0.6 7.9 %copy-start.1 = (f32[4,64,128]{2,1,0:T(8,128)S(1)}, f32[4,64,128]{2,1,0:T(8,128)}, u32[]{:S(2)}) copy-start(f32[4,64,128]{2,1,0:T(8,128)} %water.5) | copy-start | bytes 393220
  0.6 7.9 %copy-start.2 = (f32[1,1,5,16384]{3,1,2,0:T(1,128)S(1)}, f32[1,1,5,16384]{3,1,2,0:T(1,128)}, u32[]{:S(2)}) copy-start(f32[1,1,5,16384]{3,1,2,0:T(1,128)} %param.18) | copy-start | bytes 983044
  0.7 7.9 %copy-start.3 = (f32[1,1,5,16384]{3,1,2,0:T(1,128)S(1)}, f32[1,1,5,16384]{3,1,2,0:T(1,128)}, u32[]{:S(2)}) copy-start(f32[1,1,5,16384]{3,1,2,0:T(1,128)} %param.19) | copy-start | bytes 983044
  0.7 7.9 %copy-start.4 = (f32[1,1,2,16384]{3,2,1,0:T(2,128)S(1)}, f32[1,1,2,16384]{3,2,1,0:T(2,128)}, u32[]{:S(2)}) copy-start(f32[1,1,2,16384]{3,2,1,0:T(2,128)} %param.20) | copy-start | bytes 393220
  3.2 7.6 %collective-permute-start.2 = (bf16[336,128]{1,0:T(8,128)(2,1)}, bf16[336,128]{1,0:T(8,128)(2,1)S(1)}, u32[]{:S(2)}, u32[]{:S(2)}) collective-permute-start(bf16[336,128]{1,0:T(8,128)(2,1)} %get-tuple-element.32), channel_id=1, source_target_pairs={{0,1},{1,0},{2,3},{3,2},{4,5},{5,4},{6,7},{7,6},{8,9},{9,8},{10,11... | collective-permute-start | bytes 258056 | tf_op jit(solution)/shard_map/ppermute | solution.py:636
  3.7 4.8 %collective-permute-start = (bf16[144,128]{1,0:T(8,128)(2,1)}, bf16[144,128]{1,0:T(8,128)(2,1)S(1)}, u32[]{:S(2)}, u32[]{:S(2)}) collective-permute-start(bf16[144,128]{1,0:T(8,128)(2,1)} %get-tuple-element.30), channel_id=1, source_target_pairs={{0,2},{1,3},{2,0},{3,1},{4,6},{5,7},{6,4},{7,5},{8,10},{9,11},{10,... | collective-permute-start | bytes 110600 | tf_op jit(solution)/shard_map/ppermute | solution.py:682
  6.3 4.5 %collective-permute-start.3 = (bf16[192,128]{1,0:T(8,128)(2,1)}, bf16[192,128]{1,0:T(8,128)(2,1)S(1)}, u32[]{:S(2)}, u32[]{:S(2)}) collective-permute-start(bf16[192,128]{1,0:T(8,128)(2,1)} %get-tuple-element.33), channel_id=1, source_target_pairs={{0,2},{1,3},{2,0},{3,1},{4,6},{5,7},{6,4},{7,5},{8,10},{9,11},{10,... | collective-permute-start | bytes 147464 | tf_op jit(solution)/shard_map/ppermute | solution.py:636
  6.3 4.5 %collective-permute-start.4 = (bf16[192,128]{1,0:T(8,128)(2,1)}, bf16[192,128]{1,0:T(8,128)(2,1)S(1)}, u32[]{:S(2)}, u32[]{:S(2)}) collective-permute-start(bf16[192,128]{1,0:T(8,128)(2,1)} %get-tuple-element.34), channel_id=1, source_target_pairs={{0,3},{1,2},{2,1},{3,0},{4,7},{5,6},{6,5},{7,4},{8,11},{9,10},{10,... | collective-permute-start | bytes 147464 | tf_op jit(solution)/shard_map/ppermute | solution.py:636
  8.5 2.3 %collective-permute-start.1 = (bf16[144,128]{1,0:T(8,128)(2,1)S(1)}, bf16[144,128]{1,0:T(8,128)(2,1)S(1)}, u32[]{:S(2)}, u32[]{:S(2)}) collective-permute-start(bf16[144,128]{1,0:T(8,128)(2,1)S(1)} %collective-permute-done.refs_0_.refs_8_), channel_id=1, source_target_pairs={{0,1},{1,0},{2,3},{3,2},{4,5},{5,4},{6,7},{7,6},{8,9},{9,8},{10,11... | collective-permute-start | bytes 110600 | tf_op jit(solution)/shard_map/ppermute | solution.py:683
  8.6 2.3 %copy-start = (bf16[336,128]{1,0:T(8,128)(2,1)S(1)}, bf16[336,128]{1,0:T(8,128)(2,1)}, u32[]{:S(2)}) copy-start(bf16[336,128]{1,0:T(8,128)(2,1)} %get-tuple-element.31.refs_2_.refs_4_.refs_0_) | copy-start | bytes 258052
  8.6 2.2 %copy-start.5 = (f32[1,1,2,16384]{3,2,1,0:T(2,128)S(1)}, f32[1,1,2,16384]{3,2,1,0:T(2,128)}, u32[]{:S(2)}) copy-start(f32[1,1,2,16384]{3,2,1,0:T(2,128)} %param.21) | copy-start | bytes 393220
  10.8 9.1 %copy-start.6 = (f32[64,128]{1,0:T(8,128)S(1)}, f32[64,128]{1,0:T(8,128)}, u32[]{:S(2)}) copy-start(f32[64,128]{1,0:T(8,128)} %mixing.2) | copy-start | bytes 98308
  11.4 4.8 %collective-permute-start.7 = (bf16[112,128]{1,0:T(8,128)(2,1)S(1)}, bf16[112,128]{1,0:T(8,128)(2,1)S(1)}, u32[]{:S(2)}, u32[]{:S(2)}) collective-permute-start(bf16[112,128]{1,0:T(8,128)(2,1)S(1)} %get-tuple-element.35.refs_0_), channel_id=1, source_target_pairs={{0,8},{4,12},{8,0},{12,4},{1,9},{5,13},{9,1},{13,5},{2,10},{6,14},... | collective-permute-start | bytes 86024 | tf_op jit(solution)/shard_map/ppermute | solution.py:619
  14.3 5.7 %collective-permute-start.6 = (bf16[112,128]{1,0:T(8,128)(2,1)S(1)}, bf16[112,128]{1,0:T(8,128)(2,1)S(1)}, u32[]{:S(2)}, u32[]{:S(2)}) collective-permute-start(bf16[112,128]{1,0:T(8,128)(2,1)S(1)} %get-tuple-element.35.refs_0_), channel_id=1, source_target_pairs={{0,12},{4,8},{8,4},{12,0},{1,13},{5,9},{9,5},{13,1},{2,14},{6,10},... | collective-permute-start | bytes 86024 | tf_op jit(solution)/shard_map/ppermute | solution.py:619
  15.6 4.3 %collective-permute-start.5 = (bf16[112,128]{1,0:T(8,128)(2,1)S(1)}, bf16[112,128]{1,0:T(8,128)(2,1)S(1)}, u32[]{:S(2)}, u32[]{:S(2)}) collective-permute-start(bf16[112,128]{1,0:T(8,128)(2,1)S(1)} %get-tuple-element.35.refs_0_), channel_id=1, source_target_pairs={{0,4},{4,0},{8,12},{12,8},{1,5},{5,1},{9,13},{13,9},{2,6},{6,2},{1... | collective-permute-start | bytes 86024 | tf_op jit(solution)/shard_map/ppermute | solution.py:619
  20.4 4.7 %collective-permute-start.9 = (bf16[384,128]{1,0:T(8,128)(2,1)S(1)}, bf16[384,128]{1,0:T(8,128)(2,1)S(1)}, u32[]{:S(2)}, u32[]{:S(2)}) collective-permute-start(bf16[384,128]{1,0:T(8,128)(2,1)S(1)} %shard_map.133.refs_4_), channel_id=1, source_target_pairs={{0,2},{1,3},{2,0},{3,1},{4,6},{5,7},{6,4},{7,5},{8,10},{9,11},{10,... | collective-permute-start | bytes 294920 | tf_op jit(solution)/shard_map/ppermute | solution.py:624
  21.9 3.3 %collective-permute-start.8 = (bf16[384,128]{1,0:T(8,128)(2,1)S(1)}, bf16[384,128]{1,0:T(8,128)(2,1)S(1)}, u32[]{:S(2)}, u32[]{:S(2)}) collective-permute-start(bf16[384,128]{1,0:T(8,128)(2,1)S(1)} %shard_map.133.refs_4_), channel_id=1, source_target_pairs={{0,1},{1,0},{2,3},{3,2},{4,5},{5,4},{6,7},{7,6},{8,9},{9,8},{10,11... | collective-permute-start | bytes 294920 | tf_op jit(solution)/shard_map/ppermute | solution.py:630
  25.1 1.3 %collective-permute-start.10 = (bf16[384,128]{1,0:T(8,128)(2,1)S(1)}, bf16[384,128]{1,0:T(8,128)(2,1)S(1)}, u32[]{:S(2)}, u32[]{:S(2)}) collective-permute-start(bf16[384,128]{1,0:T(8,128)(2,1)S(1)} %collective-permute-done.9.refs_6_), channel_id=1, source_target_pairs={{0,1},{1,0},{2,3},{3,2},{4,5},{5,4},{6,7},{7,6},{8,9},{9,8},{10,11... | collective-permute-start | bytes 294920 | tf_op jit(solution)/shard_map/ppermute | solution.py:630
  29.0 1.4 %collective-permute-start.11 = (bf16[384,128]{1,0:T(8,128)(2,1)S(1)}, bf16[384,128]{1,0:T(8,128)(2,1)S(1)}, u32[]{:S(2)}, u32[]{:S(2)}) collective-permute-start(bf16[384,128]{1,0:T(8,128)(2,1)S(1)} %get-tuple-element.46), channel_id=1, source_target_pairs={{0,1},{1,0},{2,3},{3,2},{4,5},{5,4},{6,7},{7,6},{8,9},{9,8},{10,11... | collective-permute-start | bytes 294920 | tf_op jit(solution)/shard_map/ppermute | solution.py:750
  30.3 4.2 %collective-permute-start.12 = (bf16[192,128]{1,0:T(8,128)(2,1)S(1)}, bf16[192,128]{1,0:T(8,128)(2,1)S(1)}, u32[]{:S(2)}, u32[]{:S(2)}) collective-permute-start(bf16[192,128]{1,0:T(8,128)(2,1)S(1)} %shard_map.137), channel_id=1, source_target_pairs={{0,2},{1,3},{2,0},{3,1},{4,6},{5,7},{6,4},{7,5},{8,10},{9,11},{10,... | collective-permute-start | bytes 147464 | tf_op jit(solution)/shard_map/ppermute | solution.py:755
  31.8 2.7 %copy-start.7 = (f32[2,64,128]{2,1,0:T(8,128)S(1)}, f32[2,64,128]{2,1,0:T(8,128)}, u32[]{:S(2)}) copy-start(f32[2,64,128]{2,1,0:T(8,128)} %currents.1) | copy-start | bytes 196612

commit v19 on v17

--- a/solution.py
+++ b/solution.py
@@ -167,9 +167,15 @@
             base += 1
 
 
+def apart(pairs, wide):
+    rows = pairs.shape[0]
+    wide[0:rows] = pairs[...]
+    return [wide[pl.ds(c, rows // 2, stride=2), :] for c in range(2)]
+
+
 def rims_kernel(
     thick, conc, ice, water, out, viscous_o, gain_o, mass_o, drag_o, conduct_o,
-    speed_o,
+    speed_o, wide,
 ):
     size = thick.shape[1]
     cover = jnp.zeros((size, size), F32)
@@ -184,8 +190,7 @@
     viscous = VISCOUS_STEP * (volume * jnp.exp(-STRENGTH_DECAY * (1.0 - cover))) / mass
     step_mass = SUBCYCLE_STEP / mass
     gain = 1.0 / (1.0 + step_mass * cover)
-    speed_x = ice[pl.ds(0, size, stride=2), :]
-    speed_y = ice[pl.ds(1, size, stride=2), :]
+    speed_x, speed_y = apart(ice, wide)
     viscous_o[...] = viscous
     gain_o[...] = gain
     mass_o[...] = step_mass
@@ -239,7 +244,8 @@
 
 def forcing_kernel(group, side, levels, subs, place, mass, drag, wind, early, *refs):
     chunks = refs[:group][::-1]
-    hops, (out, current_o, push_o, store) = refs[group:-4], refs[-4:]
+    hops, (out, current_o, push_o, store, wide) = refs[group:-5], refs[-5:]
+    forces = apart(wind, wide)
     size = mass.shape[0]
     depth = chunks[0].shape[1]
     tails = tails_of(chunks, hops)
@@ -249,8 +255,7 @@
     for c in range(2):
         current = total[c * size : (c + 1) * size]
         current_o[c] = current
-        force = wind[pl.ds(c, size, stride=2), :]
-        push = mass[...] * (force + drag[...] * current)
+        push = mass[...] * (forces[c] + drag[...] * current)
         push_o[c] = push
         pushes.append(push)
     store[0:EARLY_ROWS] = early[0:EARLY_ROWS]
@@ -552,7 +557,7 @@
     size = speed.shape[1]
     for c in range(2):
         flat[pl.ds(c, size, stride=2), :] = speed[c]
-    copy = pltpu.make_async_copy(flat, flat_o, left)
+    copy = pltpu.make_async_copy(flat.at[pl.ds(0, flat_o.shape[0])], flat_o, left)
     copy.start()
     rows = total_o.shape[0]
     total_o[...] = own[0:rows] + beside[0:rows].astype(F32)
@@ -691,13 +696,17 @@
             interleaved(ice_velocity),
             water_heat_state,
         ),
+        scratch=[pltpu.VMEM((2 * size + 8, size), F32)],
     )
     extra_rows = -(-(1 + 5 * levels) // TILE_ROWS) * TILE_ROWS
     message, current_ice, push = call(
         functools.partial(forcing_kernel, group, side, levels, sub_count, member_place),
         [shape(BLOCK_ROWS + extra_rows, size, dtype=BF16), planes, planes],
         (step_mass, drag, wind, early, *chunks[::-1], *hops),
-        scratch=[pltpu.VMEM((BLOCK_ROWS + extra_rows, size), F32)],
+        scratch=[
+            pltpu.VMEM((BLOCK_ROWS + extra_rows, size), F32),
+            pltpu.VMEM((2 * size + 8, size), F32),
+        ],
     )
     messages = swap(message, "tile", tile_count)
 
@@ -759,7 +768,7 @@
         settle_kernel,
         [shape(2 * size, size), shape(step, width)],
         (speed, own, beside),
-        scratch=[pltpu.VMEM((2 * size, size), F32), pltpu.SemaphoreType.DMA],
+        scratch=[pltpu.VMEM((2 * size + 8, size), F32), pltpu.SemaphoreType.DMA],
         out_spaces=(pltpu.HBM, pltpu.VMEM),
     )
     if lev_count > 1:

time: 34.9 us -> 34.9 us (level)
  no operation moved by 1% of the time
where the time goes in v19:
time: 34.9 us; the launch traced here: 34.7 us
  waiting for transfers between devices  12.7 us (36%)
  starting transfers between devices  12.2 us (35%)
  Pallas kernels  8.81 us (25%)
  between operations  0.78 us (2%)
    pallas_call x9, Pallas kernels, call(): pl.pallas_call(kernel, out_shape=outs, in_specs=specs, out_specs=jax.tree...  8.81 us
    ppermute x3, starting transfers between devices, swap(): got[k] = lax.ppermute(value, axes, [(i, i ^ k) for i in range(count)])  4.66 us
    ppermute x3, waiting for transfers between devices, swap(): got[k] = lax.ppermute(value, axes, [(i, i ^ k) for i in range(count)])  4.09 us
    ppermute x3, waiting for transfers between devices, swap_each(): lax.ppermute(values[k], group_axes, [(i, i ^ k) for i in range(group)])  3.22 us
    ppermute x3, starting transfers between devices, swap_each(): lax.ppermute(values[k], group_axes, [(i, i ^ k) for i in range(group)])  3.21 us
    ppermute x1, starting transfers between devices, shards(): lax.ppermute(value, group_axes, [(i, i ^ 2 * k + 2) for i in range(group)])  2.05 us
    ppermute x1, starting transfers between devices, swap_chips(): lax.ppermute(value, group_axes, [(i, i ^ k) for i in range(group)])  2.05 us
    ppermute x1, waiting for transfers between devices, shards(): lax.ppermute(value, group_axes, [(i, i ^ 2 * k + 2) for i in range(group)])  1.43 us
  transfers between devices with their start and end apart: 12, of which 9 were waited for; matrix products, arithmetic and copies ran while one was open for 1% of the time, Pallas kernels for 6%

profile of v19, /device:TPU:0, one launch (start us, length us, event | category | flops | bytes accessed | tf_op | source)
XLA Modules:
  0.0 34.7 jit_solution(16705983135034119638)
XLA Ops:
  0.6 0.0 copy-start.1
  0.6 0.0 copy-start.2
  0.7 0.0 copy-start.3
  0.7 0.0 copy-start.4
  0.7 2.5 %shard_map.131 = (bf16[336,128]{1,0:T(8,128)(2,1)}, bf16[336,128]{1,0:T(8,128)(2,1)}, bf16[336,128]{1,0:T(8,128)(2,1)}, bf16[192,128]{1,0:T(8,128)(2,1)}) custom-call(s32[1,1,4]{2,1,0:T(1,128)} %links_h.1, s32[1,4]{1,0:T(1,128)} %blocks_h.1, bf16[4,64,128]{2,1,0:T(8,128)(2,1)} %bitcast.27, bf16[4,128,128]{2,1,0:T(8,128)(2,1)} %bitcast.25, ...), custom_call_target="tpu_custom_call" | custom-call | flops 11500000256 | bytes 393248 | tf_op jit(solution)/shard_map/pallas_call | solution.py:45
  3.2 3.0 %collective-permute-start.1 = (bf16[336,128]{1,0:T(8,128)(2,1)}, bf16[336,128]{1,0:T(8,128)(2,1)S(1)}, u32[]{:S(2)}, u32[]{:S(2)}) collective-permute-start(bf16[336,128]{1,0:T(8,128)(2,1)} %get-tuple-element.30), channel_id=1, source_target_pairs={{0,2},{1,3},{2,0},{3,1},{4,6},{5,7},{6,4},{7,5},{8,10},{9,11},{10,... | collective-permute-start | bytes 258056 | tf_op jit(solution)/shard_map/ppermute | solution.py:639
  6.2 0.0 collective-permute-start.2
  6.2 0.2 collective-permute-start
  6.4 2.5 %collective-permute-done.1.refs_1_.refs_6_.refs_2_ = bf16[336,128]{1,0:T(8,128)(2,1)S(1)} collective-permute-done((bf16[336,128]{1,0:T(8,128)(2,1)}, bf16[336,128]{1,0:T(8,128)(2,1)S(1)}, u32[]{:S(2)}, u32[]{:S(2)}) %collective-permute-start.1) | collective-permute-done | bytes 86048 | tf_op jit(solution)/shard_map/ppermute | solution.py:639
  8.9 0.0 collective-permute-start.3
  8.9 0.0 copy-done.1
  8.9 0.0 copy-done.2
  8.9 0.0 copy-done.3
  8.9 0.0 copy-done.4
  9.0 0.0 copy-start
  9.0 0.0 copy-start.5
  9.0 0.2 shard_map.130
  9.2 0.7 %collective-permute-done.refs_0_.refs_7_.refs_3_ = bf16[192,128]{1,0:T(8,128)(2,1)S(1)} collective-permute-done((bf16[192,128]{1,0:T(8,128)(2,1)}, bf16[192,128]{1,0:T(8,128)(2,1)S(1)}, u32[]{:S(2)}, u32[]{:S(2)}) %collective-permute-start) | collective-permute-done | bytes 49184 | tf_op jit(solution)/shard_map/ppermute | solution.py:639
  9.9 0.0 collective-permute-done.2.refs_2_.refs_5_.refs_1_
  9.9 0.2 collective-permute-done.3.refs_4_.refs_8_
  10.1 0.0 copy-done
  10.1 0.0 copy-done.5
  10.1 0.0 copy-start.6
  10.1 0.6 %shard_map.132 = (bf16[112,128]{1,0:T(8,128)(2,1)S(1)}, f32[2,128,128]{2,1,0:T(8,128)S(1)}, f32[2,128,128]{2,1,0:T(8,128)S(1)}) custom-call(f32[128,128]{1,0:T(8,128)S(1)} %get-tuple-element.26.mass, f32[128,128]{1,0:T(8,128)S(1)} %get-tuple-element.27.drag, f32[256,128]{1,0:T(8,128)S(1)} %bitcast.24, f32[72,128]{1,0:T(8,128)S(1)} %get-tuple-element.28.early, ...), custom_call_target="tpu_custom_call" | custom-call | flops 11500000 | bytes 643072 | tf_op jit(solution)/shard_map/pallas_call | solution.py:45
  10.7 3.1 %collective-permute-start.6 = (bf16[112,128]{1,0:T(8,128)(2,1)S(1)}, bf16[112,128]{1,0:T(8,128)(2,1)S(1)}, u32[]{:S(2)}, u32[]{:S(2)}) collective-permute-start(bf16[112,128]{1,0:T(8,128)(2,1)S(1)} %get-tuple-element.33.refs_0_), channel_id=1, source_target_pairs={{0,8},{4,12},{8,0},{12,4},{1,9},{5,13},{9,1},{13,5},{2,10},{6,14},... | collective-permute-start | bytes 86024 | tf_op jit(solution)/shard_map/ppermute | solution.py:622
  13.8 1.3 %collective-permute-start.5 = (bf16[112,128]{1,0:T(8,128)(2,1)S(1)}, bf16[112,128]{1,0:T(8,128)(2,1)S(1)}, u32[]{:S(2)}, u32[]{:S(2)}) collective-permute-start(bf16[112,128]{1,0:T(8,128)(2,1)S(1)} %get-tuple-element.33.refs_0_), channel_id=1, source_target_pairs={{0,12},{4,8},{8,4},{12,0},{1,13},{5,9},{9,5},{13,1},{2,14},{6,10},... | collective-permute-start | bytes 86024 | tf_op jit(solution)/shard_map/ppermute | solution.py:622
  15.2 0.2 collective-permute-start.4
  15.4 0.3 collective-permute-done.6.refs_3_
  15.7 3.8 %collective-permute-done.5.refs_2_ = bf16[112,128]{1,0:T(8,128)(2,1)S(1)} collective-permute-done((bf16[112,128]{1,0:T(8,128)(2,1)S(1)}, bf16[112,128]{1,0:T(8,128)(2,1)S(1)}, u32[]{:S(2)}, u32[]{:S(2)}) %collective-permute-start.5) | collective-permute-done | bytes 28704 | tf_op jit(solution)/shard_map/ppermute | solution.py:622
  19.5 0.0 collective-permute-done.4.refs_1_
  19.5 0.0 copy-done.6
  19.5 0.4 %shard_map.133.refs_4_ = bf16[384,128]{1,0:T(8,128)(2,1)S(1)} custom-call(f32[4,64,128]{2,1,0:T(8,128)S(1)} %copy-done.1, f32[64,128]{1,0:T(8,128)S(1)} %copy-done.6, bf16[112,128]{1,0:T(8,128)(2,1)S(1)} %get-tuple-element.33.refs_0_, bf16[112,128]{1,0:T(8,128)(2,1)S(1)} %collective-permute-done.4.refs_1_, ...), custom_call_target="tpu_custom_call" | custom-call | flops 11500000 | bytes 622592 | tf_op jit(solution)/shard_map/pallas_call | solution.py:45
  19.9 2.0 %collective-permute-start.8 = (bf16[384,128]{1,0:T(8,128)(2,1)S(1)}, bf16[384,128]{1,0:T(8,128)(2,1)S(1)}, u32[]{:S(2)}, u32[]{:S(2)}) collective-permute-start(bf16[384,128]{1,0:T(8,128)(2,1)S(1)} %shard_map.133.refs_4_), channel_id=1, source_target_pairs={{0,2},{1,3},{2,0},{3,1},{4,6},{5,7},{6,4},{7,5},{8,10},{9,11},{10,... | collective-permute-start | bytes 294920 | tf_op jit(solution)/shard_map/ppermute | solution.py:627
  22.0 0.0 collective-permute-start.7
  22.0 0.1 reshape.41
  22.1 1.1 %shard_map.134.warm = f32[4,64,128]{2,1,0:T(8,128)S(1)} custom-call(f32[4,64,128]{2,1,0:T(8,128)S(1)} %copy-done.1, f32[64,128]{1,0:T(8,128)S(1)} %copy-done.6, bf16[112,128]{1,0:T(8,128)(2,1)S(1)} %get-tuple-element.33.refs_0_, bf16[112,128]{1,0:T(8,128)(2,1)S(1)} %collective-permute-done.4.refs_1_, bf16[112,128]{1,0:T(8,128)(2,1)S(1)} %collective-permute-done.5.refs_2_, ...), custom_call_target="tpu_custom_call" | custom-call | flops 11500000 | bytes 622592 | tf_op jit(solution)/shard_map/pallas_call | solution.py:45
  23.2 1.4 %collective-permute-done.8.refs_6_ = bf16[384,128]{1,0:T(8,128)(2,1)S(1)} collective-permute-done((bf16[384,128]{1,0:T(8,128)(2,1)S(1)}, bf16[384,128]{1,0:T(8,128)(2,1)S(1)}, u32[]{:S(2)}, u32[]{:S(2)}) %collective-permute-start.8) | collective-permute-done | bytes 98336 | tf_op jit(solution)/shard_map/ppermute | solution.py:627
  24.6 0.0 collective-permute-start.9
  24.6 0.1 xor_select_fusion.table
  24.7 0.0 collective-permute-done.7.refs_5_
  24.7 1.2 %collective-permute-done.9.refs_7_ = bf16[384,128]{1,0:T(8,128)(2,1)S(1)} collective-permute-done((bf16[384,128]{1,0:T(8,128)(2,1)S(1)}, bf16[384,128]{1,0:T(8,128)(2,1)S(1)}, u32[]{:S(2)}, u32[]{:S(2)}) %collective-permute-start.9) | collective-permute-done | bytes 98336 | tf_op jit(solution)/shard_map/ppermute | solution.py:633
  25.9 2.6 %shard_map.135 = (f32[2,128,128]{2,1,0:T(8,128)S(1)}, f32[384,128]{1,0:T(8,128)S(1)}, bf16[384,128]{1,0:T(8,128)(2,1)S(1)}) custom-call(s32[16,4]{1,0:T(8,128)S(1)} %xor_select_fusion.table, f32[128,128]{1,0:T(8,128)S(1)} %get-tuple-element.35.viscous, f32[128,128]{1,0:T(8,128)S(1)} %get-tuple-element.36.gain, f32[128,128]{1,0:T(8,128)S(1)} %get-tuple-element.27.drag, ...), custom_call_target="tpu_custom_call" | custom-call | flops 11500000 | bytes 1356032 | tf_op jit(solution)/shard_map/pallas_call | solution.py:45
  28.5 0.2 collective-permute-start.10
  28.7 1.1 %collective-permute-done.10.beside = bf16[384,128]{1,0:T(8,128)(2,1)S(1)} collective-permute-done((bf16[384,128]{1,0:T(8,128)(2,1)S(1)}, bf16[384,128]{1,0:T(8,128)(2,1)S(1)}, u32[]{:S(2)}, u32[]{:S(2)}) %collective-permute-start.10) | collective-permute-done | bytes 98336 | tf_op jit(solution)/shard_map/ppermute | solution.py:759
  29.9 2.0 %collective-permute-start.11 = (bf16[192,128]{1,0:T(8,128)(2,1)S(1)}, bf16[192,128]{1,0:T(8,128)(2,1)S(1)}, u32[]{:S(2)}, u32[]{:S(2)}) collective-permute-start(bf16[192,128]{1,0:T(8,128)(2,1)S(1)} %shard_map.137), channel_id=1, source_target_pairs={{0,2},{1,3},{2,0},{3,1},{4,6},{5,7},{6,4},{7,5},{8,10},{9,11},{10,... | collective-permute-start | bytes 147464 | tf_op jit(solution)/shard_map/ppermute | solution.py:764
  31.9 0.0 copy-start.7
  31.9 0.7 %shard_map.136 = (f32[256,128]{1,0:T(8,128)}, f32[192,128]{1,0:T(8,128)S(1)}) custom-call(f32[2,128,128]{2,1,0:T(8,128)S(1)} %get-tuple-element.42.speed, f32[384,128]{1,0:T(8,128)S(1)} %get-tuple-element.43.own, bf16[384,128]{1,0:T(8,128)(2,1)S(1)} %collective-permute-done.10.beside), custom_call_target="tpu_custom_call" | custom-call | flops 11500000 | bytes 425984 | tf_op jit(solution)/shard_map/pallas_call | solution.py:45
  32.6 1.4 %collective-permute-done.11.refs_0_ = bf16[192,128]{1,0:T(8,128)(2,1)S(1)} collective-permute-done((bf16[192,128]{1,0:T(8,128)(2,1)S(1)}, bf16[192,128]{1,0:T(8,128)(2,1)S(1)}, u32[]{:S(2)}, u32[]{:S(2)}) %collective-permute-start.11) | collective-permute-done | bytes 49184 | tf_op jit(solution)/shard_map/ppermute | solution.py:764
  34.0 0.0 copy-done.7
  34.0 0.7 %shard_map.138 = (f32[4,64,128]{2,1,0:T(8,128)}, f32[2,64,128]{2,1,0:T(8,128)}) custom-call(f32[4,64,128]{2,1,0:T(8,128)S(1)} %shard_map.134.warm, f32[2,64,128]{2,1,0:T(8,128)S(1)} %copy-done.7, f32[192,128]{1,0:T(8,128)S(1)} %get-tuple-element.45.total, bf16[192,128]{1,0:T(8,128)(2,1)S(1)} %collective-permute-done.11.refs_0_), custom_call_target="tpu_custom_call" | custom-call | flops 11500000 | bytes 344064 | tf_op jit(solution)/shard_map/pallas_call | solution.py:45
  (7 shorter events, 0.0 us)
Async XLA Ops:
  0.6 8.3 %copy-start.1 = (f32[4,64,128]{2,1,0:T(8,128)S(1)}, f32[4,64,128]{2,1,0:T(8,128)}, u32[]{:S(2)}) copy-start(f32[4,64,128]{2,1,0:T(8,128)} %water.5) | copy-start | bytes 393220
  0.6 8.3 %copy-start.2 = (f32[1,1,5,16384]{3,1,2,0:T(1,128)S(1)}, f32[1,1,5,16384]{3,1,2,0:T(1,128)}, u32[]{:S(2)}) copy-start(f32[1,1,5,16384]{3,1,2,0:T(1,128)} %param.18) | copy-start | bytes 983044
  0.7 8.3 %copy-start.3 = (f32[1,1,5,16384]{3,1,2,0:T(1,128)S(1)}, f32[1,1,5,16384]{3,1,2,0:T(1,128)}, u32[]{:S(2)}) copy-start(f32[1,1,5,16384]{3,1,2,0:T(1,128)} %param.19) | copy-start | bytes 983044
  0.7 8.3 %copy-start.4 = (f32[1,1,2,16384]{3,2,1,0:T(2,128)S(1)}, f32[1,1,2,16384]{3,2,1,0:T(2,128)}, u32[]{:S(2)}) copy-start(f32[1,1,2,16384]{3,2,1,0:T(2,128)} %param.20) | copy-start | bytes 393220
  3.2 5.7 %collective-permute-start.1 = (bf16[336,128]{1,0:T(8,128)(2,1)}, bf16[336,128]{1,0:T(8,128)(2,1)S(1)}, u32[]{:S(2)}, u32[]{:S(2)}) collective-permute-start(bf16[336,128]{1,0:T(8,128)(2,1)} %get-tuple-element.30), channel_id=1, source_target_pairs={{0,2},{1,3},{2,0},{3,1},{4,6},{5,7},{6,4},{7,5},{8,10},{9,11},{10,... | collective-permute-start | bytes 258056 | tf_op jit(solution)/shard_map/ppermute | solution.py:639
  6.2 3.7 %collective-permute-start.2 = (bf16[336,128]{1,0:T(8,128)(2,1)}, bf16[336,128]{1,0:T(8,128)(2,1)S(1)}, u32[]{:S(2)}, u32[]{:S(2)}) collective-permute-start(bf16[336,128]{1,0:T(8,128)(2,1)} %get-tuple-element.31), channel_id=1, source_target_pairs={{0,1},{1,0},{2,3},{3,2},{4,5},{5,4},{6,7},{7,6},{8,9},{9,8},{10,11... | collective-permute-start | bytes 258056 | tf_op jit(solution)/shard_map/ppermute | solution.py:639
  6.2 3.7 %collective-permute-start = (bf16[192,128]{1,0:T(8,128)(2,1)}, bf16[192,128]{1,0:T(8,128)(2,1)S(1)}, u32[]{:S(2)}, u32[]{:S(2)}) collective-permute-start(bf16[192,128]{1,0:T(8,128)(2,1)} %get-tuple-element.29), channel_id=1, source_target_pairs={{0,3},{1,2},{2,1},{3,0},{4,7},{5,6},{6,5},{7,4},{8,11},{9,10},{10,... | collective-permute-start | bytes 147464 | tf_op jit(solution)/shard_map/ppermute | solution.py:639
  8.9 1.2 %collective-permute-start.3 = (bf16[144,128]{1,0:T(8,128)(2,1)S(1)}, bf16[144,128]{1,0:T(8,128)(2,1)S(1)}, u32[]{:S(2)}, u32[]{:S(2)}) collective-permute-start(bf16[144,128]{1,0:T(8,128)(2,1)S(1)} %slice.28), channel_id=1, source_target_pairs={{0,1},{1,0},{2,3},{3,2},{4,5},{5,4},{6,7},{7,6},{8,9},{9,8},{10,11... | collective-permute-start | bytes 110600 | tf_op jit(solution)/shard_map/ppermute | solution.py:686
  9.0 1.2 %copy-start = (bf16[336,128]{1,0:T(8,128)(2,1)S(1)}, bf16[336,128]{1,0:T(8,128)(2,1)}, u32[]{:S(2)}) copy-start(bf16[336,128]{1,0:T(8,128)(2,1)} %get-tuple-element.32.refs_3_.refs_4_.refs_0_) | copy-start | bytes 258052
  9.0 1.2 %copy-start.5 = (f32[1,1,2,16384]{3,2,1,0:T(2,128)S(1)}, f32[1,1,2,16384]{3,2,1,0:T(2,128)}, u32[]{:S(2)}) copy-start(f32[1,1,2,16384]{3,2,1,0:T(2,128)} %param.21) | copy-start | bytes 393220
  10.1 9.3 %copy-start.6 = (f32[64,128]{1,0:T(8,128)S(1)}, f32[64,128]{1,0:T(8,128)}, u32[]{:S(2)}) copy-start(f32[64,128]{1,0:T(8,128)} %mixing.2) | copy-start | bytes 98308
  10.7 4.9 %collective-permute-start.6 = (bf16[112,128]{1,0:T(8,128)(2,1)S(1)}, bf16[112,128]{1,0:T(8,128)(2,1)S(1)}, u32[]{:S(2)}, u32[]{:S(2)}) collective-permute-start(bf16[112,128]{1,0:T(8,128)(2,1)S(1)} %get-tuple-element.33.refs_0_), channel_id=1, source_target_pairs={{0,8},{4,12},{8,0},{12,4},{1,9},{5,13},{9,1},{13,5},{2,10},{6,14},... | collective-permute-start | bytes 86024 | tf_op jit(solution)/shard_map/ppermute | solution.py:622
  13.8 5.7 %collective-permute-start.5 = (bf16[112,128]{1,0:T(8,128)(2,1)S(1)}, bf16[112,128]{1,0:T(8,128)(2,1)S(1)}, u32[]{:S(2)}, u32[]{:S(2)}) collective-permute-start(bf16[112,128]{1,0:T(8,128)(2,1)S(1)} %get-tuple-element.33.refs_0_), channel_id=1, source_target_pairs={{0,12},{4,8},{8,4},{12,0},{1,13},{5,9},{9,5},{13,1},{2,14},{6,10},... | collective-permute-start | bytes 86024 | tf_op jit(solution)/shard_map/ppermute | solution.py:622
  15.2 4.3 %collective-permute-start.4 = (bf16[112,128]{1,0:T(8,128)(2,1)S(1)}, bf16[112,128]{1,0:T(8,128)(2,1)S(1)}, u32[]{:S(2)}, u32[]{:S(2)}) collective-permute-start(bf16[112,128]{1,0:T(8,128)(2,1)S(1)} %get-tuple-element.33.refs_0_), channel_id=1, source_target_pairs={{0,4},{4,0},{8,12},{12,8},{1,5},{5,1},{9,13},{13,9},{2,6},{6,2},{1... | collective-permute-start | bytes 86024 | tf_op jit(solution)/shard_map/ppermute | solution.py:622
  19.9 4.7 %collective-permute-start.8 = (bf16[384,128]{1,0:T(8,128)(2,1)S(1)}, bf16[384,128]{1,0:T(8,128)(2,1)S(1)}, u32[]{:S(2)}, u32[]{:S(2)}) collective-permute-start(bf16[384,128]{1,0:T(8,128)(2,1)S(1)} %shard_map.133.refs_4_), channel_id=1, source_target_pairs={{0,2},{1,3},{2,0},{3,1},{4,6},{5,7},{6,4},{7,5},{8,10},{9,11},{10,... | collective-permute-start | bytes 294920 | tf_op jit(solution)/shard_map/ppermute | solution.py:627
  22.0 2.7 %collective-permute-start.7 = (bf16[384,128]{1,0:T(8,128)(2,1)S(1)}, bf16[384,128]{1,0:T(8,128)(2,1)S(1)}, u32[]{:S(2)}, u32[]{:S(2)}) collective-permute-start(bf16[384,128]{1,0:T(8,128)(2,1)S(1)} %shard_map.133.refs_4_), channel_id=1, source_target_pairs={{0,1},{1,0},{2,3},{3,2},{4,5},{5,4},{6,7},{7,6},{8,9},{9,8},{10,11... | collective-permute-start | bytes 294920 | tf_op jit(solution)/shard_map/ppermute | solution.py:633
  24.6 1.3 %collective-permute-start.9 = (bf16[384,128]{1,0:T(8,128)(2,1)S(1)}, bf16[384,128]{1,0:T(8,128)(2,1)S(1)}, u32[]{:S(2)}, u32[]{:S(2)}) collective-permute-start(bf16[384,128]{1,0:T(8,128)(2,1)S(1)} %collective-permute-done.8.refs_6_), channel_id=1, source_target_pairs={{0,1},{1,0},{2,3},{3,2},{4,5},{5,4},{6,7},{7,6},{8,9},{9,8},{10,11... | collective-permute-start | bytes 294920 | tf_op jit(solution)/shard_map/ppermute | solution.py:633
  28.5 1.4 %collective-permute-start.10 = (bf16[384,128]{1,0:T(8,128)(2,1)S(1)}, bf16[384,128]{1,0:T(8,128)(2,1)S(1)}, u32[]{:S(2)}, u32[]{:S(2)}) collective-permute-start(bf16[384,128]{1,0:T(8,128)(2,1)S(1)} %get-tuple-element.44), channel_id=1, source_target_pairs={{0,1},{1,0},{2,3},{3,2},{4,5},{5,4},{6,7},{7,6},{8,9},{9,8},{10,11... | collective-permute-start | bytes 294920 | tf_op jit(solution)/shard_map/ppermute | solution.py:759
  29.9 4.2 %collective-permute-start.11 = (bf16[192,128]{1,0:T(8,128)(2,1)S(1)}, bf16[192,128]{1,0:T(8,128)(2,1)S(1)}, u32[]{:S(2)}, u32[]{:S(2)}) collective-permute-start(bf16[192,128]{1,0:T(8,128)(2,1)S(1)} %shard_map.137), channel_id=1, source_target_pairs={{0,2},{1,3},{2,0},{3,1},{4,6},{5,7},{6,4},{7,5},{8,10},{9,11},{10,... | collective-permute-start | bytes 147464 | tf_op jit(solution)/shard_map/ppermute | solution.py:764
  31.9 2.1 %copy-start.7 = (f32[2,64,128]{2,1,0:T(8,128)S(1)}, f32[2,64,128]{2,1,0:T(8,128)}, u32[]{:S(2)}) copy-start(f32[2,64,128]{2,1,0:T(8,128)} %currents.1) | copy-start | bytes 196612

commit v20 on v19

--- a/solution.py
+++ b/solution.py
@@ -107,13 +107,30 @@
             )
         )
     ]
-    for load in loads:
-        load.start()
+    for i in (5, 2, 0, 1, 4, 3):
+        loads[i].start()
+    for i in (0, 2, 5):
+        loads[i].wait()
+    for c in range(2):
+        fields[c * side : (c + 1) * side] = currents[c].astype(BF16)
+    lane = iota((1, width), 1)
+    numbers = jnp.zeros((1, width), F32)
+    for q in range(4):
+        numbers = jnp.where(lane == q, (links[0, 0, q] >> 7).astype(F32), numbers)
+        numbers = jnp.where(lane == 4 + q, (links[0, 0, q] & 127).astype(F32), numbers)
+    ends = ocean_columns(water) + [numbers]
+    blank = jnp.zeros((fields.shape[0] - 2 * side - len(ends), width), F32)
+    fields[2 * side :] = jnp.concatenate(ends + [blank], axis=0).astype(BF16)
+    copies = []
+    for k, out in enumerate(outs):
+        if out.shape[0] > both:
+            target = out.at[pl.ds(both, fields.shape[0])]
+            copies.append(pltpu.make_async_copy(fields, target, left.at[2 * k + 1]))
+            copies[-1].start()
     for i in (1, 3, 4):
         loads[i].wait()
     me = place()
     owners = [lax.rem(lax.rem(blocks[0, m], devices), members) for m in range(pairs)]
-    copies = []
     for k, out in enumerate(outs):
         partner = me ^ k
         pair = jnp.int32(0)
@@ -126,23 +143,6 @@
             source = kept.at[k]
         copies.append(pltpu.make_async_copy(source, out.at[pl.ds(0, both)], left.at[2 * k]))
         copies[-1].start()
-    for i in (0, 2, 5):
-        loads[i].wait()
-    for c in range(2):
-        fields[c * side : (c + 1) * side] = currents[c].astype(BF16)
-    lane = iota((1, width), 1)
-    numbers = jnp.zeros((1, width), F32)
-    for q in range(4):
-        numbers = jnp.where(lane == q, (links[0, 0, q] >> 7).astype(F32), numbers)
-        numbers = jnp.where(lane == 4 + q, (links[0, 0, q] & 127).astype(F32), numbers)
-    ends = ocean_columns(water) + [numbers]
-    blank = jnp.zeros((fields.shape[0] - 2 * side - len(ends), width), F32)
-    fields[2 * side :] = jnp.concatenate(ends + [blank], axis=0).astype(BF16)
-    for k, out in enumerate(outs):
-        if out.shape[0] > both:
-            target = out.at[pl.ds(both, fields.shape[0])]
-            copies.append(pltpu.make_async_copy(fields, target, left.at[2 * k + 1]))
-            copies[-1].start()
     for copy in copies:
         copy.wait()
 

time: 34.9 us -> 34.9 us (level)
  no operation moved by 1% of the time
where the time goes in v20:
time: 34.9 us; the launch traced here: 34.7 us
  waiting for transfers between devices  12.7 us (36%)
  starting transfers between devices  12.2 us (35%)
  Pallas kernels  8.8 us (25%)
  between operations  0.78 us (2%)
    pallas_call x9, Pallas kernels, call(): pl.pallas_call(kernel, out_shape=outs, in_specs=specs, out_specs=jax.tree...  8.8 us
    ppermute x3, starting transfers between devices, swap(): got[k] = lax.ppermute(value, axes, [(i, i ^ k) for i in range(count)])  4.67 us
    ppermute x3, waiting for transfers between devices, swap(): got[k] = lax.ppermute(value, axes, [(i, i ^ k) for i in range(count)])  4.09 us
    ppermute x3, waiting for transfers between devices, swap_each(): lax.ppermute(values[k], group_axes, [(i, i ^ k) for i in range(group)])  3.22 us
    ppermute x3, starting transfers between devices, swap_each(): lax.ppermute(values[k], group_axes, [(i, i ^ k) for i in range(group)])  3.21 us
    ppermute x1, starting transfers between devices, shards(): lax.ppermute(value, group_axes, [(i, i ^ 2 * k + 2) for i in range(group)])  2.05 us
    ppermute x1, starting transfers between devices, swap_chips(): lax.ppermute(value, group_axes, [(i, i ^ k) for i in range(group)])  2.05 us
    ppermute x1, waiting for transfers between devices, shards(): lax.ppermute(value, group_axes, [(i, i ^ 2 * k + 2) for i in range(group)])  1.43 us
  transfers between devices with their start and end apart: 12, of which 9 were waited for; matrix products, arithmetic and copies ran while one was open for 1% of the time, Pallas kernels for 6%

profile of v20, /device:TPU:0, one launch (start us, length us, event | category | flops | bytes accessed | tf_op | source)
XLA Modules:
  0.0 34.7 jit_solution(15842977881585570270)
XLA Ops:
  0.6 0.0 copy-start.1
  0.6 0.0 copy-start.2
  0.7 0.0 copy-start.3
  0.7 0.0 copy-start.4
  0.7 2.5 %shard_map.131 = (bf16[336,128]{1,0:T(8,128)(2,1)}, bf16[336,128]{1,0:T(8,128)(2,1)}, bf16[336,128]{1,0:T(8,128)(2,1)}, bf16[192,128]{1,0:T(8,128)(2,1)}) custom-call(s32[1,1,4]{2,1,0:T(1,128)} %links_h.1, s32[1,4]{1,0:T(1,128)} %blocks_h.1, bf16[4,64,128]{2,1,0:T(8,128)(2,1)} %bitcast.27, bf16[4,128,128]{2,1,0:T(8,128)(2,1)} %bitcast.25, ...), custom_call_target="tpu_custom_call" | custom-call | flops 11500000256 | bytes 393248 | tf_op jit(solution)/shard_map/pallas_call | solution.py:45
  3.2 3.0 %collective-permute-start.1 = (bf16[336,128]{1,0:T(8,128)(2,1)}, bf16[336,128]{1,0:T(8,128)(2,1)S(1)}, u32[]{:S(2)}, u32[]{:S(2)}) collective-permute-start(bf16[336,128]{1,0:T(8,128)(2,1)} %get-tuple-element.30), channel_id=1, source_target_pairs={{0,2},{1,3},{2,0},{3,1},{4,6},{5,7},{6,4},{7,5},{8,10},{9,11},{10,... | collective-permute-start | bytes 258056 | tf_op jit(solution)/shard_map/ppermute | solution.py:639
  6.2 0.0 collective-permute-start.2
  6.2 0.2 collective-permute-start
  6.4 2.5 %collective-permute-done.1.refs_1_.refs_6_.refs_2_ = bf16[336,128]{1,0:T(8,128)(2,1)S(1)} collective-permute-done((bf16[336,128]{1,0:T(8,128)(2,1)}, bf16[336,128]{1,0:T(8,128)(2,1)S(1)}, u32[]{:S(2)}, u32[]{:S(2)}) %collective-permute-start.1) | collective-permute-done | bytes 86048 | tf_op jit(solution)/shard_map/ppermute | solution.py:639
  8.9 0.0 collective-permute-start.3
  8.9 0.0 copy-done.1
  8.9 0.0 copy-done.2
  8.9 0.0 copy-done.3
  8.9 0.0 copy-done.4
  8.9 0.0 copy-start
  9.0 0.0 copy-start.5
  9.0 0.2 shard_map.130
  9.2 0.7 %collective-permute-done.refs_0_.refs_7_.refs_3_ = bf16[192,128]{1,0:T(8,128)(2,1)S(1)} collective-permute-done((bf16[192,128]{1,0:T(8,128)(2,1)}, bf16[192,128]{1,0:T(8,128)(2,1)S(1)}, u32[]{:S(2)}, u32[]{:S(2)}) %collective-permute-start) | collective-permute-done | bytes 49184 | tf_op jit(solution)/shard_map/ppermute | solution.py:639
  9.9 0.0 collective-permute-done.2.refs_2_.refs_5_.refs_1_
  9.9 0.2 collective-permute-done.3.refs_4_.refs_8_
  10.1 0.0 copy-done
  10.1 0.0 copy-done.5
  10.1 0.0 copy-start.6
  10.1 0.6 %shard_map.132 = (bf16[112,128]{1,0:T(8,128)(2,1)S(1)}, f32[2,128,128]{2,1,0:T(8,128)S(1)}, f32[2,128,128]{2,1,0:T(8,128)S(1)}) custom-call(f32[128,128]{1,0:T(8,128)S(1)} %get-tuple-element.26.mass, f32[128,128]{1,0:T(8,128)S(1)} %get-tuple-element.27.drag, f32[256,128]{1,0:T(8,128)S(1)} %bitcast.24, f32[72,128]{1,0:T(8,128)S(1)} %get-tuple-element.28.early, ...), custom_call_target="tpu_custom_call" | custom-call | flops 11500000 | bytes 643072 | tf_op jit(solution)/shard_map/pallas_call | solution.py:45
  10.7 3.1 %collective-permute-start.6 = (bf16[112,128]{1,0:T(8,128)(2,1)S(1)}, bf16[112,128]{1,0:T(8,128)(2,1)S(1)}, u32[]{:S(2)}, u32[]{:S(2)}) collective-permute-start(bf16[112,128]{1,0:T(8,128)(2,1)S(1)} %get-tuple-element.33.refs_0_), channel_id=1, source_target_pairs={{0,8},{4,12},{8,0},{12,4},{1,9},{5,13},{9,1},{13,5},{2,10},{6,14},... | collective-permute-start | bytes 86024 | tf_op jit(solution)/shard_map/ppermute | solution.py:622
  13.8 1.3 %collective-permute-start.5 = (bf16[112,128]{1,0:T(8,128)(2,1)S(1)}, bf16[112,128]{1,0:T(8,128)(2,1)S(1)}, u32[]{:S(2)}, u32[]{:S(2)}) collective-permute-start(bf16[112,128]{1,0:T(8,128)(2,1)S(1)} %get-tuple-element.33.refs_0_), channel_id=1, source_target_pairs={{0,12},{4,8},{8,4},{12,0},{1,13},{5,9},{9,5},{13,1},{2,14},{6,10},... | collective-permute-start | bytes 86024 | tf_op jit(solution)/shard_map/ppermute | solution.py:622
  15.1 0.2 collective-permute-start.4
  15.4 0.3 collective-permute-done.6.refs_3_
  15.6 3.8 %collective-permute-done.5.refs_2_ = bf16[112,128]{1,0:T(8,128)(2,1)S(1)} collective-permute-done((bf16[112,128]{1,0:T(8,128)(2,1)S(1)}, bf16[112,128]{1,0:T(8,128)(2,1)S(1)}, u32[]{:S(2)}, u32[]{:S(2)}) %collective-permute-start.5) | collective-permute-done | bytes 28704 | tf_op jit(solution)/shard_map/ppermute | solution.py:622
  19.5 0.0 collective-permute-done.4.refs_1_
  19.5 0.0 copy-done.6
  19.5 0.4 %shard_map.133.refs_4_ = bf16[384,128]{1,0:T(8,128)(2,1)S(1)} custom-call(f32[4,64,128]{2,1,0:T(8,128)S(1)} %copy-done.1, f32[64,128]{1,0:T(8,128)S(1)} %copy-done.6, bf16[112,128]{1,0:T(8,128)(2,1)S(1)} %get-tuple-element.33.refs_0_, bf16[112,128]{1,0:T(8,128)(2,1)S(1)} %collective-permute-done.4.refs_1_, ...), custom_call_target="tpu_custom_call" | custom-call | flops 11500000 | bytes 622592 | tf_op jit(solution)/shard_map/pallas_call | solution.py:45
  19.9 2.0 %collective-permute-start.8 = (bf16[384,128]{1,0:T(8,128)(2,1)S(1)}, bf16[384,128]{1,0:T(8,128)(2,1)S(1)}, u32[]{:S(2)}, u32[]{:S(2)}) collective-permute-start(bf16[384,128]{1,0:T(8,128)(2,1)S(1)} %shard_map.133.refs_4_), channel_id=1, source_target_pairs={{0,2},{1,3},{2,0},{3,1},{4,6},{5,7},{6,4},{7,5},{8,10},{9,11},{10,... | collective-permute-start | bytes 294920 | tf_op jit(solution)/shard_map/ppermute | solution.py:627
  22.0 0.0 collective-permute-start.7
  22.0 0.1 reshape.41
  22.1 1.1 %shard_map.134.warm = f32[4,64,128]{2,1,0:T(8,128)S(1)} custom-call(f32[4,64,128]{2,1,0:T(8,128)S(1)} %copy-done.1, f32[64,128]{1,0:T(8,128)S(1)} %copy-done.6, bf16[112,128]{1,0:T(8,128)(2,1)S(1)} %get-tuple-element.33.refs_0_, bf16[112,128]{1,0:T(8,128)(2,1)S(1)} %collective-permute-done.4.refs_1_, bf16[112,128]{1,0:T(8,128)(2,1)S(1)} %collective-permute-done.5.refs_2_, ...), custom_call_target="tpu_custom_call" | custom-call | flops 11500000 | bytes 622592 | tf_op jit(solution)/shard_map/pallas_call | solution.py:45
  23.2 1.4 %collective-permute-done.8.refs_6_ = bf16[384,128]{1,0:T(8,128)(2,1)S(1)} collective-permute-done((bf16[384,128]{1,0:T(8,128)(2,1)S(1)}, bf16[384,128]{1,0:T(8,128)(2,1)S(1)}, u32[]{:S(2)}, u32[]{:S(2)}) %collective-permute-start.8) | collective-permute-done | bytes 98336 | tf_op jit(solution)/shard_map/ppermute | solution.py:627
  24.6 0.0 collective-permute-start.9
  24.6 0.1 xor_select_fusion.table
  24.7 0.0 collective-permute-done.7.refs_5_
  24.7 1.2 %collective-permute-done.9.refs_7_ = bf16[384,128]{1,0:T(8,128)(2,1)S(1)} collective-permute-done((bf16[384,128]{1,0:T(8,128)(2,1)S(1)}, bf16[384,128]{1,0:T(8,128)(2,1)S(1)}, u32[]{:S(2)}, u32[]{:S(2)}) %collective-permute-start.9) | collective-permute-done | bytes 98336 | tf_op jit(solution)/shard_map/ppermute | solution.py:633
  25.9 2.6 %shard_map.135 = (f32[2,128,128]{2,1,0:T(8,128)S(1)}, f32[384,128]{1,0:T(8,128)S(1)}, bf16[384,128]{1,0:T(8,128)(2,1)S(1)}) custom-call(s32[16,4]{1,0:T(8,128)S(1)} %xor_select_fusion.table, f32[128,128]{1,0:T(8,128)S(1)} %get-tuple-element.35.viscous, f32[128,128]{1,0:T(8,128)S(1)} %get-tuple-element.36.gain, f32[128,128]{1,0:T(8,128)S(1)} %get-tuple-element.27.drag, ...), custom_call_target="tpu_custom_call" | custom-call | flops 11500000 | bytes 1356032 | tf_op jit(solution)/shard_map/pallas_call | solution.py:45
  28.5 0.2 collective-permute-start.10
  28.7 1.1 %collective-permute-done.10.beside = bf16[384,128]{1,0:T(8,128)(2,1)S(1)} collective-permute-done((bf16[384,128]{1,0:T(8,128)(2,1)S(1)}, bf16[384,128]{1,0:T(8,128)(2,1)S(1)}, u32[]{:S(2)}, u32[]{:S(2)}) %collective-permute-start.10) | collective-permute-done | bytes 98336 | tf_op jit(solution)/shard_map/ppermute | solution.py:759
  29.9 2.0 %collective-permute-start.11 = (bf16[192,128]{1,0:T(8,128)(2,1)S(1)}, bf16[192,128]{1,0:T(8,128)(2,1)S(1)}, u32[]{:S(2)}, u32[]{:S(2)}) collective-permute-start(bf16[192,128]{1,0:T(8,128)(2,1)S(1)} %shard_map.137), channel_id=1, source_target_pairs={{0,2},{1,3},{2,0},{3,1},{4,6},{5,7},{6,4},{7,5},{8,10},{9,11},{10,... | collective-permute-start | bytes 147464 | tf_op jit(solution)/shard_map/ppermute | solution.py:764
  31.9 0.0 copy-start.7
  31.9 0.7 %shard_map.136 = (f32[256,128]{1,0:T(8,128)}, f32[192,128]{1,0:T(8,128)S(1)}) custom-call(f32[2,128,128]{2,1,0:T(8,128)S(1)} %get-tuple-element.42.speed, f32[384,128]{1,0:T(8,128)S(1)} %get-tuple-element.43.own, bf16[384,128]{1,0:T(8,128)(2,1)S(1)} %collective-permute-done.10.beside), custom_call_target="tpu_custom_call" | custom-call | flops 11500000 | bytes 425984 | tf_op jit(solution)/shard_map/pallas_call | solution.py:45
  32.6 1.4 %collective-permute-done.11.refs_0_ = bf16[192,128]{1,0:T(8,128)(2,1)S(1)} collective-permute-done((bf16[192,128]{1,0:T(8,128)(2,1)S(1)}, bf16[192,128]{1,0:T(8,128)(2,1)S(1)}, u32[]{:S(2)}, u32[]{:S(2)}) %collective-permute-start.11) | collective-permute-done | bytes 49184 | tf_op jit(solution)/shard_map/ppermute | solution.py:764
  34.0 0.0 copy-done.7
  34.0 0.7 %shard_map.138 = (f32[4,64,128]{2,1,0:T(8,128)}, f32[2,64,128]{2,1,0:T(8,128)}) custom-call(f32[4,64,128]{2,1,0:T(8,128)S(1)} %shard_map.134.warm, f32[2,64,128]{2,1,0:T(8,128)S(1)} %copy-done.7, f32[192,128]{1,0:T(8,128)S(1)} %get-tuple-element.45.total, bf16[192,128]{1,0:T(8,128)(2,1)S(1)} %collective-permute-done.11.refs_0_), custom_call_target="tpu_custom_call" | custom-call | flops 11500000 | bytes 344064 | tf_op jit(solution)/shard_map/pallas_call | solution.py:45
  (7 shorter events, 0.0 us)
Async XLA Ops:
  0.6 8.3 %copy-start.1 = (f32[4,64,128]{2,1,0:T(8,128)S(1)}, f32[4,64,128]{2,1,0:T(8,128)}, u32[]{:S(2)}) copy-start(f32[4,64,128]{2,1,0:T(8,128)} %water.5) | copy-start | bytes 393220
  0.6 8.3 %copy-start.2 = (f32[1,1,5,16384]{3,1,2,0:T(1,128)S(1)}, f32[1,1,5,16384]{3,1,2,0:T(1,128)}, u32[]{:S(2)}) copy-start(f32[1,1,5,16384]{3,1,2,0:T(1,128)} %param.18) | copy-start | bytes 983044
  0.7 8.3 %copy-start.3 = (f32[1,1,5,16384]{3,1,2,0:T(1,128)S(1)}, f32[1,1,5,16384]{3,1,2,0:T(1,128)}, u32[]{:S(2)}) copy-start(f32[1,1,5,16384]{3,1,2,0:T(1,128)} %param.19) | copy-start | bytes 983044
  0.7 8.3 %copy-start.4 = (f32[1,1,2,16384]{3,2,1,0:T(2,128)S(1)}, f32[1,1,2,16384]{3,2,1,0:T(2,128)}, u32[]{:S(2)}) copy-start(f32[1,1,2,16384]{3,2,1,0:T(2,128)} %param.20) | copy-start | bytes 393220
  3.2 5.7 %collective-permute-start.1 = (bf16[336,128]{1,0:T(8,128)(2,1)}, bf16[336,128]{1,0:T(8,128)(2,1)S(1)}, u32[]{:S(2)}, u32[]{:S(2)}) collective-permute-start(bf16[336,128]{1,0:T(8,128)(2,1)} %get-tuple-element.30), channel_id=1, source_target_pairs={{0,2},{1,3},{2,0},{3,1},{4,6},{5,7},{6,4},{7,5},{8,10},{9,11},{10,... | collective-permute-start | bytes 258056 | tf_op jit(solution)/shard_map/ppermute | solution.py:639
  6.2 3.7 %collective-permute-start.2 = (bf16[336,128]{1,0:T(8,128)(2,1)}, bf16[336,128]{1,0:T(8,128)(2,1)S(1)}, u32[]{:S(2)}, u32[]{:S(2)}) collective-permute-start(bf16[336,128]{1,0:T(8,128)(2,1)} %get-tuple-element.31), channel_id=1, source_target_pairs={{0,1},{1,0},{2,3},{3,2},{4,5},{5,4},{6,7},{7,6},{8,9},{9,8},{10,11... | collective-permute-start | bytes 258056 | tf_op jit(solution)/shard_map/ppermute | solution.py:639
  6.2 3.7 %collective-permute-start = (bf16[192,128]{1,0:T(8,128)(2,1)}, bf16[192,128]{1,0:T(8,128)(2,1)S(1)}, u32[]{:S(2)}, u32[]{:S(2)}) collective-permute-start(bf16[192,128]{1,0:T(8,128)(2,1)} %get-tuple-element.29), channel_id=1, source_target_pairs={{0,3},{1,2},{2,1},{3,0},{4,7},{5,6},{6,5},{7,4},{8,11},{9,10},{10,... | collective-permute-start | bytes 147464 | tf_op jit(solution)/shard_map/ppermute | solution.py:639
  8.9 1.2 %collective-permute-start.3 = (bf16[144,128]{1,0:T(8,128)(2,1)S(1)}, bf16[144,128]{1,0:T(8,128)(2,1)S(1)}, u32[]{:S(2)}, u32[]{:S(2)}) collective-permute-start(bf16[144,128]{1,0:T(8,128)(2,1)S(1)} %slice.28), channel_id=1, source_target_pairs={{0,1},{1,0},{2,3},{3,2},{4,5},{5,4},{6,7},{7,6},{8,9},{9,8},{10,11... | collective-permute-start | bytes 110600 | tf_op jit(solution)/shard_map/ppermute | solution.py:686
  8.9 1.2 %copy-start = (bf16[336,128]{1,0:T(8,128)(2,1)S(1)}, bf16[336,128]{1,0:T(8,128)(2,1)}, u32[]{:S(2)}) copy-start(bf16[336,128]{1,0:T(8,128)(2,1)} %get-tuple-element.32.refs_3_.refs_4_.refs_0_) | copy-start | bytes 258052
  9.0 1.2 %copy-start.5 = (f32[1,1,2,16384]{3,2,1,0:T(2,128)S(1)}, f32[1,1,2,16384]{3,2,1,0:T(2,128)}, u32[]{:S(2)}) copy-start(f32[1,1,2,16384]{3,2,1,0:T(2,128)} %param.21) | copy-start | bytes 393220
  10.1 9.3 %copy-start.6 = (f32[64,128]{1,0:T(8,128)S(1)}, f32[64,128]{1,0:T(8,128)}, u32[]{:S(2)}) copy-start(f32[64,128]{1,0:T(8,128)} %mixing.2) | copy-start | bytes 98308
  10.7 4.9 %collective-permute-start.6 = (bf16[112,128]{1,0:T(8,128)(2,1)S(1)}, bf16[112,128]{1,0:T(8,128)(2,1)S(1)}, u32[]{:S(2)}, u32[]{:S(2)}) collective-permute-start(bf16[112,128]{1,0:T(8,128)(2,1)S(1)} %get-tuple-element.33.refs_0_), channel_id=1, source_target_pairs={{0,8},{4,12},{8,0},{12,4},{1,9},{5,13},{9,1},{13,5},{2,10},{6,14},... | collective-permute-start | bytes 86024 | tf_op jit(solution)/shard_map/ppermute | solution.py:622
  13.8 5.7 %collective-permute-start.5 = (bf16[112,128]{1,0:T(8,128)(2,1)S(1)}, bf16[112,128]{1,0:T(8,128)(2,1)S(1)}, u32[]{:S(2)}, u32[]{:S(2)}) collective-permute-start(bf16[112,128]{1,0:T(8,128)(2,1)S(1)} %get-tuple-element.33.refs_0_), channel_id=1, source_target_pairs={{0,12},{4,8},{8,4},{12,0},{1,13},{5,9},{9,5},{13,1},{2,14},{6,10},... | collective-permute-start | bytes 86024 | tf_op jit(solution)/shard_map/ppermute | solution.py:622
  15.1 4.3 %collective-permute-start.4 = (bf16[112,128]{1,0:T(8,128)(2,1)S(1)}, bf16[112,128]{1,0:T(8,128)(2,1)S(1)}, u32[]{:S(2)}, u32[]{:S(2)}) collective-permute-start(bf16[112,128]{1,0:T(8,128)(2,1)S(1)} %get-tuple-element.33.refs_0_), channel_id=1, source_target_pairs={{0,4},{4,0},{8,12},{12,8},{1,5},{5,1},{9,13},{13,9},{2,6},{6,2},{1... | collective-permute-start | bytes 86024 | tf_op jit(solution)/shard_map/ppermute | solution.py:622
  19.9 4.7 %collective-permute-start.8 = (bf16[384,128]{1,0:T(8,128)(2,1)S(1)}, bf16[384,128]{1,0:T(8,128)(2,1)S(1)}, u32[]{:S(2)}, u32[]{:S(2)}) collective-permute-start(bf16[384,128]{1,0:T(8,128)(2,1)S(1)} %shard_map.133.refs_4_), channel_id=1, source_target_pairs={{0,2},{1,3},{2,0},{3,1},{4,6},{5,7},{6,4},{7,5},{8,10},{9,11},{10,... | collective-permute-start | bytes 294920 | tf_op jit(solution)/shard_map/ppermute | solution.py:627
  22.0 2.7 %collective-permute-start.7 = (bf16[384,128]{1,0:T(8,128)(2,1)S(1)}, bf16[384,128]{1,0:T(8,128)(2,1)S(1)}, u32[]{:S(2)}, u32[]{:S(2)}) collective-permute-start(bf16[384,128]{1,0:T(8,128)(2,1)S(1)} %shard_map.133.refs_4_), channel_id=1, source_target_pairs={{0,1},{1,0},{2,3},{3,2},{4,5},{5,4},{6,7},{7,6},{8,9},{9,8},{10,11... | collective-permute-start | bytes 294920 | tf_op jit(solution)/shard_map/ppermute | solution.py:633
  24.6 1.3 %collective-permute-start.9 = (bf16[384,128]{1,0:T(8,128)(2,1)S(1)}, bf16[384,128]{1,0:T(8,128)(2,1)S(1)}, u32[]{:S(2)}, u32[]{:S(2)}) collective-permute-start(bf16[384,128]{1,0:T(8,128)(2,1)S(1)} %collective-permute-done.8.refs_6_), channel_id=1, source_target_pairs={{0,1},{1,0},{2,3},{3,2},{4,5},{5,4},{6,7},{7,6},{8,9},{9,8},{10,11... | collective-permute-start | bytes 294920 | tf_op jit(solution)/shard_map/ppermute | solution.py:633
  28.5 1.4 %collective-permute-start.10 = (bf16[384,128]{1,0:T(8,128)(2,1)S(1)}, bf16[384,128]{1,0:T(8,128)(2,1)S(1)}, u32[]{:S(2)}, u32[]{:S(2)}) collective-permute-start(bf16[384,128]{1,0:T(8,128)(2,1)S(1)} %get-tuple-element.44), channel_id=1, source_target_pairs={{0,1},{1,0},{2,3},{3,2},{4,5},{5,4},{6,7},{7,6},{8,9},{9,8},{10,11... | collective-permute-start | bytes 294920 | tf_op jit(solution)/shard_map/ppermute | solution.py:759
  29.9 4.2 %collective-permute-start.11 = (bf16[192,128]{1,0:T(8,128)(2,1)S(1)}, bf16[192,128]{1,0:T(8,128)(2,1)S(1)}, u32[]{:S(2)}, u32[]{:S(2)}) collective-permute-start(bf16[192,128]{1,0:T(8,128)(2,1)S(1)} %shard_map.137), channel_id=1, source_target_pairs={{0,2},{1,3},{2,0},{3,1},{4,6},{5,7},{6,4},{7,5},{8,10},{9,11},{10,... | collective-permute-start | bytes 147464 | tf_op jit(solution)/shard_map/ppermute | solution.py:764
  31.9 2.1 %copy-start.7 = (f32[2,64,128]{2,1,0:T(8,128)S(1)}, f32[2,64,128]{2,1,0:T(8,128)}, u32[]{:S(2)}) copy-start(f32[2,64,128]{2,1,0:T(8,128)} %currents.1) | copy-start | bytes 196612
